TPU v7x, 32 devices: a whole 2x2x4 slice. The times are simulated.
32 devices in a mesh: row: 8 (over z, core), col: 4 (over y, x).
Axes of the slice: x: 2, y: 2, z: 4, core: 2. Of those that a mesh axis runs over, the one named last changes fastest.
Arguments:
- specimen: float32 [2, 1024, 512], P(None, 'row', 'col'), may hold values from -4 to 4
- probe_mode_stack: float32 [4, 2, 256, 256], replicated, may hold values from -4 to 4
- measured: float32 [8, 4, 1, 256, 256], P('row', 'col'), may hold values from 0.3 to 3
- centers: int32 [8, 4, 2, 2], P('row', 'col'), may hold values from 1 to 127
- frame_counts: int32 [8, 4], P('row', 'col'), may hold values from 0 to 2, as said below
- helper_cols: int32 [8, 4, 2], P('row', 'col'), may hold values from 0 to 3, as said below
Outputs:
- gradient: float32 [2, 1024, 512], P(None, 'row', 'col')
Inputs may be any that keep to these rules, and one draw needn't show every extreme that they name: `frame_counts`: in every row of tiles the counts sum to 1 times the number of tiles in the row, and some tile of every row holds 2 frames. `helper_cols`: among a tile's live slots the helper columns are distinct; in every row of tiles each column is named by exactly one live slot; slots past a tile's count hold arbitrary columns.
All inputs are finite; a program needn't handle non-finite values.
Results may differ from a plain program's by a relative error of at most 0.007.
Values may be sent and summed in bfloat16 or wider, within the bound.
No kernel may reach another device: no remote copies, remote signals or barrier semaphores. Data moves between devices by JAX's collectives and lax.ppermute only.
A program may use at most 64 MiB of HBM per device.

v0:
```python
import functools
import math

import jax
import jax.numpy as jnp
import numpy as np
from jax import lax
from jax.experimental import pallas as pl
from jax.experimental.pallas import tpu as pltpu
from jax.sharding import PartitionSpec as P

F32 = jnp.float32
BF16 = jnp.bfloat16
INFO = 16
VMEM = pl.BlockSpec(memory_space=pltpu.VMEM)
ANY = pl.BlockSpec(memory_space=pl.ANY)


def dft_tables(extent):
    half = extent // 2
    steps = np.arange(extent, dtype=np.int32)
    angles = (steps[:, None] * steps[None, :] % extent).astype(np.float32)
    angles = angles * np.float32(2.0 * math.pi / extent)
    scaling = np.float32(1.0 / math.sqrt(extent))
    real = (np.cos(angles) * scaling).astype(BF16)
    imag = (-np.sin(angles) * scaling).astype(BF16)
    tables = []
    for parity in (0, 1):
        re, im = real[:half, parity::2], imag[:half, parity::2]
        right = np.concatenate(
            [np.concatenate([re, im], 1), np.concatenate([-im, re], 1)], 0
        )
        tables += [right, np.ascontiguousarray(right.T)]
    return jnp.asarray(np.stack(tables))


def dot(a, b):
    return jnp.dot(a, b, preferred_element_type=F32)


def quarters(tl, tr, bl, br):
    return jnp.concatenate(
        [jnp.concatenate([tl, tr], 1), jnp.concatenate([bl, br], 1)], 0
    )


def iota(shape, dim):
    return lax.broadcasted_iota(jnp.int32, shape, dim)


def fetch(pairs, sems):
    copies = [
        pltpu.make_async_copy(source, target, sems.at[i])
        for i, (source, target) in enumerate(pairs)
    ]
    for copy in copies:
        copy.start()
    return copies


def pack_kernel(specimen, centers, counts, helpers, out, tile_v, cen, cnt, hlp, sems):
    copies = fetch(
        ((specimen, tile_v), (centers, cen), (counts, cnt), (helpers, hlp)), sems
    )
    for copy in copies:
        copy.wait()
    tile = tile_v.shape[1]
    lanes = tile_v.shape[2]
    rows, cols = iota((INFO, lanes), 0), iota((INFO, lanes), 1)
    info = jnp.where(rows == 0, -1.0, 0.0)
    for j in range(centers.shape[2]):
        helper = jnp.where(j < cnt[0, 0], hlp[0, 0, j], -1)
        for r, value in enumerate((helper, cen[0, 0, j, 0], cen[0, 0, j, 1])):
            info = jnp.where((rows == r) & (cols == j), value.astype(F32), info)
    info = info.astype(BF16)
    for c in range(out.shape[0]):
        for p in range(2):
            out[c, p * tile : (p + 1) * tile] = tile_v[p].astype(BF16)
        out[c, 2 * tile :] = info


def load_kernel(probe, measured, tables, probe_out, amplitude, tables_out, raw, sems):
    copies = fetch(
        ((measured, raw), (probe, probe_out), (tables, tables_out)), sems
    )
    copies[0].wait()
    extent = raw.shape[-1]
    half = extent // 2
    shape = (extent, extent)

    def source(i):
        return jnp.where(i < half, 2 * i, 2 * (i - half) + 1)

    sort = (iota(shape, 1) == source(iota(shape, 0))).astype(F32).astype(BF16)
    sort_t = (iota(shape, 0) == source(iota(shape, 1))).astype(F32).astype(BF16)
    value = raw[0, 0, 0]
    coarse = value.astype(BF16)
    fine = (value - coarse.astype(F32)).astype(BF16)
    amplitude[...] = sum(
        dot(dot(sort, part).astype(BF16), sort_t) for part in (coarse, fine)
    )
    for copy in copies[1:]:
        copy.wait()


def frame_kernel(
    band, first, second, probe, amplitude, tables,
    to_first, to_second, centre, wide, far, spread,
):
    columns = band.shape[0]
    lanes = band.shape[2]
    tile = (band.shape[1] - INFO) // 2
    extent = probe.shape[-1]
    half = extent // 2
    modes = probe.shape[0]
    odd = lax.axis_index("row") % 2 == 1
    me = lax.axis_index("col").astype(F32)

    code = jnp.zeros((1, lanes), F32)
    for c in range(columns):
        info = band[c, 2 * tile :].astype(F32)
        hit = info[0:1] == me
        code += jnp.where(hit, c * 128.0 * 128.0 + info[1:2] * 128.0 + info[2:3], 0.0)
    code = jnp.sum(code).astype(jnp.int32)
    source = code // (128 * 128)
    row = code // 128 % 128
    col = code % 128

    for d in range(3):
        c = source + d - 1
        inside = (c >= 0) & (c < columns)
        c = jnp.clip(c, 0, columns - 1)
        for p in range(2):
            part = pl.ds(p * tile, tile)
            above = jnp.where(odd, first[c, part], second[c, part])
            below = jnp.where(odd, second[c, part], first[c, part])
            for i, block in enumerate((above, band[c, part], below)):
                wide[p, i * tile : (i + 1) * tile, d * tile : (d + 1) * tile] = jnp.where(
                    inside, block.astype(F32), 0.0
                )
    groups = extent // 8 + 1
    base = pl.multiple_of(row // 8 * 8, 8)
    step = row % 8
    window = pl.ds(base, 8 * groups)
    lane = iota((8 * groups, tile), 1)
    sub = iota((groups - 1, 8, extent), 1)
    patch = []
    for p in range(2):
        turned = [
            pltpu.roll(wide[p, window, d * tile : (d + 1) * tile], tile - col, 1)
            for d in range(3)
        ]
        shifted = jnp.concatenate(
            [jnp.where(lane < tile - col, turned[d], turned[d + 1]) for d in range(2)], 1
        )
        turned = pltpu.roll(shifted.reshape(groups, 8, extent), (8 - step) % 8, 1)
        patch.append(
            jnp.where(sub < 8 - step, turned[:-1], turned[1:]).reshape(extent, extent)
        )

    right = (tables[0], tables[2])
    left = (tables[1], tables[3])
    intensity = [jnp.zeros((half, extent), F32) for _ in range(2)]
    for k in range(modes):
        pr, pi = probe[k, 0], probe[k, 1]
        wr = pr * patch[0] - pi * patch[1]
        wi = pr * patch[1] + pi * patch[0]
        spectra = []
        for parity, sign in ((0, 1), (1, -1)):
            folded = jnp.concatenate(
                [wr[:, :half] + sign * wr[:, half:], wi[:, :half] + sign * wi[:, half:]], 1
            ).astype(BF16)
            spectra.append(dot(folded, right[parity]))
        even, odds = spectra
        for parity, sign in ((0, 1), (1, -1)):
            e = even[:half] + sign * even[half:]
            o = odds[:half] + sign * odds[half:]
            folded = quarters(e[:, :half], o[:, :half], e[:, half:], o[:, half:])
            f = dot(left[parity], folded.astype(BF16))
            far[k, parity] = f
            intensity[parity] += f[:half] * f[:half] + f[half:] * f[half:]
    factor = [
        1.0
        - amplitude[i * half : (i + 1) * half]
        * lax.rsqrt(jnp.maximum(intensity[i], 0.25))
        for i in range(2)
    ]
    grad = [[jnp.zeros((half, extent), F32) for _ in range(2)] for _ in range(2)]
    for k in range(modes):
        c = []
        for parity in range(2):
            f = far[k, parity]
            c.append(
                (f * jnp.concatenate([factor[parity], factor[parity]], 0)).astype(BF16)
            )
        a = dot(
            quarters(c[0][:half, :half], c[0][half:, :half], c[1][:half, :half], c[1][half:, :half]),
            left[0],
        )
        b = dot(
            quarters(c[0][:half, half:], c[0][half:, half:], c[1][:half, half:], c[1][half:, half:]),
            left[1],
        )
        lo, hi = (a + b).astype(BF16), (a - b).astype(BF16)
        turned = []
        for parity in range(2):
            l = lo[parity * half : (parity + 1) * half]
            h = hi[parity * half : (parity + 1) * half]
            turned.append(
                dot(
                    right[parity],
                    quarters(l[:, :half], h[:, :half], l[:, half:], h[:, half:]),
                )
            )
        for i, chi in enumerate((turned[0] + turned[1], turned[0] - turned[1])):
            cr, ci = chi[:half], chi[half:]
            pr = probe[k, 0, i * half : (i + 1) * half]
            pi = probe[k, 1, i * half : (i + 1) * half]
            grad[0][i] += pr * cr + pi * ci
            grad[1][i] += pr * ci - pi * cr

    to_first[...] = jnp.zeros_like(to_first)
    to_second[...] = jnp.zeros_like(to_second)
    centre[...] = jnp.zeros_like(centre)
    spread[...] = jnp.zeros_like(spread)
    for p in range(2):
        g = jnp.concatenate(grad[p], 0).astype(BF16).astype(F32)
        turned = pltpu.roll(g.reshape(groups - 1, 8, extent), step, 1)
        none = jnp.zeros((1, 8, extent), F32)
        g = jnp.where(
            iota((groups, 8, extent), 1) >= step,
            jnp.concatenate([turned, none], 0),
            jnp.concatenate([none, turned], 0),
        ).reshape(8 * groups, extent)
        turned = [pltpu.roll(g[:, d * tile : (d + 1) * tile], col, 1) for d in range(2)]
        spread[p, window, 0:tile] = jnp.where(lane >= col, turned[0], 0.0)
        spread[p, window, tile : 2 * tile] = jnp.where(lane >= col, turned[1], turned[0])
        spread[p, window, 2 * tile :] = jnp.where(lane < col, turned[1], 0.0)
    for d in range(3):
        c = source + d - 1

        @pl.when((c >= 0) & (c < columns))
        def _():
            for p in range(2):
                part = pl.ds(p * tile, tile)
                above, own, below = (
                    spread[p, i * tile : (i + 1) * tile, d * tile : (d + 1) * tile].astype(BF16)
                    for i in range(3)
                )
                to_first[c, part] = jnp.where(odd, above, below)
                to_second[c, part] = jnp.where(odd, below, above)
                centre[c, part] = own


def call(kernel, name, out_shape, in_specs, scratch, flops, moved, *args):
    return pl.pallas_call(
        kernel,
        out_shape=out_shape,
        in_specs=in_specs,
        out_specs=jax.tree.map(lambda _: VMEM, out_shape),
        scratch_shapes=scratch,
        compiler_params=pltpu.CompilerParams(vmem_limit_bytes=24 * 2**20),
        cost_estimate=pl.CostEstimate(flops=flops, bytes_accessed=moved, transcendentals=0),
        name=name,
    )(*args)


def per_device(specimen, probe, measured, centers, frame_counts, helper_cols):
    extent = probe.shape[-1]
    half = extent // 2
    tile = specimen.shape[1]
    modes = probe.shape[0]
    columns = lax.axis_size("col")
    height = 2 * tile
    block = jax.ShapeDtypeStruct((columns, height, tile), BF16)
    dma = pltpu.SemaphoreType.DMA

    packed = call(
        pack_kernel, "pack",
        jax.ShapeDtypeStruct((columns, height + INFO, tile), BF16),
        [ANY] * 4,
        [
            pltpu.VMEM(specimen.shape, F32),
            pltpu.SMEM(centers.shape, jnp.int32),
            pltpu.SMEM(frame_counts.shape, jnp.int32),
            pltpu.SMEM(helper_cols.shape, jnp.int32),
            dma((4,)),
        ],
        10**5, 2**19,
        specimen, centers, frame_counts, helper_cols,
    )
    tables = dft_tables(extent)
    probe, amplitude, tables = call(
        load_kernel, "load",
        (
            jax.ShapeDtypeStruct(probe.shape, F32),
            jax.ShapeDtypeStruct((extent, extent), F32),
            jax.ShapeDtypeStruct(tables.shape, BF16),
        ),
        [ANY] * 3,
        [pltpu.VMEM(measured.shape, F32), dma((3,))],
        10**8, 2**22,
        probe, measured, tables,
    )
    band = lax.all_to_all(packed, "col", split_axis=0, concat_axis=0, tiled=True)

    rows = lax.axis_size("row")
    swaps = []
    for start in (0, 1):
        pairs = [(i, i + 1) for i in range(start, rows - 1, 2)]
        swaps.append(pairs + [(b, a) for a, b in pairs])
    second = lax.ppermute(band, "row", swaps[1])
    first = lax.ppermute(band, "row", swaps[0])
    to_first, to_second, centre = call(
        frame_kernel, "frame",
        (block, block, block),
        [VMEM] * 6,
        [
            pltpu.VMEM((2, tile + 2 * half, 3 * tile), F32),
            pltpu.VMEM((modes, 2, extent, extent), F32),
            pltpu.VMEM((2, tile + 2 * half, 3 * tile), F32),
        ],
        2 * 10**9, 2**22,
        band, first, second, probe, amplitude, tables,
    )
    from_second = lax.ppermute(to_second, "row", swaps[1])
    from_first = lax.ppermute(to_first, "row", swaps[0])
    summed = centre.astype(F32) + from_second.astype(F32) + from_first.astype(F32)
    shares = lax.all_to_all(
        summed.astype(BF16), "col", split_axis=0, concat_axis=0, tiled=True
    )
    return jnp.sum(shares.astype(F32), axis=0).reshape(2, tile, tile)


def solution(mesh):
    return jax.shard_map(
        per_device,
        mesh=mesh,
        in_specs=(
            P(None, "row", "col"),
            P(),
            P("row", "col", None, None, None),
            P("row", "col", None, None),
            P("row", "col"),
            P("row", "col", None),
        ),
        out_specs=P(None, "row", "col"),
        check_vma=False,
    )
```

profile of v0, /device:TPU:8, one launch (start us, length us, event | category | flops | bytes accessed | tf_op | source)
XLA Modules:
  0.0 42.1 jit_solution(15454918685644170643)
XLA Ops:
  0.7 0.0 copy-start.3
  0.7 0.9 %copy-done.3 = f32[2,128,128]{2,1,0:T(8,128)S(1)} copy-done((f32[2,128,128]{2,1,0:T(8,128)S(1)}, f32[2,128,128]{2,1,0:T(8,128)}, u32[]{:S(2)}) %copy-start.3) | copy-done | bytes 131096
  1.6 0.0 copy-start.4
  1.6 0.7 %copy-done.4 = s32[1,1,2,2]{3,2,1,0:T(2,128)S(1)} copy-done((s32[1,1,2,2]{3,2,1,0:T(2,128)S(1)}, s32[1,1,2,2]{3,2,1,0:T(2,128)}, u32[]{:S(2)}) %copy-start.4) | copy-done | bytes 40
  2.2 0.0 copy-start.5
  2.2 0.7 %copy-done.5 = s32[1,1,2]{2,1,0:T(1,128)S(1)} copy-done((s32[1,1,2]{2,1,0:T(1,128)S(1)}, s32[1,1,2]{2,1,0:T(1,128)}, u32[]{:S(2)}) %copy-start.5) | copy-done | bytes 32
  2.9 0.8 %pack.1 = bf16[4,272,128]{2,1,0:T(8,128)(2,1)S(1)} custom-call(f32[2,128,128]{2,1,0:T(8,128)S(1)} %copy-done.3, s32[1,1,2,2]{3,2,1,0:T(2,128)S(1)} %copy-done.4, s32[1,1]{1,0:T(1,128)S(6)} %copy.8.counts, s32[1,1,2]{2,1,0:T(1,128)S(1)} %copy-done.5), custom_call_target="tpu_custom_call" | custom-call | flops 100000 | bytes 524288 | tf_op jit(solution)/shard_map/pack/pallas_call | solution.py:256
  3.7 9.7 %all_to_all.10.band = bf16[4,272,128]{2,1,0:T(8,128)(2,1)S(1)} all-to-all(bf16[4,272,128]{2,1,0:T(8,128)(2,1)S(1)} %pack.1), channel_id=1, replica_groups=mesh['row'=8,'col'=4] {'col'}, dimensions={0} | all-to-all | bytes 557056 | tf_op jit(solution)/shard_map/all_to_all | solution.py:305
  13.4 1.9 %collective-permute-start.1 = (bf16[4,272,128]{2,1,0:T(8,128)(2,1)S(1)}, bf16[4,272,128]{2,1,0:T(8,128)(2,1)S(1)}, u32[]{:S(2)}, u32[]{:S(2)}) collective-permute-start(bf16[4,272,128]{2,1,0:T(8,128)(2,1)S(1)} %all_to_all.10.band), channel_id=1, source_target_pairs={{4,8},{12,16},{20,24},{8,4},{16,12},{24,20},{5,9},{13,17},{21,25},... | collective-permute-start | bytes 835592 | tf_op jit(solution)/shard_map/ppermute | solution.py:312
  15.3 1.7 %collective-permute-start = (bf16[4,272,128]{2,1,0:T(8,128)(2,1)S(1)}, bf16[4,272,128]{2,1,0:T(8,128)(2,1)S(1)}, u32[]{:S(2)}, u32[]{:S(2)}) collective-permute-start(bf16[4,272,128]{2,1,0:T(8,128)(2,1)S(1)} %all_to_all.10.band), channel_id=1, source_target_pairs={{0,4},{8,12},{16,20},{24,28},{4,0},{12,8},{20,16},{28,24},{1,5},{9... | collective-permute-start | bytes 835592 | tf_op jit(solution)/shard_map/ppermute | solution.py:313
  17.0 0.0 copy-start
  17.0 1.6 %copy-done = f32[4,2,256,256]{3,2,1,0:T(8,128)S(1)} copy-done((f32[4,2,256,256]{3,2,1,0:T(8,128)S(1)}, f32[4,2,256,256]{3,2,1,0:T(8,128)}, u32[]{:S(2)}) %copy-start) | copy-done | bytes 2097176
  18.6 0.0 copy-start.1
  18.6 1.0 %copy-done.1 = bf16[4,256,256]{2,1,0:T(8,128)(2,1)S(1)} copy-done((bf16[4,256,256]{2,1,0:T(8,128)(2,1)S(1)}, bf16[4,256,256]{2,1,0:T(8,128)(2,1)}, u32[]{:S(2)}) %copy-start.1) | copy-done | bytes 524312
  19.7 0.0 copy-start.2
  19.7 0.9 %copy-done.2 = f32[1,1,1,256,256]{4,3,2,1,0:T(8,128)S(1)} copy-done((f32[1,1,1,256,256]{4,3,2,1,0:T(8,128)S(1)}, f32[1,1,1,256,256]{4,3,2,1,0:T(8,128)}, u32[]{:S(2)}) %copy-start.2) | copy-done | bytes 262168
  20.6 0.7 %load.1 = (f32[4,2,256,256]{3,2,1,0:T(8,128)S(1)}, f32[256,256]{1,0:T(8,128)S(1)}, bf16[4,256,256]{2,1,0:T(8,128)(2,1)S(1)}) custom-call(f32[4,2,256,256]{3,2,1,0:T(8,128)S(1)} %copy-done, f32[1,1,1,256,256]{4,3,2,1,0:T(8,128)S(1)} %copy-done.2, bf16[4,256,256]{2,1,0:T(8,128)(2,1)S(1)} %copy-done.1), custom_call_target="tpu_custom_call" | custom-call | flops 100000000 | bytes 4194304 | tf_op jit(solution)/shard_map/load/pallas_call | solution.py:256
  21.3 0.0 collective-permute-done.1.second
  21.3 0.0 collective-permute-done.first
  21.3 3.6 %frame.1 = (bf16[4,256,128]{2,1,0:T(8,128)(2,1)S(1)}, bf16[4,256,128]{2,1,0:T(8,128)(2,1)S(1)}, bf16[4,256,128]{2,1,0:T(8,128)(2,1)S(1)}) custom-call(bf16[4,272,128]{2,1,0:T(8,128)(2,1)S(1)} %all_to_all.10.band, bf16[4,272,128]{2,1,0:T(8,128)(2,1)S(1)} %collective-permute-done.first, bf16[4,272,128]{2,1,0:T(8,128)(2,1)S(1)} %collective-permute-done.1.second, ...), custom_call_target="tpu_custom_call" | custom-call | flops 2000000000 | bytes 4194304 | tf_op jit(solution)/shard_map/frame/pallas_call | solution.py:256
  25.0 2.0 %collective-permute-start.2 = (bf16[4,256,128]{2,1,0:T(8,128)(2,1)S(1)}, bf16[4,256,128]{2,1,0:T(8,128)(2,1)S(1)}, u32[]{:S(2)}, u32[]{:S(2)}) collective-permute-start(bf16[4,256,128]{2,1,0:T(8,128)(2,1)S(1)} %get-tuple-element.15), channel_id=1, source_target_pairs={{4,8},{12,16},{20,24},{8,4},{16,12},{24,20},{5,9},{13,17},{21,25},... | collective-permute-start | bytes 786440 | tf_op jit(solution)/shard_map/ppermute | solution.py:326
  26.9 1.7 %collective-permute-start.3 = (bf16[4,256,128]{2,1,0:T(8,128)(2,1)S(1)}, bf16[4,256,128]{2,1,0:T(8,128)(2,1)S(1)}, u32[]{:S(2)}, u32[]{:S(2)}) collective-permute-start(bf16[4,256,128]{2,1,0:T(8,128)(2,1)S(1)} %get-tuple-element.16), channel_id=1, source_target_pairs={{0,4},{8,12},{16,20},{24,28},{4,0},{12,8},{20,16},{28,24},{1,5},{9... | collective-permute-start | bytes 786440 | tf_op jit(solution)/shard_map/ppermute | solution.py:327
  28.7 4.0 %collective-permute-done.2 = bf16[4,256,128]{2,1,0:T(8,128)(2,1)S(1)} collective-permute-done((bf16[4,256,128]{2,1,0:T(8,128)(2,1)S(1)}, bf16[4,256,128]{2,1,0:T(8,128)(2,1)S(1)}, u32[]{:S(2)}, u32[]{:S(2)}) %collective-permute-start.2) | collective-permute-done | bytes 262176 | tf_op jit(solution)/shard_map/ppermute | solution.py:326
  32.6 0.0 collective-permute-done.3
  32.6 0.1 add_convert_fusion
  32.8 8.7 %all_to_all.11 = bf16[4,256,128]{2,1,0:T(8,128)(2,1)S(1)} all-to-all(bf16[4,256,128]{2,1,0:T(8,128)(2,1)S(1)} %add_convert_fusion), channel_id=1, replica_groups=mesh['row'=8,'col'=4] {'col'}, dimensions={0} | all-to-all | bytes 524288 | tf_op jit(solution)/shard_map/all_to_all | solution.py:329
  41.4 0.7 %convert_reduce_fusion = f32[256,128]{1,0:T(8,128)} fusion(bf16[4,256,128]{2,1,0:T(8,128)(2,1)S(1)} %all_to_all.11), kind=kLoop, calls=%fused_computation | loop fusion | flops 229376 | bytes 393216 | tf_op jit(solution)/shard_map/reduce_sum | solution.py:332
Async XLA Ops:
  0.7 0.9 %copy-start.3 = (f32[2,128,128]{2,1,0:T(8,128)S(1)}, f32[2,128,128]{2,1,0:T(8,128)}, u32[]{:S(2)}) copy-start(f32[2,128,128]{2,1,0:T(8,128)} %specimen.1) | copy-start | bytes 393220
  1.6 0.7 %copy-start.4 = (s32[1,1,2,2]{3,2,1,0:T(2,128)S(1)}, s32[1,1,2,2]{3,2,1,0:T(2,128)}, u32[]{:S(2)}) copy-start(s32[1,1,2,2]{3,2,1,0:T(2,128)} %centers.1) | copy-start | bytes 52
  2.2 0.7 %copy-start.5 = (s32[1,1,2]{2,1,0:T(1,128)S(1)}, s32[1,1,2]{2,1,0:T(1,128)}, u32[]{:S(2)}) copy-start(s32[1,1,2]{2,1,0:T(1,128)} %helpers.1) | copy-start | bytes 28
  13.4 8.0 %collective-permute-start.1 = (bf16[4,272,128]{2,1,0:T(8,128)(2,1)S(1)}, bf16[4,272,128]{2,1,0:T(8,128)(2,1)S(1)}, u32[]{:S(2)}, u32[]{:S(2)}) collective-permute-start(bf16[4,272,128]{2,1,0:T(8,128)(2,1)S(1)} %all_to_all.10.band), channel_id=1, source_target_pairs={{4,8},{12,16},{20,24},{8,4},{16,12},{24,20},{5,9},{13,17},{21,25},... | collective-permute-start | bytes 835592 | tf_op jit(solution)/shard_map/ppermute | solution.py:312
  15.3 6.0 %collective-permute-start = (bf16[4,272,128]{2,1,0:T(8,128)(2,1)S(1)}, bf16[4,272,128]{2,1,0:T(8,128)(2,1)S(1)}, u32[]{:S(2)}, u32[]{:S(2)}) collective-permute-start(bf16[4,272,128]{2,1,0:T(8,128)(2,1)S(1)} %all_to_all.10.band), channel_id=1, source_target_pairs={{0,4},{8,12},{16,20},{24,28},{4,0},{12,8},{20,16},{28,24},{1,5},{9... | collective-permute-start | bytes 835592 | tf_op jit(solution)/shard_map/ppermute | solution.py:313
  17.0 1.6 %copy-start = (f32[4,2,256,256]{3,2,1,0:T(8,128)S(1)}, f32[4,2,256,256]{3,2,1,0:T(8,128)}, u32[]{:S(2)}) copy-start(f32[4,2,256,256]{3,2,1,0:T(8,128)} %probe.1) | copy-start | bytes 6291460
  18.6 1.0 %copy-start.1 = (bf16[4,256,256]{2,1,0:T(8,128)(2,1)S(1)}, bf16[4,256,256]{2,1,0:T(8,128)(2,1)}, u32[]{:S(2)}) copy-start(bf16[4,256,256]{2,1,0:T(8,128)(2,1)} %constant.4.clone.tables) | copy-start | bytes 1572868
  19.7 0.9 %copy-start.2 = (f32[1,1,1,256,256]{4,3,2,1,0:T(8,128)S(1)}, f32[1,1,1,256,256]{4,3,2,1,0:T(8,128)}, u32[]{:S(2)}) copy-start(f32[1,1,1,256,256]{4,3,2,1,0:T(8,128)} %measured.1) | copy-start | bytes 786436
  25.0 7.7 %collective-permute-start.2 = (bf16[4,256,128]{2,1,0:T(8,128)(2,1)S(1)}, bf16[4,256,128]{2,1,0:T(8,128)(2,1)S(1)}, u32[]{:S(2)}, u32[]{:S(2)}) collective-permute-start(bf16[4,256,128]{2,1,0:T(8,128)(2,1)S(1)} %get-tuple-element.15), channel_id=1, source_target_pairs={{4,8},{12,16},{20,24},{8,4},{16,12},{24,20},{5,9},{13,17},{21,25},... | collective-permute-start | bytes 786440 | tf_op jit(solution)/shard_map/ppermute | solution.py:326
  26.9 5.7 %collective-permute-start.3 = (bf16[4,256,128]{2,1,0:T(8,128)(2,1)S(1)}, bf16[4,256,128]{2,1,0:T(8,128)(2,1)S(1)}, u32[]{:S(2)}, u32[]{:S(2)}) collective-permute-start(bf16[4,256,128]{2,1,0:T(8,128)(2,1)S(1)} %get-tuple-element.16), channel_id=1, source_target_pairs={{0,4},{8,12},{16,20},{24,28},{4,0},{12,8},{20,16},{28,24},{1,5},{9... | collective-permute-start | bytes 786440 | tf_op jit(solution)/shard_map/ppermute | solution.py:327
where the time goes:
time: 42.5 us; the launch traced here: 42.1 us
  blocking collectives  18.4 us (43%)
  starting transfers between devices  7.34 us (17%)
  local copies, waits for them, and re-layouts  5.81 us (14%)
  Pallas kernels  5.06 us (12%)
  waiting for transfers between devices  4 us (9%)
  other arithmetic  0.79 us (2%)
  between operations  0.73 us (2%)
    all_to_all x1, blocking collectives, per_device(): lax.all_to_all(packed, 'col', split_axis=0, concat_axis=0, tiled=True)  9.71 us
    all_to_all x1, blocking collectives, per_device(): lax.all_to_all(summed.astype(BF16), 'col', split_axis=0, concat_axis=0, t...  8.66 us
    unnamed x12, local copies, waits for them, and re-layouts  5.81 us
    pallas_call x3, Pallas kernels, call(): pl.pallas_call(kernel, out_shape=out_shape, in_specs=in_specs, out_specs=...  5.06 us
    ppermute x1, waiting for transfers between devices, per_device(): from_second = lax.ppermute(to_second, 'row', swaps[1])  3.99 us
    ppermute x1, starting transfers between devices, per_device(): from_second = lax.ppermute(to_second, 'row', swaps[1])  1.98 us
    ppermute x1, starting transfers between devices, per_device(): second = lax.ppermute(band, 'row', swaps[1])  1.91 us
    ppermute x1, starting transfers between devices, per_device(): first = lax.ppermute(band, 'row', swaps[0])  1.74 us
  transfers between devices with their start and end apart: 4, of which 1 were waited for; matrix products, arithmetic and copies ran while one was open for 0% of the time, Pallas kernels for 2%

commit v1 on v0

--- a/solution.py
+++ b/solution.py
@@ -13,7 +13,8 @@
 BF16 = jnp.bfloat16
 INFO = 16
 VMEM = pl.BlockSpec(memory_space=pltpu.VMEM)
-ANY = pl.BlockSpec(memory_space=pl.ANY)
+SMEM = pl.BlockSpec(memory_space=pltpu.SMEM)
+HBM = pl.BlockSpec(memory_space=pltpu.HBM)
 
 
 def dft_tables(extent):
@@ -58,10 +59,8 @@
     return copies
 
 
-def pack_kernel(specimen, centers, counts, helpers, out, tile_v, cen, cnt, hlp, sems):
-    copies = fetch(
-        ((specimen, tile_v), (centers, cen), (counts, cnt), (helpers, hlp)), sems
-    )
+def pack_kernel(specimen, centers, cnt, helpers, out, tile_v, cen, hlp, sems):
+    copies = fetch(((specimen, tile_v), (centers, cen), (helpers, hlp)), sems)
     for copy in copies:
         copy.wait()
     tile = tile_v.shape[1]
@@ -219,40 +218,52 @@
             grad[0][i] += pr * cr + pi * ci
             grad[1][i] += pr * ci - pi * cr
 
-    to_first[...] = jnp.zeros_like(to_first)
-    to_second[...] = jnp.zeros_like(to_second)
-    centre[...] = jnp.zeros_like(centre)
     spread[...] = jnp.zeros_like(spread)
     for p in range(2):
         g = jnp.concatenate(grad[p], 0).astype(BF16).astype(F32)
         turned = pltpu.roll(g.reshape(groups - 1, 8, extent), step, 1)
         none = jnp.zeros((1, 8, extent), F32)
-        g = jnp.where(
+        spread[p, window, :] = jnp.where(
             iota((groups, 8, extent), 1) >= step,
             jnp.concatenate([turned, none], 0),
             jnp.concatenate([none, turned], 0),
         ).reshape(8 * groups, extent)
-        turned = [pltpu.roll(g[:, d * tile : (d + 1) * tile], col, 1) for d in range(2)]
-        spread[p, window, 0:tile] = jnp.where(lane >= col, turned[0], 0.0)
-        spread[p, window, tile : 2 * tile] = jnp.where(lane >= col, turned[1], turned[0])
-        spread[p, window, 2 * tile :] = jnp.where(lane < col, turned[1], 0.0)
-    for d in range(3):
-        c = source + d - 1
-
-        @pl.when((c >= 0) & (c < columns))
-        def _():
-            for p in range(2):
-                part = pl.ds(p * tile, tile)
-                above, own, below = (
-                    spread[p, i * tile : (i + 1) * tile, d * tile : (d + 1) * tile].astype(BF16)
-                    for i in range(3)
-                )
-                to_first[c, part] = jnp.where(odd, above, below)
-                to_second[c, part] = jnp.where(odd, below, above)
-                centre[c, part] = own
+    which = iota((INFO, extent), 0)
+    info = jnp.where(which == 0, source, col).astype(F32).astype(BF16)
+    for p in range(2):
+        part = pl.ds(p * tile, tile)
+        above, own, below = (
+            spread[p, i * tile : (i + 1) * tile].astype(BF16) for i in range(3)
+        )
+        to_first[part] = jnp.where(odd, above, below)
+        to_second[part] = jnp.where(odd, below, above)
+        centre[part] = own
+    for out in (to_first, to_second, centre):
+        out[2 * tile :] = info
+
+
+def fold_kernel(centre, first, second, out):
+    columns, height, tile = out.shape
+    extent = centre.shape[1]
+    half = extent // 2
+    gradients, places = [], []
+    for part in (centre, first, second):
+        source = part[height : height + 1, :].astype(F32).astype(jnp.int32)
+        col = part[height + 1 : height + 2, :].astype(F32).astype(jnp.int32)
+        start = jnp.concatenate([source * tile + col - half] * (columns * tile // extent), 1)
+        shape = (extent, columns * tile)
+        places.append((iota(shape, 1) - iota(shape, 0) == start).astype(F32).astype(BF16))
+        gradients.append(part[:height])
+    total = dot(jnp.concatenate(gradients, 1), jnp.concatenate(places, 0))
+    for c in range(columns):
+        out[c] = total[:, c * tile : (c + 1) * tile].astype(BF16)
 
 
 def call(kernel, name, out_shape, in_specs, scratch, flops, moved, *args):
+    args = [
+        pltpu.with_memory_space_constraint(arg, pltpu.HBM) if spec is HBM else arg
+        for arg, spec in zip(args, in_specs)
+    ]
     return pl.pallas_call(
         kernel,
         out_shape=out_shape,
@@ -272,19 +283,18 @@
     modes = probe.shape[0]
     columns = lax.axis_size("col")
     height = 2 * tile
-    block = jax.ShapeDtypeStruct((columns, height, tile), BF16)
+    part = jax.ShapeDtypeStruct((height + INFO, extent), BF16)
     dma = pltpu.SemaphoreType.DMA
 
     packed = call(
         pack_kernel, "pack",
         jax.ShapeDtypeStruct((columns, height + INFO, tile), BF16),
-        [ANY] * 4,
+        [HBM, HBM, SMEM, HBM],
         [
             pltpu.VMEM(specimen.shape, F32),
             pltpu.SMEM(centers.shape, jnp.int32),
-            pltpu.SMEM(frame_counts.shape, jnp.int32),
             pltpu.SMEM(helper_cols.shape, jnp.int32),
-            dma((4,)),
+            dma((3,)),
         ],
         10**5, 2**19,
         specimen, centers, frame_counts, helper_cols,
@@ -297,7 +307,7 @@
             jax.ShapeDtypeStruct((extent, extent), F32),
             jax.ShapeDtypeStruct(tables.shape, BF16),
         ),
-        [ANY] * 3,
+        [HBM] * 3,
         [pltpu.VMEM(measured.shape, F32), dma((3,))],
         10**8, 2**22,
         probe, measured, tables,
@@ -313,22 +323,27 @@
     first = lax.ppermute(band, "row", swaps[0])
     to_first, to_second, centre = call(
         frame_kernel, "frame",
-        (block, block, block),
+        (part, part, part),
         [VMEM] * 6,
         [
             pltpu.VMEM((2, tile + 2 * half, 3 * tile), F32),
             pltpu.VMEM((modes, 2, extent, extent), F32),
-            pltpu.VMEM((2, tile + 2 * half, 3 * tile), F32),
+            pltpu.VMEM((2, tile + 2 * half, extent), F32),
         ],
         2 * 10**9, 2**22,
         band, first, second, probe, amplitude, tables,
     )
     from_second = lax.ppermute(to_second, "row", swaps[1])
     from_first = lax.ppermute(to_first, "row", swaps[0])
-    summed = centre.astype(F32) + from_second.astype(F32) + from_first.astype(F32)
-    shares = lax.all_to_all(
-        summed.astype(BF16), "col", split_axis=0, concat_axis=0, tiled=True
-    )
+    summed = call(
+        fold_kernel, "fold",
+        jax.ShapeDtypeStruct((columns, height, tile), BF16),
+        [VMEM] * 3,
+        [],
+        10**9, 2**20,
+        centre, from_first, from_second,
+    )
+    shares = lax.all_to_all(summed, "col", split_axis=0, concat_axis=0, tiled=True)
     return jnp.sum(shares.astype(F32), axis=0).reshape(2, tile, tile)
 
 

time: 42.5 us -> 39.5 us (0.929)
  local copies, waits for them, and re-layouts: 5.81 us -> 0 us
  waiting for transfers between devices: 4 us -> 6.85 us
  starting transfers between devices: 7.34 us -> 5.74 us
  Pallas kernels: 5.06 us -> 6.54 us
    unnamed x12 -> x0, local copies, waits for them, and re-layouts: 5.81 us -> none
    ppermute x1, waiting for transfers between devices: 0.01 us -> 2.41 us  [per_device(): second = lax.ppermute(band, 'row', swaps[1])]
    ppermute x1, starting transfers between devices: 1.7 us -> 0.18 us  [per_device(): from_first = lax.ppermute(to_first, 'row', swaps[0])]
    pallas_call x3 -> x4, Pallas kernels: 5.06 us -> 6.54 us  [call(): pl.pallas_call(kernel, out_shape=out_shape, in_specs=in_specs, out_specs=...]
    ppermute x1, waiting for transfers between devices: 3.99 us -> 4.44 us  [per_device(): from_second = lax.ppermute(to_second, 'row', swaps[1])]
  transfers between devices with their start and end apart: 4 -> 4, of which waited for: 1 -> 2; matrix products, arithmetic and copies ran while one was open for 0% -> 0% of each run, Pallas kernels for 2% -> 5%
where the time goes in v1:
time: 39.5 us; the launch traced here: 39.2 us
  blocking collectives  18.7 us (47%)
  waiting for transfers between devices  6.85 us (17%)
  Pallas kernels  6.54 us (17%)
  starting transfers between devices  5.74 us (15%)
  between operations  0.71 us (2%)
  other arithmetic  0.69 us (2%)
    all_to_all x1, blocking collectives, per_device(): lax.all_to_all(packed, 'col', split_axis=0, concat_axis=0, tiled=True)  9.71 us
    all_to_all x1, blocking collectives, per_device(): lax.all_to_all(summed, 'col', split_axis=0, concat_axis=0, tiled=True)  8.97 us
    pallas_call x4, Pallas kernels, call(): pl.pallas_call(kernel, out_shape=out_shape, in_specs=in_specs, out_specs=...  6.54 us
    ppermute x1, waiting for transfers between devices, per_device(): from_second = lax.ppermute(to_second, 'row', swaps[1])  4.44 us
    ppermute x1, waiting for transfers between devices, per_device(): second = lax.ppermute(band, 'row', swaps[1])  2.41 us
    ppermute x1, starting transfers between devices, per_device(): second = lax.ppermute(band, 'row', swaps[1])  1.91 us
    ppermute x1, starting transfers between devices, per_device(): from_second = lax.ppermute(to_second, 'row', swaps[1])  1.91 us
    ppermute x1, starting transfers between devices, per_device(): first = lax.ppermute(band, 'row', swaps[0])  1.74 us
  transfers between devices with their start and end apart: 4, of which 2 were waited for; matrix products, arithmetic and copies ran while one was open for 0% of the time, Pallas kernels for 5%

profile of v1, /device:TPU:8, one launch (start us, length us, event | category | flops | bytes accessed | tf_op | source)
XLA Modules:
  0.0 39.2 jit_solution(8754562141979415670)
XLA Ops:
  0.7 1.0 %pack.1 = bf16[4,272,128]{2,1,0:T(8,128)(2,1)S(1)} custom-call(f32[2,128,128]{2,1,0:T(8,128)} %specimen.1, s32[1,1,2,2]{3,2,1,0:T(2,128)} %centers.1, s32[1,1]{1,0:T(1,128)S(6)} %copy.8.cnt, s32[1,1,2]{2,1,0:T(1,128)} %helpers.1), custom_call_target="tpu_custom_call" | custom-call | flops 100000 | bytes 524288 | tf_op jit(solution)/shard_map/pack/pallas_call | solution.py:267
  1.6 9.7 %all_to_all.10.band = bf16[4,272,128]{2,1,0:T(8,128)(2,1)S(1)} all-to-all(bf16[4,272,128]{2,1,0:T(8,128)(2,1)S(1)} %pack.1), channel_id=1, replica_groups=mesh['row'=8,'col'=4] {'col'}, dimensions={0} | all-to-all | bytes 557056 | tf_op jit(solution)/shard_map/all_to_all | solution.py:315
  11.3 1.9 %collective-permute-start.1 = (bf16[4,272,128]{2,1,0:T(8,128)(2,1)S(1)}, bf16[4,272,128]{2,1,0:T(8,128)(2,1)S(1)}, u32[]{:S(2)}, u32[]{:S(2)}) collective-permute-start(bf16[4,272,128]{2,1,0:T(8,128)(2,1)S(1)} %all_to_all.10.band), channel_id=1, source_target_pairs={{4,8},{12,16},{20,24},{8,4},{16,12},{24,20},{5,9},{13,17},{21,25},... | collective-permute-start | bytes 835592 | tf_op jit(solution)/shard_map/ppermute | solution.py:322
  13.3 1.7 %collective-permute-start = (bf16[4,272,128]{2,1,0:T(8,128)(2,1)S(1)}, bf16[4,272,128]{2,1,0:T(8,128)(2,1)S(1)}, u32[]{:S(2)}, u32[]{:S(2)}) collective-permute-start(bf16[4,272,128]{2,1,0:T(8,128)(2,1)S(1)} %all_to_all.10.band), channel_id=1, source_target_pairs={{0,4},{8,12},{16,20},{24,28},{4,0},{12,8},{20,16},{28,24},{1,5},{9... | collective-permute-start | bytes 835592 | tf_op jit(solution)/shard_map/ppermute | solution.py:323
  15.0 1.8 %load.1 = (f32[4,2,256,256]{3,2,1,0:T(8,128)S(1)}, f32[256,256]{1,0:T(8,128)S(1)}, bf16[4,256,256]{2,1,0:T(8,128)(2,1)S(1)}) custom-call(f32[4,2,256,256]{3,2,1,0:T(8,128)} %probe.1, f32[1,1,1,256,256]{4,3,2,1,0:T(8,128)} %measured.1, bf16[4,256,256]{2,1,0:T(8,128)(2,1)} %constant.4.clone.tables), custom_call_target="tpu_custom_call" | custom-call | flops 100000000 | bytes 4194304 | tf_op jit(solution)/shard_map/load/pallas_call | solution.py:267
  16.8 2.4 %collective-permute-done.1.second = bf16[4,272,128]{2,1,0:T(8,128)(2,1)S(1)} collective-permute-done((bf16[4,272,128]{2,1,0:T(8,128)(2,1)S(1)}, bf16[4,272,128]{2,1,0:T(8,128)(2,1)S(1)}, u32[]{:S(2)}, u32[]{:S(2)}) %collective-permute-start.1) | collective-permute-done | bytes 278560 | tf_op jit(solution)/shard_map/ppermute | solution.py:322
  19.2 0.0 collective-permute-done.first
  19.2 3.4 %frame.1 = (bf16[272,256]{1,0:T(8,128)(2,1)S(1)}, bf16[272,256]{1,0:T(8,128)(2,1)S(1)}, bf16[272,256]{1,0:T(8,128)(2,1)S(1)}) custom-call(bf16[4,272,128]{2,1,0:T(8,128)(2,1)S(1)} %all_to_all.10.band, bf16[4,272,128]{2,1,0:T(8,128)(2,1)S(1)} %collective-permute-done.first, bf16[4,272,128]{2,1,0:T(8,128)(2,1)S(1)} %collective-permute-done.1.second, ...), custom_call_target="tpu_custom_call" | custom-call | flops 2000000000 | bytes 4194304 | tf_op jit(solution)/shard_map/frame/pallas_call | solution.py:267
  22.6 0.2 collective-permute-start.2
  22.8 1.9 %collective-permute-start.3 = (bf16[272,256]{1,0:T(8,128)(2,1)S(1)}, bf16[272,256]{1,0:T(8,128)(2,1)S(1)}, u32[]{:S(2)}, u32[]{:S(2)}) collective-permute-start(bf16[272,256]{1,0:T(8,128)(2,1)S(1)} %get-tuple-element.16), channel_id=1, source_target_pairs={{4,8},{12,16},{20,24},{8,4},{16,12},{24,20},{5,9},{13,17},{21,25},... | collective-permute-start | bytes 417800 | tf_op jit(solution)/shard_map/ppermute | solution.py:336
  24.7 0.0 collective-permute-done.2.first
  24.7 4.4 %collective-permute-done.3.second = bf16[272,256]{1,0:T(8,128)(2,1)S(1)} collective-permute-done((bf16[272,256]{1,0:T(8,128)(2,1)S(1)}, bf16[272,256]{1,0:T(8,128)(2,1)S(1)}, u32[]{:S(2)}, u32[]{:S(2)}) %collective-permute-start.3) | collective-permute-done | bytes 139296 | tf_op jit(solution)/shard_map/ppermute | solution.py:336
  29.1 0.4 %fold.1 = bf16[4,256,128]{2,1,0:T(8,128)(2,1)S(1)} custom-call(bf16[272,256]{1,0:T(8,128)(2,1)S(1)} %get-tuple-element.14.centre, bf16[272,256]{1,0:T(8,128)(2,1)S(1)} %collective-permute-done.2.first, bf16[272,256]{1,0:T(8,128)(2,1)S(1)} %collective-permute-done.3.second), custom_call_target="tpu_custom_call" | custom-call | flops 1000000000 | bytes 1048576 | tf_op jit(solution)/shard_map/fold/pallas_call | solution.py:267
  29.5 9.0 %all_to_all.11 = bf16[4,256,128]{2,1,0:T(8,128)(2,1)S(1)} all-to-all(bf16[4,256,128]{2,1,0:T(8,128)(2,1)S(1)} %fold.1), channel_id=1, replica_groups=mesh['row'=8,'col'=4] {'col'}, dimensions={0} | all-to-all | bytes 524288 | tf_op jit(solution)/shard_map/all_to_all | solution.py:346
  38.5 0.7 %convert_reduce_fusion = f32[256,128]{1,0:T(8,128)} fusion(bf16[4,256,128]{2,1,0:T(8,128)(2,1)S(1)} %all_to_all.11), kind=kLoop, calls=%fused_computation | loop fusion | flops 229376 | bytes 393216 | tf_op jit(solution)/shard_map/reduce_sum | solution.py:347
Async XLA Ops:
  11.3 7.9 %collective-permute-start.1 = (bf16[4,272,128]{2,1,0:T(8,128)(2,1)S(1)}, bf16[4,272,128]{2,1,0:T(8,128)(2,1)S(1)}, u32[]{:S(2)}, u32[]{:S(2)}) collective-permute-start(bf16[4,272,128]{2,1,0:T(8,128)(2,1)S(1)} %all_to_all.10.band), channel_id=1, source_target_pairs={{4,8},{12,16},{20,24},{8,4},{16,12},{24,20},{5,9},{13,17},{21,25},... | collective-permute-start | bytes 835592 | tf_op jit(solution)/shard_map/ppermute | solution.py:322
  13.3 5.9 %collective-permute-start = (bf16[4,272,128]{2,1,0:T(8,128)(2,1)S(1)}, bf16[4,272,128]{2,1,0:T(8,128)(2,1)S(1)}, u32[]{:S(2)}, u32[]{:S(2)}) collective-permute-start(bf16[4,272,128]{2,1,0:T(8,128)(2,1)S(1)} %all_to_all.10.band), channel_id=1, source_target_pairs={{0,4},{8,12},{16,20},{24,28},{4,0},{12,8},{20,16},{28,24},{1,5},{9... | collective-permute-start | bytes 835592 | tf_op jit(solution)/shard_map/ppermute | solution.py:323
  22.6 2.1 %collective-permute-start.2 = (bf16[272,256]{1,0:T(8,128)(2,1)S(1)}, bf16[272,256]{1,0:T(8,128)(2,1)S(1)}, u32[]{:S(2)}, u32[]{:S(2)}) collective-permute-start(bf16[272,256]{1,0:T(8,128)(2,1)S(1)} %get-tuple-element.15), channel_id=1, source_target_pairs={{0,4},{8,12},{16,20},{24,28},{4,0},{12,8},{20,16},{28,24},{1,5},{9... | collective-permute-start | bytes 417800 | tf_op jit(solution)/shard_map/ppermute | solution.py:337
  22.8 6.4 %collective-permute-start.3 = (bf16[272,256]{1,0:T(8,128)(2,1)S(1)}, bf16[272,256]{1,0:T(8,128)(2,1)S(1)}, u32[]{:S(2)}, u32[]{:S(2)}) collective-permute-start(bf16[272,256]{1,0:T(8,128)(2,1)S(1)} %get-tuple-element.16), channel_id=1, source_target_pairs={{4,8},{12,16},{20,24},{8,4},{16,12},{24,20},{5,9},{13,17},{21,25},... | collective-permute-start | bytes 417800 | tf_op jit(solution)/shard_map/ppermute | solution.py:336

commit v2 on v1

--- a/solution.py
+++ b/solution.py
@@ -72,10 +72,9 @@
         for r, value in enumerate((helper, cen[0, 0, j, 0], cen[0, 0, j, 1])):
             info = jnp.where((rows == r) & (cols == j), value.astype(F32), info)
     info = info.astype(BF16)
-    for c in range(out.shape[0]):
-        for p in range(2):
-            out[c, p * tile : (p + 1) * tile] = tile_v[p].astype(BF16)
-        out[c, 2 * tile :] = info
+    for p in range(2):
+        out[p * tile : (p + 1) * tile] = tile_v[p].astype(BF16)
+    out[2 * tile :] = info
 
 
 def load_kernel(probe, measured, tables, probe_out, amplitude, tables_out, raw, sems):
@@ -104,7 +103,7 @@
 
 def frame_kernel(
     band, first, second, probe, amplitude, tables,
-    to_first, to_second, centre, wide, far, spread,
+    to_second, to_first, centre, wide, far, spread,
 ):
     columns = band.shape[0]
     lanes = band.shape[2]
@@ -288,7 +287,7 @@
 
     packed = call(
         pack_kernel, "pack",
-        jax.ShapeDtypeStruct((columns, height + INFO, tile), BF16),
+        jax.ShapeDtypeStruct((height + INFO, tile), BF16),
         [HBM, HBM, SMEM, HBM],
         [
             pltpu.VMEM(specimen.shape, F32),
@@ -312,7 +311,7 @@
         10**8, 2**22,
         probe, measured, tables,
     )
-    band = lax.all_to_all(packed, "col", split_axis=0, concat_axis=0, tiled=True)
+    band = lax.all_gather(packed, "col")
 
     rows = lax.axis_size("row")
     swaps = []
@@ -321,7 +320,7 @@
         swaps.append(pairs + [(b, a) for a, b in pairs])
     second = lax.ppermute(band, "row", swaps[1])
     first = lax.ppermute(band, "row", swaps[0])
-    to_first, to_second, centre = call(
+    to_second, to_first, centre = call(
         frame_kernel, "frame",
         (part, part, part),
         [VMEM] * 6,

time: 39.5 us -> 38.8 us (0.982)
  blocking collectives: 18.7 us -> 18.1 us
    all_to_all x1 -> x0, blocking collectives: 9.71 us -> none  [per_device(): lax.all_to_all(packed, 'col', split_axis=0, concat_axis=0, tiled=True)]
    all_gather x0 -> x1, blocking collectives: none -> 9.13 us  [per_device(): band = lax.all_gather(packed, 'col')]
where the time goes in v2:
time: 38.8 us; the launch traced here: 38.6 us
  blocking collectives  18.1 us (47%)
  waiting for transfers between devices  6.85 us (18%)
  Pallas kernels  6.53 us (17%)
  starting transfers between devices  5.74 us (15%)
  between operations  0.71 us (2%)
  other arithmetic  0.69 us (2%)
    all_gather x1, blocking collectives, per_device(): band = lax.all_gather(packed, 'col')  9.13 us
    all_to_all x1, blocking collectives, per_device(): lax.all_to_all(summed, 'col', split_axis=0, concat_axis=0, tiled=True)  8.96 us
    pallas_call x4, Pallas kernels, call(): pl.pallas_call(kernel, out_shape=out_shape, in_specs=in_specs, out_specs=...  6.53 us
    ppermute x1, waiting for transfers between devices, per_device(): from_second = lax.ppermute(to_second, 'row', swaps[1])  4.44 us
    ppermute x1, waiting for transfers between devices, per_device(): second = lax.ppermute(band, 'row', swaps[1])  2.41 us
    ppermute x1, starting transfers between devices, per_device(): second = lax.ppermute(band, 'row', swaps[1])  1.91 us
    ppermute x1, starting transfers between devices, per_device(): from_second = lax.ppermute(to_second, 'row', swaps[1])  1.91 us
    ppermute x1, starting transfers between devices, per_device(): first = lax.ppermute(band, 'row', swaps[0])  1.74 us
  transfers between devices with their start and end apart: 4, of which 2 were waited for; matrix products, arithmetic and copies ran while one was open for 0% of the time, Pallas kernels for 5%

profile of v2, /device:TPU:8, one launch (start us, length us, event | category | flops | bytes accessed | tf_op | source)
XLA Modules:
  0.0 38.6 jit_solution(4792655758841139921)
XLA Ops:
  0.7 1.0 %pack.1 = bf16[272,128]{1,0:T(8,128)(2,1)S(1)} custom-call(f32[2,128,128]{2,1,0:T(8,128)} %specimen.1, s32[1,1,2,2]{3,2,1,0:T(2,128)} %centers.1, s32[1,1]{1,0:T(1,128)S(6)} %copy.8.cnt, s32[1,1,2]{2,1,0:T(1,128)} %helpers.1), custom_call_target="tpu_custom_call" | custom-call | flops 100000 | bytes 524288 | tf_op jit(solution)/shard_map/pack/pallas_call | solution.py:266
  1.6 9.1 %all-gather = bf16[1088,128]{1,0:T(8,128)(2,1)S(1)} all-gather(bf16[272,128]{1,0:T(8,128)(2,1)S(1)} %pack.1), channel_id=2, replica_groups=mesh['row'=8,'col'=4] {'col'}, dimensions={0}, use_global_device_ids=true | all-gather | bytes 348160 | tf_op jit(solution)/shard_map/all_gather | solution.py:314
  10.8 1.9 %collective-permute-start.1 = (bf16[4,272,128]{2,1,0:T(8,128)(2,1)S(1)}, bf16[4,272,128]{2,1,0:T(8,128)(2,1)S(1)}, u32[]{:S(2)}, u32[]{:S(2)}) collective-permute-start(bf16[4,272,128]{2,1,0:T(8,128)(2,1)S(1)} %bitcast.2), channel_id=1, source_target_pairs={{4,8},{12,16},{20,24},{8,4},{16,12},{24,20},{5,9},{13,17},{21,25},... | collective-permute-start | bytes 835592 | tf_op jit(solution)/shard_map/ppermute | solution.py:321
  12.7 1.7 %collective-permute-start = (bf16[4,272,128]{2,1,0:T(8,128)(2,1)S(1)}, bf16[4,272,128]{2,1,0:T(8,128)(2,1)S(1)}, u32[]{:S(2)}, u32[]{:S(2)}) collective-permute-start(bf16[4,272,128]{2,1,0:T(8,128)(2,1)S(1)} %bitcast.3), channel_id=1, source_target_pairs={{0,4},{8,12},{16,20},{24,28},{4,0},{12,8},{20,16},{28,24},{1,5},{9... | collective-permute-start | bytes 835592 | tf_op jit(solution)/shard_map/ppermute | solution.py:322
  14.4 1.8 %load.1 = (f32[4,2,256,256]{3,2,1,0:T(8,128)S(1)}, f32[256,256]{1,0:T(8,128)S(1)}, bf16[4,256,256]{2,1,0:T(8,128)(2,1)S(1)}) custom-call(f32[4,2,256,256]{3,2,1,0:T(8,128)} %probe.1, f32[1,1,1,256,256]{4,3,2,1,0:T(8,128)} %measured.1, bf16[4,256,256]{2,1,0:T(8,128)(2,1)} %constant.4.clone.tables), custom_call_target="tpu_custom_call" | custom-call | flops 100000000 | bytes 4194304 | tf_op jit(solution)/shard_map/load/pallas_call | solution.py:266
  16.2 2.4 %collective-permute-done.1.second = bf16[4,272,128]{2,1,0:T(8,128)(2,1)S(1)} collective-permute-done((bf16[4,272,128]{2,1,0:T(8,128)(2,1)S(1)}, bf16[4,272,128]{2,1,0:T(8,128)(2,1)S(1)}, u32[]{:S(2)}, u32[]{:S(2)}) %collective-permute-start.1) | collective-permute-done | bytes 278560 | tf_op jit(solution)/shard_map/ppermute | solution.py:321
  18.6 0.0 collective-permute-done.first
  18.6 3.4 %frame.1 = (bf16[272,256]{1,0:T(8,128)(2,1)S(1)}, bf16[272,256]{1,0:T(8,128)(2,1)S(1)}, bf16[272,256]{1,0:T(8,128)(2,1)S(1)}) custom-call(bf16[4,272,128]{2,1,0:T(8,128)(2,1)S(1)} %bitcast.4, bf16[4,272,128]{2,1,0:T(8,128)(2,1)S(1)} %collective-permute-done.first, bf16[4,272,128]{2,1,0:T(8,128)(2,1)S(1)} %collective-permute-done.1.second, ...), custom_call_target="tpu_custom_call" | custom-call | flops 2000000000 | bytes 4194304 | tf_op jit(solution)/shard_map/frame/pallas_call | solution.py:266
  22.0 0.2 collective-permute-start.2
  22.2 1.9 %collective-permute-start.3 = (bf16[272,256]{1,0:T(8,128)(2,1)S(1)}, bf16[272,256]{1,0:T(8,128)(2,1)S(1)}, u32[]{:S(2)}, u32[]{:S(2)}) collective-permute-start(bf16[272,256]{1,0:T(8,128)(2,1)S(1)} %get-tuple-element.16), channel_id=1, source_target_pairs={{4,8},{12,16},{20,24},{8,4},{16,12},{24,20},{5,9},{13,17},{21,25},... | collective-permute-start | bytes 417800 | tf_op jit(solution)/shard_map/ppermute | solution.py:335
  24.1 0.0 collective-permute-done.2.first
  24.1 4.4 %collective-permute-done.3.second = bf16[272,256]{1,0:T(8,128)(2,1)S(1)} collective-permute-done((bf16[272,256]{1,0:T(8,128)(2,1)S(1)}, bf16[272,256]{1,0:T(8,128)(2,1)S(1)}, u32[]{:S(2)}, u32[]{:S(2)}) %collective-permute-start.3) | collective-permute-done | bytes 139296 | tf_op jit(solution)/shard_map/ppermute | solution.py:335
  28.5 0.4 %fold.1 = bf16[4,256,128]{2,1,0:T(8,128)(2,1)S(1)} custom-call(bf16[272,256]{1,0:T(8,128)(2,1)S(1)} %get-tuple-element.14.centre, bf16[272,256]{1,0:T(8,128)(2,1)S(1)} %collective-permute-done.2.first, bf16[272,256]{1,0:T(8,128)(2,1)S(1)} %collective-permute-done.3.second), custom_call_target="tpu_custom_call" | custom-call | flops 1000000000 | bytes 1048576 | tf_op jit(solution)/shard_map/fold/pallas_call | solution.py:266
  28.9 9.0 %all_to_all.5 = bf16[4,256,128]{2,1,0:T(8,128)(2,1)S(1)} all-to-all(bf16[4,256,128]{2,1,0:T(8,128)(2,1)S(1)} %fold.1), channel_id=1, replica_groups=mesh['row'=8,'col'=4] {'col'}, dimensions={0} | all-to-all | bytes 524288 | tf_op jit(solution)/shard_map/all_to_all | solution.py:345
  37.9 0.7 %convert_reduce_fusion = f32[256,128]{1,0:T(8,128)} fusion(bf16[4,256,128]{2,1,0:T(8,128)(2,1)S(1)} %all_to_all.5), kind=kLoop, calls=%fused_computation | loop fusion | flops 229376 | bytes 393216 | tf_op jit(solution)/shard_map/reduce_sum | solution.py:346
Async XLA Ops:
  10.8 7.9 %collective-permute-start.1 = (bf16[4,272,128]{2,1,0:T(8,128)(2,1)S(1)}, bf16[4,272,128]{2,1,0:T(8,128)(2,1)S(1)}, u32[]{:S(2)}, u32[]{:S(2)}) collective-permute-start(bf16[4,272,128]{2,1,0:T(8,128)(2,1)S(1)} %bitcast.2), channel_id=1, source_target_pairs={{4,8},{12,16},{20,24},{8,4},{16,12},{24,20},{5,9},{13,17},{21,25},... | collective-permute-start | bytes 835592 | tf_op jit(solution)/shard_map/ppermute | solution.py:321
  12.7 5.9 %collective-permute-start = (bf16[4,272,128]{2,1,0:T(8,128)(2,1)S(1)}, bf16[4,272,128]{2,1,0:T(8,128)(2,1)S(1)}, u32[]{:S(2)}, u32[]{:S(2)}) collective-permute-start(bf16[4,272,128]{2,1,0:T(8,128)(2,1)S(1)} %bitcast.3), channel_id=1, source_target_pairs={{0,4},{8,12},{16,20},{24,28},{4,0},{12,8},{20,16},{28,24},{1,5},{9... | collective-permute-start | bytes 835592 | tf_op jit(solution)/shard_map/ppermute | solution.py:322
  22.0 2.1 %collective-permute-start.2 = (bf16[272,256]{1,0:T(8,128)(2,1)S(1)}, bf16[272,256]{1,0:T(8,128)(2,1)S(1)}, u32[]{:S(2)}, u32[]{:S(2)}) collective-permute-start(bf16[272,256]{1,0:T(8,128)(2,1)S(1)} %get-tuple-element.15), channel_id=1, source_target_pairs={{0,4},{8,12},{16,20},{24,28},{4,0},{12,8},{20,16},{28,24},{1,5},{9... | collective-permute-start | bytes 417800 | tf_op jit(solution)/shard_map/ppermute | solution.py:336
  22.2 6.4 %collective-permute-start.3 = (bf16[272,256]{1,0:T(8,128)(2,1)S(1)}, bf16[272,256]{1,0:T(8,128)(2,1)S(1)}, u32[]{:S(2)}, u32[]{:S(2)}) collective-permute-start(bf16[272,256]{1,0:T(8,128)(2,1)S(1)} %get-tuple-element.16), channel_id=1, source_target_pairs={{4,8},{12,16},{20,24},{8,4},{16,12},{24,20},{5,9},{13,17},{21,25},... | collective-permute-start | bytes 417800 | tf_op jit(solution)/shard_map/ppermute | solution.py:335

commit v3 on v2

--- a/solution.py
+++ b/solution.py
@@ -102,7 +102,7 @@
 
 
 def frame_kernel(
-    band, first, second, probe, amplitude, tables,
+    band, first, second_lo, second_hi, probe, amplitude, tables,
     to_second, to_first, centre, wide, far, spread,
 ):
     columns = band.shape[0]
@@ -130,8 +130,14 @@
         c = jnp.clip(c, 0, columns - 1)
         for p in range(2):
             part = pl.ds(p * tile, tile)
-            above = jnp.where(odd, first[c, part], second[c, part])
-            below = jnp.where(odd, second[c, part], first[c, part])
+            pair = second_lo.shape[0]
+            other = jnp.where(
+                c < pair,
+                second_lo[jnp.minimum(c, pair - 1), part],
+                second_hi[jnp.maximum(c - pair, 0), part],
+            )
+            above = jnp.where(odd, first[c, part], other)
+            below = jnp.where(odd, other, first[c, part])
             for i, block in enumerate((above, band[c, part], below)):
                 wide[p, i * tile : (i + 1) * tile, d * tile : (d + 1) * tile] = jnp.where(
                     inside, block.astype(F32), 0.0
@@ -241,7 +247,7 @@
         out[2 * tile :] = info
 
 
-def fold_kernel(centre, first, second, out):
+def fold_kernel(centre, second, first, out):
     columns, height, tile = out.shape
     extent = centre.shape[1]
     half = extent // 2
@@ -318,29 +324,32 @@
     for start in (0, 1):
         pairs = [(i, i + 1) for i in range(start, rows - 1, 2)]
         swaps.append(pairs + [(b, a) for a, b in pairs])
-    second = lax.ppermute(band, "row", swaps[1])
+    pair = columns // 2
+    second = [
+        lax.ppermute(part, "row", swaps[1]) for part in (band[:pair], band[pair:])
+    ]
     first = lax.ppermute(band, "row", swaps[0])
     to_second, to_first, centre = call(
         frame_kernel, "frame",
         (part, part, part),
-        [VMEM] * 6,
+        [VMEM] * 7,
         [
             pltpu.VMEM((2, tile + 2 * half, 3 * tile), F32),
             pltpu.VMEM((modes, 2, extent, extent), F32),
             pltpu.VMEM((2, tile + 2 * half, extent), F32),
         ],
         2 * 10**9, 2**22,
-        band, first, second, probe, amplitude, tables,
-    )
+        band, first, *second, probe, amplitude, tables,
+    )
+    from_first = lax.ppermute(to_first, "row", swaps[0])
     from_second = lax.ppermute(to_second, "row", swaps[1])
-    from_first = lax.ppermute(to_first, "row", swaps[0])
     summed = call(
         fold_kernel, "fold",
         jax.ShapeDtypeStruct((columns, height, tile), BF16),
         [VMEM] * 3,
         [],
         10**9, 2**20,
-        centre, from_first, from_second,
+        centre, from_second, from_first,
     )
     shares = lax.all_to_all(summed, "col", split_axis=0, concat_axis=0, tiled=True)
     return jnp.sum(shares.astype(F32), axis=0).reshape(2, tile, tile)

time: 38.8 us -> 40.4 us (1.041)
  starting transfers between devices: 5.74 us -> 9.23 us
  waiting for transfers between devices: 6.85 us -> 4.18 us
    ppermute x1 -> x2, starting transfers between devices: 1.91 us -> 5.56 us  [per_device(): lax.ppermute(part, 'row', swaps[1])]
    ppermute x1, starting transfers between devices: 1.74 us -> 0.01 us  [per_device(): first = lax.ppermute(band, 'row', swaps[0])]
    ppermute x1, waiting for transfers between devices: 4.44 us -> 2.7 us  [per_device(): from_second = lax.ppermute(to_second, 'row', swaps[1])]
    ppermute x1, starting transfers between devices: 1.91 us -> 3.09 us  [per_device(): from_second = lax.ppermute(to_second, 'row', swaps[1])]
    ppermute x1 -> x2, waiting for transfers between devices: 2.41 us -> 1.47 us  [per_device(): lax.ppermute(part, 'row', swaps[1])]
    ppermute x1, starting transfers between devices: 0.17 us -> 0.58 us  [per_device(): from_first = lax.ppermute(to_first, 'row', swaps[0])]
  transfers between devices with their start and end apart: 4 -> 5, of which waited for: 2 -> 2; matrix products, arithmetic and copies ran while one was open for 0% -> 0% of each run, Pallas kernels for 5% -> 4%
where the time goes in v3:
time: 40.4 us; the launch traced here: 39.9 us
  blocking collectives  18.5 us (46%)
  starting transfers between devices  9.23 us (23%)
  Pallas kernels  6.57 us (16%)
  waiting for transfers between devices  4.18 us (10%)
  between operations  0.73 us (2%)
  other arithmetic  0.69 us (2%)
    all_to_all x1, blocking collectives, per_device(): lax.all_to_all(summed, 'col', split_axis=0, concat_axis=0, tiled=True)  9.33 us
    all_gather x1, blocking collectives, per_device(): band = lax.all_gather(packed, 'col')  9.13 us
    pallas_call x4, Pallas kernels, call(): pl.pallas_call(kernel, out_shape=out_shape, in_specs=in_specs, out_specs=...  6.57 us
    ppermute x2, starting transfers between devices, per_device(): lax.ppermute(part, 'row', swaps[1])  5.56 us
    ppermute x1, starting transfers between devices, per_device(): from_second = lax.ppermute(to_second, 'row', swaps[1])  3.09 us
    ppermute x1, waiting for transfers between devices, per_device(): from_second = lax.ppermute(to_second, 'row', swaps[1])  2.7 us
    ppermute x2, waiting for transfers between devices, per_device(): lax.ppermute(part, 'row', swaps[1])  1.47 us
  transfers between devices with their start and end apart: 5, of which 2 were waited for; matrix products, arithmetic and copies ran while one was open for 0% of the time, Pallas kernels for 4%

profile of v3, /device:TPU:8, one launch (start us, length us, event | category | flops | bytes accessed | tf_op | source)
XLA Modules:
  0.0 39.9 jit_solution(14298741245353836551)
XLA Ops:
  0.7 1.0 %pack.1 = bf16[272,128]{1,0:T(8,128)(2,1)S(1)} custom-call(f32[2,128,128]{2,1,0:T(8,128)} %specimen.1, s32[1,1,2,2]{3,2,1,0:T(2,128)} %centers.1, s32[1,1]{1,0:T(1,128)S(6)} %copy.8.cnt, s32[1,1,2]{2,1,0:T(1,128)} %helpers.1), custom_call_target="tpu_custom_call" | custom-call | flops 100000 | bytes 524288 | tf_op jit(solution)/shard_map/pack/pallas_call | solution.py:272
  1.6 9.1 %all-gather = bf16[1088,128]{1,0:T(8,128)(2,1)S(1)} all-gather(bf16[272,128]{1,0:T(8,128)(2,1)S(1)} %pack.1), channel_id=2, replica_groups=mesh['row'=8,'col'=4] {'col'}, dimensions={0}, use_global_device_ids=true | all-gather | bytes 348160 | tf_op jit(solution)/shard_map/all_gather | solution.py:320
  10.8 0.0 collective-permute-start
  10.8 2.5 %collective-permute-start.1 = (bf16[2,272,128]{2,1,0:T(8,128)(2,1)S(1)}, bf16[2,272,128]{2,1,0:T(8,128)(2,1)S(1)}, u32[]{:S(2)}, u32[]{:S(2)}) collective-permute-start(bf16[2,272,128]{2,1,0:T(8,128)(2,1)S(1)} %bitcast.7), channel_id=1, source_target_pairs={{4,8},{12,16},{20,24},{8,4},{16,12},{24,20},{5,9},{13,17},{21,25},... | collective-permute-start | bytes 417800 | tf_op jit(solution)/shard_map/ppermute | solution.py:329
  13.3 3.1 %collective-permute-start.2 = (bf16[2,272,128]{2,1,0:T(8,128)(2,1)S(1)}, bf16[2,272,128]{2,1,0:T(8,128)(2,1)S(1)}, u32[]{:S(2)}, u32[]{:S(2)}) collective-permute-start(bf16[2,272,128]{2,1,0:T(8,128)(2,1)S(1)} %bitcast.6), channel_id=1, source_target_pairs={{4,8},{12,16},{20,24},{8,4},{16,12},{24,20},{5,9},{13,17},{21,25},... | collective-permute-start | bytes 417800 | tf_op jit(solution)/shard_map/ppermute | solution.py:329
  16.4 1.8 %load.1 = (f32[4,2,256,256]{3,2,1,0:T(8,128)S(1)}, f32[256,256]{1,0:T(8,128)S(1)}, bf16[4,256,256]{2,1,0:T(8,128)(2,1)S(1)}) custom-call(f32[4,2,256,256]{3,2,1,0:T(8,128)} %probe.1, f32[1,1,1,256,256]{4,3,2,1,0:T(8,128)} %measured.1, bf16[4,256,256]{2,1,0:T(8,128)(2,1)} %constant.4.clone.tables), custom_call_target="tpu_custom_call" | custom-call | flops 100000000 | bytes 4194304 | tf_op jit(solution)/shard_map/load/pallas_call | solution.py:272
  18.2 0.0 collective-permute-done.1.second_lo
  18.2 1.5 %collective-permute-done.2.second_hi = bf16[2,272,128]{2,1,0:T(8,128)(2,1)S(1)} collective-permute-done((bf16[2,272,128]{2,1,0:T(8,128)(2,1)S(1)}, bf16[2,272,128]{2,1,0:T(8,128)(2,1)S(1)}, u32[]{:S(2)}, u32[]{:S(2)}) %collective-permute-start.2) | collective-permute-done | bytes 139296 | tf_op jit(solution)/shard_map/ppermute | solution.py:329
  19.6 0.0 collective-permute-done.first
  19.6 3.4 %frame.1 = (bf16[272,256]{1,0:T(8,128)(2,1)S(1)}, bf16[272,256]{1,0:T(8,128)(2,1)S(1)}, bf16[272,256]{1,0:T(8,128)(2,1)S(1)}) custom-call(bf16[4,272,128]{2,1,0:T(8,128)(2,1)S(1)} %bitcast.5, bf16[4,272,128]{2,1,0:T(8,128)(2,1)S(1)} %collective-permute-done.first, bf16[2,272,128]{2,1,0:T(8,128)(2,1)S(1)} %collective-permute-done.1.second_lo, ...), custom_call_target="tpu_custom_call" | custom-call | flops 2000000000 | bytes 4194304 | tf_op jit(solution)/shard_map/frame/pallas_call | solution.py:272
  23.1 3.1 %collective-permute-start.3 = (bf16[272,256]{1,0:T(8,128)(2,1)S(1)}, bf16[272,256]{1,0:T(8,128)(2,1)S(1)}, u32[]{:S(2)}, u32[]{:S(2)}) collective-permute-start(bf16[272,256]{1,0:T(8,128)(2,1)S(1)} %get-tuple-element.15), channel_id=1, source_target_pairs={{4,8},{12,16},{20,24},{8,4},{16,12},{24,20},{5,9},{13,17},{21,25},... | collective-permute-start | bytes 417800 | tf_op jit(solution)/shard_map/ppermute | solution.py:345
  26.2 0.6 %collective-permute-start.4 = (bf16[272,256]{1,0:T(8,128)(2,1)S(1)}, bf16[272,256]{1,0:T(8,128)(2,1)S(1)}, u32[]{:S(2)}, u32[]{:S(2)}) collective-permute-start(bf16[272,256]{1,0:T(8,128)(2,1)S(1)} %get-tuple-element.16), channel_id=1, source_target_pairs={{0,4},{8,12},{16,20},{24,28},{4,0},{12,8},{20,16},{28,24},{1,5},{9... | collective-permute-start | bytes 417800 | tf_op jit(solution)/shard_map/ppermute | solution.py:344
  26.7 2.7 %collective-permute-done.3.second = bf16[272,256]{1,0:T(8,128)(2,1)S(1)} collective-permute-done((bf16[272,256]{1,0:T(8,128)(2,1)S(1)}, bf16[272,256]{1,0:T(8,128)(2,1)S(1)}, u32[]{:S(2)}, u32[]{:S(2)}) %collective-permute-start.3) | collective-permute-done | bytes 139296 | tf_op jit(solution)/shard_map/ppermute | solution.py:345
  29.4 0.0 collective-permute-done.4.first
  29.4 0.4 %fold.1 = bf16[4,256,128]{2,1,0:T(8,128)(2,1)S(1)} custom-call(bf16[272,256]{1,0:T(8,128)(2,1)S(1)} %get-tuple-element.14.centre, bf16[272,256]{1,0:T(8,128)(2,1)S(1)} %collective-permute-done.3.second, bf16[272,256]{1,0:T(8,128)(2,1)S(1)} %collective-permute-done.4.first), custom_call_target="tpu_custom_call" | custom-call | flops 1000000000 | bytes 1048576 | tf_op jit(solution)/shard_map/fold/pallas_call | solution.py:272
  29.9 9.3 %all_to_all.5 = bf16[4,256,128]{2,1,0:T(8,128)(2,1)S(1)} all-to-all(bf16[4,256,128]{2,1,0:T(8,128)(2,1)S(1)} %fold.1), channel_id=1, replica_groups=mesh['row'=8,'col'=4] {'col'}, dimensions={0} | all-to-all | bytes 524288 | tf_op jit(solution)/shard_map/all_to_all | solution.py:354
  39.2 0.7 %convert_reduce_fusion = f32[256,128]{1,0:T(8,128)} fusion(bf16[4,256,128]{2,1,0:T(8,128)(2,1)S(1)} %all_to_all.5), kind=kLoop, calls=%fused_computation | loop fusion | flops 229376 | bytes 393216 | tf_op jit(solution)/shard_map/reduce_sum | solution.py:355
  (1 shorter events, 0.0 us)
Async XLA Ops:
  10.8 8.9 %collective-permute-start = (bf16[4,272,128]{2,1,0:T(8,128)(2,1)S(1)}, bf16[4,272,128]{2,1,0:T(8,128)(2,1)S(1)}, u32[]{:S(2)}, u32[]{:S(2)}) collective-permute-start(bf16[4,272,128]{2,1,0:T(8,128)(2,1)S(1)} %bitcast.4), channel_id=1, source_target_pairs={{0,4},{8,12},{16,20},{24,28},{4,0},{12,8},{20,16},{28,24},{1,5},{9... | collective-permute-start | bytes 835592 | tf_op jit(solution)/shard_map/ppermute | solution.py:331
  10.8 7.4 %collective-permute-start.1 = (bf16[2,272,128]{2,1,0:T(8,128)(2,1)S(1)}, bf16[2,272,128]{2,1,0:T(8,128)(2,1)S(1)}, u32[]{:S(2)}, u32[]{:S(2)}) collective-permute-start(bf16[2,272,128]{2,1,0:T(8,128)(2,1)S(1)} %bitcast.7), channel_id=1, source_target_pairs={{4,8},{12,16},{20,24},{8,4},{16,12},{24,20},{5,9},{13,17},{21,25},... | collective-permute-start | bytes 417800 | tf_op jit(solution)/shard_map/ppermute | solution.py:329
  13.3 6.4 %collective-permute-start.2 = (bf16[2,272,128]{2,1,0:T(8,128)(2,1)S(1)}, bf16[2,272,128]{2,1,0:T(8,128)(2,1)S(1)}, u32[]{:S(2)}, u32[]{:S(2)}) collective-permute-start(bf16[2,272,128]{2,1,0:T(8,128)(2,1)S(1)} %bitcast.6), channel_id=1, source_target_pairs={{4,8},{12,16},{20,24},{8,4},{16,12},{24,20},{5,9},{13,17},{21,25},... | collective-permute-start | bytes 417800 | tf_op jit(solution)/shard_map/ppermute | solution.py:329
  23.1 6.4 %collective-permute-start.3 = (bf16[272,256]{1,0:T(8,128)(2,1)S(1)}, bf16[272,256]{1,0:T(8,128)(2,1)S(1)}, u32[]{:S(2)}, u32[]{:S(2)}) collective-permute-start(bf16[272,256]{1,0:T(8,128)(2,1)S(1)} %get-tuple-element.15), channel_id=1, source_target_pairs={{4,8},{12,16},{20,24},{8,4},{16,12},{24,20},{5,9},{13,17},{21,25},... | collective-permute-start | bytes 417800 | tf_op jit(solution)/shard_map/ppermute | solution.py:345
  26.2 3.3 %collective-permute-start.4 = (bf16[272,256]{1,0:T(8,128)(2,1)S(1)}, bf16[272,256]{1,0:T(8,128)(2,1)S(1)}, u32[]{:S(2)}, u32[]{:S(2)}) collective-permute-start(bf16[272,256]{1,0:T(8,128)(2,1)S(1)} %get-tuple-element.16), channel_id=1, source_target_pairs={{0,4},{8,12},{16,20},{24,28},{4,0},{12,8},{20,16},{28,24},{1,5},{9... | collective-permute-start | bytes 417800 | tf_op jit(solution)/shard_map/ppermute | solution.py:344

commit v4 on v2

v4 whole, which is shorter than its diff:
```python
import functools
import math

import jax
import jax.numpy as jnp
import numpy as np
from jax import lax
from jax.experimental import pallas as pl
from jax.experimental.pallas import tpu as pltpu
from jax.sharding import PartitionSpec as P

F32 = jnp.float32
BF16 = jnp.bfloat16
INFO = 16
VMEM = pl.BlockSpec(memory_space=pltpu.VMEM)
SMEM = pl.BlockSpec(memory_space=pltpu.SMEM)
HBM = pl.BlockSpec(memory_space=pltpu.HBM)


def dft_tables(extent):
    half = extent // 2
    steps = np.arange(extent, dtype=np.int32)
    angles = (steps[:, None] * steps[None, :] % extent).astype(np.float32)
    angles = angles * np.float32(2.0 * math.pi / extent)
    scaling = np.float32(1.0 / math.sqrt(extent))
    real = (np.cos(angles) * scaling).astype(BF16)
    imag = (-np.sin(angles) * scaling).astype(BF16)
    tables = []
    for parity in (0, 1):
        re, im = real[:half, parity::2], imag[:half, parity::2]
        right = np.concatenate(
            [np.concatenate([re, im], 1), np.concatenate([-im, re], 1)], 0
        )
        tables += [right, np.ascontiguousarray(right.T)]
    return jnp.asarray(np.stack(tables))


def dot(a, b):
    return jnp.dot(a, b, preferred_element_type=F32)


def quarters(tl, tr, bl, br):
    return jnp.concatenate(
        [jnp.concatenate([tl, tr], 1), jnp.concatenate([bl, br], 1)], 0
    )


def iota(shape, dim):
    return lax.broadcasted_iota(jnp.int32, shape, dim)


def fetch(pairs, sems):
    copies = [
        pltpu.make_async_copy(source, target, sems.at[i])
        for i, (source, target) in enumerate(pairs)
    ]
    for copy in copies:
        copy.start()
    return copies


def pack_kernel(specimen, centers, cnt, helpers, out, tile_v, cen, hlp, sems):
    copies = fetch(((specimen, tile_v), (centers, cen), (helpers, hlp)), sems)
    for copy in copies:
        copy.wait()
    tile = tile_v.shape[1]
    lanes = tile_v.shape[2]
    rows, cols = iota((INFO, lanes), 0), iota((INFO, lanes), 1)
    info = jnp.where(rows == 0, -1.0, 0.0)
    for j in range(centers.shape[2]):
        helper = jnp.where(j < cnt[0, 0], hlp[0, 0, j], -1)
        for r, value in enumerate((helper, cen[0, 0, j, 0], cen[0, 0, j, 1])):
            info = jnp.where((rows == r) & (cols == j), value.astype(F32), info)
    info = info.astype(BF16)
    for p in range(2):
        out[p * tile : (p + 1) * tile] = tile_v[p].astype(BF16)
    out[2 * tile :] = info


def gather_columns(get, source, col, columns, shape):
    lane = iota(shape, 1)
    beside = own = jnp.zeros(shape, F32)
    for c in range(columns):
        block = get(c)
        near = ((source == c + 1) & (lane >= col)) | ((source == c - 1) & (lane < col))
        beside = jnp.where(near, block, beside)
        own = jnp.where(source == c, block, own)
    return jnp.concatenate([beside, own], 1)


def first_product(probe, patch, tables):
    half = patch[0].shape[1] // 2
    wr = probe[0] * patch[0] - probe[1] * patch[1]
    wi = probe[0] * patch[1] + probe[1] * patch[0]
    out = []
    for sign, table in zip((1, -1), tables):
        folded = jnp.concatenate(
            [wr[:, :half] + sign * wr[:, half:], wi[:, :half] + sign * wi[:, half:]], 1
        )
        out.append(dot(folded.astype(BF16), table))
    return out


def prepare_kernel(
    band, probe, measured, tables,
    info_out, amplitude, tables_out, probe_out, half_out, raw, raw_tables, raw_probe, groups, sems,
):
    copies = fetch(
        ((measured, raw), (tables, raw_tables), (probe, raw_probe)), sems
    )
    columns = band.shape[0]
    lanes = band.shape[2]
    tile = (band.shape[1] - INFO) // 2
    extent = raw.shape[-1]
    half = extent // 2
    modes = raw_probe.shape[0]
    me = lax.axis_index("col").astype(F32)

    code = jnp.zeros((1, lanes), F32)
    for c in range(columns):
        info = band[c, 2 * tile :].astype(F32)
        hit = info[0:1] == me
        code += jnp.where(hit, c * 128.0 * 128.0 + info[1:2] * 128.0 + info[2:3], 0.0)
    code = jnp.sum(code).astype(jnp.int32)
    source = code // (128 * 128)
    row = code // 128 % 128
    col = code % 128
    which = iota((INFO, extent), 0)
    info = jnp.where(which == 0, source, jnp.where(which == 1, col, row))
    info_out[...] = info.astype(F32).astype(BF16)

    shape = (extent, extent)

    def original(i):
        return jnp.where(i < half, 2 * i, 2 * (i - half) + 1)

    copies[0].wait()
    sort = (iota(shape, 1) == original(iota(shape, 0))).astype(F32).astype(BF16)
    sort_t = (iota(shape, 0) == original(iota(shape, 1))).astype(F32).astype(BF16)
    value = raw[0, 0, 0]
    coarse = value.astype(BF16)
    fine = (value - coarse.astype(F32)).astype(BF16)
    amplitude[...] = sum(
        dot(dot(sort, part).astype(BF16), sort_t) for part in (coarse, fine)
    )

    def roller(old, new, shift, parity):
        wrapped = new % half < shift
        hit = (old + shift - jnp.where(old % half + shift >= half, half, 0)) == new
        sign = jnp.where(wrapped, -1.0, 1.0) if parity else 1.0
        return jnp.where(hit, sign, 0.0).astype(BF16)

    copies[1].wait()
    i, j = iota(shape, 0), iota(shape, 1)
    for parity in range(2):
        right, left = raw_tables[2 * parity], raw_tables[2 * parity + 1]
        for axis, shift in enumerate((col, row)):
            rolled = dot(left, roller(i, j, shift, parity)).astype(BF16)
            rolled_t = dot(roller(j, i, shift, parity), right).astype(BF16)
            tables_out[4 * axis + parity] = rolled_t if axis == 0 else rolled
            tables_out[4 * axis + 2 + parity] = rolled if axis == 0 else rolled_t

    copies[2].wait()
    count = extent // 8
    base = row // 8
    step = row % 8
    lane = iota((extent, half), 1)
    sub = iota((count, 8, extent), 1)
    for k in range(modes):
        for p in range(2):
            lo = pltpu.roll(raw_probe[k, p, :, :half], col, 1)
            hi = pltpu.roll(raw_probe[k, p, :, half:], col, 1)
            turned = jnp.concatenate(
                [jnp.where(lane < col, hi, lo), jnp.where(lane < col, lo, hi)], 1
            )
            turned = pltpu.roll(turned.reshape(count, 8, extent), step, 1)
            turned = jnp.where(
                sub < step, jnp.concatenate([turned[-1:], turned[:-1]], 0), turned
            )
            groups[:count] = turned
            groups[count:] = turned
            probe_out[k, p] = groups[pl.ds(count - base, count)].reshape(extent, extent)

    patch = [
        gather_columns(
            lambda c: band[c, p * tile : (p + 1) * tile].astype(F32),
            source, col, columns, (tile, tile),
        )
        for p in range(2)
    ]
    for k in range(modes):
        products = first_product(
            [probe_out[k, p, half:] for p in range(2)], patch, (tables_out[0], tables_out[1])
        )
        for parity in range(2):
            half_out[k, parity] = products[parity]


def frame_kernel(
    first, second, info, amplitude, tables, probe, half_own,
    to_rows, centre, far,
):
    columns = first.shape[0]
    tile = (first.shape[1] - INFO) // 2
    extent = probe.shape[-1]
    half = extent // 2
    modes = probe.shape[0]
    odd = lax.axis_index("row") % 2
    source, col, row = (
        info[r : r + 1, :tile].astype(F32).astype(jnp.int32) for r in range(3)
    )
    from_above = (iota((tile, tile), 0) >= row).astype(jnp.int32)
    from_first = from_above == odd
    patch = []
    for p in range(2):
        part = slice(p * tile, (p + 1) * tile)
        patch.append(
            gather_columns(
                lambda c: jnp.where(
                    from_first, first[c, part].astype(F32), second[c, part].astype(F32)
                ),
                source, col, columns, (tile, tile),
            )
        )

    right, right_back = (tables[0], tables[1]), (tables[2], tables[3])
    left, left_back = (tables[4], tables[5]), (tables[6], tables[7])
    intensity = [jnp.zeros((half, extent), F32) for _ in range(2)]
    for k in range(modes):
        even, odds = first_product(
            [probe[k, p, :half] for p in range(2)], patch, right
        )
        for parity, sign in ((0, 1), (1, -1)):
            e = even + sign * half_own[k, 0]
            o = odds + sign * half_own[k, 1]
            folded = quarters(e[:, :half], o[:, :half], e[:, half:], o[:, half:])
            f = dot(left[parity], folded.astype(BF16))
            far[k, parity] = f
            intensity[parity] += f[:half] * f[:half] + f[half:] * f[half:]
    factor = [
        1.0
        - amplitude[i * half : (i + 1) * half]
        * lax.rsqrt(jnp.maximum(intensity[i], 0.25))
        for i in range(2)
    ]
    grad = [[jnp.zeros((half, extent), F32) for _ in range(2)] for _ in range(2)]
    for k in range(modes):
        c = []
        for parity in range(2):
            f = far[k, parity]
            c.append(
                (f * jnp.concatenate([factor[parity], factor[parity]], 0)).astype(BF16)
            )
        a = dot(
            quarters(c[0][:half, :half], c[0][half:, :half], c[1][:half, :half], c[1][half:, :half]),
            right_back[0],
        )
        b = dot(
            quarters(c[0][:half, half:], c[0][half:, half:], c[1][:half, half:], c[1][half:, half:]),
            right_back[1],
        )
        lo, hi = (a + b).astype(BF16), (a - b).astype(BF16)
        turned = []
        for parity in range(2):
            l = lo[parity * half : (parity + 1) * half]
            h = hi[parity * half : (parity + 1) * half]
            turned.append(
                dot(
                    left_back[parity],
                    quarters(l[:, :half], h[:, :half], l[:, half:], h[:, half:]),
                )
            )
        for i, chi in enumerate((turned[0] + turned[1], turned[0] - turned[1])):
            cr, ci = chi[:half], chi[half:]
            pr = probe[k, 0, i * half : (i + 1) * half]
            pi = probe[k, 1, i * half : (i + 1) * half]
            grad[0][i] += pr * cr + pi * ci
            grad[1][i] += pr * ci - pi * cr
    for p in range(2):
        to_rows[p * tile : (p + 1) * tile] = grad[p][0].astype(BF16)
        centre[p * tile : (p + 1) * tile] = grad[p][1].astype(BF16)
    for out in (to_rows, centre):
        out[2 * tile :] = info[...]


def fold_kernel(centre, second, first, out):
    columns, height, tile = out.shape
    odd = lax.axis_index("row") % 2
    shape = (tile, tile)
    lane = iota(shape, 1)
    totals = [[jnp.zeros(shape, F32) for _ in range(columns)] for _ in range(2)]
    for which, part in enumerate((centre, second, first)):
        source, col, row = (
            part[height + r : height + r + 1, :tile].astype(F32).astype(jnp.int32)
            for r in range(3)
        )
        before = (iota(shape, 0) < row).astype(jnp.int32)
        taken = before == (odd if which == 2 else 1 - odd)
        for p in range(2):
            block = part[p * tile : (p + 1) * tile].astype(F32)
            beside, own = block[:, :tile], block[:, tile:]
            if which:
                beside, own = jnp.where(taken, beside, 0.0), jnp.where(taken, own, 0.0)
            for c in range(columns):
                near = ((source == c + 1) & (lane >= col)) | ((source == c - 1) & (lane < col))
                totals[p][c] += jnp.where(near, beside, 0.0) + jnp.where(source == c, own, 0.0)
    for p in range(2):
        for c in range(columns):
            out[c, p * tile : (p + 1) * tile] = totals[p][c].astype(BF16)


def call(kernel, name, out_shape, in_specs, scratch, flops, moved, *args):
    args = [
        pltpu.with_memory_space_constraint(arg, pltpu.HBM) if spec is HBM else arg
        for arg, spec in zip(args, in_specs)
    ]
    return pl.pallas_call(
        kernel,
        out_shape=out_shape,
        in_specs=in_specs,
        out_specs=jax.tree.map(lambda _: VMEM, out_shape),
        scratch_shapes=scratch,
        compiler_params=pltpu.CompilerParams(vmem_limit_bytes=24 * 2**20),
        cost_estimate=pl.CostEstimate(flops=flops, bytes_accessed=moved, transcendentals=0),
        name=name,
    )(*args)


def per_device(specimen, probe, measured, centers, frame_counts, helper_cols):
    extent = probe.shape[-1]
    half = extent // 2
    tile = specimen.shape[1]
    modes = probe.shape[0]
    columns = lax.axis_size("col")
    height = 2 * tile
    part = jax.ShapeDtypeStruct((height + INFO, extent), BF16)
    dma = pltpu.SemaphoreType.DMA

    packed = call(
        pack_kernel, "pack",
        jax.ShapeDtypeStruct((height + INFO, tile), BF16),
        [HBM, HBM, SMEM, HBM],
        [
            pltpu.VMEM(specimen.shape, F32),
            pltpu.SMEM(centers.shape, jnp.int32),
            pltpu.SMEM(helper_cols.shape, jnp.int32),
            dma((3,)),
        ],
        10**5, 2**19,
        specimen, centers, frame_counts, helper_cols,
    )
    band = lax.all_gather(packed, "col")

    rows = lax.axis_size("row")
    swaps = []
    for start in (0, 1):
        pairs = [(i, i + 1) for i in range(start, rows - 1, 2)]
        swaps.append(pairs + [(b, a) for a, b in pairs])
    second = lax.ppermute(band, "row", swaps[1])
    first = lax.ppermute(band, "row", swaps[0])
    tables = dft_tables(extent)
    prepared = call(
        prepare_kernel, "prepare",
        (
            jax.ShapeDtypeStruct((INFO, extent), BF16),
            jax.ShapeDtypeStruct((extent, extent), F32),
            jax.ShapeDtypeStruct((8, extent, extent), BF16),
            jax.ShapeDtypeStruct(probe.shape, F32),
            jax.ShapeDtypeStruct((modes, 2, tile, extent), F32),
        ),
        [VMEM, HBM, HBM, HBM],
        [
            pltpu.VMEM(measured.shape, F32),
            pltpu.VMEM(tables.shape, BF16),
            pltpu.VMEM(probe.shape, F32),
            pltpu.VMEM((extent // 4, 8, extent), F32),
            dma((3,)),
        ],
        10**9, 2**22,
        band, probe, measured, tables,
    )
    to_rows, centre = call(
        frame_kernel, "frame",
        (part, part),
        [VMEM] * 7,
        [pltpu.VMEM((modes, 2, extent, extent), F32)],
        2 * 10**9, 2**22,
        first, second, *prepared,
    )
    from_first = lax.ppermute(to_rows, "row", swaps[0])
    from_second = lax.ppermute(to_rows, "row", swaps[1])
    summed = call(
        fold_kernel, "fold",
        jax.ShapeDtypeStruct((columns, height, tile), BF16),
        [VMEM] * 3,
        [],
        10**9, 2**20,
        centre, from_second, from_first,
    )
    shares = lax.all_to_all(summed, "col", split_axis=0, concat_axis=0, tiled=True)
    return jnp.sum(shares.astype(F32), axis=0).reshape(2, tile, tile)


def solution(mesh):
    return jax.shard_map(
        per_device,
        mesh=mesh,
        in_specs=(
            P(None, "row", "col"),
            P(),
            P("row", "col", None, None, None),
            P("row", "col", None, None),
            P("row", "col"),
            P("row", "col", None),
        ),
        out_specs=P(None, "row", "col"),
        check_vma=False,
    )
```

time: 38.8 us -> 38.2 us (0.985)
  waiting for transfers between devices: 6.85 us -> 5.65 us
  Pallas kernels: 6.53 us -> 7.1 us
    ppermute x1, waiting for transfers between devices: 2.41 us -> 1.21 us  [per_device(): second = lax.ppermute(band, 'row', swaps[1])]
    pallas_call x4, Pallas kernels: 6.53 us -> 7.1 us  [call(): pl.pallas_call(kernel, out_shape=out_shape, in_specs=in_specs, out_specs=...]
  transfers between devices with their start and end apart: 4 -> 4, of which waited for: 2 -> 2; matrix products, arithmetic and copies ran while one was open for 0% -> 0% of each run, Pallas kernels for 5% -> 8%
where the time goes in v4:
time: 38.2 us; the launch traced here: 38 us
  blocking collectives  18.1 us (47%)
  Pallas kernels  7.1 us (19%)
  starting transfers between devices  5.74 us (15%)
  waiting for transfers between devices  5.65 us (15%)
  between operations  0.7 us (2%)
  other arithmetic  0.69 us (2%)
    all_gather x1, blocking collectives, per_device(): band = lax.all_gather(packed, 'col')  9.13 us
    all_to_all x1, blocking collectives, per_device(): lax.all_to_all(summed, 'col', split_axis=0, concat_axis=0, tiled=True)  8.94 us
    pallas_call x4, Pallas kernels, call(): pl.pallas_call(kernel, out_shape=out_shape, in_specs=in_specs, out_specs=...  7.1 us
    ppermute x1, waiting for transfers between devices, per_device(): from_second = lax.ppermute(to_rows, 'row', swaps[1])  4.44 us
    ppermute x1, starting transfers between devices, per_device(): second = lax.ppermute(band, 'row', swaps[1])  1.91 us
    ppermute x1, starting transfers between devices, per_device(): from_second = lax.ppermute(to_rows, 'row', swaps[1])  1.91 us
    ppermute x1, starting transfers between devices, per_device(): first = lax.ppermute(band, 'row', swaps[0])  1.74 us
    ppermute x1, waiting for transfers between devices, per_device(): second = lax.ppermute(band, 'row', swaps[1])  1.21 us
  transfers between devices with their start and end apart: 4, of which 2 were waited for; matrix products, arithmetic and copies ran while one was open for 0% of the time, Pallas kernels for 8%

profile of v4, /device:TPU:8, one launch (start us, length us, event | category | flops | bytes accessed | tf_op | source)
XLA Modules:
  0.0 38.0 jit_solution(9175852454539662841)
XLA Ops:
  0.7 1.0 %pack.1 = bf16[272,128]{1,0:T(8,128)(2,1)S(1)} custom-call(f32[2,128,128]{2,1,0:T(8,128)} %specimen.1, s32[1,1,2,2]{3,2,1,0:T(2,128)} %centers.1, s32[1,1]{1,0:T(1,128)S(6)} %copy.8.cnt, s32[1,1,2]{2,1,0:T(1,128)} %helpers.1), custom_call_target="tpu_custom_call" | custom-call | flops 100000 | bytes 524288 | tf_op jit(solution)/shard_map/pack/pallas_call | solution.py:317
  1.6 9.1 %all-gather = bf16[1088,128]{1,0:T(8,128)(2,1)S(1)} all-gather(bf16[272,128]{1,0:T(8,128)(2,1)S(1)} %pack.1), channel_id=2, replica_groups=mesh['row'=8,'col'=4] {'col'}, dimensions={0}, use_global_device_ids=true | all-gather | bytes 348160 | tf_op jit(solution)/shard_map/all_gather | solution.py:352
  10.8 1.9 %collective-permute-start.1 = (bf16[4,272,128]{2,1,0:T(8,128)(2,1)S(1)}, bf16[4,272,128]{2,1,0:T(8,128)(2,1)S(1)}, u32[]{:S(2)}, u32[]{:S(2)}) collective-permute-start(bf16[4,272,128]{2,1,0:T(8,128)(2,1)S(1)} %bitcast.2), channel_id=1, source_target_pairs={{4,8},{12,16},{20,24},{8,4},{16,12},{24,20},{5,9},{13,17},{21,25},... | collective-permute-start | bytes 835592 | tf_op jit(solution)/shard_map/ppermute | solution.py:359
  12.7 1.7 %collective-permute-start = (bf16[4,272,128]{2,1,0:T(8,128)(2,1)S(1)}, bf16[4,272,128]{2,1,0:T(8,128)(2,1)S(1)}, u32[]{:S(2)}, u32[]{:S(2)}) collective-permute-start(bf16[4,272,128]{2,1,0:T(8,128)(2,1)S(1)} %bitcast.3), channel_id=1, source_target_pairs={{0,4},{8,12},{16,20},{24,28},{4,0},{12,8},{20,16},{28,24},{1,5},{9... | collective-permute-start | bytes 835592 | tf_op jit(solution)/shard_map/ppermute | solution.py:360
  14.4 3.0 %prepare.1 = (bf16[16,256]{1,0:T(8,128)(2,1)S(1)}, f32[256,256]{1,0:T(8,128)S(1)}, bf16[8,256,256]{2,1,0:T(8,128)(2,1)S(1)}, f32[4,2,256,256]{3,2,1,0:T(8,128)S(1)}, f32[4,2,128,256]{3,2,1,0:T(8,128)S(1)}) custom-call(bf16[4,272,128]{2,1,0:T(8,128)(2,1)S(1)} %bitcast.4, f32[4,2,256,256]{3,2,1,0:T(8,128)} %probe.1, f32[1,1,1,256,256]{4,3,2,1,0:T(8,128)} %measured.1, ...), custom_call_target="tpu_custom_call" | custom-call | flops 1000000000 | bytes 4194304 | tf_op jit(solution)/shard_map/prepare/pallas_call | solution.py:317
  17.4 1.2 %collective-permute-done.1.second = bf16[4,272,128]{2,1,0:T(8,128)(2,1)S(1)} collective-permute-done((bf16[4,272,128]{2,1,0:T(8,128)(2,1)S(1)}, bf16[4,272,128]{2,1,0:T(8,128)(2,1)S(1)}, u32[]{:S(2)}, u32[]{:S(2)}) %collective-permute-start.1) | collective-permute-done | bytes 278560 | tf_op jit(solution)/shard_map/ppermute | solution.py:359
  18.6 0.0 collective-permute-done.first
  18.6 2.9 %frame.1 = (bf16[272,256]{1,0:T(8,128)(2,1)S(1)}, bf16[272,256]{1,0:T(8,128)(2,1)S(1)}) custom-call(bf16[4,272,128]{2,1,0:T(8,128)(2,1)S(1)} %collective-permute-done.first, bf16[4,272,128]{2,1,0:T(8,128)(2,1)S(1)} %collective-permute-done.1.second, bf16[16,256]{1,0:T(8,128)(2,1)S(1)} %get-tuple-element.12.info, f32[256,256]{1,0:T(8,128)S(1)} %get-tuple-element.13.amplitude, ...), custom_call_target="tpu_custom_call" | custom-call | flops 2000000000 | bytes 4194304 | tf_op jit(solution)/shard_map/frame/pallas_call | solution.py:317
  21.5 0.2 collective-permute-start.3
  21.7 1.9 %collective-permute-start.2 = (bf16[272,256]{1,0:T(8,128)(2,1)S(1)}, bf16[272,256]{1,0:T(8,128)(2,1)S(1)}, u32[]{:S(2)}, u32[]{:S(2)}) collective-permute-start(bf16[272,256]{1,0:T(8,128)(2,1)S(1)} %get-tuple-element.18), channel_id=1, source_target_pairs={{4,8},{12,16},{20,24},{8,4},{16,12},{24,20},{5,9},{13,17},{21,25},... | collective-permute-start | bytes 417800 | tf_op jit(solution)/shard_map/ppermute | solution.py:391
  23.6 0.0 collective-permute-done.3.first
  23.6 4.4 %collective-permute-done.2.second = bf16[272,256]{1,0:T(8,128)(2,1)S(1)} collective-permute-done((bf16[272,256]{1,0:T(8,128)(2,1)S(1)}, bf16[272,256]{1,0:T(8,128)(2,1)S(1)}, u32[]{:S(2)}, u32[]{:S(2)}) %collective-permute-start.2) | collective-permute-done | bytes 139296 | tf_op jit(solution)/shard_map/ppermute | solution.py:391
  28.0 0.3 fold.1
  28.3 8.9 %all_to_all.5 = bf16[4,256,128]{2,1,0:T(8,128)(2,1)S(1)} all-to-all(bf16[4,256,128]{2,1,0:T(8,128)(2,1)S(1)} %fold.1), channel_id=1, replica_groups=mesh['row'=8,'col'=4] {'col'}, dimensions={0} | all-to-all | bytes 524288 | tf_op jit(solution)/shard_map/all_to_all | solution.py:400
  37.3 0.7 %convert_reduce_fusion = f32[256,128]{1,0:T(8,128)} fusion(bf16[4,256,128]{2,1,0:T(8,128)(2,1)S(1)} %all_to_all.5), kind=kLoop, calls=%fused_computation | loop fusion | flops 229376 | bytes 393216 | tf_op jit(solution)/shard_map/reduce_sum | solution.py:401
Async XLA Ops:
  10.8 7.9 %collective-permute-start.1 = (bf16[4,272,128]{2,1,0:T(8,128)(2,1)S(1)}, bf16[4,272,128]{2,1,0:T(8,128)(2,1)S(1)}, u32[]{:S(2)}, u32[]{:S(2)}) collective-permute-start(bf16[4,272,128]{2,1,0:T(8,128)(2,1)S(1)} %bitcast.2), channel_id=1, source_target_pairs={{4,8},{12,16},{20,24},{8,4},{16,12},{24,20},{5,9},{13,17},{21,25},... | collective-permute-start | bytes 835592 | tf_op jit(solution)/shard_map/ppermute | solution.py:359
  12.7 5.9 %collective-permute-start = (bf16[4,272,128]{2,1,0:T(8,128)(2,1)S(1)}, bf16[4,272,128]{2,1,0:T(8,128)(2,1)S(1)}, u32[]{:S(2)}, u32[]{:S(2)}) collective-permute-start(bf16[4,272,128]{2,1,0:T(8,128)(2,1)S(1)} %bitcast.3), channel_id=1, source_target_pairs={{0,4},{8,12},{16,20},{24,28},{4,0},{12,8},{20,16},{28,24},{1,5},{9... | collective-permute-start | bytes 835592 | tf_op jit(solution)/shard_map/ppermute | solution.py:360
  21.5 2.1 %collective-permute-start.3 = (bf16[272,256]{1,0:T(8,128)(2,1)S(1)}, bf16[272,256]{1,0:T(8,128)(2,1)S(1)}, u32[]{:S(2)}, u32[]{:S(2)}) collective-permute-start(bf16[272,256]{1,0:T(8,128)(2,1)S(1)} %get-tuple-element.18), channel_id=1, source_target_pairs={{0,4},{8,12},{16,20},{24,28},{4,0},{12,8},{20,16},{28,24},{1,5},{9... | collective-permute-start | bytes 417800 | tf_op jit(solution)/shard_map/ppermute | solution.py:390
  21.7 6.4 %collective-permute-start.2 = (bf16[272,256]{1,0:T(8,128)(2,1)S(1)}, bf16[272,256]{1,0:T(8,128)(2,1)S(1)}, u32[]{:S(2)}, u32[]{:S(2)}) collective-permute-start(bf16[272,256]{1,0:T(8,128)(2,1)S(1)} %get-tuple-element.18), channel_id=1, source_target_pairs={{4,8},{12,16},{20,24},{8,4},{16,12},{24,20},{5,9},{13,17},{21,25},... | collective-permute-start | bytes 417800 | tf_op jit(solution)/shard_map/ppermute | solution.py:391

commit v5 on v4

--- a/solution.py
+++ b/solution.py
@@ -387,8 +387,8 @@
         2 * 10**9, 2**22,
         first, second, *prepared,
     )
+    from_second = lax.ppermute(to_rows, "row", swaps[1])
     from_first = lax.ppermute(to_rows, "row", swaps[0])
-    from_second = lax.ppermute(to_rows, "row", swaps[1])
     summed = call(
         fold_kernel, "fold",
         jax.ShapeDtypeStruct((columns, height, tile), BF16),
@@ -397,8 +397,8 @@
         10**9, 2**20,
         centre, from_second, from_first,
     )
-    shares = lax.all_to_all(summed, "col", split_axis=0, concat_axis=0, tiled=True)
-    return jnp.sum(shares.astype(F32), axis=0).reshape(2, tile, tile)
+    share = lax.psum_scatter(summed, "col", scatter_dimension=0)
+    return share.astype(F32).reshape(2, tile, tile)
 
 
 def solution(mesh):

time: 38.2 us -> 70.1 us (1.84)
  the two profiles are of different devices: /device:TPU:8 before, /device:TPU:0 now
where the time goes in v5:
time: 70.1 us; the launch traced here: 69.8 us
  waiting for transfers between devices  30.3 us (43%)
  between operations  14.1 us (20%)
  blocking collectives  10.6 us (15%)
  Pallas kernels  7.8 us (11%)
  starting transfers between devices  5.53 us (8%)
  other arithmetic  1.5 us (2%)
    unnamed x2, waiting for transfers between devices  30 us
    all_gather x1, blocking collectives, per_device(): band = lax.all_gather(packed, 'col')  10.6 us
    pallas_call x4, Pallas kernels, call(): pl.pallas_call(kernel, out_shape=out_shape, in_specs=in_specs, out_specs=...  7.8 us
    ppermute x1, starting transfers between devices, per_device(): first = lax.ppermute(band, 'row', swaps[0])  2.99 us
    convert_element_type x1, other arithmetic, per_device(): return share.astype(F32).reshape(2, tile, tile)  1.5 us
  transfers between devices with their start and end apart: 5, of which 2 were waited for; matrix products, arithmetic and copies ran while one was open for 0% of the time, Pallas kernels for 4%

profile of v5, /device:TPU:0, one launch (start us, length us, event | category | flops | bytes accessed | tf_op | source)
XLA Modules:
  0.0 69.8 jit_solution(2797658290719357649)
XLA Ops:
  6.5 0.0 reduce-scatter.4.cloned.1.call-start
  7.2 1.0 %pack.1 = bf16[272,128]{1,0:T(8,128)(2,1)S(1)} custom-call(f32[2,128,128]{2,1,0:T(8,128)} %specimen.1, s32[1,1,2,2]{3,2,1,0:T(2,128)} %centers.1, s32[1,1]{1,0:T(1,128)S(6)} %copy.8.cnt, s32[1,1,2]{2,1,0:T(1,128)} %helpers.1), custom_call_target="tpu_custom_call" | custom-call | flops 100000 | bytes 524288 | tf_op jit(solution)/shard_map/pack/pallas_call | solution.py:317
  8.2 10.6 %all-gather = bf16[1088,128]{1,0:T(8,128)(2,1)S(1)} all-gather(bf16[272,128]{1,0:T(8,128)(2,1)S(1)} %pack.1), channel_id=2, replica_groups=mesh['row'=8,'col'=4] {'col'}, dimensions={0}, use_global_device_ids=true | all-gather | bytes 348160 | tf_op jit(solution)/shard_map/all_gather | solution.py:352
  18.7 0.7 collective-permute-start.1
  19.4 3.0 %collective-permute-start = (bf16[4,272,128]{2,1,0:T(8,128)(2,1)S(1)}, bf16[4,272,128]{2,1,0:T(8,128)(2,1)S(1)}, u32[]{:S(2)}, u32[]{:S(2)}) collective-permute-start(bf16[4,272,128]{2,1,0:T(8,128)(2,1)S(1)} %bitcast.5), channel_id=1, source_target_pairs={{0,4},{8,12},{16,20},{24,28},{4,0},{12,8},{20,16},{28,24},{1,5},{9... | collective-permute-start | bytes 835592 | tf_op jit(solution)/shard_map/ppermute | solution.py:360
  22.4 3.0 %prepare.1 = (bf16[16,256]{1,0:T(8,128)(2,1)S(1)}, f32[256,256]{1,0:T(8,128)S(1)}, bf16[8,256,256]{2,1,0:T(8,128)(2,1)S(1)}, f32[4,2,256,256]{3,2,1,0:T(8,128)S(1)}, f32[4,2,128,256]{3,2,1,0:T(8,128)S(1)}) custom-call(bf16[4,272,128]{2,1,0:T(8,128)(2,1)S(1)} %bitcast.6, f32[4,2,256,256]{3,2,1,0:T(8,128)} %probe.1, f32[1,1,1,256,256]{4,3,2,1,0:T(8,128)} %measured.1, ...), custom_call_target="tpu_custom_call" | custom-call | flops 1000000000 | bytes 4194304 | tf_op jit(solution)/shard_map/prepare/pallas_call | solution.py:317
  25.4 0.0 collective-permute-done.1.second
  25.4 0.0 collective-permute-done.first
  25.4 2.9 %frame.1 = (bf16[272,256]{1,0:T(8,128)(2,1)S(1)}, bf16[272,256]{1,0:T(8,128)(2,1)S(1)}) custom-call(bf16[4,272,128]{2,1,0:T(8,128)(2,1)S(1)} %collective-permute-done.first, bf16[4,272,128]{2,1,0:T(8,128)(2,1)S(1)} %collective-permute-done.1.second, bf16[16,256]{1,0:T(8,128)(2,1)S(1)} %get-tuple-element.12.info, f32[256,256]{1,0:T(8,128)S(1)} %get-tuple-element.13.amplitude, ...), custom_call_target="tpu_custom_call" | custom-call | flops 2000000000 | bytes 4194304 | tf_op jit(solution)/shard_map/frame/pallas_call | solution.py:317
  28.3 1.2 %collective-permute-start.3 = (bf16[272,256]{1,0:T(8,128)(2,1)S(1)}, bf16[272,256]{1,0:T(8,128)(2,1)S(1)}, u32[]{:S(2)}, u32[]{:S(2)}) collective-permute-start(bf16[272,256]{1,0:T(8,128)(2,1)S(1)} %get-tuple-element.18), channel_id=1, source_target_pairs={{0,4},{8,12},{16,20},{24,28},{4,0},{12,8},{20,16},{28,24},{1,5},{9... | collective-permute-start | bytes 417800 | tf_op jit(solution)/shard_map/ppermute | solution.py:391
  29.5 0.7 collective-permute-start.2
  30.2 0.3 collective-permute-done.3.first
  30.5 0.0 collective-permute-done.2.second
  30.5 1.0 %fold.1 = bf16[4,256,128]{2,1,0:T(8,128)(2,1)} custom-call(bf16[272,256]{1,0:T(8,128)(2,1)S(1)} %get-tuple-element.17.centre, bf16[272,256]{1,0:T(8,128)(2,1)S(1)} %collective-permute-done.2.second, bf16[272,256]{1,0:T(8,128)(2,1)S(1)} %collective-permute-done.3.first), custom_call_target="tpu_custom_call" | custom-call | flops 1000000000 | bytes 1048576 | tf_op jit(solution)/shard_map/fold/pallas_call | solution.py:317
  31.5 0.0 reduce-scatter.4.cloned.1.call-update
  31.5 30.0 %reduce-scatter.4.cloned.1.call-done = bf16[1,256,128]{2,1,0:T(8,128)(2,1)} async-done(((bf16[4,256,128]{2,1,0:T(8,128)(2,1)}), bf16[1,256,128]{2,1,0:T(8,128)(2,1)}) %reduce-scatter.4.cloned.1.call-update) | async-done | bytes 65552
  61.5 1.5 %convert.1 = f32[2,128,128]{2,1,0:T(8,128)} convert(bf16[2,128,128]{2,1,0:T(8,128)(2,1)} %bitcast.7) | non-fusion elementwise | flops 32768 | bytes 196608 | tf_op jit(solution)/shard_map/convert_element_type | solution.py:401
Async XLA Ops:
  6.5 54.9 %reduce-scatter.4.cloned.1.call-start = ((), (), s32[]{:S(2)}) async-start(), calls=%async_computation.1 | async-start | bytes 327680
  18.7 6.6 %collective-permute-start.1 = (bf16[4,272,128]{2,1,0:T(8,128)(2,1)S(1)}, bf16[4,272,128]{2,1,0:T(8,128)(2,1)S(1)}, u32[]{:S(2)}, u32[]{:S(2)}) collective-permute-start(bf16[4,272,128]{2,1,0:T(8,128)(2,1)S(1)} %bitcast.4), channel_id=1, source_target_pairs={{4,8},{12,16},{20,24},{8,4},{16,12},{24,20},{5,9},{13,17},{21,25},... | collective-permute-start | bytes 835592 | tf_op jit(solution)/shard_map/ppermute | solution.py:359
  19.4 6.0 %collective-permute-start = (bf16[4,272,128]{2,1,0:T(8,128)(2,1)S(1)}, bf16[4,272,128]{2,1,0:T(8,128)(2,1)S(1)}, u32[]{:S(2)}, u32[]{:S(2)}) collective-permute-start(bf16[4,272,128]{2,1,0:T(8,128)(2,1)S(1)} %bitcast.5), channel_id=1, source_target_pairs={{0,4},{8,12},{16,20},{24,28},{4,0},{12,8},{20,16},{28,24},{1,5},{9... | collective-permute-start | bytes 835592 | tf_op jit(solution)/shard_map/ppermute | solution.py:360
  28.3 2.2 %collective-permute-start.3 = (bf16[272,256]{1,0:T(8,128)(2,1)S(1)}, bf16[272,256]{1,0:T(8,128)(2,1)S(1)}, u32[]{:S(2)}, u32[]{:S(2)}) collective-permute-start(bf16[272,256]{1,0:T(8,128)(2,1)S(1)} %get-tuple-element.18), channel_id=1, source_target_pairs={{0,4},{8,12},{16,20},{24,28},{4,0},{12,8},{20,16},{28,24},{1,5},{9... | collective-permute-start | bytes 417800 | tf_op jit(solution)/shard_map/ppermute | solution.py:391
  29.5 1.0 %collective-permute-start.2 = (bf16[272,256]{1,0:T(8,128)(2,1)S(1)}, bf16[272,256]{1,0:T(8,128)(2,1)S(1)}, u32[]{:S(2)}, u32[]{:S(2)}) collective-permute-start(bf16[272,256]{1,0:T(8,128)(2,1)S(1)} %get-tuple-element.18), channel_id=1, source_target_pairs={{4,8},{12,16},{20,24},{8,4},{16,12},{24,20},{5,9},{13,17},{21,25},... | collective-permute-start | bytes 417800 | tf_op jit(solution)/shard_map/ppermute | solution.py:390
Sparse Core Ops, SparseCore 0:
  31.6 29.7 reduce-scatter.3

commit v6 on v4

--- a/solution.py
+++ b/solution.py
@@ -12,6 +12,7 @@
 F32 = jnp.float32
 BF16 = jnp.bfloat16
 INFO = 16
+STRIP = 16
 VMEM = pl.BlockSpec(memory_space=pltpu.VMEM)
 SMEM = pl.BlockSpec(memory_space=pltpu.SMEM)
 HBM = pl.BlockSpec(memory_space=pltpu.HBM)
@@ -198,7 +199,7 @@
 
 def frame_kernel(
     first, second, info, amplitude, tables, probe, half_own,
-    to_rows, centre, far,
+    to_rows, centre, patch, folded, half_far, mixed, far, corrected, product, mixed_back, turned,
 ):
     columns = first.shape[0]
     tile = (first.shape[1] - INFO) // 2
@@ -209,76 +210,121 @@
     source, col, row = (
         info[r : r + 1, :tile].astype(F32).astype(jnp.int32) for r in range(3)
     )
-    from_above = (iota((tile, tile), 0) >= row).astype(jnp.int32)
-    from_first = from_above == odd
-    patch = []
-    for p in range(2):
-        part = slice(p * tile, (p + 1) * tile)
-        patch.append(
-            gather_columns(
+    strips = [pl.ds(r, STRIP) for r in range(0, half, STRIP)]
+    lower = [pl.ds(half + r, STRIP) for r in range(0, half, STRIP)]
+
+    def split(x):
+        return x[:, :half], x[:, half:]
+
+    def join(x, y):
+        return jnp.concatenate([x, y], 1).astype(BF16)
+
+    def gather(s):
+        rows = iota((STRIP, tile), 0) + s.start
+        from_first = (rows >= row).astype(jnp.int32) == odd
+        for p in range(2):
+            part = pl.ds(p * tile + s.start, STRIP)
+            patch[p, s] = gather_columns(
                 lambda c: jnp.where(
                     from_first, first[c, part].astype(F32), second[c, part].astype(F32)
                 ),
-                source, col, columns, (tile, tile),
+                source, col, columns, (STRIP, tile),
             )
-        )
-
-    right, right_back = (tables[0], tables[1]), (tables[2], tables[3])
-    left, left_back = (tables[4], tables[5]), (tables[6], tables[7])
-    intensity = [jnp.zeros((half, extent), F32) for _ in range(2)]
-    for k in range(modes):
-        even, odds = first_product(
-            [probe[k, p, :half] for p in range(2)], patch, right
-        )
-        for parity, sign in ((0, 1), (1, -1)):
-            e = even + sign * half_own[k, 0]
-            o = odds + sign * half_own[k, 1]
-            folded = quarters(e[:, :half], o[:, :half], e[:, half:], o[:, half:])
-            f = dot(left[parity], folded.astype(BF16))
-            far[k, parity] = f
-            intensity[parity] += f[:half] * f[:half] + f[half:] * f[half:]
-    factor = [
-        1.0
-        - amplitude[i * half : (i + 1) * half]
-        * lax.rsqrt(jnp.maximum(intensity[i], 0.25))
-        for i in range(2)
-    ]
-    grad = [[jnp.zeros((half, extent), F32) for _ in range(2)] for _ in range(2)]
-    for k in range(modes):
-        c = []
-        for parity in range(2):
-            f = far[k, parity]
-            c.append(
-                (f * jnp.concatenate([factor[parity], factor[parity]], 0)).astype(BF16)
-            )
-        a = dot(
-            quarters(c[0][:half, :half], c[0][half:, :half], c[1][:half, :half], c[1][half:, :half]),
-            right_back[0],
-        )
-        b = dot(
-            quarters(c[0][:half, half:], c[0][half:, half:], c[1][:half, half:], c[1][half:, half:]),
-            right_back[1],
-        )
-        lo, hi = (a + b).astype(BF16), (a - b).astype(BF16)
-        turned = []
-        for parity in range(2):
-            l = lo[parity * half : (parity + 1) * half]
-            h = hi[parity * half : (parity + 1) * half]
-            turned.append(
-                dot(
-                    left_back[parity],
-                    quarters(l[:, :half], h[:, :half], l[:, half:], h[:, half:]),
-                )
-            )
-        for i, chi in enumerate((turned[0] + turned[1], turned[0] - turned[1])):
-            cr, ci = chi[:half], chi[half:]
-            pr = probe[k, 0, i * half : (i + 1) * half]
-            pi = probe[k, 1, i * half : (i + 1) * half]
-            grad[0][i] += pr * cr + pi * ci
-            grad[1][i] += pr * ci - pi * cr
-    for p in range(2):
-        to_rows[p * tile : (p + 1) * tile] = grad[p][0].astype(BF16)
-        centre[p * tile : (p + 1) * tile] = grad[p][1].astype(BF16)
+
+    def wave(k):
+        for s in strips:
+            pr, pi, xr, xi = probe[k, 0, s], probe[k, 1, s], patch[0, s], patch[1, s]
+            re = split(pr * xr - pi * xi)
+            im = split(pr * xi + pi * xr)
+            folded[k, 0, s] = join(re[0] + re[1], im[0] + im[1])
+            folded[k, 1, s] = join(re[0] - re[1], im[0] - im[1])
+
+    def along_rows(k):
+        for q in range(2):
+            half_far[k, q] = dot(folded[k, q], tables[q])
+
+    def mix(k):
+        for s, t in zip(strips, lower):
+            even, odds = half_far[k, 0, s], half_far[k, 1, s]
+            even_own, odds_own = half_own[k, 0, s], half_own[k, 1, s]
+            for q, (e, o) in enumerate(
+                ((even + even_own, odds + odds_own), (even - even_own, odds - odds_own))
+            ):
+                (er, ei), (our, oui) = split(e), split(o)
+                mixed[k, q, s] = join(er, our)
+                mixed[k, q, t] = join(ei, oui)
+
+    def along_columns(k, q):
+        far[k, q] = dot(tables[4 + q], mixed[k, q])
+
+    def correct(q, which):
+        for s, t in list(zip(strips, lower))[which]:
+            re = [far[k, q, s] for k in range(modes)]
+            im = [far[k, q, t] for k in range(modes)]
+            intensity = sum(x * x for x in re + im)
+            size = amplitude[pl.ds(q * half + s.start, STRIP)]
+            factor = 1.0 - size * lax.rsqrt(jnp.maximum(intensity, 0.25))
+            out = pl.ds(q * half + s.start, STRIP)
+            for k in range(modes):
+                (re_even, re_odd), (im_even, im_odd) = split(re[k] * factor), split(im[k] * factor)
+                corrected[k, 0, out] = join(re_even, im_even)
+                corrected[k, 1, out] = join(re_odd, im_odd)
+
+    def back_along_rows(k, q):
+        part = pl.ds(q * half, half)
+        for c in range(2):
+            product[k, c, part] = dot(corrected[k, c, part], tables[2 + c])
+
+    def mix_back(k, q):
+        for s, t in zip(strips, lower):
+            part = pl.ds(q * half + s.start, STRIP)
+            x, y = product[k, 0, part], product[k, 1, part]
+            (lr, li), (hr, hi) = split(x + y), split(x - y)
+            mixed_back[k, q, s] = join(lr, hr)
+            mixed_back[k, q, t] = join(li, hi)
+
+    def back_along_columns(k, q):
+        turned[k, q] = dot(tables[6 + q], mixed_back[k, q])
+
+    def accumulate(s, t):
+        total = [[0.0, 0.0], [0.0, 0.0]]
+        for k in range(modes):
+            er, ei, our, oui = turned[k, 0, s], turned[k, 0, t], turned[k, 1, s], turned[k, 1, t]
+            for i, (cr, ci, rows) in enumerate(
+                ((er + our, ei + oui, s), (er - our, ei - oui, t))
+            ):
+                pr, pi = probe[k, 0, rows], probe[k, 1, rows]
+                total[i][0] += pr * cr + pi * ci
+                total[i][1] += pr * ci - pi * cr
+        for out, parts in zip((to_rows, centre), total):
+            for p in range(2):
+                out[pl.ds(p * tile + s.start, STRIP)] = parts[p].astype(BF16)
+
+    for s in strips:
+        gather(s)
+    for k in range(modes + 1):
+        if k < modes:
+            wave(k)
+            along_rows(k)
+        if k > 0:
+            mix(k - 1)
+            along_columns(k - 1, 0)
+    share = -(-len(strips) // modes)
+    for k in range(modes):
+        along_columns(k, 1)
+        correct(0, slice(k * share, (k + 1) * share))
+    for k in range(modes):
+        back_along_rows(k, 0)
+        correct(1, slice(k * share, (k + 1) * share))
+    for k in range(modes):
+        mix_back(k, 0)
+        back_along_columns(k, 0)
+        back_along_rows(k, 1)
+    for k in range(modes):
+        mix_back(k, 1)
+        back_along_columns(k, 1)
+    for s, t in zip(strips, lower):
+        accumulate(s, t)
     for out in (to_rows, centre):
         out[2 * tile :] = info[...]
 
@@ -320,7 +366,7 @@
         in_specs=in_specs,
         out_specs=jax.tree.map(lambda _: VMEM, out_shape),
         scratch_shapes=scratch,
-        compiler_params=pltpu.CompilerParams(vmem_limit_bytes=24 * 2**20),
+        compiler_params=pltpu.CompilerParams(vmem_limit_bytes=32 * 2**20),
         cost_estimate=pl.CostEstimate(flops=flops, bytes_accessed=moved, transcendentals=0),
         name=name,
     )(*args)
@@ -383,7 +429,17 @@
         frame_kernel, "frame",
         (part, part),
         [VMEM] * 7,
-        [pltpu.VMEM((modes, 2, extent, extent), F32)],
+        [
+            pltpu.VMEM((2, tile, extent), F32),
+            pltpu.VMEM((modes, 2, half, extent), BF16),
+            pltpu.VMEM((modes, 2, half, extent), F32),
+            pltpu.VMEM((modes, 2, extent, extent), BF16),
+            pltpu.VMEM((modes, 2, extent, extent), F32),
+            pltpu.VMEM((modes, 2, extent, extent), BF16),
+            pltpu.VMEM((modes, 2, extent, extent), F32),
+            pltpu.VMEM((modes, 2, extent, extent), BF16),
+            pltpu.VMEM((modes, 2, extent, extent), F32),
+        ],
         2 * 10**9, 2**22,
         first, second, *prepared,
     )

time: 38.2 us -> 37.5 us (0.982)
  Pallas kernels: 7.1 us -> 6.45 us
    pallas_call x4, Pallas kernels: 7.1 us -> 6.45 us  [call(): pl.pallas_call(kernel, out_shape=out_shape, in_specs=in_specs, out_specs=...]
where the time goes in v6:
time: 37.5 us; the launch traced here: 37.3 us
  blocking collectives  18.1 us (48%)
  Pallas kernels  6.45 us (17%)
  starting transfers between devices  5.74 us (15%)
  waiting for transfers between devices  5.64 us (15%)
  between operations  0.7 us (2%)
  other arithmetic  0.69 us (2%)
    all_gather x1, blocking collectives, per_device(): band = lax.all_gather(packed, 'col')  9.13 us
    all_to_all x1, blocking collectives, per_device(): lax.all_to_all(summed, 'col', split_axis=0, concat_axis=0, tiled=True)  8.94 us
    pallas_call x4, Pallas kernels, call(): pl.pallas_call(kernel, out_shape=out_shape, in_specs=in_specs, out_specs=...  6.45 us
    ppermute x1, waiting for transfers between devices, per_device(): from_second = lax.ppermute(to_rows, 'row', swaps[1])  4.44 us
    ppermute x1, starting transfers between devices, per_device(): second = lax.ppermute(band, 'row', swaps[1])  1.91 us
    ppermute x1, starting transfers between devices, per_device(): from_second = lax.ppermute(to_rows, 'row', swaps[1])  1.91 us
    ppermute x1, starting transfers between devices, per_device(): first = lax.ppermute(band, 'row', swaps[0])  1.74 us
    ppermute x1, waiting for transfers between devices, per_device(): second = lax.ppermute(band, 'row', swaps[1])  1.2 us
  transfers between devices with their start and end apart: 4, of which 2 were waited for; matrix products, arithmetic and copies ran while one was open for 0% of the time, Pallas kernels for 8%

profile of v6, /device:TPU:8, one launch (start us, length us, event | category | flops | bytes accessed | tf_op | source)
XLA Modules:
  0.0 37.3 jit_solution(14987867669958983923)
XLA Ops:
  0.7 1.0 %pack.1 = bf16[272,128]{1,0:T(8,128)(2,1)S(1)} custom-call(f32[2,128,128]{2,1,0:T(8,128)} %specimen.1, s32[1,1,2,2]{3,2,1,0:T(2,128)} %centers.1, s32[1,1]{1,0:T(1,128)S(6)} %copy.8.cnt, s32[1,1,2]{2,1,0:T(1,128)} %helpers.1), custom_call_target="tpu_custom_call" | custom-call | flops 100000 | bytes 524288 | tf_op jit(solution)/shard_map/pack/pallas_call | solution.py:363
  1.6 9.1 %all-gather = bf16[1088,128]{1,0:T(8,128)(2,1)S(1)} all-gather(bf16[272,128]{1,0:T(8,128)(2,1)S(1)} %pack.1), channel_id=2, replica_groups=mesh['row'=8,'col'=4] {'col'}, dimensions={0}, use_global_device_ids=true | all-gather | bytes 348160 | tf_op jit(solution)/shard_map/all_gather | solution.py:398
  10.8 1.9 %collective-permute-start.1 = (bf16[4,272,128]{2,1,0:T(8,128)(2,1)S(1)}, bf16[4,272,128]{2,1,0:T(8,128)(2,1)S(1)}, u32[]{:S(2)}, u32[]{:S(2)}) collective-permute-start(bf16[4,272,128]{2,1,0:T(8,128)(2,1)S(1)} %bitcast.2), channel_id=1, source_target_pairs={{4,8},{12,16},{20,24},{8,4},{16,12},{24,20},{5,9},{13,17},{21,25},... | collective-permute-start | bytes 835592 | tf_op jit(solution)/shard_map/ppermute | solution.py:405
  12.7 1.7 %collective-permute-start = (bf16[4,272,128]{2,1,0:T(8,128)(2,1)S(1)}, bf16[4,272,128]{2,1,0:T(8,128)(2,1)S(1)}, u32[]{:S(2)}, u32[]{:S(2)}) collective-permute-start(bf16[4,272,128]{2,1,0:T(8,128)(2,1)S(1)} %bitcast.3), channel_id=1, source_target_pairs={{0,4},{8,12},{16,20},{24,28},{4,0},{12,8},{20,16},{28,24},{1,5},{9... | collective-permute-start | bytes 835592 | tf_op jit(solution)/shard_map/ppermute | solution.py:406
  14.4 3.0 %prepare.1 = (bf16[16,256]{1,0:T(8,128)(2,1)S(1)}, f32[256,256]{1,0:T(8,128)S(1)}, bf16[8,256,256]{2,1,0:T(8,128)(2,1)S(1)}, f32[4,2,256,256]{3,2,1,0:T(8,128)S(1)}, f32[4,2,128,256]{3,2,1,0:T(8,128)S(1)}) custom-call(bf16[4,272,128]{2,1,0:T(8,128)(2,1)S(1)} %bitcast.4, f32[4,2,256,256]{3,2,1,0:T(8,128)} %probe.1, f32[1,1,1,256,256]{4,3,2,1,0:T(8,128)} %measured.1, ...), custom_call_target="tpu_custom_call" | custom-call | flops 1000000000 | bytes 4194304 | tf_op jit(solution)/shard_map/prepare/pallas_call | solution.py:363
  17.4 1.2 %collective-permute-done.1.second = bf16[4,272,128]{2,1,0:T(8,128)(2,1)S(1)} collective-permute-done((bf16[4,272,128]{2,1,0:T(8,128)(2,1)S(1)}, bf16[4,272,128]{2,1,0:T(8,128)(2,1)S(1)}, u32[]{:S(2)}, u32[]{:S(2)}) %collective-permute-start.1) | collective-permute-done | bytes 278560 | tf_op jit(solution)/shard_map/ppermute | solution.py:405
  18.6 0.0 collective-permute-done.first
  18.6 2.2 %frame.1 = (bf16[272,256]{1,0:T(8,128)(2,1)S(1)}, bf16[272,256]{1,0:T(8,128)(2,1)S(1)}) custom-call(bf16[4,272,128]{2,1,0:T(8,128)(2,1)S(1)} %collective-permute-done.first, bf16[4,272,128]{2,1,0:T(8,128)(2,1)S(1)} %collective-permute-done.1.second, bf16[16,256]{1,0:T(8,128)(2,1)S(1)} %get-tuple-element.12.info, f32[256,256]{1,0:T(8,128)S(1)} %get-tuple-element.13.amplitude, ...), custom_call_target="tpu_custom_call" | custom-call | flops 2000000000 | bytes 4194304 | tf_op jit(solution)/shard_map/frame/pallas_call | solution.py:363
  20.8 0.2 collective-permute-start.3
  21.0 1.9 %collective-permute-start.2 = (bf16[272,256]{1,0:T(8,128)(2,1)S(1)}, bf16[272,256]{1,0:T(8,128)(2,1)S(1)}, u32[]{:S(2)}, u32[]{:S(2)}) collective-permute-start(bf16[272,256]{1,0:T(8,128)(2,1)S(1)} %get-tuple-element.18), channel_id=1, source_target_pairs={{4,8},{12,16},{20,24},{8,4},{16,12},{24,20},{5,9},{13,17},{21,25},... | collective-permute-start | bytes 417800 | tf_op jit(solution)/shard_map/ppermute | solution.py:447
  22.9 0.0 collective-permute-done.3.first
  22.9 4.4 %collective-permute-done.2.second = bf16[272,256]{1,0:T(8,128)(2,1)S(1)} collective-permute-done((bf16[272,256]{1,0:T(8,128)(2,1)S(1)}, bf16[272,256]{1,0:T(8,128)(2,1)S(1)}, u32[]{:S(2)}, u32[]{:S(2)}) %collective-permute-start.2) | collective-permute-done | bytes 139296 | tf_op jit(solution)/shard_map/ppermute | solution.py:447
  27.4 0.3 fold.1
  27.7 8.9 %all_to_all.5 = bf16[4,256,128]{2,1,0:T(8,128)(2,1)S(1)} all-to-all(bf16[4,256,128]{2,1,0:T(8,128)(2,1)S(1)} %fold.1), channel_id=1, replica_groups=mesh['row'=8,'col'=4] {'col'}, dimensions={0} | all-to-all | bytes 524288 | tf_op jit(solution)/shard_map/all_to_all | solution.py:456
  36.6 0.7 %convert_reduce_fusion = f32[256,128]{1,0:T(8,128)} fusion(bf16[4,256,128]{2,1,0:T(8,128)(2,1)S(1)} %all_to_all.5), kind=kLoop, calls=%fused_computation | loop fusion | flops 229376 | bytes 393216 | tf_op jit(solution)/shard_map/reduce_sum | solution.py:457
Async XLA Ops:
  10.8 7.9 %collective-permute-start.1 = (bf16[4,272,128]{2,1,0:T(8,128)(2,1)S(1)}, bf16[4,272,128]{2,1,0:T(8,128)(2,1)S(1)}, u32[]{:S(2)}, u32[]{:S(2)}) collective-permute-start(bf16[4,272,128]{2,1,0:T(8,128)(2,1)S(1)} %bitcast.2), channel_id=1, source_target_pairs={{4,8},{12,16},{20,24},{8,4},{16,12},{24,20},{5,9},{13,17},{21,25},... | collective-permute-start | bytes 835592 | tf_op jit(solution)/shard_map/ppermute | solution.py:405
  12.7 5.9 %collective-permute-start = (bf16[4,272,128]{2,1,0:T(8,128)(2,1)S(1)}, bf16[4,272,128]{2,1,0:T(8,128)(2,1)S(1)}, u32[]{:S(2)}, u32[]{:S(2)}) collective-permute-start(bf16[4,272,128]{2,1,0:T(8,128)(2,1)S(1)} %bitcast.3), channel_id=1, source_target_pairs={{0,4},{8,12},{16,20},{24,28},{4,0},{12,8},{20,16},{28,24},{1,5},{9... | collective-permute-start | bytes 835592 | tf_op jit(solution)/shard_map/ppermute | solution.py:406
  20.8 2.1 %collective-permute-start.3 = (bf16[272,256]{1,0:T(8,128)(2,1)S(1)}, bf16[272,256]{1,0:T(8,128)(2,1)S(1)}, u32[]{:S(2)}, u32[]{:S(2)}) collective-permute-start(bf16[272,256]{1,0:T(8,128)(2,1)S(1)} %get-tuple-element.18), channel_id=1, source_target_pairs={{0,4},{8,12},{16,20},{24,28},{4,0},{12,8},{20,16},{28,24},{1,5},{9... | collective-permute-start | bytes 417800 | tf_op jit(solution)/shard_map/ppermute | solution.py:446
  21.0 6.4 %collective-permute-start.2 = (bf16[272,256]{1,0:T(8,128)(2,1)S(1)}, bf16[272,256]{1,0:T(8,128)(2,1)S(1)}, u32[]{:S(2)}, u32[]{:S(2)}) collective-permute-start(bf16[272,256]{1,0:T(8,128)(2,1)S(1)} %get-tuple-element.18), channel_id=1, source_target_pairs={{4,8},{12,16},{20,24},{8,4},{16,12},{24,20},{5,9},{13,17},{21,25},... | collective-permute-start | bytes 417800 | tf_op jit(solution)/shard_map/ppermute | solution.py:447

commit v7 on v6

--- a/solution.py
+++ b/solution.py
@@ -329,30 +329,39 @@
         out[2 * tile :] = info[...]
 
 
-def fold_kernel(centre, second, first, out):
-    columns, height, tile = out.shape
-    odd = lax.axis_index("row") % 2
+def fold_kernel(centre, to_rows, first, out):
+    _, height, tile = out.shape
+    columns = out.shape[0] // 2
+    me = lax.axis_index("row")
+    odd = me % 2
     shape = (tile, tile)
     lane = iota(shape, 1)
-    totals = [[jnp.zeros(shape, F32) for _ in range(columns)] for _ in range(2)]
-    for which, part in enumerate((centre, second, first)):
+    outer = (me > 0) & (me < lax.axis_size("row") - 1)
+    own_row = [[jnp.zeros(shape, F32) for _ in range(columns)] for _ in range(2)]
+    other_row = [[jnp.zeros(shape, F32) for _ in range(columns)] for _ in range(2)]
+    for part, totals, wanted in (
+        (centre, own_row, None), (first, own_row, odd), (to_rows, other_row, odd)
+    ):
         source, col, row = (
             part[height + r : height + r + 1, :tile].astype(F32).astype(jnp.int32)
             for r in range(3)
         )
-        before = (iota(shape, 0) < row).astype(jnp.int32)
-        taken = before == (odd if which == 2 else 1 - odd)
+        taken = (iota(shape, 0) < row).astype(jnp.int32) == odd
+        if totals is other_row:
+            taken = taken & outer
         for p in range(2):
             block = part[p * tile : (p + 1) * tile].astype(F32)
             beside, own = block[:, :tile], block[:, tile:]
-            if which:
+            if wanted is not None:
                 beside, own = jnp.where(taken, beside, 0.0), jnp.where(taken, own, 0.0)
             for c in range(columns):
                 near = ((source == c + 1) & (lane >= col)) | ((source == c - 1) & (lane < col))
                 totals[p][c] += jnp.where(near, beside, 0.0) + jnp.where(source == c, own, 0.0)
     for p in range(2):
+        part = slice(p * tile, (p + 1) * tile)
         for c in range(columns):
-            out[c, p * tile : (p + 1) * tile] = totals[p][c].astype(BF16)
+            out[(1 - odd) * columns + c, part] = own_row[p][c].astype(BF16)
+            out[odd * columns + c, part] = other_row[p][c].astype(BF16)
 
 
 def call(kernel, name, out_shape, in_specs, scratch, flops, moved, *args):
@@ -444,16 +453,21 @@
         first, second, *prepared,
     )
     from_first = lax.ppermute(to_rows, "row", swaps[0])
-    from_second = lax.ppermute(to_rows, "row", swaps[1])
     summed = call(
         fold_kernel, "fold",
-        jax.ShapeDtypeStruct((columns, height, tile), BF16),
+        jax.ShapeDtypeStruct((2 * columns, height, tile), BF16),
         [VMEM] * 3,
         [],
-        10**9, 2**20,
-        centre, from_second, from_first,
-    )
-    shares = lax.all_to_all(summed, "col", split_axis=0, concat_axis=0, tiled=True)
+        10**7, 2**20,
+        centre, to_rows, from_first,
+    )
+    groups = [
+        [r * columns + c for r in (start, (start + 1) % rows) for c in range(columns)]
+        for start in range(1, rows, 2)
+    ]
+    shares = lax.all_to_all(
+        summed, ("row", "col"), split_axis=0, concat_axis=0, axis_index_groups=groups, tiled=True
+    )
     return jnp.sum(shares.astype(F32), axis=0).reshape(2, tile, tile)
 
 

time: 37.5 us -> 38.4 us (1.024)
  the two profiles are of different devices: /device:TPU:8 before, /device:TPU:1 now
where the time goes in v7:
time: 38.4 us; the launch traced here: 38.2 us
  blocking collectives  21.9 us (57%)
  Pallas kernels  6.42 us (17%)
  starting transfers between devices  5.92 us (15%)
  waiting for transfers between devices  2.5 us (7%)
  other arithmetic  0.72 us (2%)
  between operations  0.7 us (2%)
    all_to_all x1, blocking collectives, per_device(): lax.all_to_all(summed, ('row', 'col'), split_axis=0, concat_axis=0, axis_...  14 us
    all_gather x1, blocking collectives, per_device(): band = lax.all_gather(packed, 'col')  7.94 us
    pallas_call x4, Pallas kernels, call(): pl.pallas_call(kernel, out_shape=out_shape, in_specs=in_specs, out_specs=...  6.42 us
    ppermute x1, starting transfers between devices, per_device(): second = lax.ppermute(band, 'row', swaps[1])  5.77 us
    ppermute x1, waiting for transfers between devices, per_device(): from_first = lax.ppermute(to_rows, 'row', swaps[0])  1.35 us
    ppermute x1, waiting for transfers between devices, per_device(): second = lax.ppermute(band, 'row', swaps[1])  1.15 us
  transfers between devices with their start and end apart: 3, of which 2 were waited for; matrix products, arithmetic and copies ran while one was open for 0% of the time, Pallas kernels for 8%

profile of v7, /device:TPU:1, one launch (start us, length us, event | category | flops | bytes accessed | tf_op | source)
XLA Modules:
  0.0 38.2 jit_solution(18149722722210954767)
XLA Ops:
  0.7 1.0 %pack.1 = bf16[272,128]{1,0:T(8,128)(2,1)S(1)} custom-call(f32[2,128,128]{2,1,0:T(8,128)} %specimen.1, s32[1,1,2,2]{3,2,1,0:T(2,128)} %centers.1, s32[1,1]{1,0:T(1,128)S(6)} %copy.8.cnt, s32[1,1,2]{2,1,0:T(1,128)} %helpers.1), custom_call_target="tpu_custom_call" | custom-call | flops 100000 | bytes 524288 | tf_op jit(solution)/shard_map/pack/pallas_call | solution.py:372
  1.6 7.9 %all-gather = bf16[1088,128]{1,0:T(8,128)(2,1)S(1)} all-gather(bf16[272,128]{1,0:T(8,128)(2,1)S(1)} %pack.1), channel_id=2, replica_groups=mesh['row'=8,'col'=4] {'col'}, dimensions={0}, use_global_device_ids=true | all-gather | bytes 348160 | tf_op jit(solution)/shard_map/all_gather | solution.py:407
  9.6 5.8 %collective-permute-start.1 = (bf16[4,272,128]{2,1,0:T(8,128)(2,1)S(1)}, bf16[4,272,128]{2,1,0:T(8,128)(2,1)S(1)}, u32[]{:S(2)}, u32[]{:S(2)}) collective-permute-start(bf16[4,272,128]{2,1,0:T(8,128)(2,1)S(1)} %bitcast.2), channel_id=1, source_target_pairs={{4,8},{12,16},{20,24},{8,4},{16,12},{24,20},{5,9},{13,17},{21,25},... | collective-permute-start | bytes 835592 | tf_op jit(solution)/shard_map/ppermute | solution.py:414
  15.3 0.1 collective-permute-start
  15.4 3.0 %prepare.1 = (bf16[16,256]{1,0:T(8,128)(2,1)S(1)}, f32[256,256]{1,0:T(8,128)S(1)}, bf16[8,256,256]{2,1,0:T(8,128)(2,1)S(1)}, f32[4,2,256,256]{3,2,1,0:T(8,128)S(1)}, f32[4,2,128,256]{3,2,1,0:T(8,128)S(1)}) custom-call(bf16[4,272,128]{2,1,0:T(8,128)(2,1)S(1)} %bitcast.4, f32[4,2,256,256]{3,2,1,0:T(8,128)} %probe.1, f32[1,1,1,256,256]{4,3,2,1,0:T(8,128)} %measured.1, ...), custom_call_target="tpu_custom_call" | custom-call | flops 1000000000 | bytes 4194304 | tf_op jit(solution)/shard_map/prepare/pallas_call | solution.py:372
  18.4 1.2 %collective-permute-done.1.second = bf16[4,272,128]{2,1,0:T(8,128)(2,1)S(1)} collective-permute-done((bf16[4,272,128]{2,1,0:T(8,128)(2,1)S(1)}, bf16[4,272,128]{2,1,0:T(8,128)(2,1)S(1)}, u32[]{:S(2)}, u32[]{:S(2)}) %collective-permute-start.1) | collective-permute-done | bytes 278560 | tf_op jit(solution)/shard_map/ppermute | solution.py:414
  19.6 0.0 collective-permute-done.first
  19.6 2.2 %frame.1 = (bf16[272,256]{1,0:T(8,128)(2,1)S(1)}, bf16[272,256]{1,0:T(8,128)(2,1)S(1)}) custom-call(bf16[4,272,128]{2,1,0:T(8,128)(2,1)S(1)} %collective-permute-done.first, bf16[4,272,128]{2,1,0:T(8,128)(2,1)S(1)} %collective-permute-done.1.second, bf16[16,256]{1,0:T(8,128)(2,1)S(1)} %get-tuple-element.12.info, f32[256,256]{1,0:T(8,128)S(1)} %get-tuple-element.13.amplitude, ...), custom_call_target="tpu_custom_call" | custom-call | flops 2000000000 | bytes 4194304 | tf_op jit(solution)/shard_map/frame/pallas_call | solution.py:372
  21.8 0.1 collective-permute-start.2
  21.9 1.3 %collective-permute-done.2.first = bf16[272,256]{1,0:T(8,128)(2,1)S(1)} collective-permute-done((bf16[272,256]{1,0:T(8,128)(2,1)S(1)}, bf16[272,256]{1,0:T(8,128)(2,1)S(1)}, u32[]{:S(2)}, u32[]{:S(2)}) %collective-permute-start.2) | collective-permute-done | bytes 139296 | tf_op jit(solution)/shard_map/ppermute | solution.py:455
  23.2 0.3 fold.1
  23.5 14.0 %all_to_all.5 = bf16[8,256,128]{2,1,0:T(8,128)(2,1)S(1)} all-to-all(bf16[8,256,128]{2,1,0:T(8,128)(2,1)S(1)} %fold.1), channel_id=1, replica_groups={{4,5,6,7,8,9,10,11},{12,13,14,15,16,17,18,19},{20,21,22,23,24,25,26,27}..., dimensions={0} | all-to-all | bytes 1048576 | tf_op jit(solution)/shard_map/all_to_all | solution.py:468
  37.5 0.7 %convert_reduce_fusion = f32[256,128]{1,0:T(8,128)} fusion(bf16[8,256,128]{2,1,0:T(8,128)(2,1)S(1)} %all_to_all.5), kind=kLoop, calls=%fused_computation | loop fusion | flops 491520 | bytes 655360 | tf_op jit(solution)/shard_map/reduce_sum | solution.py:471
Async XLA Ops:
  9.6 10.0 %collective-permute-start.1 = (bf16[4,272,128]{2,1,0:T(8,128)(2,1)S(1)}, bf16[4,272,128]{2,1,0:T(8,128)(2,1)S(1)}, u32[]{:S(2)}, u32[]{:S(2)}) collective-permute-start(bf16[4,272,128]{2,1,0:T(8,128)(2,1)S(1)} %bitcast.2), channel_id=1, source_target_pairs={{4,8},{12,16},{20,24},{8,4},{16,12},{24,20},{5,9},{13,17},{21,25},... | collective-permute-start | bytes 835592 | tf_op jit(solution)/shard_map/ppermute | solution.py:414
  15.3 4.2 %collective-permute-start = (bf16[4,272,128]{2,1,0:T(8,128)(2,1)S(1)}, bf16[4,272,128]{2,1,0:T(8,128)(2,1)S(1)}, u32[]{:S(2)}, u32[]{:S(2)}) collective-permute-start(bf16[4,272,128]{2,1,0:T(8,128)(2,1)S(1)} %bitcast.3), channel_id=1, source_target_pairs={{0,4},{8,12},{16,20},{24,28},{4,0},{12,8},{20,16},{28,24},{1,5},{9... | collective-permute-start | bytes 835592 | tf_op jit(solution)/shard_map/ppermute | solution.py:415
  21.8 1.4 %collective-permute-start.2 = (bf16[272,256]{1,0:T(8,128)(2,1)S(1)}, bf16[272,256]{1,0:T(8,128)(2,1)S(1)}, u32[]{:S(2)}, u32[]{:S(2)}) collective-permute-start(bf16[272,256]{1,0:T(8,128)(2,1)S(1)} %get-tuple-element.18.to_rows), channel_id=1, source_target_pairs={{0,4},{8,12},{16,20},{24,28},{4,0},{12,8},{20,16},{28,24},{1,5},{9... | collective-permute-start | bytes 417800 | tf_op jit(solution)/shard_map/ppermute | solution.py:455

commit v8 on v6

--- a/solution.py
+++ b/solution.py
@@ -102,6 +102,18 @@
     return out
 
 
+def frame_of(band):
+    columns, height, lanes = band.shape
+    me = lax.axis_index("col").astype(F32)
+    code = jnp.zeros((1, lanes), F32)
+    for c in range(columns):
+        info = band[c, height - INFO :].astype(F32)
+        hit = info[0:1] == me
+        code += jnp.where(hit, c * 128.0 * 128.0 + info[1:2] * 128.0 + info[2:3], 0.0)
+    code = jnp.sum(code).astype(jnp.int32)
+    return code // (128 * 128), code // 128 % 128, code % 128
+
+
 def prepare_kernel(
     band, probe, measured, tables,
     info_out, amplitude, tables_out, probe_out, half_out, raw, raw_tables, raw_probe, groups, sems,
@@ -110,22 +122,11 @@
         ((measured, raw), (tables, raw_tables), (probe, raw_probe)), sems
     )
     columns = band.shape[0]
-    lanes = band.shape[2]
     tile = (band.shape[1] - INFO) // 2
     extent = raw.shape[-1]
     half = extent // 2
     modes = raw_probe.shape[0]
-    me = lax.axis_index("col").astype(F32)
-
-    code = jnp.zeros((1, lanes), F32)
-    for c in range(columns):
-        info = band[c, 2 * tile :].astype(F32)
-        hit = info[0:1] == me
-        code += jnp.where(hit, c * 128.0 * 128.0 + info[1:2] * 128.0 + info[2:3], 0.0)
-    code = jnp.sum(code).astype(jnp.int32)
-    source = code // (128 * 128)
-    row = code // 128 % 128
-    col = code % 128
+    source, row, col = frame_of(band)
     which = iota((INFO, extent), 0)
     info = jnp.where(which == 0, source, jnp.where(which == 1, col, row))
     info_out[...] = info.astype(F32).astype(BF16)
@@ -199,7 +200,7 @@
 
 def frame_kernel(
     first, second, info, amplitude, tables, probe, half_own,
-    to_rows, centre, patch, folded, half_far, mixed, far, corrected, product, mixed_back, turned,
+    to_rows, turned, patch, folded, half_far, mixed, far, corrected, product, mixed_back,
 ):
     columns = first.shape[0]
     tile = (first.shape[1] - INFO) // 2
@@ -285,20 +286,6 @@
 
     def back_along_columns(k, q):
         turned[k, q] = dot(tables[6 + q], mixed_back[k, q])
-
-    def accumulate(s, t):
-        total = [[0.0, 0.0], [0.0, 0.0]]
-        for k in range(modes):
-            er, ei, our, oui = turned[k, 0, s], turned[k, 0, t], turned[k, 1, s], turned[k, 1, t]
-            for i, (cr, ci, rows) in enumerate(
-                ((er + our, ei + oui, s), (er - our, ei - oui, t))
-            ):
-                pr, pi = probe[k, 0, rows], probe[k, 1, rows]
-                total[i][0] += pr * cr + pi * ci
-                total[i][1] += pr * ci - pi * cr
-        for out, parts in zip((to_rows, centre), total):
-            for p in range(2):
-                out[pl.ds(p * tile + s.start, STRIP)] = parts[p].astype(BF16)
 
     for s in strips:
         gather(s)
@@ -324,35 +311,71 @@
         mix_back(k, 1)
         back_along_columns(k, 1)
     for s, t in zip(strips, lower):
-        accumulate(s, t)
-    for out in (to_rows, centre):
-        out[2 * tile :] = info[...]
-
-
-def fold_kernel(centre, second, first, out):
+        accumulate(to_rows, turned, probe, s, t, s, 1)
+
+
+def accumulate(out, turned, probe, s, t, rows, sign):
+    tile = out.shape[0] // 2
+    re = im = 0.0
+    for k in range(probe.shape[0]):
+        pr, pi = probe[k, 0, rows], probe[k, 1, rows]
+        cr = turned[k, 0, s] + sign * turned[k, 1, s]
+        ci = turned[k, 0, t] + sign * turned[k, 1, t]
+        re += pr * cr + pi * ci
+        im += pr * ci - pi * cr
+    out[s] = re.astype(BF16)
+    out[pl.ds(tile + s.start, STRIP)] = im.astype(BF16)
+
+
+def place(block, columns, source, col, taken):
+    tile = block.shape[1] // 2
+    beside, own = block[:, :tile], block[:, tile:]
+    lane = iota(own.shape, 1)
+    if taken is not None:
+        beside, own = jnp.where(taken, beside, 0.0), jnp.where(taken, own, 0.0)
+    out = []
+    for c in range(columns):
+        near = ((source == c + 1) & (lane >= col)) | ((source == c - 1) & (lane < col))
+        out.append(jnp.where(near, beside, 0.0) + jnp.where(source == c, own, 0.0))
+    return out
+
+
+def finish_kernel(
+    band, first_band, second_band, turned, probe, first, partial, second_info, centre,
+):
+    columns = band.shape[0]
+    tile = (band.shape[1] - INFO) // 2
+    odd = lax.axis_index("row") % 2
+    own_frame, first_frame, second_frame = (
+        frame_of(b) for b in (band, first_band, second_band)
+    )
+    which = iota(second_info.shape, 0)
+    second_info[...] = jnp.where(
+        which == 0, second_frame[0], jnp.where(which == 1, second_frame[1], second_frame[2])
+    )
+    for r in range(0, tile, STRIP):
+        s, t = pl.ds(r, STRIP), pl.ds(tile + r, STRIP)
+        accumulate(centre, turned, probe, s, t, t, -1)
+        before = (iota((STRIP, tile), 0) + r < first_frame[1]).astype(jnp.int32)
+        for part in (s, t):
+            mine = place(centre[part].astype(F32), columns, own_frame[0], own_frame[2], None)
+            other = place(
+                first[part].astype(F32), columns, first_frame[0], first_frame[2], before == odd
+            )
+            for c in range(columns):
+                partial[c, part] = mine[c] + other[c]
+
+
+def fold_kernel(partial, second, second_info, out):
     columns, height, tile = out.shape
     odd = lax.axis_index("row") % 2
-    shape = (tile, tile)
-    lane = iota(shape, 1)
-    totals = [[jnp.zeros(shape, F32) for _ in range(columns)] for _ in range(2)]
-    for which, part in enumerate((centre, second, first)):
-        source, col, row = (
-            part[height + r : height + r + 1, :tile].astype(F32).astype(jnp.int32)
-            for r in range(3)
-        )
-        before = (iota(shape, 0) < row).astype(jnp.int32)
-        taken = before == (odd if which == 2 else 1 - odd)
-        for p in range(2):
-            block = part[p * tile : (p + 1) * tile].astype(F32)
-            beside, own = block[:, :tile], block[:, tile:]
-            if which:
-                beside, own = jnp.where(taken, beside, 0.0), jnp.where(taken, own, 0.0)
-            for c in range(columns):
-                near = ((source == c + 1) & (lane >= col)) | ((source == c - 1) & (lane < col))
-                totals[p][c] += jnp.where(near, beside, 0.0) + jnp.where(source == c, own, 0.0)
-    for p in range(2):
+    source, row, col = (second_info[r : r + 1] for r in range(3))
+    for r in range(0, height, STRIP):
+        s = pl.ds(r, STRIP)
+        before = (iota((STRIP, tile), 0) + r % tile < row).astype(jnp.int32)
+        other = place(second[s].astype(F32), columns, source, col, before == 1 - odd)
         for c in range(columns):
-            out[c, p * tile : (p + 1) * tile] = totals[p][c].astype(BF16)
+            out[c, s] = (partial[c, s] + other[c]).astype(BF16)
 
 
 def call(kernel, name, out_shape, in_specs, scratch, flops, moved, *args):
@@ -379,7 +402,7 @@
     modes = probe.shape[0]
     columns = lax.axis_size("col")
     height = 2 * tile
-    part = jax.ShapeDtypeStruct((height + INFO, extent), BF16)
+    part = jax.ShapeDtypeStruct((height, extent), BF16)
     dma = pltpu.SemaphoreType.DMA
 
     packed = call(
@@ -425,33 +448,44 @@
         10**9, 2**22,
         band, probe, measured, tables,
     )
-    to_rows, centre = call(
+    full = (modes, 2, extent, extent)
+    to_rows, turned = call(
         frame_kernel, "frame",
-        (part, part),
+        (part, jax.ShapeDtypeStruct(full, F32)),
         [VMEM] * 7,
         [
             pltpu.VMEM((2, tile, extent), F32),
             pltpu.VMEM((modes, 2, half, extent), BF16),
             pltpu.VMEM((modes, 2, half, extent), F32),
-            pltpu.VMEM((modes, 2, extent, extent), BF16),
-            pltpu.VMEM((modes, 2, extent, extent), F32),
-            pltpu.VMEM((modes, 2, extent, extent), BF16),
-            pltpu.VMEM((modes, 2, extent, extent), F32),
-            pltpu.VMEM((modes, 2, extent, extent), BF16),
-            pltpu.VMEM((modes, 2, extent, extent), F32),
+            pltpu.VMEM(full, BF16),
+            pltpu.VMEM(full, F32),
+            pltpu.VMEM(full, BF16),
+            pltpu.VMEM(full, F32),
+            pltpu.VMEM(full, BF16),
         ],
         2 * 10**9, 2**22,
         first, second, *prepared,
     )
     from_first = lax.ppermute(to_rows, "row", swaps[0])
     from_second = lax.ppermute(to_rows, "row", swaps[1])
+    partial, second_info = call(
+        finish_kernel, "finish",
+        (
+            jax.ShapeDtypeStruct((columns, height, tile), F32),
+            jax.ShapeDtypeStruct((8, tile), jnp.int32),
+        ),
+        [VMEM] * 6,
+        [pltpu.VMEM((height, extent), BF16)],
+        10**7, 2**22,
+        band, first, second, turned, prepared[3], from_first,
+    )
     summed = call(
         fold_kernel, "fold",
         jax.ShapeDtypeStruct((columns, height, tile), BF16),
         [VMEM] * 3,
         [],
-        10**9, 2**20,
-        centre, from_second, from_first,
+        10**7, 2**20,
+        partial, from_second, second_info,
     )
     shares = lax.all_to_all(summed, "col", split_axis=0, concat_axis=0, tiled=True)
     return jnp.sum(shares.astype(F32), axis=0).reshape(2, tile, tile)

time: 37.5 us -> 36.8 us (0.981)
  waiting for transfers between devices: 5.64 us -> 5.1 us
    ppermute x1, waiting for transfers between devices: 4.44 us -> 3.88 us  [per_device(): from_second = lax.ppermute(to_rows, 'row', swaps[1])]
    pallas_call x4 -> x5, Pallas kernels: 6.45 us -> 6.25 us  [call(): pl.pallas_call(kernel, out_shape=out_shape, in_specs=in_specs, out_specs=...]
  transfers between devices with their start and end apart: 4 -> 4, of which waited for: 2 -> 2; matrix products, arithmetic and copies ran while one was open for 0% -> 0% of each run, Pallas kernels for 8% -> 9%
where the time goes in v8:
time: 36.8 us; the launch traced here: 36.6 us
  blocking collectives  18.1 us (49%)
  Pallas kernels  6.25 us (17%)
  starting transfers between devices  5.74 us (16%)
  waiting for transfers between devices  5.1 us (14%)
  between operations  0.71 us (2%)
  other arithmetic  0.69 us (2%)
    all_gather x1, blocking collectives, per_device(): band = lax.all_gather(packed, 'col')  9.13 us
    all_to_all x1, blocking collectives, per_device(): lax.all_to_all(summed, 'col', split_axis=0, concat_axis=0, tiled=True)  8.94 us
    pallas_call x5, Pallas kernels, call(): pl.pallas_call(kernel, out_shape=out_shape, in_specs=in_specs, out_specs=...  6.25 us
    ppermute x1, waiting for transfers between devices, per_device(): from_second = lax.ppermute(to_rows, 'row', swaps[1])  3.88 us
    ppermute x1, starting transfers between devices, per_device(): second = lax.ppermute(band, 'row', swaps[1])  1.91 us
    ppermute x1, starting transfers between devices, per_device(): from_second = lax.ppermute(to_rows, 'row', swaps[1])  1.91 us
    ppermute x1, starting transfers between devices, per_device(): first = lax.ppermute(band, 'row', swaps[0])  1.74 us
    ppermute x1, waiting for transfers between devices, per_device(): second = lax.ppermute(band, 'row', swaps[1])  1.22 us
  transfers between devices with their start and end apart: 4, of which 2 were waited for; matrix products, arithmetic and copies ran while one was open for 0% of the time, Pallas kernels for 9%

profile of v8, /device:TPU:8, one launch (start us, length us, event | category | flops | bytes accessed | tf_op | source)
XLA Modules:
  0.0 36.6 jit_solution(6626646565582964711)
XLA Ops:
  0.7 1.0 %pack.1 = bf16[272,128]{1,0:T(8,128)(2,1)S(1)} custom-call(f32[2,128,128]{2,1,0:T(8,128)} %specimen.1, s32[1,1,2,2]{3,2,1,0:T(2,128)} %centers.1, s32[1,1]{1,0:T(1,128)S(6)} %copy.8.cnt, s32[1,1,2]{2,1,0:T(1,128)} %helpers.1), custom_call_target="tpu_custom_call" | custom-call | flops 100000 | bytes 524288 | tf_op jit(solution)/shard_map/pack/pallas_call | solution.py:386
  1.6 9.1 %all-gather = bf16[1088,128]{1,0:T(8,128)(2,1)S(1)} all-gather(bf16[272,128]{1,0:T(8,128)(2,1)S(1)} %pack.1), channel_id=2, replica_groups=mesh['row'=8,'col'=4] {'col'}, dimensions={0}, use_global_device_ids=true | all-gather | bytes 348160 | tf_op jit(solution)/shard_map/all_gather | solution.py:421
  10.8 1.9 %collective-permute-start.1 = (bf16[4,272,128]{2,1,0:T(8,128)(2,1)S(1)}, bf16[4,272,128]{2,1,0:T(8,128)(2,1)S(1)}, u32[]{:S(2)}, u32[]{:S(2)}) collective-permute-start(bf16[4,272,128]{2,1,0:T(8,128)(2,1)S(1)} %bitcast.2), channel_id=1, source_target_pairs={{4,8},{12,16},{20,24},{8,4},{16,12},{24,20},{5,9},{13,17},{21,25},... | collective-permute-start | bytes 835592 | tf_op jit(solution)/shard_map/ppermute | solution.py:428
  12.7 1.7 %collective-permute-start = (bf16[4,272,128]{2,1,0:T(8,128)(2,1)S(1)}, bf16[4,272,128]{2,1,0:T(8,128)(2,1)S(1)}, u32[]{:S(2)}, u32[]{:S(2)}) collective-permute-start(bf16[4,272,128]{2,1,0:T(8,128)(2,1)S(1)} %bitcast.3), channel_id=1, source_target_pairs={{0,4},{8,12},{16,20},{24,28},{4,0},{12,8},{20,16},{28,24},{1,5},{9... | collective-permute-start | bytes 835592 | tf_op jit(solution)/shard_map/ppermute | solution.py:429
  14.4 3.0 %prepare.1 = (bf16[16,256]{1,0:T(8,128)(2,1)S(1)}, f32[256,256]{1,0:T(8,128)S(1)}, bf16[8,256,256]{2,1,0:T(8,128)(2,1)S(1)}, f32[4,2,256,256]{3,2,1,0:T(8,128)S(1)}, f32[4,2,128,256]{3,2,1,0:T(8,128)S(1)}) custom-call(bf16[4,272,128]{2,1,0:T(8,128)(2,1)S(1)} %bitcast.4, f32[4,2,256,256]{3,2,1,0:T(8,128)} %probe.1, f32[1,1,1,256,256]{4,3,2,1,0:T(8,128)} %measured.1, ...), custom_call_target="tpu_custom_call" | custom-call | flops 1000000000 | bytes 4194304 | tf_op jit(solution)/shard_map/prepare/pallas_call | solution.py:386
  17.4 1.2 %collective-permute-done.1.second.second_band = bf16[4,272,128]{2,1,0:T(8,128)(2,1)S(1)} collective-permute-done((bf16[4,272,128]{2,1,0:T(8,128)(2,1)S(1)}, bf16[4,272,128]{2,1,0:T(8,128)(2,1)S(1)}, u32[]{:S(2)}, u32[]{:S(2)}) %collective-permute-start.1) | collective-permute-done | bytes 278560 | tf_op jit(solution)/shard_map/ppermute | solution.py:428
  18.6 0.0 collective-permute-done.first.first_band
  18.6 1.7 %frame.1 = (bf16[256,256]{1,0:T(8,128)(2,1)S(1)}, f32[4,2,256,256]{3,2,1,0:T(8,128)S(1)}) custom-call(bf16[4,272,128]{2,1,0:T(8,128)(2,1)S(1)} %collective-permute-done.first.first_band, bf16[4,272,128]{2,1,0:T(8,128)(2,1)S(1)} %collective-permute-done.1.second.second_band, bf16[16,256]{1,0:T(8,128)(2,1)S(1)} %get-tuple-element.14.info, ...), custom_call_target="tpu_custom_call" | custom-call | flops 2000000000 | bytes 4194304 | tf_op jit(solution)/shard_map/frame/pallas_call | solution.py:386
  20.4 0.2 collective-permute-start.2
  20.5 1.9 %collective-permute-start.3 = (bf16[256,256]{1,0:T(8,128)(2,1)S(1)}, bf16[256,256]{1,0:T(8,128)(2,1)S(1)}, u32[]{:S(2)}, u32[]{:S(2)}) collective-permute-start(bf16[256,256]{1,0:T(8,128)(2,1)S(1)} %get-tuple-element.20), channel_id=1, source_target_pairs={{4,8},{12,16},{20,24},{8,4},{16,12},{24,20},{5,9},{13,17},{21,25},... | collective-permute-start | bytes 393224 | tf_op jit(solution)/shard_map/ppermute | solution.py:470
  22.5 0.0 collective-permute-done.2.first
  22.5 0.5 %finish.1 = (f32[4,256,128]{2,1,0:T(8,128)S(1)}, s32[8,128]{1,0:T(8,128)S(1)}) custom-call(bf16[4,272,128]{2,1,0:T(8,128)(2,1)S(1)} %bitcast.5, bf16[4,272,128]{2,1,0:T(8,128)(2,1)S(1)} %collective-permute-done.first.first_band, bf16[4,272,128]{2,1,0:T(8,128)(2,1)S(1)} %collective-permute-done.1.second.second_band, ...), custom_call_target="tpu_custom_call" | custom-call | flops 10000000 | bytes 4194304 | tf_op jit(solution)/shard_map/finish/pallas_call | solution.py:386
  22.9 3.9 %collective-permute-done.3.second = bf16[256,256]{1,0:T(8,128)(2,1)S(1)} collective-permute-done((bf16[256,256]{1,0:T(8,128)(2,1)S(1)}, bf16[256,256]{1,0:T(8,128)(2,1)S(1)}, u32[]{:S(2)}, u32[]{:S(2)}) %collective-permute-start.3) | collective-permute-done | bytes 131104 | tf_op jit(solution)/shard_map/ppermute | solution.py:470
  26.8 0.1 fold.1
  26.9 8.9 %all_to_all.5 = bf16[4,256,128]{2,1,0:T(8,128)(2,1)S(1)} all-to-all(bf16[4,256,128]{2,1,0:T(8,128)(2,1)S(1)} %fold.1), channel_id=1, replica_groups=mesh['row'=8,'col'=4] {'col'}, dimensions={0} | all-to-all | bytes 524288 | tf_op jit(solution)/shard_map/all_to_all | solution.py:490
  35.9 0.7 %convert_reduce_fusion = f32[256,128]{1,0:T(8,128)} fusion(bf16[4,256,128]{2,1,0:T(8,128)(2,1)S(1)} %all_to_all.5), kind=kLoop, calls=%fused_computation | loop fusion | flops 229376 | bytes 393216 | tf_op jit(solution)/shard_map/reduce_sum | solution.py:491
Async XLA Ops:
  10.8 7.9 %collective-permute-start.1 = (bf16[4,272,128]{2,1,0:T(8,128)(2,1)S(1)}, bf16[4,272,128]{2,1,0:T(8,128)(2,1)S(1)}, u32[]{:S(2)}, u32[]{:S(2)}) collective-permute-start(bf16[4,272,128]{2,1,0:T(8,128)(2,1)S(1)} %bitcast.2), channel_id=1, source_target_pairs={{4,8},{12,16},{20,24},{8,4},{16,12},{24,20},{5,9},{13,17},{21,25},... | collective-permute-start | bytes 835592 | tf_op jit(solution)/shard_map/ppermute | solution.py:428
  12.7 5.9 %collective-permute-start = (bf16[4,272,128]{2,1,0:T(8,128)(2,1)S(1)}, bf16[4,272,128]{2,1,0:T(8,128)(2,1)S(1)}, u32[]{:S(2)}, u32[]{:S(2)}) collective-permute-start(bf16[4,272,128]{2,1,0:T(8,128)(2,1)S(1)} %bitcast.3), channel_id=1, source_target_pairs={{0,4},{8,12},{16,20},{24,28},{4,0},{12,8},{20,16},{28,24},{1,5},{9... | collective-permute-start | bytes 835592 | tf_op jit(solution)/shard_map/ppermute | solution.py:429
  20.4 2.1 %collective-permute-start.2 = (bf16[256,256]{1,0:T(8,128)(2,1)S(1)}, bf16[256,256]{1,0:T(8,128)(2,1)S(1)}, u32[]{:S(2)}, u32[]{:S(2)}) collective-permute-start(bf16[256,256]{1,0:T(8,128)(2,1)S(1)} %get-tuple-element.20), channel_id=1, source_target_pairs={{0,4},{8,12},{16,20},{24,28},{4,0},{12,8},{20,16},{28,24},{1,5},{9... | collective-permute-start | bytes 393224 | tf_op jit(solution)/shard_map/ppermute | solution.py:469
  20.5 6.3 %collective-permute-start.3 = (bf16[256,256]{1,0:T(8,128)(2,1)S(1)}, bf16[256,256]{1,0:T(8,128)(2,1)S(1)}, u32[]{:S(2)}, u32[]{:S(2)}) collective-permute-start(bf16[256,256]{1,0:T(8,128)(2,1)S(1)} %get-tuple-element.20), channel_id=1, source_target_pairs={{4,8},{12,16},{20,24},{8,4},{16,12},{24,20},{5,9},{13,17},{21,25},... | collective-permute-start | bytes 393224 | tf_op jit(solution)/shard_map/ppermute | solution.py:470

commit v9 on v8

--- a/solution.py
+++ b/solution.py
@@ -102,31 +102,37 @@
     return out
 
 
-def frame_of(band):
-    columns, height, lanes = band.shape
+def frame_of(band, base, columns):
+    _, height, lanes = band.shape
     me = lax.axis_index("col").astype(F32)
     code = jnp.zeros((1, lanes), F32)
     for c in range(columns):
-        info = band[c, height - INFO :].astype(F32)
+        info = band[base + c, height - INFO :].astype(F32)
         hit = info[0:1] == me
         code += jnp.where(hit, c * 128.0 * 128.0 + info[1:2] * 128.0 + info[2:3], 0.0)
     code = jnp.sum(code).astype(jnp.int32)
     return code // (128 * 128), code // 128 % 128, code % 128
 
 
+def halves(bands):
+    columns = bands.shape[0] // 2
+    odd = lax.axis_index("row") % 2
+    return odd * columns, (1 - odd) * columns, columns
+
+
 def prepare_kernel(
-    band, probe, measured, tables,
+    bands, probe, measured, tables,
     info_out, amplitude, tables_out, probe_out, half_out, raw, raw_tables, raw_probe, groups, sems,
 ):
     copies = fetch(
         ((measured, raw), (tables, raw_tables), (probe, raw_probe)), sems
     )
-    columns = band.shape[0]
-    tile = (band.shape[1] - INFO) // 2
+    mine, _, columns = halves(bands)
+    tile = (bands.shape[1] - INFO) // 2
     extent = raw.shape[-1]
     half = extent // 2
     modes = raw_probe.shape[0]
-    source, row, col = frame_of(band)
+    source, row, col = frame_of(bands, mine, columns)
     which = iota((INFO, extent), 0)
     info = jnp.where(which == 0, source, jnp.where(which == 1, col, row))
     info_out[...] = info.astype(F32).astype(BF16)
@@ -185,7 +191,7 @@
 
     patch = [
         gather_columns(
-            lambda c: band[c, p * tile : (p + 1) * tile].astype(F32),
+            lambda c: bands[mine + c, p * tile : (p + 1) * tile].astype(F32),
             source, col, columns, (tile, tile),
         )
         for p in range(2)
@@ -199,11 +205,11 @@
 
 
 def frame_kernel(
-    first, second, info, amplitude, tables, probe, half_own,
+    bands, second, info, amplitude, tables, probe, half_own,
     to_rows, turned, patch, folded, half_far, mixed, far, corrected, product, mixed_back,
 ):
-    columns = first.shape[0]
-    tile = (first.shape[1] - INFO) // 2
+    _, theirs, columns = halves(bands)
+    tile = (bands.shape[1] - INFO) // 2
     extent = probe.shape[-1]
     half = extent // 2
     modes = probe.shape[0]
@@ -227,7 +233,7 @@
             part = pl.ds(p * tile + s.start, STRIP)
             patch[p, s] = gather_columns(
                 lambda c: jnp.where(
-                    from_first, first[c, part].astype(F32), second[c, part].astype(F32)
+                    from_first, bands[theirs + c, part].astype(F32), second[c, part].astype(F32)
                 ),
                 source, col, columns, (STRIP, tile),
             )
@@ -341,13 +347,14 @@
 
 
 def finish_kernel(
-    band, first_band, second_band, turned, probe, first, partial, second_info, centre,
+    bands, second_band, turned, probe, first, partial, second_info, centre,
 ):
-    columns = band.shape[0]
-    tile = (band.shape[1] - INFO) // 2
+    mine, theirs, columns = halves(bands)
+    tile = (bands.shape[1] - INFO) // 2
     odd = lax.axis_index("row") % 2
     own_frame, first_frame, second_frame = (
-        frame_of(b) for b in (band, first_band, second_band)
+        frame_of(ref, base, columns)
+        for ref, base in ((bands, mine), (bands, theirs), (second_band, 0))
     )
     which = iota(second_info.shape, 0)
     second_info[...] = jnp.where(
@@ -358,12 +365,12 @@
         accumulate(centre, turned, probe, s, t, t, -1)
         before = (iota((STRIP, tile), 0) + r < first_frame[1]).astype(jnp.int32)
         for part in (s, t):
-            mine = place(centre[part].astype(F32), columns, own_frame[0], own_frame[2], None)
+            own = place(centre[part].astype(F32), columns, own_frame[0], own_frame[2], None)
             other = place(
                 first[part].astype(F32), columns, first_frame[0], first_frame[2], before == odd
             )
             for c in range(columns):
-                partial[c, part] = mine[c] + other[c]
+                partial[c, part] = own[c] + other[c]
 
 
 def fold_kernel(partial, second, second_info, out):
@@ -418,15 +425,18 @@
         10**5, 2**19,
         specimen, centers, frame_counts, helper_cols,
     )
-    band = lax.all_gather(packed, "col")
-
     rows = lax.axis_size("row")
     swaps = []
     for start in (0, 1):
         pairs = [(i, i + 1) for i in range(start, rows - 1, 2)]
         swaps.append(pairs + [(b, a) for a, b in pairs])
+    groups = [
+        [r * columns + c for r in (start, start + 1) for c in range(columns)]
+        for start in range(0, rows, 2)
+    ]
+    bands = lax.all_gather(packed, ("row", "col"), axis_index_groups=groups)
+    band = lax.dynamic_slice_in_dim(bands, lax.axis_index("row") % 2 * columns, columns)
     second = lax.ppermute(band, "row", swaps[1])
-    first = lax.ppermute(band, "row", swaps[0])
     tables = dft_tables(extent)
     prepared = call(
         prepare_kernel, "prepare",
@@ -446,7 +456,7 @@
             dma((3,)),
         ],
         10**9, 2**22,
-        band, probe, measured, tables,
+        bands, probe, measured, tables,
     )
     full = (modes, 2, extent, extent)
     to_rows, turned = call(
@@ -464,7 +474,7 @@
             pltpu.VMEM(full, BF16),
         ],
         2 * 10**9, 2**22,
-        first, second, *prepared,
+        bands, second, *prepared,
     )
     from_first = lax.ppermute(to_rows, "row", swaps[0])
     from_second = lax.ppermute(to_rows, "row", swaps[1])
@@ -474,10 +484,10 @@
             jax.ShapeDtypeStruct((columns, height, tile), F32),
             jax.ShapeDtypeStruct((8, tile), jnp.int32),
         ),
-        [VMEM] * 6,
+        [VMEM] * 5,
         [pltpu.VMEM((height, extent), BF16)],
         10**7, 2**22,
-        band, first, second, turned, prepared[3], from_first,
+        bands, second, turned, prepared[3], from_first,
     )
     summed = call(
         fold_kernel, "fold",

time: 36.8 us -> 53.2 us (1.45)
  blocking collectives: 18.1 us -> 34.3 us
  starting transfers between devices: 5.74 us -> 4.01 us
  waiting for transfers between devices: 5.1 us -> 6.81 us
    all_gather x1, blocking collectives: 9.13 us -> 25 us  [per_device(): bands = lax.all_gather(packed, ('row', 'col'), axis_index_groups=groups)]
    ppermute x1 -> x0, starting transfers between devices: 1.74 us -> none  [per_device(): first = lax.ppermute(band, 'row', swaps[0])]
    ppermute x1, waiting for transfers between devices: 1.22 us -> 2.94 us  [per_device(): second = lax.ppermute(band, 'row', swaps[1])]
  transfers between devices with their start and end apart: 4 -> 3, of which waited for: 2 -> 2; matrix products, arithmetic and copies ran while one was open for 0% -> 0% of each run, Pallas kernels for 9% -> 7%
where the time goes in v9:
time: 53.2 us; the launch traced here: 53 us
  blocking collectives  34.3 us (64%)
  waiting for transfers between devices  6.81 us (13%)
  Pallas kernels  6.45 us (12%)
  starting transfers between devices  4.01 us (8%)
  between operations  0.71 us (1%)
  other arithmetic  0.69 us (1%)
    all_gather x1, blocking collectives, per_device(): bands = lax.all_gather(packed, ('row', 'col'), axis_index_groups=groups)  25 us
    all_to_all x1, blocking collectives, per_device(): lax.all_to_all(summed, 'col', split_axis=0, concat_axis=0, tiled=True)  9.33 us
    pallas_call x5, Pallas kernels, call(): pl.pallas_call(kernel, out_shape=out_shape, in_specs=in_specs, out_specs=...  6.45 us
    ppermute x1, waiting for transfers between devices, per_device(): from_second = lax.ppermute(to_rows, 'row', swaps[1])  3.87 us
    ppermute x1, waiting for transfers between devices, per_device(): second = lax.ppermute(band, 'row', swaps[1])  2.94 us
    ppermute x1, starting transfers between devices, per_device(): second = lax.ppermute(band, 'row', swaps[1])  1.92 us
    ppermute x1, starting transfers between devices, per_device(): from_second = lax.ppermute(to_rows, 'row', swaps[1])  1.91 us
  transfers between devices with their start and end apart: 3, of which 2 were waited for; matrix products, arithmetic and copies ran while one was open for 0% of the time, Pallas kernels for 7%

profile of v9, /device:TPU:8, one launch (start us, length us, event | category | flops | bytes accessed | tf_op | source)
XLA Modules:
  0.0 53.0 jit_solution(17510771555800963817)
XLA Ops:
  0.7 1.0 %pack.1 = bf16[272,128]{1,0:T(8,128)(2,1)S(1)} custom-call(f32[2,128,128]{2,1,0:T(8,128)} %specimen.1, s32[1,1,2,2]{3,2,1,0:T(2,128)} %centers.1, s32[1,1]{1,0:T(1,128)S(6)} %copy.8.cnt, s32[1,1,2]{2,1,0:T(1,128)} %helpers.1), custom_call_target="tpu_custom_call" | custom-call | flops 100000 | bytes 524288 | tf_op jit(solution)/shard_map/pack/pallas_call | solution.py:393
  1.6 25.0 %all-gather = bf16[2176,128]{1,0:T(8,128)(2,1)S(1)} all-gather(bf16[272,128]{1,0:T(8,128)(2,1)S(1)} %pack.1), channel_id=2, replica_groups={{0,1,2,3,4,5,6,7},{8,9,10,11,12,13,14,15},{16,17,18,19,20,21,22,23},{24..., dimensions={0}, use_global_device_ids=true | all-gather | bytes 626688 | tf_op jit(solution)/shard_map/all_gather | solution.py:437
  26.6 1.9 %collective-permute-start = (bf16[4,272,128]{2,1,0:T(8,128)(2,1)S(1)}, bf16[4,272,128]{2,1,0:T(8,128)(2,1)S(1)}, u32[]{:S(2)}, u32[]{:S(2)}) collective-permute-start(bf16[4,272,128]{2,1,0:T(8,128)(2,1)S(1)} %constant_dynamic-slice_fusion), channel_id=1, source_target_pairs={{4,8},{12,16},{20,24},{8,4},{16,12},{24,20},{5,9},{13,17},{21,25},... | collective-permute-start | bytes 835592 | tf_op jit(solution)/shard_map/ppermute | solution.py:439
  28.5 3.0 %prepare.1 = (bf16[16,256]{1,0:T(8,128)(2,1)S(1)}, f32[256,256]{1,0:T(8,128)S(1)}, bf16[8,256,256]{2,1,0:T(8,128)(2,1)S(1)}, f32[4,2,256,256]{3,2,1,0:T(8,128)S(1)}, f32[4,2,128,256]{3,2,1,0:T(8,128)S(1)}) custom-call(bf16[8,272,128]{2,1,0:T(8,128)(2,1)S(1)} %bitcast.3, f32[4,2,256,256]{3,2,1,0:T(8,128)} %probe.1, f32[1,1,1,256,256]{4,3,2,1,0:T(8,128)} %measured.1, ...), custom_call_target="tpu_custom_call" | custom-call | flops 1000000000 | bytes 4194304 | tf_op jit(solution)/shard_map/prepare/pallas_call | solution.py:393
  31.5 2.9 %collective-permute-done.second.second_band = bf16[4,272,128]{2,1,0:T(8,128)(2,1)S(1)} collective-permute-done((bf16[4,272,128]{2,1,0:T(8,128)(2,1)S(1)}, bf16[4,272,128]{2,1,0:T(8,128)(2,1)S(1)}, u32[]{:S(2)}, u32[]{:S(2)}) %collective-permute-start) | collective-permute-done | bytes 278560 | tf_op jit(solution)/shard_map/ppermute | solution.py:439
  34.5 1.9 %frame.1 = (bf16[256,256]{1,0:T(8,128)(2,1)S(1)}, f32[4,2,256,256]{3,2,1,0:T(8,128)S(1)}) custom-call(bf16[8,272,128]{2,1,0:T(8,128)(2,1)S(1)} %bitcast.4, bf16[4,272,128]{2,1,0:T(8,128)(2,1)S(1)} %collective-permute-done.second.second_band, bf16[16,256]{1,0:T(8,128)(2,1)S(1)} %get-tuple-element.14.info, f32[256,256]{1,0:T(8,128)S(1)} %get-tuple-element.15.amplitude, ...), custom_call_target="tpu_custom_call" | custom-call | flops 2000000000 | bytes 4194304 | tf_op jit(solution)/shard_map/frame/pallas_call | solution.py:393
  36.4 0.2 collective-permute-start.1
  36.6 1.9 %collective-permute-start.2 = (bf16[256,256]{1,0:T(8,128)(2,1)S(1)}, bf16[256,256]{1,0:T(8,128)(2,1)S(1)}, u32[]{:S(2)}, u32[]{:S(2)}) collective-permute-start(bf16[256,256]{1,0:T(8,128)(2,1)S(1)} %get-tuple-element.20), channel_id=1, source_target_pairs={{4,8},{12,16},{20,24},{8,4},{16,12},{24,20},{5,9},{13,17},{21,25},... | collective-permute-start | bytes 393224 | tf_op jit(solution)/shard_map/ppermute | solution.py:480
  38.5 0.0 collective-permute-done.1.first
  38.5 0.5 finish.1
  39.0 3.9 %collective-permute-done.2.second = bf16[256,256]{1,0:T(8,128)(2,1)S(1)} collective-permute-done((bf16[256,256]{1,0:T(8,128)(2,1)S(1)}, bf16[256,256]{1,0:T(8,128)(2,1)S(1)}, u32[]{:S(2)}, u32[]{:S(2)}) %collective-permute-start.2) | collective-permute-done | bytes 131104 | tf_op jit(solution)/shard_map/ppermute | solution.py:480
  42.9 0.1 fold.1
  43.0 9.3 %all_to_all.5 = bf16[4,256,128]{2,1,0:T(8,128)(2,1)S(1)} all-to-all(bf16[4,256,128]{2,1,0:T(8,128)(2,1)S(1)} %fold.1), channel_id=1, replica_groups=mesh['row'=8,'col'=4] {'col'}, dimensions={0} | all-to-all | bytes 524288 | tf_op jit(solution)/shard_map/all_to_all | solution.py:500
  52.3 0.7 %convert_reduce_fusion = f32[256,128]{1,0:T(8,128)} fusion(bf16[4,256,128]{2,1,0:T(8,128)(2,1)S(1)} %all_to_all.5), kind=kLoop, calls=%fused_computation | loop fusion | flops 229376 | bytes 393216 | tf_op jit(solution)/shard_map/reduce_sum | solution.py:501
  (1 shorter events, 0.0 us)
Async XLA Ops:
  26.6 7.9 %collective-permute-start = (bf16[4,272,128]{2,1,0:T(8,128)(2,1)S(1)}, bf16[4,272,128]{2,1,0:T(8,128)(2,1)S(1)}, u32[]{:S(2)}, u32[]{:S(2)}) collective-permute-start(bf16[4,272,128]{2,1,0:T(8,128)(2,1)S(1)} %constant_dynamic-slice_fusion), channel_id=1, source_target_pairs={{4,8},{12,16},{20,24},{8,4},{16,12},{24,20},{5,9},{13,17},{21,25},... | collective-permute-start | bytes 835592 | tf_op jit(solution)/shard_map/ppermute | solution.py:439
  36.4 2.1 %collective-permute-start.1 = (bf16[256,256]{1,0:T(8,128)(2,1)S(1)}, bf16[256,256]{1,0:T(8,128)(2,1)S(1)}, u32[]{:S(2)}, u32[]{:S(2)}) collective-permute-start(bf16[256,256]{1,0:T(8,128)(2,1)S(1)} %get-tuple-element.20), channel_id=1, source_target_pairs={{0,4},{8,12},{16,20},{24,28},{4,0},{12,8},{20,16},{28,24},{1,5},{9... | collective-permute-start | bytes 393224 | tf_op jit(solution)/shard_map/ppermute | solution.py:479
  36.6 6.3 %collective-permute-start.2 = (bf16[256,256]{1,0:T(8,128)(2,1)S(1)}, bf16[256,256]{1,0:T(8,128)(2,1)S(1)}, u32[]{:S(2)}, u32[]{:S(2)}) collective-permute-start(bf16[256,256]{1,0:T(8,128)(2,1)S(1)} %get-tuple-element.20), channel_id=1, source_target_pairs={{4,8},{12,16},{20,24},{8,4},{16,12},{24,20},{5,9},{13,17},{21,25},... | collective-permute-start | bytes 393224 | tf_op jit(solution)/shard_map/ppermute | solution.py:480

commit v10 on v8

--- a/solution.py
+++ b/solution.py
@@ -13,6 +13,7 @@
 BF16 = jnp.bfloat16
 INFO = 16
 STRIP = 16
+BATCH = 2
 VMEM = pl.BlockSpec(memory_space=pltpu.VMEM)
 SMEM = pl.BlockSpec(memory_space=pltpu.SMEM)
 HBM = pl.BlockSpec(memory_space=pltpu.HBM)
@@ -237,16 +238,19 @@
             pr, pi, xr, xi = probe[k, 0, s], probe[k, 1, s], patch[0, s], patch[1, s]
             re = split(pr * xr - pi * xi)
             im = split(pr * xi + pi * xr)
-            folded[k, 0, s] = join(re[0] + re[1], im[0] + im[1])
-            folded[k, 1, s] = join(re[0] - re[1], im[0] - im[1])
-
-    def along_rows(k):
+            out = pl.ds(k * half + s.start, STRIP)
+            folded[0, out] = join(re[0] + re[1], im[0] + im[1])
+            folded[1, out] = join(re[0] - re[1], im[0] - im[1])
+
+    def along_rows(k, count):
+        part = pl.ds(k * half, count * half)
         for q in range(2):
-            half_far[k, q] = dot(folded[k, q], tables[q])
+            half_far[q, part] = dot(folded[q, part], tables[q])
 
     def mix(k):
         for s, t in zip(strips, lower):
-            even, odds = half_far[k, 0, s], half_far[k, 1, s]
+            rows = pl.ds(k * half + s.start, STRIP)
+            even, odds = half_far[0, rows], half_far[1, rows]
             even_own, odds_own = half_own[k, 0, s], half_own[k, 1, s]
             for q, (e, o) in enumerate(
                 ((even + even_own, odds + odds_own), (even - even_own, odds - odds_own))
@@ -265,21 +269,20 @@
             intensity = sum(x * x for x in re + im)
             size = amplitude[pl.ds(q * half + s.start, STRIP)]
             factor = 1.0 - size * lax.rsqrt(jnp.maximum(intensity, 0.25))
-            out = pl.ds(q * half + s.start, STRIP)
             for k in range(modes):
+                out = pl.ds(k * half + s.start, STRIP)
                 (re_even, re_odd), (im_even, im_odd) = split(re[k] * factor), split(im[k] * factor)
-                corrected[k, 0, out] = join(re_even, im_even)
-                corrected[k, 1, out] = join(re_odd, im_odd)
-
-    def back_along_rows(k, q):
-        part = pl.ds(q * half, half)
+                corrected[q, 0, out] = join(re_even, im_even)
+                corrected[q, 1, out] = join(re_odd, im_odd)
+
+    def back_along_rows(q):
         for c in range(2):
-            product[k, c, part] = dot(corrected[k, c, part], tables[2 + c])
+            product[q, c] = dot(corrected[q, c], tables[2 + c])
 
     def mix_back(k, q):
         for s, t in zip(strips, lower):
-            part = pl.ds(q * half + s.start, STRIP)
-            x, y = product[k, 0, part], product[k, 1, part]
+            part = pl.ds(k * half + s.start, STRIP)
+            x, y = product[q, 0, part], product[q, 1, part]
             (lr, li), (hr, hi) = split(x + y), split(x - y)
             mixed_back[k, q, s] = join(lr, hr)
             mixed_back[k, q, t] = join(li, hi)
@@ -289,24 +292,28 @@
 
     for s in strips:
         gather(s)
-    for k in range(modes + 1):
-        if k < modes:
-            wave(k)
-            along_rows(k)
-        if k > 0:
-            mix(k - 1)
-            along_columns(k - 1, 0)
+    for k in range(0, modes, BATCH):
+        batch = range(k, min(k + BATCH, modes))
+        for m in batch:
+            wave(m)
+        along_rows(k, len(batch))
+        for m in range(k - BATCH, k):
+            if m >= 0:
+                mix(m)
+                along_columns(m, 0)
+    for m in range(modes - len(batch), modes):
+        mix(m)
+        along_columns(m, 0)
     share = -(-len(strips) // modes)
     for k in range(modes):
         along_columns(k, 1)
         correct(0, slice(k * share, (k + 1) * share))
-    for k in range(modes):
-        back_along_rows(k, 0)
-        correct(1, slice(k * share, (k + 1) * share))
+    back_along_rows(0)
+    correct(1, slice(0, None))
     for k in range(modes):
         mix_back(k, 0)
         back_along_columns(k, 0)
-        back_along_rows(k, 1)
+    back_along_rows(1)
     for k in range(modes):
         mix_back(k, 1)
         back_along_columns(k, 1)
@@ -455,12 +462,12 @@
         [VMEM] * 7,
         [
             pltpu.VMEM((2, tile, extent), F32),
-            pltpu.VMEM((modes, 2, half, extent), BF16),
-            pltpu.VMEM((modes, 2, half, extent), F32),
+            pltpu.VMEM((2, modes * half, extent), BF16),
+            pltpu.VMEM((2, modes * half, extent), F32),
             pltpu.VMEM(full, BF16),
             pltpu.VMEM(full, F32),
-            pltpu.VMEM(full, BF16),
-            pltpu.VMEM(full, F32),
+            pltpu.VMEM((2, 2, modes * half, extent), BF16),
+            pltpu.VMEM((2, 2, modes * half, extent), F32),
             pltpu.VMEM(full, BF16),
         ],
         2 * 10**9, 2**22,

time: 36.8 us -> 36.8 us (level)
  no operation moved by 1% of the time
where the time goes in v10:
time: 36.8 us; the launch traced here: 36.6 us
  blocking collectives  18.1 us (49%)
  Pallas kernels  6.27 us (17%)
  starting transfers between devices  5.74 us (16%)
  waiting for transfers between devices  5.13 us (14%)
  between operations  0.71 us (2%)
  other arithmetic  0.69 us (2%)
    all_gather x1, blocking collectives, per_device(): band = lax.all_gather(packed, 'col')  9.13 us
    all_to_all x1, blocking collectives, per_device(): lax.all_to_all(summed, 'col', split_axis=0, concat_axis=0, tiled=True)  8.94 us
    pallas_call x5, Pallas kernels, call(): pl.pallas_call(kernel, out_shape=out_shape, in_specs=in_specs, out_specs=...  6.27 us
    ppermute x1, waiting for transfers between devices, per_device(): from_second = lax.ppermute(to_rows, 'row', swaps[1])  3.88 us
    ppermute x1, starting transfers between devices, per_device(): second = lax.ppermute(band, 'row', swaps[1])  1.91 us
    ppermute x1, starting transfers between devices, per_device(): from_second = lax.ppermute(to_rows, 'row', swaps[1])  1.91 us
    ppermute x1, starting transfers between devices, per_device(): first = lax.ppermute(band, 'row', swaps[0])  1.74 us
    ppermute x1, waiting for transfers between devices, per_device(): second = lax.ppermute(band, 'row', swaps[1])  1.24 us
  transfers between devices with their start and end apart: 4, of which 2 were waited for; matrix products, arithmetic and copies ran while one was open for 0% of the time, Pallas kernels for 9%

profile of v10, /device:TPU:8, one launch (start us, length us, event | category | flops | bytes accessed | tf_op | source)
XLA Modules:
  0.0 36.6 jit_solution(7913569893404285634)
XLA Ops:
  0.7 1.0 %pack.1 = bf16[272,128]{1,0:T(8,128)(2,1)S(1)} custom-call(f32[2,128,128]{2,1,0:T(8,128)} %specimen.1, s32[1,1,2,2]{3,2,1,0:T(2,128)} %centers.1, s32[1,1]{1,0:T(1,128)S(6)} %copy.8.cnt, s32[1,1,2]{2,1,0:T(1,128)} %helpers.1), custom_call_target="tpu_custom_call" | custom-call | flops 100000 | bytes 524288 | tf_op jit(solution)/shard_map/pack/pallas_call | solution.py:393
  1.6 9.1 %all-gather = bf16[1088,128]{1,0:T(8,128)(2,1)S(1)} all-gather(bf16[272,128]{1,0:T(8,128)(2,1)S(1)} %pack.1), channel_id=2, replica_groups=mesh['row'=8,'col'=4] {'col'}, dimensions={0}, use_global_device_ids=true | all-gather | bytes 348160 | tf_op jit(solution)/shard_map/all_gather | solution.py:428
  10.8 1.9 %collective-permute-start.1 = (bf16[4,272,128]{2,1,0:T(8,128)(2,1)S(1)}, bf16[4,272,128]{2,1,0:T(8,128)(2,1)S(1)}, u32[]{:S(2)}, u32[]{:S(2)}) collective-permute-start(bf16[4,272,128]{2,1,0:T(8,128)(2,1)S(1)} %bitcast.2), channel_id=1, source_target_pairs={{4,8},{12,16},{20,24},{8,4},{16,12},{24,20},{5,9},{13,17},{21,25},... | collective-permute-start | bytes 835592 | tf_op jit(solution)/shard_map/ppermute | solution.py:435
  12.7 1.7 %collective-permute-start = (bf16[4,272,128]{2,1,0:T(8,128)(2,1)S(1)}, bf16[4,272,128]{2,1,0:T(8,128)(2,1)S(1)}, u32[]{:S(2)}, u32[]{:S(2)}) collective-permute-start(bf16[4,272,128]{2,1,0:T(8,128)(2,1)S(1)} %bitcast.3), channel_id=1, source_target_pairs={{0,4},{8,12},{16,20},{24,28},{4,0},{12,8},{20,16},{28,24},{1,5},{9... | collective-permute-start | bytes 835592 | tf_op jit(solution)/shard_map/ppermute | solution.py:436
  14.4 2.9 %prepare.1 = (bf16[16,256]{1,0:T(8,128)(2,1)S(1)}, f32[256,256]{1,0:T(8,128)S(1)}, bf16[8,256,256]{2,1,0:T(8,128)(2,1)S(1)}, f32[4,2,256,256]{3,2,1,0:T(8,128)S(1)}, f32[4,2,128,256]{3,2,1,0:T(8,128)S(1)}) custom-call(bf16[4,272,128]{2,1,0:T(8,128)(2,1)S(1)} %bitcast.4, f32[4,2,256,256]{3,2,1,0:T(8,128)} %probe.1, f32[1,1,1,256,256]{4,3,2,1,0:T(8,128)} %measured.1, ...), custom_call_target="tpu_custom_call" | custom-call | flops 1000000000 | bytes 4194304 | tf_op jit(solution)/shard_map/prepare/pallas_call | solution.py:393
  17.4 1.2 %collective-permute-done.1.second.second_band = bf16[4,272,128]{2,1,0:T(8,128)(2,1)S(1)} collective-permute-done((bf16[4,272,128]{2,1,0:T(8,128)(2,1)S(1)}, bf16[4,272,128]{2,1,0:T(8,128)(2,1)S(1)}, u32[]{:S(2)}, u32[]{:S(2)}) %collective-permute-start.1) | collective-permute-done | bytes 278560 | tf_op jit(solution)/shard_map/ppermute | solution.py:435
  18.6 0.0 collective-permute-done.first.first_band
  18.6 1.8 %frame.1 = (bf16[256,256]{1,0:T(8,128)(2,1)S(1)}, f32[4,2,256,256]{3,2,1,0:T(8,128)S(1)}) custom-call(bf16[4,272,128]{2,1,0:T(8,128)(2,1)S(1)} %collective-permute-done.first.first_band, bf16[4,272,128]{2,1,0:T(8,128)(2,1)S(1)} %collective-permute-done.1.second.second_band, bf16[16,256]{1,0:T(8,128)(2,1)S(1)} %get-tuple-element.14.info, ...), custom_call_target="tpu_custom_call" | custom-call | flops 2000000000 | bytes 4194304 | tf_op jit(solution)/shard_map/frame/pallas_call | solution.py:393
  20.4 0.2 collective-permute-start.2
  20.6 1.9 %collective-permute-start.3 = (bf16[256,256]{1,0:T(8,128)(2,1)S(1)}, bf16[256,256]{1,0:T(8,128)(2,1)S(1)}, u32[]{:S(2)}, u32[]{:S(2)}) collective-permute-start(bf16[256,256]{1,0:T(8,128)(2,1)S(1)} %get-tuple-element.20), channel_id=1, source_target_pairs={{4,8},{12,16},{20,24},{8,4},{16,12},{24,20},{5,9},{13,17},{21,25},... | collective-permute-start | bytes 393224 | tf_op jit(solution)/shard_map/ppermute | solution.py:477
  22.5 0.0 collective-permute-done.2.first
  22.5 0.5 %finish.1 = (f32[4,256,128]{2,1,0:T(8,128)S(1)}, s32[8,128]{1,0:T(8,128)S(1)}) custom-call(bf16[4,272,128]{2,1,0:T(8,128)(2,1)S(1)} %bitcast.5, bf16[4,272,128]{2,1,0:T(8,128)(2,1)S(1)} %collective-permute-done.first.first_band, bf16[4,272,128]{2,1,0:T(8,128)(2,1)S(1)} %collective-permute-done.1.second.second_band, ...), custom_call_target="tpu_custom_call" | custom-call | flops 10000000 | bytes 4194304 | tf_op jit(solution)/shard_map/finish/pallas_call | solution.py:393
  23.0 3.9 %collective-permute-done.3.second = bf16[256,256]{1,0:T(8,128)(2,1)S(1)} collective-permute-done((bf16[256,256]{1,0:T(8,128)(2,1)S(1)}, bf16[256,256]{1,0:T(8,128)(2,1)S(1)}, u32[]{:S(2)}, u32[]{:S(2)}) %collective-permute-start.3) | collective-permute-done | bytes 131104 | tf_op jit(solution)/shard_map/ppermute | solution.py:477
  26.9 0.1 fold.1
  27.0 8.9 %all_to_all.5 = bf16[4,256,128]{2,1,0:T(8,128)(2,1)S(1)} all-to-all(bf16[4,256,128]{2,1,0:T(8,128)(2,1)S(1)} %fold.1), channel_id=1, replica_groups=mesh['row'=8,'col'=4] {'col'}, dimensions={0} | all-to-all | bytes 524288 | tf_op jit(solution)/shard_map/all_to_all | solution.py:497
  35.9 0.7 %convert_reduce_fusion = f32[256,128]{1,0:T(8,128)} fusion(bf16[4,256,128]{2,1,0:T(8,128)(2,1)S(1)} %all_to_all.5), kind=kLoop, calls=%fused_computation | loop fusion | flops 229376 | bytes 393216 | tf_op jit(solution)/shard_map/reduce_sum | solution.py:498
Async XLA Ops:
  10.8 7.9 %collective-permute-start.1 = (bf16[4,272,128]{2,1,0:T(8,128)(2,1)S(1)}, bf16[4,272,128]{2,1,0:T(8,128)(2,1)S(1)}, u32[]{:S(2)}, u32[]{:S(2)}) collective-permute-start(bf16[4,272,128]{2,1,0:T(8,128)(2,1)S(1)} %bitcast.2), channel_id=1, source_target_pairs={{4,8},{12,16},{20,24},{8,4},{16,12},{24,20},{5,9},{13,17},{21,25},... | collective-permute-start | bytes 835592 | tf_op jit(solution)/shard_map/ppermute | solution.py:435
  12.7 5.9 %collective-permute-start = (bf16[4,272,128]{2,1,0:T(8,128)(2,1)S(1)}, bf16[4,272,128]{2,1,0:T(8,128)(2,1)S(1)}, u32[]{:S(2)}, u32[]{:S(2)}) collective-permute-start(bf16[4,272,128]{2,1,0:T(8,128)(2,1)S(1)} %bitcast.3), channel_id=1, source_target_pairs={{0,4},{8,12},{16,20},{24,28},{4,0},{12,8},{20,16},{28,24},{1,5},{9... | collective-permute-start | bytes 835592 | tf_op jit(solution)/shard_map/ppermute | solution.py:436
  20.4 2.1 %collective-permute-start.2 = (bf16[256,256]{1,0:T(8,128)(2,1)S(1)}, bf16[256,256]{1,0:T(8,128)(2,1)S(1)}, u32[]{:S(2)}, u32[]{:S(2)}) collective-permute-start(bf16[256,256]{1,0:T(8,128)(2,1)S(1)} %get-tuple-element.20), channel_id=1, source_target_pairs={{0,4},{8,12},{16,20},{24,28},{4,0},{12,8},{20,16},{28,24},{1,5},{9... | collective-permute-start | bytes 393224 | tf_op jit(solution)/shard_map/ppermute | solution.py:476
  20.6 6.3 %collective-permute-start.3 = (bf16[256,256]{1,0:T(8,128)(2,1)S(1)}, bf16[256,256]{1,0:T(8,128)(2,1)S(1)}, u32[]{:S(2)}, u32[]{:S(2)}) collective-permute-start(bf16[256,256]{1,0:T(8,128)(2,1)S(1)} %get-tuple-element.20), channel_id=1, source_target_pairs={{4,8},{12,16},{20,24},{8,4},{16,12},{24,20},{5,9},{13,17},{21,25},... | collective-permute-start | bytes 393224 | tf_op jit(solution)/shard_map/ppermute | solution.py:477

commit v11 on v8

--- a/solution.py
+++ b/solution.py
@@ -200,7 +200,7 @@
 
 def frame_kernel(
     first, second, info, amplitude, tables, probe, half_own,
-    to_rows, turned, patch, folded, half_far, mixed, far, corrected, product, mixed_back,
+    to_rows, mixed_back, patch, folded, mixed, far, corrected, total,
 ):
     columns = first.shape[0]
     tile = (first.shape[1] - INFO) // 2
@@ -240,13 +240,10 @@
             folded[k, 0, s] = join(re[0] + re[1], im[0] + im[1])
             folded[k, 1, s] = join(re[0] - re[1], im[0] - im[1])
 
-    def along_rows(k):
-        for q in range(2):
-            half_far[k, q] = dot(folded[k, q], tables[q])
-
     def mix(k):
+        both = [dot(folded[k, q], tables[q]) for q in range(2)]
         for s, t in zip(strips, lower):
-            even, odds = half_far[k, 0, s], half_far[k, 1, s]
+            even, odds = (x[s.start : s.start + STRIP] for x in both)
             even_own, odds_own = half_own[k, 0, s], half_own[k, 1, s]
             for q, (e, o) in enumerate(
                 ((even + even_own, odds + odds_own), (even - even_own, odds - odds_own))
@@ -271,28 +268,36 @@
                 corrected[k, 0, out] = join(re_even, im_even)
                 corrected[k, 1, out] = join(re_odd, im_odd)
 
-    def back_along_rows(k, q):
+    def mix_back(k, q):
         part = pl.ds(q * half, half)
-        for c in range(2):
-            product[k, c, part] = dot(corrected[k, c, part], tables[2 + c])
-
-    def mix_back(k, q):
+        both = [dot(corrected[k, c, part], tables[2 + c]) for c in range(2)]
         for s, t in zip(strips, lower):
-            part = pl.ds(q * half + s.start, STRIP)
-            x, y = product[k, 0, part], product[k, 1, part]
+            x, y = (z[s.start : s.start + STRIP] for z in both)
             (lr, li), (hr, hi) = split(x + y), split(x - y)
             mixed_back[k, q, s] = join(lr, hr)
             mixed_back[k, q, t] = join(li, hi)
 
-    def back_along_columns(k, q):
-        turned[k, q] = dot(tables[6 + q], mixed_back[k, q])
+    both_back = jnp.concatenate([tables[6], tables[7]], 1)
+
+    def accumulate(k):
+        chi = dot(both_back, mixed_back[k].reshape(2 * extent, extent))
+        for s in strips:
+            pr, pi = probe[k, 0, s], probe[k, 1, s]
+            cr, ci = (chi[r : r + STRIP] for r in (s.start, half + s.start))
+            re, im = pr * cr + pi * ci, pr * ci - pi * cr
+            if k > 0:
+                re, im = re + total[0, s], im + total[1, s]
+            if k < modes - 1:
+                total[0, s], total[1, s] = re, im
+            else:
+                to_rows[s] = re.astype(BF16)
+                to_rows[pl.ds(tile + s.start, STRIP)] = im.astype(BF16)
 
     for s in strips:
         gather(s)
     for k in range(modes + 1):
         if k < modes:
             wave(k)
-            along_rows(k)
         if k > 0:
             mix(k - 1)
             along_columns(k - 1, 0)
@@ -301,30 +306,13 @@
         along_columns(k, 1)
         correct(0, slice(k * share, (k + 1) * share))
     for k in range(modes):
-        back_along_rows(k, 0)
+        mix_back(k, 0)
         correct(1, slice(k * share, (k + 1) * share))
     for k in range(modes):
-        mix_back(k, 0)
-        back_along_columns(k, 0)
-        back_along_rows(k, 1)
-    for k in range(modes):
         mix_back(k, 1)
-        back_along_columns(k, 1)
-    for s, t in zip(strips, lower):
-        accumulate(to_rows, turned, probe, s, t, s, 1)
-
-
-def accumulate(out, turned, probe, s, t, rows, sign):
-    tile = out.shape[0] // 2
-    re = im = 0.0
-    for k in range(probe.shape[0]):
-        pr, pi = probe[k, 0, rows], probe[k, 1, rows]
-        cr = turned[k, 0, s] + sign * turned[k, 1, s]
-        ci = turned[k, 0, t] + sign * turned[k, 1, t]
-        re += pr * cr + pi * ci
-        im += pr * ci - pi * cr
-    out[s] = re.astype(BF16)
-    out[pl.ds(tile + s.start, STRIP)] = im.astype(BF16)
+        if k > 0:
+            accumulate(k - 1)
+    accumulate(modes - 1)
 
 
 def place(block, columns, source, col, taken):
@@ -341,9 +329,12 @@
 
 
 def finish_kernel(
-    band, first_band, second_band, turned, probe, first, partial, second_info, centre,
+    band, first_band, second_band, mixed_back, tables, probe, first,
+    partial, second_info, total, centre,
 ):
     columns = band.shape[0]
+    extent = probe.shape[-1]
+    modes = probe.shape[0]
     tile = (band.shape[1] - INFO) // 2
     odd = lax.axis_index("row") % 2
     own_frame, first_frame, second_frame = (
@@ -353,9 +344,22 @@
     second_info[...] = jnp.where(
         which == 0, second_frame[0], jnp.where(which == 1, second_frame[1], second_frame[2])
     )
+    both_back = jnp.concatenate([tables[6], -tables[7]], 1)
+    for k in range(modes):
+        chi = dot(both_back, mixed_back[k].reshape(2 * extent, extent))
+        for r in range(0, tile, STRIP):
+            s, t = pl.ds(r, STRIP), pl.ds(tile + r, STRIP)
+            pr, pi = probe[k, 0, t], probe[k, 1, t]
+            cr, ci = (chi[i : i + STRIP] for i in (r, tile + r))
+            re, im = pr * cr + pi * ci, pr * ci - pi * cr
+            if k > 0:
+                re, im = re + total[0, s], im + total[1, s]
+            if k < modes - 1:
+                total[0, s], total[1, s] = re, im
+            else:
+                centre[s], centre[t] = re.astype(BF16), im.astype(BF16)
     for r in range(0, tile, STRIP):
         s, t = pl.ds(r, STRIP), pl.ds(tile + r, STRIP)
-        accumulate(centre, turned, probe, s, t, t, -1)
         before = (iota((STRIP, tile), 0) + r < first_frame[1]).astype(jnp.int32)
         for part in (s, t):
             mine = place(centre[part].astype(F32), columns, own_frame[0], own_frame[2], None)
@@ -449,19 +453,17 @@
         band, probe, measured, tables,
     )
     full = (modes, 2, extent, extent)
-    to_rows, turned = call(
+    to_rows, mixed_back = call(
         frame_kernel, "frame",
-        (part, jax.ShapeDtypeStruct(full, F32)),
+        (part, jax.ShapeDtypeStruct(full, BF16)),
         [VMEM] * 7,
         [
             pltpu.VMEM((2, tile, extent), F32),
             pltpu.VMEM((modes, 2, half, extent), BF16),
-            pltpu.VMEM((modes, 2, half, extent), F32),
             pltpu.VMEM(full, BF16),
             pltpu.VMEM(full, F32),
             pltpu.VMEM(full, BF16),
-            pltpu.VMEM(full, F32),
-            pltpu.VMEM(full, BF16),
+            pltpu.VMEM((2, tile, extent), F32),
         ],
         2 * 10**9, 2**22,
         first, second, *prepared,
@@ -474,10 +476,10 @@
             jax.ShapeDtypeStruct((columns, height, tile), F32),
             jax.ShapeDtypeStruct((8, tile), jnp.int32),
         ),
-        [VMEM] * 6,
-        [pltpu.VMEM((height, extent), BF16)],
-        10**7, 2**22,
-        band, first, second, turned, prepared[3], from_first,
+        [VMEM] * 7,
+        [pltpu.VMEM((2, tile, extent), F32), pltpu.VMEM((height, extent), BF16)],
+        5 * 10**8, 2**22,
+        band, first, second, mixed_back, prepared[2], prepared[3], from_first,
     )
     summed = call(
         fold_kernel, "fold",

time: 36.8 us -> 37 us (level)
  Pallas kernels: 6.25 us -> 6.67 us
    pallas_call x5, Pallas kernels: 6.25 us -> 6.67 us  [call(): pl.pallas_call(kernel, out_shape=out_shape, in_specs=in_specs, out_specs=...]
  transfers between devices with their start and end apart: 4 -> 4, of which waited for: 2 -> 2; matrix products, arithmetic and copies ran while one was open for 0% -> 0% of each run, Pallas kernels for 9% -> 10%
where the time goes in v11:
time: 37 us; the launch traced here: 36.7 us
  blocking collectives  18.1 us (49%)
  Pallas kernels  6.67 us (18%)
  starting transfers between devices  5.75 us (16%)
  waiting for transfers between devices  4.85 us (13%)
  between operations  0.71 us (2%)
  other arithmetic  0.69 us (2%)
    all_gather x1, blocking collectives, per_device(): band = lax.all_gather(packed, 'col')  9.13 us
    all_to_all x1, blocking collectives, per_device(): lax.all_to_all(summed, 'col', split_axis=0, concat_axis=0, tiled=True)  8.94 us
    pallas_call x5, Pallas kernels, call(): pl.pallas_call(kernel, out_shape=out_shape, in_specs=in_specs, out_specs=...  6.67 us
    ppermute x1, waiting for transfers between devices, per_device(): from_second = lax.ppermute(to_rows, 'row', swaps[1])  3.64 us
    ppermute x1, starting transfers between devices, per_device(): second = lax.ppermute(band, 'row', swaps[1])  1.91 us
    ppermute x1, starting transfers between devices, per_device(): from_second = lax.ppermute(to_rows, 'row', swaps[1])  1.91 us
    ppermute x1, starting transfers between devices, per_device(): first = lax.ppermute(band, 'row', swaps[0])  1.74 us
    ppermute x1, waiting for transfers between devices, per_device(): second = lax.ppermute(band, 'row', swaps[1])  1.21 us
  transfers between devices with their start and end apart: 4, of which 2 were waited for; matrix products, arithmetic and copies ran while one was open for 0% of the time, Pallas kernels for 10%

profile of v11, /device:TPU:8, one launch (start us, length us, event | category | flops | bytes accessed | tf_op | source)
XLA Modules:
  0.0 36.7 jit_solution(4465668123065632774)
XLA Ops:
  0.7 1.0 %pack.1 = bf16[272,128]{1,0:T(8,128)(2,1)S(1)} custom-call(f32[2,128,128]{2,1,0:T(8,128)} %specimen.1, s32[1,1,2,2]{3,2,1,0:T(2,128)} %centers.1, s32[1,1]{1,0:T(1,128)S(6)} %copy.8.cnt, s32[1,1,2]{2,1,0:T(1,128)} %helpers.1), custom_call_target="tpu_custom_call" | custom-call | flops 100000 | bytes 524288 | tf_op jit(solution)/shard_map/pack/pallas_call | solution.py:390
  1.6 9.1 %all-gather = bf16[1088,128]{1,0:T(8,128)(2,1)S(1)} all-gather(bf16[272,128]{1,0:T(8,128)(2,1)S(1)} %pack.1), channel_id=2, replica_groups=mesh['row'=8,'col'=4] {'col'}, dimensions={0}, use_global_device_ids=true | all-gather | bytes 348160 | tf_op jit(solution)/shard_map/all_gather | solution.py:425
  10.8 1.9 %collective-permute-start.1 = (bf16[4,272,128]{2,1,0:T(8,128)(2,1)S(1)}, bf16[4,272,128]{2,1,0:T(8,128)(2,1)S(1)}, u32[]{:S(2)}, u32[]{:S(2)}) collective-permute-start(bf16[4,272,128]{2,1,0:T(8,128)(2,1)S(1)} %bitcast.2), channel_id=1, source_target_pairs={{4,8},{12,16},{20,24},{8,4},{16,12},{24,20},{5,9},{13,17},{21,25},... | collective-permute-start | bytes 835592 | tf_op jit(solution)/shard_map/ppermute | solution.py:432
  12.7 1.7 %collective-permute-start = (bf16[4,272,128]{2,1,0:T(8,128)(2,1)S(1)}, bf16[4,272,128]{2,1,0:T(8,128)(2,1)S(1)}, u32[]{:S(2)}, u32[]{:S(2)}) collective-permute-start(bf16[4,272,128]{2,1,0:T(8,128)(2,1)S(1)} %bitcast.3), channel_id=1, source_target_pairs={{0,4},{8,12},{16,20},{24,28},{4,0},{12,8},{20,16},{28,24},{1,5},{9... | collective-permute-start | bytes 835592 | tf_op jit(solution)/shard_map/ppermute | solution.py:433
  14.4 3.0 %prepare.1 = (bf16[16,256]{1,0:T(8,128)(2,1)S(1)}, f32[256,256]{1,0:T(8,128)S(1)}, bf16[8,256,256]{2,1,0:T(8,128)(2,1)S(1)}, f32[4,2,256,256]{3,2,1,0:T(8,128)S(1)}, f32[4,2,128,256]{3,2,1,0:T(8,128)S(1)}) custom-call(bf16[4,272,128]{2,1,0:T(8,128)(2,1)S(1)} %bitcast.4, f32[4,2,256,256]{3,2,1,0:T(8,128)} %probe.1, f32[1,1,1,256,256]{4,3,2,1,0:T(8,128)} %measured.1, ...), custom_call_target="tpu_custom_call" | custom-call | flops 1000000000 | bytes 4194304 | tf_op jit(solution)/shard_map/prepare/pallas_call | solution.py:390
  17.4 1.2 %collective-permute-done.1.second.second_band = bf16[4,272,128]{2,1,0:T(8,128)(2,1)S(1)} collective-permute-done((bf16[4,272,128]{2,1,0:T(8,128)(2,1)S(1)}, bf16[4,272,128]{2,1,0:T(8,128)(2,1)S(1)}, u32[]{:S(2)}, u32[]{:S(2)}) %collective-permute-start.1) | collective-permute-done | bytes 278560 | tf_op jit(solution)/shard_map/ppermute | solution.py:432
  18.6 0.0 collective-permute-done.first.first_band
  18.6 1.9 %frame.1 = (bf16[256,256]{1,0:T(8,128)(2,1)S(1)}, bf16[4,2,256,256]{3,2,1,0:T(8,128)(2,1)S(1)}) custom-call(bf16[4,272,128]{2,1,0:T(8,128)(2,1)S(1)} %collective-permute-done.first.first_band, bf16[4,272,128]{2,1,0:T(8,128)(2,1)S(1)} %collective-permute-done.1.second.second_band, bf16[16,256]{1,0:T(8,128)(2,1)S(1)} %get-tuple-element.14.info, ...), custom_call_target="tpu_custom_call" | custom-call | flops 2000000000 | bytes 4194304 | tf_op jit(solution)/shard_map/frame/pallas_call | solution.py:390
  20.5 0.2 collective-permute-start.2
  20.7 1.9 %collective-permute-start.3 = (bf16[256,256]{1,0:T(8,128)(2,1)S(1)}, bf16[256,256]{1,0:T(8,128)(2,1)S(1)}, u32[]{:S(2)}, u32[]{:S(2)}) collective-permute-start(bf16[256,256]{1,0:T(8,128)(2,1)S(1)} %get-tuple-element.20), channel_id=1, source_target_pairs={{4,8},{12,16},{20,24},{8,4},{16,12},{24,20},{5,9},{13,17},{21,25},... | collective-permute-start | bytes 393224 | tf_op jit(solution)/shard_map/ppermute | solution.py:472
  22.6 0.0 collective-permute-done.2.first
  22.6 0.7 %finish.1 = (f32[4,256,128]{2,1,0:T(8,128)S(1)}, s32[8,128]{1,0:T(8,128)S(1)}) custom-call(bf16[4,272,128]{2,1,0:T(8,128)(2,1)S(1)} %bitcast.5, bf16[4,272,128]{2,1,0:T(8,128)(2,1)S(1)} %collective-permute-done.first.first_band, bf16[4,272,128]{2,1,0:T(8,128)(2,1)S(1)} %collective-permute-done.1.second.second_band, ...), custom_call_target="tpu_custom_call" | custom-call | flops 500000000 | bytes 4194304 | tf_op jit(solution)/shard_map/finish/pallas_call | solution.py:390
  23.4 3.6 %collective-permute-done.3.second = bf16[256,256]{1,0:T(8,128)(2,1)S(1)} collective-permute-done((bf16[256,256]{1,0:T(8,128)(2,1)S(1)}, bf16[256,256]{1,0:T(8,128)(2,1)S(1)}, u32[]{:S(2)}, u32[]{:S(2)}) %collective-permute-start.3) | collective-permute-done | bytes 131104 | tf_op jit(solution)/shard_map/ppermute | solution.py:472
  27.0 0.1 fold.1
  27.1 8.9 %all_to_all.5 = bf16[4,256,128]{2,1,0:T(8,128)(2,1)S(1)} all-to-all(bf16[4,256,128]{2,1,0:T(8,128)(2,1)S(1)} %fold.1), channel_id=1, replica_groups=mesh['row'=8,'col'=4] {'col'}, dimensions={0} | all-to-all | bytes 524288 | tf_op jit(solution)/shard_map/all_to_all | solution.py:492
  36.0 0.7 %convert_reduce_fusion = f32[256,128]{1,0:T(8,128)} fusion(bf16[4,256,128]{2,1,0:T(8,128)(2,1)S(1)} %all_to_all.5), kind=kLoop, calls=%fused_computation | loop fusion | flops 229376 | bytes 393216 | tf_op jit(solution)/shard_map/reduce_sum | solution.py:493
Async XLA Ops:
  10.8 7.9 %collective-permute-start.1 = (bf16[4,272,128]{2,1,0:T(8,128)(2,1)S(1)}, bf16[4,272,128]{2,1,0:T(8,128)(2,1)S(1)}, u32[]{:S(2)}, u32[]{:S(2)}) collective-permute-start(bf16[4,272,128]{2,1,0:T(8,128)(2,1)S(1)} %bitcast.2), channel_id=1, source_target_pairs={{4,8},{12,16},{20,24},{8,4},{16,12},{24,20},{5,9},{13,17},{21,25},... | collective-permute-start | bytes 835592 | tf_op jit(solution)/shard_map/ppermute | solution.py:432
  12.7 5.9 %collective-permute-start = (bf16[4,272,128]{2,1,0:T(8,128)(2,1)S(1)}, bf16[4,272,128]{2,1,0:T(8,128)(2,1)S(1)}, u32[]{:S(2)}, u32[]{:S(2)}) collective-permute-start(bf16[4,272,128]{2,1,0:T(8,128)(2,1)S(1)} %bitcast.3), channel_id=1, source_target_pairs={{0,4},{8,12},{16,20},{24,28},{4,0},{12,8},{20,16},{28,24},{1,5},{9... | collective-permute-start | bytes 835592 | tf_op jit(solution)/shard_map/ppermute | solution.py:433
  20.5 2.1 %collective-permute-start.2 = (bf16[256,256]{1,0:T(8,128)(2,1)S(1)}, bf16[256,256]{1,0:T(8,128)(2,1)S(1)}, u32[]{:S(2)}, u32[]{:S(2)}) collective-permute-start(bf16[256,256]{1,0:T(8,128)(2,1)S(1)} %get-tuple-element.20), channel_id=1, source_target_pairs={{0,4},{8,12},{16,20},{24,28},{4,0},{12,8},{20,16},{28,24},{1,5},{9... | collective-permute-start | bytes 393224 | tf_op jit(solution)/shard_map/ppermute | solution.py:471
  20.7 6.3 %collective-permute-start.3 = (bf16[256,256]{1,0:T(8,128)(2,1)S(1)}, bf16[256,256]{1,0:T(8,128)(2,1)S(1)}, u32[]{:S(2)}, u32[]{:S(2)}) collective-permute-start(bf16[256,256]{1,0:T(8,128)(2,1)S(1)} %get-tuple-element.20), channel_id=1, source_target_pairs={{4,8},{12,16},{20,24},{8,4},{16,12},{24,20},{5,9},{13,17},{21,25},... | collective-permute-start | bytes 393224 | tf_op jit(solution)/shard_map/ppermute | solution.py:472

commit v12 on v8

--- a/solution.py
+++ b/solution.py
@@ -418,7 +418,10 @@
         10**5, 2**19,
         specimen, centers, frame_counts, helper_cols,
     )
-    band = lax.all_gather(packed, "col")
+    near = [[c, c + 1] for c in range(0, columns, 2)]
+    far = [list(range(c, columns, 2)) for c in range(2)]
+    band = lax.all_gather(packed, "col", axis_index_groups=near)
+    band = lax.all_gather(band, "col", axis_index_groups=far, tiled=True)
 
     rows = lax.axis_size("row")
     swaps = []

time: 36.8 us -> 39.2 us (1.065)
  blocking collectives: 18.1 us -> 20.5 us
    all_gather x1 -> x2, blocking collectives: 9.13 us -> 10.7 us  [the longest x1 5.72 us: per_device(): band = lax.all_gather(band, 'col', axis_index_groups=far, tiled=True)]
    all_to_all x1, blocking collectives: 8.94 us -> 9.82 us  [per_device(): lax.all_to_all(summed, 'col', split_axis=0, concat_axis=0, tiled=True)]
where the time goes in v12:
time: 39.2 us; the launch traced here: 39 us
  blocking collectives  20.5 us (52%)
  Pallas kernels  6.22 us (16%)
  starting transfers between devices  5.74 us (15%)
  waiting for transfers between devices  5.13 us (13%)
  between operations  0.71 us (2%)
  other arithmetic  0.69 us (2%)
    all_to_all x1, blocking collectives, per_device(): lax.all_to_all(summed, 'col', split_axis=0, concat_axis=0, tiled=True)  9.82 us
    pallas_call x5, Pallas kernels, call(): pl.pallas_call(kernel, out_shape=out_shape, in_specs=in_specs, out_specs=...  6.22 us
    all_gather x1, blocking collectives, per_device(): band = lax.all_gather(band, 'col', axis_index_groups=far, tiled=True)  5.72 us
    all_gather x1, blocking collectives, per_device(): band = lax.all_gather(packed, 'col', axis_index_groups=near)  4.99 us
    ppermute x1, waiting for transfers between devices, per_device(): from_second = lax.ppermute(to_rows, 'row', swaps[1])  3.88 us
    ppermute x1, starting transfers between devices, per_device(): second = lax.ppermute(band, 'row', swaps[1])  1.91 us
    ppermute x1, starting transfers between devices, per_device(): from_second = lax.ppermute(to_rows, 'row', swaps[1])  1.91 us
    ppermute x1, starting transfers between devices, per_device(): first = lax.ppermute(band, 'row', swaps[0])  1.74 us
  transfers between devices with their start and end apart: 4, of which 2 were waited for; matrix products, arithmetic and copies ran while one was open for 0% of the time, Pallas kernels for 9%

profile of v12, /device:TPU:8, one launch (start us, length us, event | category | flops | bytes accessed | tf_op | source)
XLA Modules:
  0.0 39.0 jit_solution(3474195872831482659)
XLA Ops:
  0.7 1.0 %pack.1 = bf16[272,128]{1,0:T(8,128)(2,1)S(1)} custom-call(f32[2,128,128]{2,1,0:T(8,128)} %specimen.1, s32[1,1,2,2]{3,2,1,0:T(2,128)} %centers.1, s32[1,1]{1,0:T(1,128)S(6)} %copy.8.cnt, s32[1,1,2]{2,1,0:T(1,128)} %helpers.1), custom_call_target="tpu_custom_call" | custom-call | flops 100000 | bytes 524288 | tf_op jit(solution)/shard_map/pack/pallas_call | solution.py:386
  1.6 5.0 %all-gather = bf16[544,128]{1,0:T(8,128)(2,1)S(1)} all-gather(bf16[272,128]{1,0:T(8,128)(2,1)S(1)} %pack.1), channel_id=2, replica_groups={{0,1},{2,3},{4,5},{6,7},{8,9},{10,11},{12,13},{14,15},{16,17},{18,19},{..., dimensions={0}, use_global_device_ids=true | all-gather | bytes 208896 | tf_op jit(solution)/shard_map/all_gather | solution.py:423
  6.6 5.7 %all_gather.11.band = bf16[4,272,128]{2,1,0:T(8,128)(2,1)S(1)} all-gather(bf16[2,272,128]{2,1,0:T(8,128)(2,1)S(1)} %bitcast.2), channel_id=1, replica_groups={{0,2},{1,3},{4,6},{5,7},{8,10},{9,11},{12,14},{13,15},{16,18},{17,19},{..., dimensions={0}, use_global_device_ids=true | all-gather | bytes 417792 | tf_op jit(solution)/shard_map/all_gather | solution.py:424
  12.3 1.9 %collective-permute-start.1 = (bf16[4,272,128]{2,1,0:T(8,128)(2,1)S(1)}, bf16[4,272,128]{2,1,0:T(8,128)(2,1)S(1)}, u32[]{:S(2)}, u32[]{:S(2)}) collective-permute-start(bf16[4,272,128]{2,1,0:T(8,128)(2,1)S(1)} %all_gather.11.band), channel_id=1, source_target_pairs={{4,8},{12,16},{20,24},{8,4},{16,12},{24,20},{5,9},{13,17},{21,25},... | collective-permute-start | bytes 835592 | tf_op jit(solution)/shard_map/ppermute | solution.py:431
  14.2 1.7 %collective-permute-start = (bf16[4,272,128]{2,1,0:T(8,128)(2,1)S(1)}, bf16[4,272,128]{2,1,0:T(8,128)(2,1)S(1)}, u32[]{:S(2)}, u32[]{:S(2)}) collective-permute-start(bf16[4,272,128]{2,1,0:T(8,128)(2,1)S(1)} %all_gather.11.band), channel_id=1, source_target_pairs={{0,4},{8,12},{16,20},{24,28},{4,0},{12,8},{20,16},{28,24},{1,5},{9... | collective-permute-start | bytes 835592 | tf_op jit(solution)/shard_map/ppermute | solution.py:432
  16.0 2.9 %prepare.1 = (bf16[16,256]{1,0:T(8,128)(2,1)S(1)}, f32[256,256]{1,0:T(8,128)S(1)}, bf16[8,256,256]{2,1,0:T(8,128)(2,1)S(1)}, f32[4,2,256,256]{3,2,1,0:T(8,128)S(1)}, f32[4,2,128,256]{3,2,1,0:T(8,128)S(1)}) custom-call(bf16[4,272,128]{2,1,0:T(8,128)(2,1)S(1)} %all_gather.11.band, f32[4,2,256,256]{3,2,1,0:T(8,128)} %probe.1, f32[1,1,1,256,256]{4,3,2,1,0:T(8,128)} %measured.1, ...), custom_call_target="tpu_custom_call" | custom-call | flops 1000000000 | bytes 4194304 | tf_op jit(solution)/shard_map/prepare/pallas_call | solution.py:386
  18.9 1.2 %collective-permute-done.1.second.second_band = bf16[4,272,128]{2,1,0:T(8,128)(2,1)S(1)} collective-permute-done((bf16[4,272,128]{2,1,0:T(8,128)(2,1)S(1)}, bf16[4,272,128]{2,1,0:T(8,128)(2,1)S(1)}, u32[]{:S(2)}, u32[]{:S(2)}) %collective-permute-start.1) | collective-permute-done | bytes 278560 | tf_op jit(solution)/shard_map/ppermute | solution.py:431
  20.2 0.0 collective-permute-done.first.first_band
  20.2 1.7 %frame.1 = (bf16[256,256]{1,0:T(8,128)(2,1)S(1)}, f32[4,2,256,256]{3,2,1,0:T(8,128)S(1)}) custom-call(bf16[4,272,128]{2,1,0:T(8,128)(2,1)S(1)} %collective-permute-done.first.first_band, bf16[4,272,128]{2,1,0:T(8,128)(2,1)S(1)} %collective-permute-done.1.second.second_band, bf16[16,256]{1,0:T(8,128)(2,1)S(1)} %get-tuple-element.14.info, ...), custom_call_target="tpu_custom_call" | custom-call | flops 2000000000 | bytes 4194304 | tf_op jit(solution)/shard_map/frame/pallas_call | solution.py:386
  21.9 0.2 collective-permute-start.2
  22.1 1.9 %collective-permute-start.3 = (bf16[256,256]{1,0:T(8,128)(2,1)S(1)}, bf16[256,256]{1,0:T(8,128)(2,1)S(1)}, u32[]{:S(2)}, u32[]{:S(2)}) collective-permute-start(bf16[256,256]{1,0:T(8,128)(2,1)S(1)} %get-tuple-element.20), channel_id=1, source_target_pairs={{4,8},{12,16},{20,24},{8,4},{16,12},{24,20},{5,9},{13,17},{21,25},... | collective-permute-start | bytes 393224 | tf_op jit(solution)/shard_map/ppermute | solution.py:473
  24.0 0.0 collective-permute-done.2.first
  24.0 0.5 %finish.1 = (f32[4,256,128]{2,1,0:T(8,128)S(1)}, s32[8,128]{1,0:T(8,128)S(1)}) custom-call(bf16[4,272,128]{2,1,0:T(8,128)(2,1)S(1)} %all_gather.11.band, bf16[4,272,128]{2,1,0:T(8,128)(2,1)S(1)} %collective-permute-done.first.first_band, bf16[4,272,128]{2,1,0:T(8,128)(2,1)S(1)} %collective-permute-done.1.second.second_band, ...), custom_call_target="tpu_custom_call" | custom-call | flops 10000000 | bytes 4194304 | tf_op jit(solution)/shard_map/finish/pallas_call | solution.py:386
  24.5 3.9 %collective-permute-done.3.second = bf16[256,256]{1,0:T(8,128)(2,1)S(1)} collective-permute-done((bf16[256,256]{1,0:T(8,128)(2,1)S(1)}, bf16[256,256]{1,0:T(8,128)(2,1)S(1)}, u32[]{:S(2)}, u32[]{:S(2)}) %collective-permute-start.3) | collective-permute-done | bytes 131104 | tf_op jit(solution)/shard_map/ppermute | solution.py:473
  28.4 0.1 fold.1
  28.5 9.8 %all_to_all.5 = bf16[4,256,128]{2,1,0:T(8,128)(2,1)S(1)} all-to-all(bf16[4,256,128]{2,1,0:T(8,128)(2,1)S(1)} %fold.1), channel_id=1, replica_groups=mesh['row'=8,'col'=4] {'col'}, dimensions={0} | all-to-all | bytes 524288 | tf_op jit(solution)/shard_map/all_to_all | solution.py:493
  38.3 0.7 %convert_reduce_fusion = f32[256,128]{1,0:T(8,128)} fusion(bf16[4,256,128]{2,1,0:T(8,128)(2,1)S(1)} %all_to_all.5), kind=kLoop, calls=%fused_computation | loop fusion | flops 229376 | bytes 393216 | tf_op jit(solution)/shard_map/reduce_sum | solution.py:494
Async XLA Ops:
  12.3 7.9 %collective-permute-start.1 = (bf16[4,272,128]{2,1,0:T(8,128)(2,1)S(1)}, bf16[4,272,128]{2,1,0:T(8,128)(2,1)S(1)}, u32[]{:S(2)}, u32[]{:S(2)}) collective-permute-start(bf16[4,272,128]{2,1,0:T(8,128)(2,1)S(1)} %all_gather.11.band), channel_id=1, source_target_pairs={{4,8},{12,16},{20,24},{8,4},{16,12},{24,20},{5,9},{13,17},{21,25},... | collective-permute-start | bytes 835592 | tf_op jit(solution)/shard_map/ppermute | solution.py:431
  14.2 5.9 %collective-permute-start = (bf16[4,272,128]{2,1,0:T(8,128)(2,1)S(1)}, bf16[4,272,128]{2,1,0:T(8,128)(2,1)S(1)}, u32[]{:S(2)}, u32[]{:S(2)}) collective-permute-start(bf16[4,272,128]{2,1,0:T(8,128)(2,1)S(1)} %all_gather.11.band), channel_id=1, source_target_pairs={{0,4},{8,12},{16,20},{24,28},{4,0},{12,8},{20,16},{28,24},{1,5},{9... | collective-permute-start | bytes 835592 | tf_op jit(solution)/shard_map/ppermute | solution.py:432
  21.9 2.1 %collective-permute-start.2 = (bf16[256,256]{1,0:T(8,128)(2,1)S(1)}, bf16[256,256]{1,0:T(8,128)(2,1)S(1)}, u32[]{:S(2)}, u32[]{:S(2)}) collective-permute-start(bf16[256,256]{1,0:T(8,128)(2,1)S(1)} %get-tuple-element.20), channel_id=1, source_target_pairs={{0,4},{8,12},{16,20},{24,28},{4,0},{12,8},{20,16},{28,24},{1,5},{9... | collective-permute-start | bytes 393224 | tf_op jit(solution)/shard_map/ppermute | solution.py:472
  22.1 6.3 %collective-permute-start.3 = (bf16[256,256]{1,0:T(8,128)(2,1)S(1)}, bf16[256,256]{1,0:T(8,128)(2,1)S(1)}, u32[]{:S(2)}, u32[]{:S(2)}) collective-permute-start(bf16[256,256]{1,0:T(8,128)(2,1)S(1)} %get-tuple-element.20), channel_id=1, source_target_pairs={{4,8},{12,16},{20,24},{8,4},{16,12},{24,20},{5,9},{13,17},{21,25},... | collective-permute-start | bytes 393224 | tf_op jit(solution)/shard_map/ppermute | solution.py:473

commit v13 on v8

--- a/solution.py
+++ b/solution.py
@@ -341,41 +341,32 @@
 
 
 def finish_kernel(
-    band, first_band, second_band, turned, probe, first, partial, second_info, centre,
+    band, first_band, second_band, turned, probe, first, pair, out, centre,
 ):
     columns = band.shape[0]
     tile = (band.shape[1] - INFO) // 2
-    odd = lax.axis_index("row") % 2
+    me = lax.axis_index("row")
+    odd = me % 2
     own_frame, first_frame, second_frame = (
         frame_of(b) for b in (band, first_band, second_band)
     )
-    which = iota(second_info.shape, 0)
-    second_info[...] = jnp.where(
-        which == 0, second_frame[0], jnp.where(which == 1, second_frame[1], second_frame[2])
-    )
+    outer = ((me > 0) & (me < lax.axis_size("row") - 1)).astype(jnp.int32)
     for r in range(0, tile, STRIP):
         s, t = pl.ds(r, STRIP), pl.ds(tile + r, STRIP)
         accumulate(centre, turned, probe, s, t, t, -1)
-        before = (iota((STRIP, tile), 0) + r < first_frame[1]).astype(jnp.int32)
+        rows = iota((STRIP, tile), 0) + r
+        from_first = (rows < first_frame[1]).astype(jnp.int32) == odd
+        from_second = (rows < second_frame[1]).astype(jnp.int32) + 2 * (1 - outer) == 1 - odd
         for part in (s, t):
-            mine = place(centre[part].astype(F32), columns, own_frame[0], own_frame[2], None)
-            other = place(
-                first[part].astype(F32), columns, first_frame[0], first_frame[2], before == odd
+            own = place(centre[part].astype(F32), columns, own_frame[0], own_frame[2], None)
+            near = place(
+                first[part].astype(F32), columns, first_frame[0], first_frame[2], from_first
+            )
+            far = place(
+                pair[odd, part].astype(F32), columns, second_frame[0], second_frame[2], from_second
             )
             for c in range(columns):
-                partial[c, part] = mine[c] + other[c]
-
-
-def fold_kernel(partial, second, second_info, out):
-    columns, height, tile = out.shape
-    odd = lax.axis_index("row") % 2
-    source, row, col = (second_info[r : r + 1] for r in range(3))
-    for r in range(0, height, STRIP):
-        s = pl.ds(r, STRIP)
-        before = (iota((STRIP, tile), 0) + r % tile < row).astype(jnp.int32)
-        other = place(second[s].astype(F32), columns, source, col, before == 1 - odd)
-        for c in range(columns):
-            out[c, s] = (partial[c, s] + other[c]).astype(BF16)
+                out[c, part] = (own[c] + near[c] + far[c]).astype(BF16)
 
 
 def call(kernel, name, out_shape, in_specs, scratch, flops, moved, *args):
@@ -467,25 +458,20 @@
         first, second, *prepared,
     )
     from_first = lax.ppermute(to_rows, "row", swaps[0])
-    from_second = lax.ppermute(to_rows, "row", swaps[1])
-    partial, second_info = call(
+    ends = [r * columns + c for r in (0, rows - 1) for c in range(columns)]
+    pairs = [ends[i : i + 2] for i in range(0, 2 * columns, 2)]
+    pairs += [
+        [r * columns + c, (r + 1) * columns + c]
+        for r in range(1, rows - 1, 2) for c in range(columns)
+    ]
+    pair = lax.all_gather(to_rows, ("row", "col"), axis_index_groups=pairs)
+    summed = call(
         finish_kernel, "finish",
-        (
-            jax.ShapeDtypeStruct((columns, height, tile), F32),
-            jax.ShapeDtypeStruct((8, tile), jnp.int32),
-        ),
-        [VMEM] * 6,
+        jax.ShapeDtypeStruct((columns, height, tile), BF16),
+        [VMEM] * 7,
         [pltpu.VMEM((height, extent), BF16)],
         10**7, 2**22,
-        band, first, second, turned, prepared[3], from_first,
-    )
-    summed = call(
-        fold_kernel, "fold",
-        jax.ShapeDtypeStruct((columns, height, tile), BF16),
-        [VMEM] * 3,
-        [],
-        10**7, 2**20,
-        partial, from_second, second_info,
+        band, first, second, turned, prepared[3], from_first, pair,
     )
     shares = lax.all_to_all(summed, "col", split_axis=0, concat_axis=0, tiled=True)
     return jnp.sum(shares.astype(F32), axis=0).reshape(2, tile, tile)

time: 36.8 us -> 37.5 us (1.019)
  the two profiles are of different devices: /device:TPU:8 before, /device:TPU:0 now
where the time goes in v13:
time: 37.5 us; the launch traced here: 37.3 us
  blocking collectives  24.6 us (66%)
  Pallas kernels  6.44 us (17%)
  starting transfers between devices  4.87 us (13%)
  between operations  0.71 us (2%)
  other arithmetic  0.69 us (2%)
    all_gather x1, blocking collectives, per_device(): band = lax.all_gather(packed, 'col')  10.6 us
    all_to_all x1, blocking collectives, per_device(): lax.all_to_all(summed, 'col', split_axis=0, concat_axis=0, tiled=True)  8.35 us
    pallas_call x4, Pallas kernels, call(): pl.pallas_call(kernel, out_shape=out_shape, in_specs=in_specs, out_specs=...  6.44 us
    all_gather x1, blocking collectives, per_device(): pair = lax.all_gather(to_rows, ('row', 'col'), axis_index_groups=pairs)  5.63 us
    ppermute x1, starting transfers between devices, per_device(): first = lax.ppermute(band, 'row', swaps[0])  2.99 us
    ppermute x1, starting transfers between devices, per_device(): from_first = lax.ppermute(to_rows, 'row', swaps[0])  1.22 us
  transfers between devices with their start and end apart: 3, of which 0 were waited for; matrix products, arithmetic and copies ran while one was open for 0% of the time, Pallas kernels for 8%

profile of v13, /device:TPU:0, one launch (start us, length us, event | category | flops | bytes accessed | tf_op | source)
XLA Modules:
  0.0 37.3 jit_solution(10900802997928894505)
XLA Ops:
  0.7 1.0 %pack.1 = bf16[272,128]{1,0:T(8,128)(2,1)S(1)} custom-call(f32[2,128,128]{2,1,0:T(8,128)} %specimen.1, s32[1,1,2,2]{3,2,1,0:T(2,128)} %centers.1, s32[1,1]{1,0:T(1,128)S(6)} %copy.8.cnt, s32[1,1,2]{2,1,0:T(1,128)} %helpers.1), custom_call_target="tpu_custom_call" | custom-call | flops 100000 | bytes 524288 | tf_op jit(solution)/shard_map/pack/pallas_call | solution.py:377
  1.6 10.6 %all-gather = bf16[1088,128]{1,0:T(8,128)(2,1)S(1)} all-gather(bf16[272,128]{1,0:T(8,128)(2,1)S(1)} %pack.1), channel_id=2, replica_groups=mesh['row'=8,'col'=4] {'col'}, dimensions={0}, use_global_device_ids=true | all-gather | bytes 348160 | tf_op jit(solution)/shard_map/all_gather | solution.py:412
  12.2 0.7 %collective-permute-start.1 = (bf16[4,272,128]{2,1,0:T(8,128)(2,1)S(1)}, bf16[4,272,128]{2,1,0:T(8,128)(2,1)S(1)}, u32[]{:S(2)}, u32[]{:S(2)}) collective-permute-start(bf16[4,272,128]{2,1,0:T(8,128)(2,1)S(1)} %bitcast.3), channel_id=1, source_target_pairs={{4,8},{12,16},{20,24},{8,4},{16,12},{24,20},{5,9},{13,17},{21,25},... | collective-permute-start | bytes 835592 | tf_op jit(solution)/shard_map/ppermute | solution.py:419
  12.9 3.0 %collective-permute-start = (bf16[4,272,128]{2,1,0:T(8,128)(2,1)S(1)}, bf16[4,272,128]{2,1,0:T(8,128)(2,1)S(1)}, u32[]{:S(2)}, u32[]{:S(2)}) collective-permute-start(bf16[4,272,128]{2,1,0:T(8,128)(2,1)S(1)} %bitcast.4), channel_id=1, source_target_pairs={{0,4},{8,12},{16,20},{24,28},{4,0},{12,8},{20,16},{28,24},{1,5},{9... | collective-permute-start | bytes 835592 | tf_op jit(solution)/shard_map/ppermute | solution.py:420
  15.9 3.0 %prepare.1 = (bf16[16,256]{1,0:T(8,128)(2,1)S(1)}, f32[256,256]{1,0:T(8,128)S(1)}, bf16[8,256,256]{2,1,0:T(8,128)(2,1)S(1)}, f32[4,2,256,256]{3,2,1,0:T(8,128)S(1)}, f32[4,2,128,256]{3,2,1,0:T(8,128)S(1)}) custom-call(bf16[4,272,128]{2,1,0:T(8,128)(2,1)S(1)} %bitcast.5, f32[4,2,256,256]{3,2,1,0:T(8,128)} %probe.1, f32[1,1,1,256,256]{4,3,2,1,0:T(8,128)} %measured.1, ...), custom_call_target="tpu_custom_call" | custom-call | flops 1000000000 | bytes 4194304 | tf_op jit(solution)/shard_map/prepare/pallas_call | solution.py:377
  18.8 0.0 collective-permute-done.1.second.second_band
  18.9 0.0 collective-permute-done.first.first_band
  18.9 1.9 %frame.1 = (bf16[256,256]{1,0:T(8,128)(2,1)S(1)}, f32[4,2,256,256]{3,2,1,0:T(8,128)S(1)}) custom-call(bf16[4,272,128]{2,1,0:T(8,128)(2,1)S(1)} %collective-permute-done.first.first_band, bf16[4,272,128]{2,1,0:T(8,128)(2,1)S(1)} %collective-permute-done.1.second.second_band, bf16[16,256]{1,0:T(8,128)(2,1)S(1)} %get-tuple-element.12.info, ...), custom_call_target="tpu_custom_call" | custom-call | flops 2000000000 | bytes 4194304 | tf_op jit(solution)/shard_map/frame/pallas_call | solution.py:377
  20.8 1.2 %collective-permute-start.2 = (bf16[256,256]{1,0:T(8,128)(2,1)S(1)}, bf16[256,256]{1,0:T(8,128)(2,1)S(1)}, u32[]{:S(2)}, u32[]{:S(2)}) collective-permute-start(bf16[256,256]{1,0:T(8,128)(2,1)S(1)} %get-tuple-element.18), channel_id=1, source_target_pairs={{0,4},{8,12},{16,20},{24,28},{4,0},{12,8},{20,16},{28,24},{1,5},{9... | collective-permute-start | bytes 393224 | tf_op jit(solution)/shard_map/ppermute | solution.py:460
  22.0 5.6 %all-gather.1 = bf16[512,256]{1,0:T(8,128)(2,1)S(1)} all-gather(bf16[256,256]{1,0:T(8,128)(2,1)S(1)} %get-tuple-element.18), channel_id=3, replica_groups={{0,1},{2,3},{28,29},{30,31},{4,8},{5,9},{6,10},{7,11},{12,16},{13,17},{..., dimensions={0}, use_global_device_ids=true | all-gather | bytes 393216 | tf_op jit(solution)/shard_map/all_gather | solution.py:467
  27.6 0.0 collective-permute-done.2.first
  27.6 0.6 %finish.1 = bf16[4,256,128]{2,1,0:T(8,128)(2,1)S(1)} custom-call(bf16[4,272,128]{2,1,0:T(8,128)(2,1)S(1)} %bitcast.6, bf16[4,272,128]{2,1,0:T(8,128)(2,1)S(1)} %collective-permute-done.first.first_band, bf16[4,272,128]{2,1,0:T(8,128)(2,1)S(1)} %collective-permute-done.1.second.second_band, f32[4,2,256,256]{3,2,1,0:T(8,128)S(1)} %get-tuple-element.17.turned, ...), custom_call_target="tpu_custom_call" | custom-call | flops 10000000 | bytes 4194304 | tf_op jit(solution)/shard_map/finish/pallas_call | solution.py:377
  28.2 8.4 %all_to_all.5 = bf16[4,256,128]{2,1,0:T(8,128)(2,1)S(1)} all-to-all(bf16[4,256,128]{2,1,0:T(8,128)(2,1)S(1)} %finish.1), channel_id=1, replica_groups=mesh['row'=8,'col'=4] {'col'}, dimensions={0} | all-to-all | bytes 524288 | tf_op jit(solution)/shard_map/all_to_all | solution.py:476
  36.6 0.7 %convert_reduce_fusion = f32[256,128]{1,0:T(8,128)} fusion(bf16[4,256,128]{2,1,0:T(8,128)(2,1)S(1)} %all_to_all.5), kind=kLoop, calls=%fused_computation | loop fusion | flops 229376 | bytes 393216 | tf_op jit(solution)/shard_map/reduce_sum | solution.py:477
Async XLA Ops:
  12.2 6.6 %collective-permute-start.1 = (bf16[4,272,128]{2,1,0:T(8,128)(2,1)S(1)}, bf16[4,272,128]{2,1,0:T(8,128)(2,1)S(1)}, u32[]{:S(2)}, u32[]{:S(2)}) collective-permute-start(bf16[4,272,128]{2,1,0:T(8,128)(2,1)S(1)} %bitcast.3), channel_id=1, source_target_pairs={{4,8},{12,16},{20,24},{8,4},{16,12},{24,20},{5,9},{13,17},{21,25},... | collective-permute-start | bytes 835592 | tf_op jit(solution)/shard_map/ppermute | solution.py:419
  12.9 6.0 %collective-permute-start = (bf16[4,272,128]{2,1,0:T(8,128)(2,1)S(1)}, bf16[4,272,128]{2,1,0:T(8,128)(2,1)S(1)}, u32[]{:S(2)}, u32[]{:S(2)}) collective-permute-start(bf16[4,272,128]{2,1,0:T(8,128)(2,1)S(1)} %bitcast.4), channel_id=1, source_target_pairs={{0,4},{8,12},{16,20},{24,28},{4,0},{12,8},{20,16},{28,24},{1,5},{9... | collective-permute-start | bytes 835592 | tf_op jit(solution)/shard_map/ppermute | solution.py:420
  20.8 6.9 %collective-permute-start.2 = (bf16[256,256]{1,0:T(8,128)(2,1)S(1)}, bf16[256,256]{1,0:T(8,128)(2,1)S(1)}, u32[]{:S(2)}, u32[]{:S(2)}) collective-permute-start(bf16[256,256]{1,0:T(8,128)(2,1)S(1)} %get-tuple-element.18), channel_id=1, source_target_pairs={{0,4},{8,12},{16,20},{24,28},{4,0},{12,8},{20,16},{28,24},{1,5},{9... | collective-permute-start | bytes 393224 | tf_op jit(solution)/shard_map/ppermute | solution.py:460

commit v14 on v8

--- a/solution.py
+++ b/solution.py
@@ -214,23 +214,28 @@
     strips = [pl.ds(r, STRIP) for r in range(0, half, STRIP)]
     lower = [pl.ds(half + r, STRIP) for r in range(0, half, STRIP)]
 
+    def strip(i, offset=0):
+        return pl.ds(pl.multiple_of(offset + i * STRIP, STRIP), STRIP)
+
     def split(x):
         return x[:, :half], x[:, half:]
 
     def join(x, y):
         return jnp.concatenate([x, y], 1).astype(BF16)
 
-    def gather(s):
+    def gather(i, carry):
+        s = strip(i)
         rows = iota((STRIP, tile), 0) + s.start
         from_first = (rows >= row).astype(jnp.int32) == odd
         for p in range(2):
-            part = pl.ds(p * tile + s.start, STRIP)
+            part = strip(i, p * tile)
             patch[p, s] = gather_columns(
                 lambda c: jnp.where(
                     from_first, first[c, part].astype(F32), second[c, part].astype(F32)
                 ),
                 source, col, columns, (STRIP, tile),
             )
+        return carry
 
     def wave(k):
         for s in strips:
@@ -255,63 +260,70 @@
                 mixed[k, q, s] = join(er, our)
                 mixed[k, q, t] = join(ei, oui)
 
-    def along_columns(k, q):
-        far[k, q] = dot(tables[4 + q], mixed[k, q])
-
-    def correct(q, which):
-        for s, t in list(zip(strips, lower))[which]:
+    def along_columns(k):
+        for q in range(2):
+            far[k, q] = dot(tables[4 + q], mixed[k, q])
+
+    def correct(i, carry):
+        for q in range(2):
+            s, t = strip(i), strip(i, half)
+            out = strip(i, q * half)
             re = [far[k, q, s] for k in range(modes)]
             im = [far[k, q, t] for k in range(modes)]
             intensity = sum(x * x for x in re + im)
-            size = amplitude[pl.ds(q * half + s.start, STRIP)]
-            factor = 1.0 - size * lax.rsqrt(jnp.maximum(intensity, 0.25))
-            out = pl.ds(q * half + s.start, STRIP)
+            factor = 1.0 - amplitude[out] * lax.rsqrt(jnp.maximum(intensity, 0.25))
             for k in range(modes):
                 (re_even, re_odd), (im_even, im_odd) = split(re[k] * factor), split(im[k] * factor)
                 corrected[k, 0, out] = join(re_even, im_even)
                 corrected[k, 1, out] = join(re_odd, im_odd)
-
-    def back_along_rows(k, q):
-        part = pl.ds(q * half, half)
+        return carry
+
+    def back_along_rows(k):
         for c in range(2):
-            product[k, c, part] = dot(corrected[k, c, part], tables[2 + c])
-
-    def mix_back(k, q):
-        for s, t in zip(strips, lower):
-            part = pl.ds(q * half + s.start, STRIP)
-            x, y = product[k, 0, part], product[k, 1, part]
-            (lr, li), (hr, hi) = split(x + y), split(x - y)
-            mixed_back[k, q, s] = join(lr, hr)
-            mixed_back[k, q, t] = join(li, hi)
-
-    def back_along_columns(k, q):
-        turned[k, q] = dot(tables[6 + q], mixed_back[k, q])
-
-    for s in strips:
-        gather(s)
-    for k in range(modes + 1):
-        if k < modes:
-            wave(k)
-            along_rows(k)
-        if k > 0:
-            mix(k - 1)
-            along_columns(k - 1, 0)
-    share = -(-len(strips) // modes)
-    for k in range(modes):
-        along_columns(k, 1)
-        correct(0, slice(k * share, (k + 1) * share))
-    for k in range(modes):
-        back_along_rows(k, 0)
-        correct(1, slice(k * share, (k + 1) * share))
-    for k in range(modes):
-        mix_back(k, 0)
-        back_along_columns(k, 0)
-        back_along_rows(k, 1)
-    for k in range(modes):
-        mix_back(k, 1)
-        back_along_columns(k, 1)
-    for s, t in zip(strips, lower):
-        accumulate(to_rows, turned, probe, s, t, s, 1)
+            product[k, c] = dot(corrected[k, c], tables[2 + c])
+
+    def mix_back(k):
+        for q in range(2):
+            for s, t in zip(strips, lower):
+                part = pl.ds(q * half + s.start, STRIP)
+                x, y = product[k, 0, part], product[k, 1, part]
+                (lr, li), (hr, hi) = split(x + y), split(x - y)
+                mixed_back[k, q, s] = join(lr, hr)
+                mixed_back[k, q, t] = join(li, hi)
+
+    def back_along_columns(k):
+        for q in range(2):
+            turned[k, q] = dot(tables[6 + q], mixed_back[k, q])
+
+    def forward(k, carry):
+        wave(k + 1)
+        along_rows(k + 1)
+        mix(k)
+        along_columns(k)
+        return carry
+
+    def backward(k, carry):
+        back_along_rows(k + 1)
+        mix_back(k)
+        back_along_columns(k)
+        return carry
+
+    def finish(i, carry):
+        accumulate(to_rows, turned, probe, strip(i), strip(i, half), strip(i), 1)
+        return carry
+
+    lax.fori_loop(0, len(strips), gather, 0)
+    wave(0)
+    along_rows(0)
+    lax.fori_loop(0, modes - 1, forward, 0)
+    mix(modes - 1)
+    along_columns(modes - 1)
+    lax.fori_loop(0, len(strips), correct, 0)
+    back_along_rows(0)
+    lax.fori_loop(0, modes - 1, backward, 0)
+    mix_back(modes - 1)
+    back_along_columns(modes - 1)
+    lax.fori_loop(0, len(strips), finish, 0)
 
 
 def accumulate(out, turned, probe, s, t, rows, sign):
@@ -324,7 +336,7 @@
         re += pr * cr + pi * ci
         im += pr * ci - pi * cr
     out[s] = re.astype(BF16)
-    out[pl.ds(tile + s.start, STRIP)] = im.astype(BF16)
+    out[pl.ds(pl.multiple_of(tile + s.start, STRIP), STRIP)] = im.astype(BF16)
 
 
 def place(block, columns, source, col, taken):

time: 36.8 us -> 38.5 us (1.046)
  Pallas kernels: 6.25 us -> 7.94 us
    pallas_call x5, Pallas kernels: 6.25 us -> 7.94 us  [call(): pl.pallas_call(kernel, out_shape=out_shape, in_specs=in_specs, out_specs=...]
where the time goes in v14:
time: 38.5 us; the launch traced here: 38.2 us
  blocking collectives  18.1 us (47%)
  Pallas kernels  7.94 us (21%)
  starting transfers between devices  5.74 us (15%)
  waiting for transfers between devices  5.1 us (13%)
  between operations  0.71 us (2%)
  other arithmetic  0.69 us (2%)
    all_gather x1, blocking collectives, per_device(): band = lax.all_gather(packed, 'col')  9.13 us
    all_to_all x1, blocking collectives, per_device(): lax.all_to_all(summed, 'col', split_axis=0, concat_axis=0, tiled=True)  8.94 us
    pallas_call x5, Pallas kernels, call(): pl.pallas_call(kernel, out_shape=out_shape, in_specs=in_specs, out_specs=...  7.94 us
    ppermute x1, waiting for transfers between devices, per_device(): from_second = lax.ppermute(to_rows, 'row', swaps[1])  3.88 us
    ppermute x1, starting transfers between devices, per_device(): second = lax.ppermute(band, 'row', swaps[1])  1.91 us
    ppermute x1, starting transfers between devices, per_device(): from_second = lax.ppermute(to_rows, 'row', swaps[1])  1.91 us
    ppermute x1, starting transfers between devices, per_device(): first = lax.ppermute(band, 'row', swaps[0])  1.74 us
    ppermute x1, waiting for transfers between devices, per_device(): second = lax.ppermute(band, 'row', swaps[1])  1.22 us
  transfers between devices with their start and end apart: 4, of which 2 were waited for; matrix products, arithmetic and copies ran while one was open for 0% of the time, Pallas kernels for 9%

profile of v14, /device:TPU:8, one launch (start us, length us, event | category | flops | bytes accessed | tf_op | source)
XLA Modules:
  0.0 38.2 jit_solution(10921532290786167345)
XLA Ops:
  0.7 1.0 %pack.1 = bf16[272,128]{1,0:T(8,128)(2,1)S(1)} custom-call(f32[2,128,128]{2,1,0:T(8,128)} %specimen.1, s32[1,1,2,2]{3,2,1,0:T(2,128)} %centers.1, s32[1,1]{1,0:T(1,128)S(6)} %copy.8.cnt, s32[1,1,2]{2,1,0:T(1,128)} %helpers.1), custom_call_target="tpu_custom_call" | custom-call | flops 100000 | bytes 524288 | tf_op jit(solution)/shard_map/pack/pallas_call | solution.py:398
  1.6 9.1 %all-gather = bf16[1088,128]{1,0:T(8,128)(2,1)S(1)} all-gather(bf16[272,128]{1,0:T(8,128)(2,1)S(1)} %pack.1), channel_id=2, replica_groups=mesh['row'=8,'col'=4] {'col'}, dimensions={0}, use_global_device_ids=true | all-gather | bytes 348160 | tf_op jit(solution)/shard_map/all_gather | solution.py:433
  10.8 1.9 %collective-permute-start.1 = (bf16[4,272,128]{2,1,0:T(8,128)(2,1)S(1)}, bf16[4,272,128]{2,1,0:T(8,128)(2,1)S(1)}, u32[]{:S(2)}, u32[]{:S(2)}) collective-permute-start(bf16[4,272,128]{2,1,0:T(8,128)(2,1)S(1)} %bitcast.2), channel_id=1, source_target_pairs={{4,8},{12,16},{20,24},{8,4},{16,12},{24,20},{5,9},{13,17},{21,25},... | collective-permute-start | bytes 835592 | tf_op jit(solution)/shard_map/ppermute | solution.py:440
  12.7 1.7 %collective-permute-start = (bf16[4,272,128]{2,1,0:T(8,128)(2,1)S(1)}, bf16[4,272,128]{2,1,0:T(8,128)(2,1)S(1)}, u32[]{:S(2)}, u32[]{:S(2)}) collective-permute-start(bf16[4,272,128]{2,1,0:T(8,128)(2,1)S(1)} %bitcast.3), channel_id=1, source_target_pairs={{0,4},{8,12},{16,20},{24,28},{4,0},{12,8},{20,16},{28,24},{1,5},{9... | collective-permute-start | bytes 835592 | tf_op jit(solution)/shard_map/ppermute | solution.py:441
  14.4 3.0 %prepare.1 = (bf16[16,256]{1,0:T(8,128)(2,1)S(1)}, f32[256,256]{1,0:T(8,128)S(1)}, bf16[8,256,256]{2,1,0:T(8,128)(2,1)S(1)}, f32[4,2,256,256]{3,2,1,0:T(8,128)S(1)}, f32[4,2,128,256]{3,2,1,0:T(8,128)S(1)}) custom-call(bf16[4,272,128]{2,1,0:T(8,128)(2,1)S(1)} %bitcast.4, f32[4,2,256,256]{3,2,1,0:T(8,128)} %probe.1, f32[1,1,1,256,256]{4,3,2,1,0:T(8,128)} %measured.1, ...), custom_call_target="tpu_custom_call" | custom-call | flops 1000000000 | bytes 4194304 | tf_op jit(solution)/shard_map/prepare/pallas_call | solution.py:398
  17.4 1.2 %collective-permute-done.1.second.second_band = bf16[4,272,128]{2,1,0:T(8,128)(2,1)S(1)} collective-permute-done((bf16[4,272,128]{2,1,0:T(8,128)(2,1)S(1)}, bf16[4,272,128]{2,1,0:T(8,128)(2,1)S(1)}, u32[]{:S(2)}, u32[]{:S(2)}) %collective-permute-start.1) | collective-permute-done | bytes 278560 | tf_op jit(solution)/shard_map/ppermute | solution.py:440
  18.6 0.0 collective-permute-done.first.first_band
  18.6 3.4 %frame.1 = (bf16[256,256]{1,0:T(8,128)(2,1)S(1)}, f32[4,2,256,256]{3,2,1,0:T(8,128)S(1)}) custom-call(bf16[4,272,128]{2,1,0:T(8,128)(2,1)S(1)} %collective-permute-done.first.first_band, bf16[4,272,128]{2,1,0:T(8,128)(2,1)S(1)} %collective-permute-done.1.second.second_band, bf16[16,256]{1,0:T(8,128)(2,1)S(1)} %get-tuple-element.14.info, ...), custom_call_target="tpu_custom_call" | custom-call | flops 2000000000 | bytes 4194304 | tf_op jit(solution)/shard_map/frame/pallas_call | solution.py:398
  22.0 0.2 collective-permute-start.2
  22.2 1.9 %collective-permute-start.3 = (bf16[256,256]{1,0:T(8,128)(2,1)S(1)}, bf16[256,256]{1,0:T(8,128)(2,1)S(1)}, u32[]{:S(2)}, u32[]{:S(2)}) collective-permute-start(bf16[256,256]{1,0:T(8,128)(2,1)S(1)} %get-tuple-element.20), channel_id=1, source_target_pairs={{4,8},{12,16},{20,24},{8,4},{16,12},{24,20},{5,9},{13,17},{21,25},... | collective-permute-start | bytes 393224 | tf_op jit(solution)/shard_map/ppermute | solution.py:482
  24.1 0.0 collective-permute-done.2.first
  24.2 0.5 %finish.1 = (f32[4,256,128]{2,1,0:T(8,128)S(1)}, s32[8,128]{1,0:T(8,128)S(1)}) custom-call(bf16[4,272,128]{2,1,0:T(8,128)(2,1)S(1)} %bitcast.5, bf16[4,272,128]{2,1,0:T(8,128)(2,1)S(1)} %collective-permute-done.first.first_band, bf16[4,272,128]{2,1,0:T(8,128)(2,1)S(1)} %collective-permute-done.1.second.second_band, ...), custom_call_target="tpu_custom_call" | custom-call | flops 10000000 | bytes 4194304 | tf_op jit(solution)/shard_map/finish/pallas_call | solution.py:398
  24.6 3.9 %collective-permute-done.3.second = bf16[256,256]{1,0:T(8,128)(2,1)S(1)} collective-permute-done((bf16[256,256]{1,0:T(8,128)(2,1)S(1)}, bf16[256,256]{1,0:T(8,128)(2,1)S(1)}, u32[]{:S(2)}, u32[]{:S(2)}) %collective-permute-start.3) | collective-permute-done | bytes 131104 | tf_op jit(solution)/shard_map/ppermute | solution.py:482
  28.5 0.1 fold.1
  28.6 8.9 %all_to_all.5 = bf16[4,256,128]{2,1,0:T(8,128)(2,1)S(1)} all-to-all(bf16[4,256,128]{2,1,0:T(8,128)(2,1)S(1)} %fold.1), channel_id=1, replica_groups=mesh['row'=8,'col'=4] {'col'}, dimensions={0} | all-to-all | bytes 524288 | tf_op jit(solution)/shard_map/all_to_all | solution.py:502
  37.6 0.7 %convert_reduce_fusion = f32[256,128]{1,0:T(8,128)} fusion(bf16[4,256,128]{2,1,0:T(8,128)(2,1)S(1)} %all_to_all.5), kind=kLoop, calls=%fused_computation | loop fusion | flops 229376 | bytes 393216 | tf_op jit(solution)/shard_map/reduce_sum | solution.py:503
Async XLA Ops:
  10.8 7.9 %collective-permute-start.1 = (bf16[4,272,128]{2,1,0:T(8,128)(2,1)S(1)}, bf16[4,272,128]{2,1,0:T(8,128)(2,1)S(1)}, u32[]{:S(2)}, u32[]{:S(2)}) collective-permute-start(bf16[4,272,128]{2,1,0:T(8,128)(2,1)S(1)} %bitcast.2), channel_id=1, source_target_pairs={{4,8},{12,16},{20,24},{8,4},{16,12},{24,20},{5,9},{13,17},{21,25},... | collective-permute-start | bytes 835592 | tf_op jit(solution)/shard_map/ppermute | solution.py:440
  12.7 5.9 %collective-permute-start = (bf16[4,272,128]{2,1,0:T(8,128)(2,1)S(1)}, bf16[4,272,128]{2,1,0:T(8,128)(2,1)S(1)}, u32[]{:S(2)}, u32[]{:S(2)}) collective-permute-start(bf16[4,272,128]{2,1,0:T(8,128)(2,1)S(1)} %bitcast.3), channel_id=1, source_target_pairs={{0,4},{8,12},{16,20},{24,28},{4,0},{12,8},{20,16},{28,24},{1,5},{9... | collective-permute-start | bytes 835592 | tf_op jit(solution)/shard_map/ppermute | solution.py:441
  22.0 2.1 %collective-permute-start.2 = (bf16[256,256]{1,0:T(8,128)(2,1)S(1)}, bf16[256,256]{1,0:T(8,128)(2,1)S(1)}, u32[]{:S(2)}, u32[]{:S(2)}) collective-permute-start(bf16[256,256]{1,0:T(8,128)(2,1)S(1)} %get-tuple-element.20), channel_id=1, source_target_pairs={{0,4},{8,12},{16,20},{24,28},{4,0},{12,8},{20,16},{28,24},{1,5},{9... | collective-permute-start | bytes 393224 | tf_op jit(solution)/shard_map/ppermute | solution.py:481
  22.2 6.3 %collective-permute-start.3 = (bf16[256,256]{1,0:T(8,128)(2,1)S(1)}, bf16[256,256]{1,0:T(8,128)(2,1)S(1)}, u32[]{:S(2)}, u32[]{:S(2)}) collective-permute-start(bf16[256,256]{1,0:T(8,128)(2,1)S(1)} %get-tuple-element.20), channel_id=1, source_target_pairs={{4,8},{12,16},{20,24},{8,4},{16,12},{24,20},{5,9},{13,17},{21,25},... | collective-permute-start | bytes 393224 | tf_op jit(solution)/shard_map/ppermute | solution.py:482

commit v15 on v8

--- a/solution.py
+++ b/solution.py
@@ -109,9 +109,9 @@
     for c in range(columns):
         info = band[c, height - INFO :].astype(F32)
         hit = info[0:1] == me
-        code += jnp.where(hit, c * 128.0 * 128.0 + info[1:2] * 128.0 + info[2:3], 0.0)
+        code += jnp.where(hit, (c * lanes + info[1:2]) * lanes + info[2:3], 0.0)
     code = jnp.sum(code).astype(jnp.int32)
-    return code // (128 * 128), code // 128 % 128, code % 128
+    return code // (lanes * lanes), code // lanes % lanes, code % lanes
 
 
 def prepare_kernel(
@@ -200,7 +200,7 @@
 
 def frame_kernel(
     first, second, info, amplitude, tables, probe, half_own,
-    to_rows, turned, patch, folded, half_far, mixed, far, corrected, product, mixed_back,
+    to_rows, mixed_back, patch, folded, half_far, mixed, far, corrected, product, chi,
 ):
     columns = first.shape[0]
     tile = (first.shape[1] - INFO) // 2
@@ -284,8 +284,10 @@
             mixed_back[k, q, s] = join(lr, hr)
             mixed_back[k, q, t] = join(li, hi)
 
-    def back_along_columns(k, q):
-        turned[k, q] = dot(tables[6 + q], mixed_back[k, q])
+    both_back = jnp.concatenate([tables[6], tables[7]], 1)
+
+    def back_along_columns(k):
+        chi[k] = dot(both_back, mixed_back[k].reshape(2 * extent, extent))
 
     for s in strips:
         gather(s)
@@ -305,22 +307,20 @@
         correct(1, slice(k * share, (k + 1) * share))
     for k in range(modes):
         mix_back(k, 0)
-        back_along_columns(k, 0)
         back_along_rows(k, 1)
     for k in range(modes):
         mix_back(k, 1)
-        back_along_columns(k, 1)
+        back_along_columns(k)
     for s, t in zip(strips, lower):
-        accumulate(to_rows, turned, probe, s, t, s, 1)
-
-
-def accumulate(out, turned, probe, s, t, rows, sign):
+        accumulate(to_rows, chi, probe, s, t, s)
+
+
+def accumulate(out, chi, probe, s, t, rows):
     tile = out.shape[0] // 2
     re = im = 0.0
     for k in range(probe.shape[0]):
         pr, pi = probe[k, 0, rows], probe[k, 1, rows]
-        cr = turned[k, 0, s] + sign * turned[k, 1, s]
-        ci = turned[k, 0, t] + sign * turned[k, 1, t]
+        cr, ci = chi[k, s], chi[k, t]
         re += pr * cr + pi * ci
         im += pr * ci - pi * cr
     out[s] = re.astype(BF16)
@@ -341,9 +341,11 @@
 
 
 def finish_kernel(
-    band, first_band, second_band, turned, probe, first, partial, second_info, centre,
+    band, first_band, second_band, mixed_back, tables, probe, first,
+    partial, second_info, chi, centre,
 ):
     columns = band.shape[0]
+    extent = probe.shape[-1]
     tile = (band.shape[1] - INFO) // 2
     odd = lax.axis_index("row") % 2
     own_frame, first_frame, second_frame = (
@@ -353,9 +355,12 @@
     second_info[...] = jnp.where(
         which == 0, second_frame[0], jnp.where(which == 1, second_frame[1], second_frame[2])
     )
+    both_back = jnp.concatenate([tables[6], -tables[7]], 1)
+    for k in range(probe.shape[0]):
+        chi[k] = dot(both_back, mixed_back[k].reshape(2 * extent, extent))
     for r in range(0, tile, STRIP):
         s, t = pl.ds(r, STRIP), pl.ds(tile + r, STRIP)
-        accumulate(centre, turned, probe, s, t, t, -1)
+        accumulate(centre, chi, probe, s, t, t)
         before = (iota((STRIP, tile), 0) + r < first_frame[1]).astype(jnp.int32)
         for part in (s, t):
             mine = place(centre[part].astype(F32), columns, own_frame[0], own_frame[2], None)
@@ -449,9 +454,9 @@
         band, probe, measured, tables,
     )
     full = (modes, 2, extent, extent)
-    to_rows, turned = call(
+    to_rows, mixed_back = call(
         frame_kernel, "frame",
-        (part, jax.ShapeDtypeStruct(full, F32)),
+        (part, jax.ShapeDtypeStruct(full, BF16)),
         [VMEM] * 7,
         [
             pltpu.VMEM((2, tile, extent), F32),
@@ -461,7 +466,7 @@
             pltpu.VMEM(full, F32),
             pltpu.VMEM(full, BF16),
             pltpu.VMEM(full, F32),
-            pltpu.VMEM(full, BF16),
+            pltpu.VMEM((modes, extent, extent), F32),
         ],
         2 * 10**9, 2**22,
         first, second, *prepared,
@@ -474,10 +479,10 @@
             jax.ShapeDtypeStruct((columns, height, tile), F32),
             jax.ShapeDtypeStruct((8, tile), jnp.int32),
         ),
-        [VMEM] * 6,
-        [pltpu.VMEM((height, extent), BF16)],
-        10**7, 2**22,
-        band, first, second, turned, prepared[3], from_first,
+        [VMEM] * 7,
+        [pltpu.VMEM((modes, extent, extent), F32), pltpu.VMEM((height, extent), BF16)],
+        5 * 10**8, 2**22,
+        band, first, second, mixed_back, prepared[2], prepared[3], from_first,
     )
     summed = call(
         fold_kernel, "fold",

time: 36.8 us -> 36.8 us (level)
  transfers between devices with their start and end apart: 4 -> 4, of which waited for: 2 -> 2; matrix products, arithmetic and copies ran while one was open for 0% -> 0% of each run, Pallas kernels for 9% -> 10%
where the time goes in v15:
time: 36.8 us; the launch traced here: 36.6 us
  blocking collectives  18.1 us (49%)
  Pallas kernels  6.52 us (18%)
  starting transfers between devices  5.74 us (16%)
  waiting for transfers between devices  4.84 us (13%)
  between operations  0.71 us (2%)
  other arithmetic  0.69 us (2%)
    all_gather x1, blocking collectives, per_device(): band = lax.all_gather(packed, 'col')  9.13 us
    all_to_all x1, blocking collectives, per_device(): lax.all_to_all(summed, 'col', split_axis=0, concat_axis=0, tiled=True)  8.94 us
    pallas_call x5, Pallas kernels, call(): pl.pallas_call(kernel, out_shape=out_shape, in_specs=in_specs, out_specs=...  6.52 us
    ppermute x1, waiting for transfers between devices, per_device(): from_second = lax.ppermute(to_rows, 'row', swaps[1])  3.64 us
    ppermute x1, starting transfers between devices, per_device(): second = lax.ppermute(band, 'row', swaps[1])  1.91 us
    ppermute x1, starting transfers between devices, per_device(): from_second = lax.ppermute(to_rows, 'row', swaps[1])  1.91 us
    ppermute x1, starting transfers between devices, per_device(): first = lax.ppermute(band, 'row', swaps[0])  1.74 us
    ppermute x1, waiting for transfers between devices, per_device(): second = lax.ppermute(band, 'row', swaps[1])  1.2 us
  transfers between devices with their start and end apart: 4, of which 2 were waited for; matrix products, arithmetic and copies ran while one was open for 0% of the time, Pallas kernels for 10%

profile of v15, /device:TPU:8, one launch (start us, length us, event | category | flops | bytes accessed | tf_op | source)
XLA Modules:
  0.0 36.6 jit_solution(13338710918158061281)
XLA Ops:
  0.7 1.0 %pack.1 = bf16[272,128]{1,0:T(8,128)(2,1)S(1)} custom-call(f32[2,128,128]{2,1,0:T(8,128)} %specimen.1, s32[1,1,2,2]{3,2,1,0:T(2,128)} %centers.1, s32[1,1]{1,0:T(1,128)S(6)} %copy.8.cnt, s32[1,1,2]{2,1,0:T(1,128)} %helpers.1), custom_call_target="tpu_custom_call" | custom-call | flops 100000 | bytes 524288 | tf_op jit(solution)/shard_map/pack/pallas_call | solution.py:391
  1.6 9.1 %all-gather = bf16[1088,128]{1,0:T(8,128)(2,1)S(1)} all-gather(bf16[272,128]{1,0:T(8,128)(2,1)S(1)} %pack.1), channel_id=2, replica_groups=mesh['row'=8,'col'=4] {'col'}, dimensions={0}, use_global_device_ids=true | all-gather | bytes 348160 | tf_op jit(solution)/shard_map/all_gather | solution.py:426
  10.8 1.9 %collective-permute-start.1 = (bf16[4,272,128]{2,1,0:T(8,128)(2,1)S(1)}, bf16[4,272,128]{2,1,0:T(8,128)(2,1)S(1)}, u32[]{:S(2)}, u32[]{:S(2)}) collective-permute-start(bf16[4,272,128]{2,1,0:T(8,128)(2,1)S(1)} %bitcast.2), channel_id=1, source_target_pairs={{4,8},{12,16},{20,24},{8,4},{16,12},{24,20},{5,9},{13,17},{21,25},... | collective-permute-start | bytes 835592 | tf_op jit(solution)/shard_map/ppermute | solution.py:433
  12.7 1.7 %collective-permute-start = (bf16[4,272,128]{2,1,0:T(8,128)(2,1)S(1)}, bf16[4,272,128]{2,1,0:T(8,128)(2,1)S(1)}, u32[]{:S(2)}, u32[]{:S(2)}) collective-permute-start(bf16[4,272,128]{2,1,0:T(8,128)(2,1)S(1)} %bitcast.3), channel_id=1, source_target_pairs={{0,4},{8,12},{16,20},{24,28},{4,0},{12,8},{20,16},{28,24},{1,5},{9... | collective-permute-start | bytes 835592 | tf_op jit(solution)/shard_map/ppermute | solution.py:434
  14.4 3.0 %prepare.1 = (bf16[16,256]{1,0:T(8,128)(2,1)S(1)}, f32[256,256]{1,0:T(8,128)S(1)}, bf16[8,256,256]{2,1,0:T(8,128)(2,1)S(1)}, f32[4,2,256,256]{3,2,1,0:T(8,128)S(1)}, f32[4,2,128,256]{3,2,1,0:T(8,128)S(1)}) custom-call(bf16[4,272,128]{2,1,0:T(8,128)(2,1)S(1)} %bitcast.4, f32[4,2,256,256]{3,2,1,0:T(8,128)} %probe.1, f32[1,1,1,256,256]{4,3,2,1,0:T(8,128)} %measured.1, ...), custom_call_target="tpu_custom_call" | custom-call | flops 1000000000 | bytes 4194304 | tf_op jit(solution)/shard_map/prepare/pallas_call | solution.py:391
  17.4 1.2 %collective-permute-done.1.second.second_band = bf16[4,272,128]{2,1,0:T(8,128)(2,1)S(1)} collective-permute-done((bf16[4,272,128]{2,1,0:T(8,128)(2,1)S(1)}, bf16[4,272,128]{2,1,0:T(8,128)(2,1)S(1)}, u32[]{:S(2)}, u32[]{:S(2)}) %collective-permute-start.1) | collective-permute-done | bytes 278560 | tf_op jit(solution)/shard_map/ppermute | solution.py:433
  18.6 0.0 collective-permute-done.first.first_band
  18.6 1.7 %frame.1 = (bf16[256,256]{1,0:T(8,128)(2,1)S(1)}, bf16[4,2,256,256]{3,2,1,0:T(8,128)(2,1)S(1)}) custom-call(bf16[4,272,128]{2,1,0:T(8,128)(2,1)S(1)} %collective-permute-done.first.first_band, bf16[4,272,128]{2,1,0:T(8,128)(2,1)S(1)} %collective-permute-done.1.second.second_band, bf16[16,256]{1,0:T(8,128)(2,1)S(1)} %get-tuple-element.14.info, ...), custom_call_target="tpu_custom_call" | custom-call | flops 2000000000 | bytes 4194304 | tf_op jit(solution)/shard_map/frame/pallas_call | solution.py:391
  20.4 0.2 collective-permute-start.2
  20.5 1.9 %collective-permute-start.3 = (bf16[256,256]{1,0:T(8,128)(2,1)S(1)}, bf16[256,256]{1,0:T(8,128)(2,1)S(1)}, u32[]{:S(2)}, u32[]{:S(2)}) collective-permute-start(bf16[256,256]{1,0:T(8,128)(2,1)S(1)} %get-tuple-element.20), channel_id=1, source_target_pairs={{4,8},{12,16},{20,24},{8,4},{16,12},{24,20},{5,9},{13,17},{21,25},... | collective-permute-start | bytes 393224 | tf_op jit(solution)/shard_map/ppermute | solution.py:475
  22.5 0.0 collective-permute-done.2.first
  22.5 0.7 %finish.1 = (f32[4,256,128]{2,1,0:T(8,128)S(1)}, s32[8,128]{1,0:T(8,128)S(1)}) custom-call(bf16[4,272,128]{2,1,0:T(8,128)(2,1)S(1)} %bitcast.5, bf16[4,272,128]{2,1,0:T(8,128)(2,1)S(1)} %collective-permute-done.first.first_band, bf16[4,272,128]{2,1,0:T(8,128)(2,1)S(1)} %collective-permute-done.1.second.second_band, ...), custom_call_target="tpu_custom_call" | custom-call | flops 500000000 | bytes 4194304 | tf_op jit(solution)/shard_map/finish/pallas_call | solution.py:391
  23.2 3.6 %collective-permute-done.3.second = bf16[256,256]{1,0:T(8,128)(2,1)S(1)} collective-permute-done((bf16[256,256]{1,0:T(8,128)(2,1)S(1)}, bf16[256,256]{1,0:T(8,128)(2,1)S(1)}, u32[]{:S(2)}, u32[]{:S(2)}) %collective-permute-start.3) | collective-permute-done | bytes 131104 | tf_op jit(solution)/shard_map/ppermute | solution.py:475
  26.8 0.1 fold.1
  26.9 8.9 %all_to_all.5 = bf16[4,256,128]{2,1,0:T(8,128)(2,1)S(1)} all-to-all(bf16[4,256,128]{2,1,0:T(8,128)(2,1)S(1)} %fold.1), channel_id=1, replica_groups=mesh['row'=8,'col'=4] {'col'}, dimensions={0} | all-to-all | bytes 524288 | tf_op jit(solution)/shard_map/all_to_all | solution.py:495
  35.9 0.7 %convert_reduce_fusion = f32[256,128]{1,0:T(8,128)} fusion(bf16[4,256,128]{2,1,0:T(8,128)(2,1)S(1)} %all_to_all.5), kind=kLoop, calls=%fused_computation | loop fusion | flops 229376 | bytes 393216 | tf_op jit(solution)/shard_map/reduce_sum | solution.py:496
Async XLA Ops:
  10.8 7.9 %collective-permute-start.1 = (bf16[4,272,128]{2,1,0:T(8,128)(2,1)S(1)}, bf16[4,272,128]{2,1,0:T(8,128)(2,1)S(1)}, u32[]{:S(2)}, u32[]{:S(2)}) collective-permute-start(bf16[4,272,128]{2,1,0:T(8,128)(2,1)S(1)} %bitcast.2), channel_id=1, source_target_pairs={{4,8},{12,16},{20,24},{8,4},{16,12},{24,20},{5,9},{13,17},{21,25},... | collective-permute-start | bytes 835592 | tf_op jit(solution)/shard_map/ppermute | solution.py:433
  12.7 5.9 %collective-permute-start = (bf16[4,272,128]{2,1,0:T(8,128)(2,1)S(1)}, bf16[4,272,128]{2,1,0:T(8,128)(2,1)S(1)}, u32[]{:S(2)}, u32[]{:S(2)}) collective-permute-start(bf16[4,272,128]{2,1,0:T(8,128)(2,1)S(1)} %bitcast.3), channel_id=1, source_target_pairs={{0,4},{8,12},{16,20},{24,28},{4,0},{12,8},{20,16},{28,24},{1,5},{9... | collective-permute-start | bytes 835592 | tf_op jit(solution)/shard_map/ppermute | solution.py:434
  20.4 2.1 %collective-permute-start.2 = (bf16[256,256]{1,0:T(8,128)(2,1)S(1)}, bf16[256,256]{1,0:T(8,128)(2,1)S(1)}, u32[]{:S(2)}, u32[]{:S(2)}) collective-permute-start(bf16[256,256]{1,0:T(8,128)(2,1)S(1)} %get-tuple-element.20), channel_id=1, source_target_pairs={{0,4},{8,12},{16,20},{24,28},{4,0},{12,8},{20,16},{28,24},{1,5},{9... | collective-permute-start | bytes 393224 | tf_op jit(solution)/shard_map/ppermute | solution.py:474
  20.5 6.3 %collective-permute-start.3 = (bf16[256,256]{1,0:T(8,128)(2,1)S(1)}, bf16[256,256]{1,0:T(8,128)(2,1)S(1)}, u32[]{:S(2)}, u32[]{:S(2)}) collective-permute-start(bf16[256,256]{1,0:T(8,128)(2,1)S(1)} %get-tuple-element.20), channel_id=1, source_target_pairs={{4,8},{12,16},{20,24},{8,4},{16,12},{24,20},{5,9},{13,17},{21,25},... | collective-permute-start | bytes 393224 | tf_op jit(solution)/shard_map/ppermute | solution.py:475

commit v16 on v15

--- a/solution.py
+++ b/solution.py
@@ -102,12 +102,18 @@
     return out
 
 
+def ring(columns):
+    if columns & (columns - 1):
+        return list(range(columns))
+    return [i ^ (i >> 1) for i in range(columns)]
+
+
 def frame_of(band):
     columns, height, lanes = band.shape
     me = lax.axis_index("col").astype(F32)
     code = jnp.zeros((1, lanes), F32)
-    for c in range(columns):
-        info = band[c, height - INFO :].astype(F32)
+    for place, c in enumerate(ring(columns)):
+        info = band[place, height - INFO :].astype(F32)
         hit = info[0:1] == me
         code += jnp.where(hit, (c * lanes + info[1:2]) * lanes + info[2:3], 0.0)
     code = jnp.sum(code).astype(jnp.int32)
@@ -183,9 +189,10 @@
             groups[count:] = turned
             probe_out[k, p] = groups[pl.ds(count - base, count)].reshape(extent, extent)
 
+    order = ring(columns)
     patch = [
         gather_columns(
-            lambda c: band[c, p * tile : (p + 1) * tile].astype(F32),
+            lambda c: band[order.index(c), p * tile : (p + 1) * tile].astype(F32),
             source, col, columns, (tile, tile),
         )
         for p in range(2)
@@ -207,6 +214,7 @@
     extent = probe.shape[-1]
     half = extent // 2
     modes = probe.shape[0]
+    order = ring(columns)
     odd = lax.axis_index("row") % 2
     source, col, row = (
         info[r : r + 1, :tile].astype(F32).astype(jnp.int32) for r in range(3)
@@ -227,7 +235,9 @@
             part = pl.ds(p * tile + s.start, STRIP)
             patch[p, s] = gather_columns(
                 lambda c: jnp.where(
-                    from_first, first[c, part].astype(F32), second[c, part].astype(F32)
+                    from_first,
+                    first[order.index(c), part].astype(F32),
+                    second[order.index(c), part].astype(F32),
                 ),
                 source, col, columns, (STRIP, tile),
             )
@@ -423,7 +433,7 @@
         10**5, 2**19,
         specimen, centers, frame_counts, helper_cols,
     )
-    band = lax.all_gather(packed, "col")
+    band = lax.all_gather(packed, "col", axis_index_groups=[ring(columns)])
 
     rows = lax.axis_size("row")
     swaps = []

time: 36.8 us -> 38.7 us (1.052)
  blocking collectives: 18.1 us -> 20 us
    all_gather x1, blocking collectives: 9.13 us -> 11.1 us  [per_device(): band = lax.all_gather(packed, 'col', axis_index_groups=[ring(columns)])]
where the time goes in v16:
time: 38.7 us; the launch traced here: 38.5 us
  blocking collectives  20 us (52%)
  Pallas kernels  6.5 us (17%)
  starting transfers between devices  5.74 us (15%)
  waiting for transfers between devices  4.86 us (13%)
  between operations  0.71 us (2%)
  other arithmetic  0.69 us (2%)
    all_gather x1, blocking collectives, per_device(): band = lax.all_gather(packed, 'col', axis_index_groups=[ring(columns)])  11.1 us
    all_to_all x1, blocking collectives, per_device(): lax.all_to_all(summed, 'col', split_axis=0, concat_axis=0, tiled=True)  8.94 us
    pallas_call x5, Pallas kernels, call(): pl.pallas_call(kernel, out_shape=out_shape, in_specs=in_specs, out_specs=...  6.5 us
    ppermute x1, waiting for transfers between devices, per_device(): from_second = lax.ppermute(to_rows, 'row', swaps[1])  3.64 us
    ppermute x1, starting transfers between devices, per_device(): second = lax.ppermute(band, 'row', swaps[1])  1.91 us
    ppermute x1, starting transfers between devices, per_device(): from_second = lax.ppermute(to_rows, 'row', swaps[1])  1.91 us
    ppermute x1, starting transfers between devices, per_device(): first = lax.ppermute(band, 'row', swaps[0])  1.74 us
    ppermute x1, waiting for transfers between devices, per_device(): second = lax.ppermute(band, 'row', swaps[1])  1.22 us
  transfers between devices with their start and end apart: 4, of which 2 were waited for; matrix products, arithmetic and copies ran while one was open for 0% of the time, Pallas kernels for 10%

profile of v16, /device:TPU:8, one launch (start us, length us, event | category | flops | bytes accessed | tf_op | source)
XLA Modules:
  0.0 38.5 jit_solution(15578546225633818560)
XLA Ops:
  0.7 1.0 %pack.1 = bf16[272,128]{1,0:T(8,128)(2,1)S(1)} custom-call(f32[2,128,128]{2,1,0:T(8,128)} %specimen.1, s32[1,1,2,2]{3,2,1,0:T(2,128)} %centers.1, s32[1,1]{1,0:T(1,128)S(6)} %copy.8.cnt, s32[1,1,2]{2,1,0:T(1,128)} %helpers.1), custom_call_target="tpu_custom_call" | custom-call | flops 100000 | bytes 524288 | tf_op jit(solution)/shard_map/pack/pallas_call | solution.py:401
  1.6 11.1 %all-gather = bf16[1088,128]{1,0:T(8,128)(2,1)S(1)} all-gather(bf16[272,128]{1,0:T(8,128)(2,1)S(1)} %pack.1), channel_id=2, replica_groups={{0,1,3,2},{4,5,7,6},{8,9,11,10},{12,13,15,14},{16,17,19,18},{20,21,23,2..., dimensions={0}, use_global_device_ids=true | all-gather | bytes 348160 | tf_op jit(solution)/shard_map/all_gather | solution.py:436
  12.7 1.9 %collective-permute-start.1 = (bf16[4,272,128]{2,1,0:T(8,128)(2,1)S(1)}, bf16[4,272,128]{2,1,0:T(8,128)(2,1)S(1)}, u32[]{:S(2)}, u32[]{:S(2)}) collective-permute-start(bf16[4,272,128]{2,1,0:T(8,128)(2,1)S(1)} %bitcast.2), channel_id=1, source_target_pairs={{4,8},{12,16},{20,24},{8,4},{16,12},{24,20},{5,9},{13,17},{21,25},... | collective-permute-start | bytes 835592 | tf_op jit(solution)/shard_map/ppermute | solution.py:443
  14.6 1.7 %collective-permute-start = (bf16[4,272,128]{2,1,0:T(8,128)(2,1)S(1)}, bf16[4,272,128]{2,1,0:T(8,128)(2,1)S(1)}, u32[]{:S(2)}, u32[]{:S(2)}) collective-permute-start(bf16[4,272,128]{2,1,0:T(8,128)(2,1)S(1)} %bitcast.3), channel_id=1, source_target_pairs={{0,4},{8,12},{16,20},{24,28},{4,0},{12,8},{20,16},{28,24},{1,5},{9... | collective-permute-start | bytes 835592 | tf_op jit(solution)/shard_map/ppermute | solution.py:444
  16.3 3.0 %prepare.1 = (bf16[16,256]{1,0:T(8,128)(2,1)S(1)}, f32[256,256]{1,0:T(8,128)S(1)}, bf16[8,256,256]{2,1,0:T(8,128)(2,1)S(1)}, f32[4,2,256,256]{3,2,1,0:T(8,128)S(1)}, f32[4,2,128,256]{3,2,1,0:T(8,128)S(1)}) custom-call(bf16[4,272,128]{2,1,0:T(8,128)(2,1)S(1)} %bitcast.4, f32[4,2,256,256]{3,2,1,0:T(8,128)} %probe.1, f32[1,1,1,256,256]{4,3,2,1,0:T(8,128)} %measured.1, ...), custom_call_target="tpu_custom_call" | custom-call | flops 1000000000 | bytes 4194304 | tf_op jit(solution)/shard_map/prepare/pallas_call | solution.py:401
  19.3 1.2 %collective-permute-done.1.second.second_band = bf16[4,272,128]{2,1,0:T(8,128)(2,1)S(1)} collective-permute-done((bf16[4,272,128]{2,1,0:T(8,128)(2,1)S(1)}, bf16[4,272,128]{2,1,0:T(8,128)(2,1)S(1)}, u32[]{:S(2)}, u32[]{:S(2)}) %collective-permute-start.1) | collective-permute-done | bytes 278560 | tf_op jit(solution)/shard_map/ppermute | solution.py:443
  20.5 0.0 collective-permute-done.first.first_band
  20.5 1.7 %frame.1 = (bf16[256,256]{1,0:T(8,128)(2,1)S(1)}, bf16[4,2,256,256]{3,2,1,0:T(8,128)(2,1)S(1)}) custom-call(bf16[4,272,128]{2,1,0:T(8,128)(2,1)S(1)} %collective-permute-done.first.first_band, bf16[4,272,128]{2,1,0:T(8,128)(2,1)S(1)} %collective-permute-done.1.second.second_band, bf16[16,256]{1,0:T(8,128)(2,1)S(1)} %get-tuple-element.14.info, ...), custom_call_target="tpu_custom_call" | custom-call | flops 2000000000 | bytes 4194304 | tf_op jit(solution)/shard_map/frame/pallas_call | solution.py:401
  22.3 0.2 collective-permute-start.2
  22.5 1.9 %collective-permute-start.3 = (bf16[256,256]{1,0:T(8,128)(2,1)S(1)}, bf16[256,256]{1,0:T(8,128)(2,1)S(1)}, u32[]{:S(2)}, u32[]{:S(2)}) collective-permute-start(bf16[256,256]{1,0:T(8,128)(2,1)S(1)} %get-tuple-element.20), channel_id=1, source_target_pairs={{4,8},{12,16},{20,24},{8,4},{16,12},{24,20},{5,9},{13,17},{21,25},... | collective-permute-start | bytes 393224 | tf_op jit(solution)/shard_map/ppermute | solution.py:485
  24.4 0.0 collective-permute-done.2.first
  24.4 0.7 %finish.1 = (f32[4,256,128]{2,1,0:T(8,128)S(1)}, s32[8,128]{1,0:T(8,128)S(1)}) custom-call(bf16[4,272,128]{2,1,0:T(8,128)(2,1)S(1)} %bitcast.5, bf16[4,272,128]{2,1,0:T(8,128)(2,1)S(1)} %collective-permute-done.first.first_band, bf16[4,272,128]{2,1,0:T(8,128)(2,1)S(1)} %collective-permute-done.1.second.second_band, ...), custom_call_target="tpu_custom_call" | custom-call | flops 500000000 | bytes 4194304 | tf_op jit(solution)/shard_map/finish/pallas_call | solution.py:401
  25.1 3.6 %collective-permute-done.3.second = bf16[256,256]{1,0:T(8,128)(2,1)S(1)} collective-permute-done((bf16[256,256]{1,0:T(8,128)(2,1)S(1)}, bf16[256,256]{1,0:T(8,128)(2,1)S(1)}, u32[]{:S(2)}, u32[]{:S(2)}) %collective-permute-start.3) | collective-permute-done | bytes 131104 | tf_op jit(solution)/shard_map/ppermute | solution.py:485
  28.8 0.1 fold.1
  28.9 8.9 %all_to_all.5 = bf16[4,256,128]{2,1,0:T(8,128)(2,1)S(1)} all-to-all(bf16[4,256,128]{2,1,0:T(8,128)(2,1)S(1)} %fold.1), channel_id=1, replica_groups=mesh['row'=8,'col'=4] {'col'}, dimensions={0} | all-to-all | bytes 524288 | tf_op jit(solution)/shard_map/all_to_all | solution.py:505
  37.8 0.7 %convert_reduce_fusion = f32[256,128]{1,0:T(8,128)} fusion(bf16[4,256,128]{2,1,0:T(8,128)(2,1)S(1)} %all_to_all.5), kind=kLoop, calls=%fused_computation | loop fusion | flops 229376 | bytes 393216 | tf_op jit(solution)/shard_map/reduce_sum | solution.py:506
Async XLA Ops:
  12.7 7.9 %collective-permute-start.1 = (bf16[4,272,128]{2,1,0:T(8,128)(2,1)S(1)}, bf16[4,272,128]{2,1,0:T(8,128)(2,1)S(1)}, u32[]{:S(2)}, u32[]{:S(2)}) collective-permute-start(bf16[4,272,128]{2,1,0:T(8,128)(2,1)S(1)} %bitcast.2), channel_id=1, source_target_pairs={{4,8},{12,16},{20,24},{8,4},{16,12},{24,20},{5,9},{13,17},{21,25},... | collective-permute-start | bytes 835592 | tf_op jit(solution)/shard_map/ppermute | solution.py:443
  14.6 5.9 %collective-permute-start = (bf16[4,272,128]{2,1,0:T(8,128)(2,1)S(1)}, bf16[4,272,128]{2,1,0:T(8,128)(2,1)S(1)}, u32[]{:S(2)}, u32[]{:S(2)}) collective-permute-start(bf16[4,272,128]{2,1,0:T(8,128)(2,1)S(1)} %bitcast.3), channel_id=1, source_target_pairs={{0,4},{8,12},{16,20},{24,28},{4,0},{12,8},{20,16},{28,24},{1,5},{9... | collective-permute-start | bytes 835592 | tf_op jit(solution)/shard_map/ppermute | solution.py:444
  22.3 2.1 %collective-permute-start.2 = (bf16[256,256]{1,0:T(8,128)(2,1)S(1)}, bf16[256,256]{1,0:T(8,128)(2,1)S(1)}, u32[]{:S(2)}, u32[]{:S(2)}) collective-permute-start(bf16[256,256]{1,0:T(8,128)(2,1)S(1)} %get-tuple-element.20), channel_id=1, source_target_pairs={{0,4},{8,12},{16,20},{24,28},{4,0},{12,8},{20,16},{28,24},{1,5},{9... | collective-permute-start | bytes 393224 | tf_op jit(solution)/shard_map/ppermute | solution.py:484
  22.5 6.3 %collective-permute-start.3 = (bf16[256,256]{1,0:T(8,128)(2,1)S(1)}, bf16[256,256]{1,0:T(8,128)(2,1)S(1)}, u32[]{:S(2)}, u32[]{:S(2)}) collective-permute-start(bf16[256,256]{1,0:T(8,128)(2,1)S(1)} %get-tuple-element.20), channel_id=1, source_target_pairs={{4,8},{12,16},{20,24},{8,4},{16,12},{24,20},{5,9},{13,17},{21,25},... | collective-permute-start | bytes 393224 | tf_op jit(solution)/shard_map/ppermute | solution.py:485

commit v17 on v9

--- a/solution.py
+++ b/solution.py
@@ -12,6 +12,7 @@
 F32 = jnp.float32
 BF16 = jnp.bfloat16
 INFO = 16
+ROW = ("pair", "core")
 STRIP = 16
 VMEM = pl.BlockSpec(memory_space=pltpu.VMEM)
 SMEM = pl.BlockSpec(memory_space=pltpu.SMEM)
@@ -116,7 +117,7 @@
 
 def halves(bands):
     columns = bands.shape[0] // 2
-    odd = lax.axis_index("row") % 2
+    odd = lax.axis_index(ROW) % 2
     return odd * columns, (1 - odd) * columns, columns
 
 
@@ -213,7 +214,7 @@
     extent = probe.shape[-1]
     half = extent // 2
     modes = probe.shape[0]
-    odd = lax.axis_index("row") % 2
+    odd = lax.axis_index(ROW) % 2
     source, col, row = (
         info[r : r + 1, :tile].astype(F32).astype(jnp.int32) for r in range(3)
     )
@@ -351,7 +352,7 @@
 ):
     mine, theirs, columns = halves(bands)
     tile = (bands.shape[1] - INFO) // 2
-    odd = lax.axis_index("row") % 2
+    odd = lax.axis_index(ROW) % 2
     own_frame, first_frame, second_frame = (
         frame_of(ref, base, columns)
         for ref, base in ((bands, mine), (bands, theirs), (second_band, 0))
@@ -375,7 +376,7 @@
 
 def fold_kernel(partial, second, second_info, out):
     columns, height, tile = out.shape
-    odd = lax.axis_index("row") % 2
+    odd = lax.axis_index(ROW) % 2
     source, row, col = (second_info[r : r + 1] for r in range(3))
     for r in range(0, height, STRIP):
         s = pl.ds(r, STRIP)
@@ -425,18 +426,14 @@
         10**5, 2**19,
         specimen, centers, frame_counts, helper_cols,
     )
-    rows = lax.axis_size("row")
+    rows = (lax.axis_size("pair") * lax.axis_size("core"))
     swaps = []
     for start in (0, 1):
         pairs = [(i, i + 1) for i in range(start, rows - 1, 2)]
         swaps.append(pairs + [(b, a) for a, b in pairs])
-    groups = [
-        [r * columns + c for r in (start, start + 1) for c in range(columns)]
-        for start in range(0, rows, 2)
-    ]
-    bands = lax.all_gather(packed, ("row", "col"), axis_index_groups=groups)
-    band = lax.dynamic_slice_in_dim(bands, lax.axis_index("row") % 2 * columns, columns)
-    second = lax.ppermute(band, "row", swaps[1])
+    bands = lax.all_gather(packed, ("core", "col"))
+    band = lax.dynamic_slice_in_dim(bands, lax.axis_index(ROW) % 2 * columns, columns)
+    second = lax.ppermute(band, ROW, swaps[1])
     tables = dft_tables(extent)
     prepared = call(
         prepare_kernel, "prepare",
@@ -476,8 +473,8 @@
         2 * 10**9, 2**22,
         bands, second, *prepared,
     )
-    from_first = lax.ppermute(to_rows, "row", swaps[0])
-    from_second = lax.ppermute(to_rows, "row", swaps[1])
+    from_first = lax.ppermute(to_rows, ROW, swaps[0])
+    from_second = lax.ppermute(to_rows, ROW, swaps[1])
     partial, second_info = call(
         finish_kernel, "finish",
         (
@@ -502,17 +499,19 @@
 
 
 def solution(mesh):
+    rows, columns = mesh.devices.shape
+    split = jax.sharding.Mesh(mesh.devices.reshape(rows // 2, 2, columns), ROW + ("col",))
     return jax.shard_map(
         per_device,
-        mesh=mesh,
+        mesh=split,
         in_specs=(
-            P(None, "row", "col"),
+            P(None, ROW, "col"),
             P(),
-            P("row", "col", None, None, None),
-            P("row", "col", None, None),
-            P("row", "col"),
-            P("row", "col", None),
+            P(ROW, "col", None, None, None),
+            P(ROW, "col", None, None),
+            P(ROW, "col"),
+            P(ROW, "col", None),
         ),
-        out_specs=P(None, "row", "col"),
+        out_specs=P(None, ROW, "col"),
         check_vma=False,
     )

time: 53.2 us -> 53.2 us (level)
  no operation moved by 1% of the time
where the time goes in v17:
time: 53.2 us; the launch traced here: 53 us
  blocking collectives  34.3 us (64%)
  waiting for transfers between devices  6.8 us (13%)
  Pallas kernels  6.47 us (12%)
  starting transfers between devices  4.01 us (8%)
  between operations  0.71 us (1%)
  other arithmetic  0.69 us (1%)
    all_gather x1, blocking collectives, per_device(): bands = lax.all_gather(packed, ('core', 'col'))  25 us
    all_to_all x1, blocking collectives, per_device(): lax.all_to_all(summed, 'col', split_axis=0, concat_axis=0, tiled=True)  9.36 us
    pallas_call x5, Pallas kernels, call(): pl.pallas_call(kernel, out_shape=out_shape, in_specs=in_specs, out_specs=...  6.47 us
    ppermute x1, waiting for transfers between devices, per_device(): from_second = lax.ppermute(to_rows, ROW, swaps[1])  3.86 us
    ppermute x1, waiting for transfers between devices, per_device(): second = lax.ppermute(band, ROW, swaps[1])  2.94 us
    ppermute x1, starting transfers between devices, per_device(): second = lax.ppermute(band, ROW, swaps[1])  1.92 us
    ppermute x1, starting transfers between devices, per_device(): from_second = lax.ppermute(to_rows, ROW, swaps[1])  1.91 us
  transfers between devices with their start and end apart: 3, of which 2 were waited for; matrix products, arithmetic and copies ran while one was open for 0% of the time, Pallas kernels for 7%

profile of v17, /device:TPU:8, one launch (start us, length us, event | category | flops | bytes accessed | tf_op | source)
XLA Modules:
  0.0 53.0 jit_solution(4314294731893554618)
XLA Ops:
  0.7 1.0 %pack.1 = bf16[272,128]{1,0:T(8,128)(2,1)S(1)} custom-call(f32[2,128,128]{2,1,0:T(8,128)} %specimen.1, s32[1,1,2,2]{3,2,1,0:T(2,128)} %centers.1, s32[1,1]{1,0:T(1,128)S(6)} %copy.8.cnt, s32[1,1,2]{2,1,0:T(1,128)} %helpers.1), custom_call_target="tpu_custom_call" | custom-call | flops 100000 | bytes 524288 | tf_op jit(solution)/shard_map/pack/pallas_call | solution.py:394
  1.6 25.0 %all-gather = bf16[2176,128]{1,0:T(8,128)(2,1)S(1)} all-gather(bf16[272,128]{1,0:T(8,128)(2,1)S(1)} %pack.1), channel_id=2, replica_groups=mesh['pair'=4,'core'=2,'col'=4] {'core','col'}, dimensions={0}, use_global_device_ids=true | all-gather | bytes 626688 | tf_op jit(solution)/shard_map/all_gather | solution.py:434
  26.6 1.9 %collective-permute-start = (bf16[4,272,128]{2,1,0:T(8,128)(2,1)S(1)}, bf16[4,272,128]{2,1,0:T(8,128)(2,1)S(1)}, u32[]{:S(2)}, u32[]{:S(2)}) collective-permute-start(bf16[4,272,128]{2,1,0:T(8,128)(2,1)S(1)} %constant_dynamic-slice_fusion), channel_id=1, source_target_pairs={{4,8},{12,16},{20,24},{8,4},{16,12},{24,20},{5,9},{13,17},{21,25},... | collective-permute-start | bytes 835592 | tf_op jit(solution)/shard_map/ppermute | solution.py:436
  28.5 3.0 %prepare.1 = (bf16[16,256]{1,0:T(8,128)(2,1)S(1)}, f32[256,256]{1,0:T(8,128)S(1)}, bf16[8,256,256]{2,1,0:T(8,128)(2,1)S(1)}, f32[4,2,256,256]{3,2,1,0:T(8,128)S(1)}, f32[4,2,128,256]{3,2,1,0:T(8,128)S(1)}) custom-call(bf16[8,272,128]{2,1,0:T(8,128)(2,1)S(1)} %bitcast.3, f32[4,2,256,256]{3,2,1,0:T(8,128)} %probe.1, f32[1,1,1,256,256]{4,3,2,1,0:T(8,128)} %measured.1, ...), custom_call_target="tpu_custom_call" | custom-call | flops 1000000000 | bytes 4194304 | tf_op jit(solution)/shard_map/prepare/pallas_call | solution.py:394
  31.5 2.9 %collective-permute-done.second.second_band = bf16[4,272,128]{2,1,0:T(8,128)(2,1)S(1)} collective-permute-done((bf16[4,272,128]{2,1,0:T(8,128)(2,1)S(1)}, bf16[4,272,128]{2,1,0:T(8,128)(2,1)S(1)}, u32[]{:S(2)}, u32[]{:S(2)}) %collective-permute-start) | collective-permute-done | bytes 278560 | tf_op jit(solution)/shard_map/ppermute | solution.py:436
  34.5 1.9 %frame.1 = (bf16[256,256]{1,0:T(8,128)(2,1)S(1)}, f32[4,2,256,256]{3,2,1,0:T(8,128)S(1)}) custom-call(bf16[8,272,128]{2,1,0:T(8,128)(2,1)S(1)} %bitcast.4, bf16[4,272,128]{2,1,0:T(8,128)(2,1)S(1)} %collective-permute-done.second.second_band, bf16[16,256]{1,0:T(8,128)(2,1)S(1)} %get-tuple-element.14.info, f32[256,256]{1,0:T(8,128)S(1)} %get-tuple-element.15.amplitude, ...), custom_call_target="tpu_custom_call" | custom-call | flops 2000000000 | bytes 4194304 | tf_op jit(solution)/shard_map/frame/pallas_call | solution.py:394
  36.4 0.2 collective-permute-start.1
  36.6 1.9 %collective-permute-start.2 = (bf16[256,256]{1,0:T(8,128)(2,1)S(1)}, bf16[256,256]{1,0:T(8,128)(2,1)S(1)}, u32[]{:S(2)}, u32[]{:S(2)}) collective-permute-start(bf16[256,256]{1,0:T(8,128)(2,1)S(1)} %get-tuple-element.20), channel_id=1, source_target_pairs={{4,8},{12,16},{20,24},{8,4},{16,12},{24,20},{5,9},{13,17},{21,25},... | collective-permute-start | bytes 393224 | tf_op jit(solution)/shard_map/ppermute | solution.py:477
  38.5 0.0 collective-permute-done.1.first
  38.5 0.5 finish.1
  39.0 3.9 %collective-permute-done.2.second = bf16[256,256]{1,0:T(8,128)(2,1)S(1)} collective-permute-done((bf16[256,256]{1,0:T(8,128)(2,1)S(1)}, bf16[256,256]{1,0:T(8,128)(2,1)S(1)}, u32[]{:S(2)}, u32[]{:S(2)}) %collective-permute-start.2) | collective-permute-done | bytes 131104 | tf_op jit(solution)/shard_map/ppermute | solution.py:477
  42.9 0.1 fold.1
  43.0 9.4 %all_to_all.5 = bf16[4,256,128]{2,1,0:T(8,128)(2,1)S(1)} all-to-all(bf16[4,256,128]{2,1,0:T(8,128)(2,1)S(1)} %fold.1), channel_id=1, replica_groups=mesh['pair'=4,'core'=2,'col'=4] {'col'}, dimensions={0} | all-to-all | bytes 524288 | tf_op jit(solution)/shard_map/all_to_all | solution.py:497
  52.3 0.7 %convert_reduce_fusion = f32[256,128]{1,0:T(8,128)} fusion(bf16[4,256,128]{2,1,0:T(8,128)(2,1)S(1)} %all_to_all.5), kind=kLoop, calls=%fused_computation | loop fusion | flops 229376 | bytes 393216 | tf_op jit(solution)/shard_map/reduce_sum | solution.py:498
  (1 shorter events, 0.0 us)
Async XLA Ops:
  26.6 7.9 %collective-permute-start = (bf16[4,272,128]{2,1,0:T(8,128)(2,1)S(1)}, bf16[4,272,128]{2,1,0:T(8,128)(2,1)S(1)}, u32[]{:S(2)}, u32[]{:S(2)}) collective-permute-start(bf16[4,272,128]{2,1,0:T(8,128)(2,1)S(1)} %constant_dynamic-slice_fusion), channel_id=1, source_target_pairs={{4,8},{12,16},{20,24},{8,4},{16,12},{24,20},{5,9},{13,17},{21,25},... | collective-permute-start | bytes 835592 | tf_op jit(solution)/shard_map/ppermute | solution.py:436
  36.4 2.1 %collective-permute-start.1 = (bf16[256,256]{1,0:T(8,128)(2,1)S(1)}, bf16[256,256]{1,0:T(8,128)(2,1)S(1)}, u32[]{:S(2)}, u32[]{:S(2)}) collective-permute-start(bf16[256,256]{1,0:T(8,128)(2,1)S(1)} %get-tuple-element.20), channel_id=1, source_target_pairs={{0,4},{8,12},{16,20},{24,28},{4,0},{12,8},{20,16},{28,24},{1,5},{9... | collective-permute-start | bytes 393224 | tf_op jit(solution)/shard_map/ppermute | solution.py:476
  36.6 6.3 %collective-permute-start.2 = (bf16[256,256]{1,0:T(8,128)(2,1)S(1)}, bf16[256,256]{1,0:T(8,128)(2,1)S(1)}, u32[]{:S(2)}, u32[]{:S(2)}) collective-permute-start(bf16[256,256]{1,0:T(8,128)(2,1)S(1)} %get-tuple-element.20), channel_id=1, source_target_pairs={{4,8},{12,16},{20,24},{8,4},{16,12},{24,20},{5,9},{13,17},{21,25},... | collective-permute-start | bytes 393224 | tf_op jit(solution)/shard_map/ppermute | solution.py:477

commit v18 on v15

--- a/solution.py
+++ b/solution.py
@@ -1,4 +1,5 @@
 import functools
+import itertools
 import math
 
 import jax
@@ -232,86 +233,99 @@
                 source, col, columns, (STRIP, tile),
             )
 
-    def wave(k):
-        for s in strips:
-            pr, pi, xr, xi = probe[k, 0, s], probe[k, 1, s], patch[0, s], patch[1, s]
-            re = split(pr * xr - pi * xi)
-            im = split(pr * xi + pi * xr)
-            folded[k, 0, s] = join(re[0] + re[1], im[0] + im[1])
-            folded[k, 1, s] = join(re[0] - re[1], im[0] - im[1])
-
-    def along_rows(k):
-        for q in range(2):
-            half_far[k, q] = dot(folded[k, q], tables[q])
-
-    def mix(k):
-        for s, t in zip(strips, lower):
-            even, odds = half_far[k, 0, s], half_far[k, 1, s]
-            even_own, odds_own = half_own[k, 0, s], half_own[k, 1, s]
-            for q, (e, o) in enumerate(
-                ((even + even_own, odds + odds_own), (even - even_own, odds - odds_own))
-            ):
-                (er, ei), (our, oui) = split(e), split(o)
-                mixed[k, q, s] = join(er, our)
-                mixed[k, q, t] = join(ei, oui)
-
-    def along_columns(k, q):
-        far[k, q] = dot(tables[4 + q], mixed[k, q])
-
-    def correct(q, which):
-        for s, t in list(zip(strips, lower))[which]:
-            re = [far[k, q, s] for k in range(modes)]
-            im = [far[k, q, t] for k in range(modes)]
-            intensity = sum(x * x for x in re + im)
-            size = amplitude[pl.ds(q * half + s.start, STRIP)]
-            factor = 1.0 - size * lax.rsqrt(jnp.maximum(intensity, 0.25))
-            out = pl.ds(q * half + s.start, STRIP)
-            for k in range(modes):
-                (re_even, re_odd), (im_even, im_odd) = split(re[k] * factor), split(im[k] * factor)
-                corrected[k, 0, out] = join(re_even, im_even)
-                corrected[k, 1, out] = join(re_odd, im_odd)
-
-    def back_along_rows(k, q):
+    def wave(k, s):
+        pr, pi, xr, xi = probe[k, 0, s], probe[k, 1, s], patch[0, s], patch[1, s]
+        re = split(pr * xr - pi * xi)
+        im = split(pr * xi + pi * xr)
+        folded[k, 0, s] = join(re[0] + re[1], im[0] + im[1])
+        folded[k, 1, s] = join(re[0] - re[1], im[0] - im[1])
+
+    def along_rows(k, q):
+        half_far[k, q] = dot(folded[k, q], tables[q])
+
+    def mix(k, s, t):
+        even, odds = half_far[k, 0, s], half_far[k, 1, s]
+        even_own, odds_own = half_own[k, 0, s], half_own[k, 1, s]
+        for q, (e, o) in enumerate(
+            ((even + even_own, odds + odds_own), (even - even_own, odds - odds_own))
+        ):
+            (er, ei), (our, oui) = split(e), split(o)
+            mixed[k, q, s] = join(er, our)
+            mixed[k, q, t] = join(ei, oui)
+
+    def along_columns(k, q, part):
+        far[k, q, part] = dot(tables[4 + q, part], mixed[k, q])
+
+    def correct(q, s, t):
+        re = [far[k, q, s] for k in range(modes)]
+        im = [far[k, q, t] for k in range(modes)]
+        intensity = sum(x * x for x in re + im)
+        out = pl.ds(q * half + s.start, STRIP)
+        factor = 1.0 - amplitude[out] * lax.rsqrt(jnp.maximum(intensity, 0.25))
+        for k in range(modes):
+            (re_even, re_odd), (im_even, im_odd) = split(re[k] * factor), split(im[k] * factor)
+            corrected[k, 0, out] = join(re_even, im_even)
+            corrected[k, 1, out] = join(re_odd, im_odd)
+
+    def back_along_rows(k, q, c):
         part = pl.ds(q * half, half)
-        for c in range(2):
-            product[k, c, part] = dot(corrected[k, c, part], tables[2 + c])
-
-    def mix_back(k, q):
-        for s, t in zip(strips, lower):
-            part = pl.ds(q * half + s.start, STRIP)
-            x, y = product[k, 0, part], product[k, 1, part]
-            (lr, li), (hr, hi) = split(x + y), split(x - y)
-            mixed_back[k, q, s] = join(lr, hr)
-            mixed_back[k, q, t] = join(li, hi)
+        product[k, c, part] = dot(corrected[k, c, part], tables[2 + c])
+
+    def mix_back(k, q, s, t):
+        part = pl.ds(q * half + s.start, STRIP)
+        x, y = product[k, 0, part], product[k, 1, part]
+        (lr, li), (hr, hi) = split(x + y), split(x - y)
+        mixed_back[k, q, s] = join(lr, hr)
+        mixed_back[k, q, t] = join(li, hi)
 
     both_back = jnp.concatenate([tables[6], tables[7]], 1)
 
-    def back_along_columns(k):
-        chi[k] = dot(both_back, mixed_back[k].reshape(2 * extent, extent))
+    def back_along_columns(k, part):
+        rows = both_back[part.start : part.start + half]
+        chi[k, part] = dot(rows, mixed_back[k].reshape(2 * extent, extent))
+
+    parts = [pl.ds(0, half), pl.ds(half, half)]
+    pairs = list(zip(strips, lower))
+    every = range(modes)
+
+    def steps(function, *lists):
+        return [functools.partial(function, *args) for args in itertools.product(*lists)]
+
+    def on_strips(function, *lists):
+        return [
+            functools.partial(function, *args, s, t)
+            for args in itertools.product(*lists) for s, t in pairs
+        ]
+
+    def run(products, strip_work):
+        count = len(products)
+        share = -(-len(strip_work) // max(count, 1))
+        for i in range(max(count, 1)):
+            if i < count:
+                products[i]()
+            for work in strip_work[i * share : (i + 1) * share]:
+                work()
 
     for s in strips:
         gather(s)
+    run([], steps(wave, [0], strips))
     for k in range(modes + 1):
-        if k < modes:
-            wave(k)
-            along_rows(k)
-        if k > 0:
-            mix(k - 1)
-            along_columns(k - 1, 0)
-    share = -(-len(strips) // modes)
-    for k in range(modes):
-        along_columns(k, 1)
-        correct(0, slice(k * share, (k + 1) * share))
-    for k in range(modes):
-        back_along_rows(k, 0)
-        correct(1, slice(k * share, (k + 1) * share))
-    for k in range(modes):
-        mix_back(k, 0)
-        back_along_rows(k, 1)
-    for k in range(modes):
-        mix_back(k, 1)
-        back_along_columns(k)
-    for s, t in zip(strips, lower):
+        run(
+            (steps(along_rows, [k], range(2)) if k < modes else [])
+            + (steps(along_columns, [k - 2], [0], parts) if k > 1 else []),
+            (on_strips(mix, [k - 1]) if k > 0 else [])
+            + (steps(wave, [k + 1], strips) if k + 1 < modes else []),
+        )
+    run(steps(along_columns, [modes - 1], [0], parts), [])
+    run(steps(along_columns, every, [1], parts), on_strips(correct, [0]))
+    run(steps(back_along_rows, every, [0], range(2)), on_strips(correct, [1]))
+    run(steps(back_along_rows, every, [1], range(2)), on_strips(mix_back, every, [0]))
+    for k in range(modes + 1):
+        run(
+            steps(back_along_columns, [k - 1], parts) if k > 0 else [],
+            on_strips(mix_back, [k], [1]) if k < modes else [],
+        )
+    for s, t in pairs:
         accumulate(to_rows, chi, probe, s, t, s)
 
 

time: 36.8 us -> 36.8 us (level)
  no operation moved by 1% of the time
where the time goes in v18:
time: 36.8 us; the launch traced here: 36.6 us
  blocking collectives  18.1 us (49%)
  Pallas kernels  6.51 us (18%)
  starting transfers between devices  5.74 us (16%)
  waiting for transfers between devices  4.84 us (13%)
  between operations  0.71 us (2%)
  other arithmetic  0.69 us (2%)
    all_gather x1, blocking collectives, per_device(): band = lax.all_gather(packed, 'col')  9.13 us
    all_to_all x1, blocking collectives, per_device(): lax.all_to_all(summed, 'col', split_axis=0, concat_axis=0, tiled=True)  8.94 us
    pallas_call x5, Pallas kernels, call(): pl.pallas_call(kernel, out_shape=out_shape, in_specs=in_specs, out_specs=...  6.51 us
    ppermute x1, waiting for transfers between devices, per_device(): from_second = lax.ppermute(to_rows, 'row', swaps[1])  3.64 us
    ppermute x1, starting transfers between devices, per_device(): second = lax.ppermute(band, 'row', swaps[1])  1.91 us
    ppermute x1, starting transfers between devices, per_device(): from_second = lax.ppermute(to_rows, 'row', swaps[1])  1.91 us
    ppermute x1, starting transfers between devices, per_device(): first = lax.ppermute(band, 'row', swaps[0])  1.74 us
    ppermute x1, waiting for transfers between devices, per_device(): second = lax.ppermute(band, 'row', swaps[1])  1.2 us
  transfers between devices with their start and end apart: 4, of which 2 were waited for; matrix products, arithmetic and copies ran while one was open for 0% of the time, Pallas kernels for 10%

profile of v18, /device:TPU:8, one launch (start us, length us, event | category | flops | bytes accessed | tf_op | source)
XLA Modules:
  0.0 36.6 jit_solution(14507011852160476408)
XLA Ops:
  0.7 1.0 %pack.1 = bf16[272,128]{1,0:T(8,128)(2,1)S(1)} custom-call(f32[2,128,128]{2,1,0:T(8,128)} %specimen.1, s32[1,1,2,2]{3,2,1,0:T(2,128)} %centers.1, s32[1,1]{1,0:T(1,128)S(6)} %copy.8.cnt, s32[1,1,2]{2,1,0:T(1,128)} %helpers.1), custom_call_target="tpu_custom_call" | custom-call | flops 100000 | bytes 524288 | tf_op jit(solution)/shard_map/pack/pallas_call | solution.py:405
  1.6 9.1 %all-gather = bf16[1088,128]{1,0:T(8,128)(2,1)S(1)} all-gather(bf16[272,128]{1,0:T(8,128)(2,1)S(1)} %pack.1), channel_id=2, replica_groups=mesh['row'=8,'col'=4] {'col'}, dimensions={0}, use_global_device_ids=true | all-gather | bytes 348160 | tf_op jit(solution)/shard_map/all_gather | solution.py:440
  10.8 1.9 %collective-permute-start.1 = (bf16[4,272,128]{2,1,0:T(8,128)(2,1)S(1)}, bf16[4,272,128]{2,1,0:T(8,128)(2,1)S(1)}, u32[]{:S(2)}, u32[]{:S(2)}) collective-permute-start(bf16[4,272,128]{2,1,0:T(8,128)(2,1)S(1)} %bitcast.2), channel_id=1, source_target_pairs={{4,8},{12,16},{20,24},{8,4},{16,12},{24,20},{5,9},{13,17},{21,25},... | collective-permute-start | bytes 835592 | tf_op jit(solution)/shard_map/ppermute | solution.py:447
  12.7 1.7 %collective-permute-start = (bf16[4,272,128]{2,1,0:T(8,128)(2,1)S(1)}, bf16[4,272,128]{2,1,0:T(8,128)(2,1)S(1)}, u32[]{:S(2)}, u32[]{:S(2)}) collective-permute-start(bf16[4,272,128]{2,1,0:T(8,128)(2,1)S(1)} %bitcast.3), channel_id=1, source_target_pairs={{0,4},{8,12},{16,20},{24,28},{4,0},{12,8},{20,16},{28,24},{1,5},{9... | collective-permute-start | bytes 835592 | tf_op jit(solution)/shard_map/ppermute | solution.py:448
  14.4 3.0 %prepare.1 = (bf16[16,256]{1,0:T(8,128)(2,1)S(1)}, f32[256,256]{1,0:T(8,128)S(1)}, bf16[8,256,256]{2,1,0:T(8,128)(2,1)S(1)}, f32[4,2,256,256]{3,2,1,0:T(8,128)S(1)}, f32[4,2,128,256]{3,2,1,0:T(8,128)S(1)}) custom-call(bf16[4,272,128]{2,1,0:T(8,128)(2,1)S(1)} %bitcast.4, f32[4,2,256,256]{3,2,1,0:T(8,128)} %probe.1, f32[1,1,1,256,256]{4,3,2,1,0:T(8,128)} %measured.1, ...), custom_call_target="tpu_custom_call" | custom-call | flops 1000000000 | bytes 4194304 | tf_op jit(solution)/shard_map/prepare/pallas_call | solution.py:405
  17.4 1.2 %collective-permute-done.1.second.second_band = bf16[4,272,128]{2,1,0:T(8,128)(2,1)S(1)} collective-permute-done((bf16[4,272,128]{2,1,0:T(8,128)(2,1)S(1)}, bf16[4,272,128]{2,1,0:T(8,128)(2,1)S(1)}, u32[]{:S(2)}, u32[]{:S(2)}) %collective-permute-start.1) | collective-permute-done | bytes 278560 | tf_op jit(solution)/shard_map/ppermute | solution.py:447
  18.6 0.0 collective-permute-done.first.first_band
  18.6 1.7 %frame.1 = (bf16[256,256]{1,0:T(8,128)(2,1)S(1)}, bf16[4,2,256,256]{3,2,1,0:T(8,128)(2,1)S(1)}) custom-call(bf16[4,272,128]{2,1,0:T(8,128)(2,1)S(1)} %collective-permute-done.first.first_band, bf16[4,272,128]{2,1,0:T(8,128)(2,1)S(1)} %collective-permute-done.1.second.second_band, bf16[16,256]{1,0:T(8,128)(2,1)S(1)} %get-tuple-element.14.info, ...), custom_call_target="tpu_custom_call" | custom-call | flops 2000000000 | bytes 4194304 | tf_op jit(solution)/shard_map/frame/pallas_call | solution.py:405
  20.4 0.2 collective-permute-start.2
  20.5 1.9 %collective-permute-start.3 = (bf16[256,256]{1,0:T(8,128)(2,1)S(1)}, bf16[256,256]{1,0:T(8,128)(2,1)S(1)}, u32[]{:S(2)}, u32[]{:S(2)}) collective-permute-start(bf16[256,256]{1,0:T(8,128)(2,1)S(1)} %get-tuple-element.20), channel_id=1, source_target_pairs={{4,8},{12,16},{20,24},{8,4},{16,12},{24,20},{5,9},{13,17},{21,25},... | collective-permute-start | bytes 393224 | tf_op jit(solution)/shard_map/ppermute | solution.py:489
  22.5 0.0 collective-permute-done.2.first
  22.5 0.7 %finish.1 = (f32[4,256,128]{2,1,0:T(8,128)S(1)}, s32[8,128]{1,0:T(8,128)S(1)}) custom-call(bf16[4,272,128]{2,1,0:T(8,128)(2,1)S(1)} %bitcast.5, bf16[4,272,128]{2,1,0:T(8,128)(2,1)S(1)} %collective-permute-done.first.first_band, bf16[4,272,128]{2,1,0:T(8,128)(2,1)S(1)} %collective-permute-done.1.second.second_band, ...), custom_call_target="tpu_custom_call" | custom-call | flops 500000000 | bytes 4194304 | tf_op jit(solution)/shard_map/finish/pallas_call | solution.py:405
  23.2 3.6 %collective-permute-done.3.second = bf16[256,256]{1,0:T(8,128)(2,1)S(1)} collective-permute-done((bf16[256,256]{1,0:T(8,128)(2,1)S(1)}, bf16[256,256]{1,0:T(8,128)(2,1)S(1)}, u32[]{:S(2)}, u32[]{:S(2)}) %collective-permute-start.3) | collective-permute-done | bytes 131104 | tf_op jit(solution)/shard_map/ppermute | solution.py:489
  26.8 0.1 fold.1
  26.9 8.9 %all_to_all.5 = bf16[4,256,128]{2,1,0:T(8,128)(2,1)S(1)} all-to-all(bf16[4,256,128]{2,1,0:T(8,128)(2,1)S(1)} %fold.1), channel_id=1, replica_groups=mesh['row'=8,'col'=4] {'col'}, dimensions={0} | all-to-all | bytes 524288 | tf_op jit(solution)/shard_map/all_to_all | solution.py:509
  35.9 0.7 %convert_reduce_fusion = f32[256,128]{1,0:T(8,128)} fusion(bf16[4,256,128]{2,1,0:T(8,128)(2,1)S(1)} %all_to_all.5), kind=kLoop, calls=%fused_computation | loop fusion | flops 229376 | bytes 393216 | tf_op jit(solution)/shard_map/reduce_sum | solution.py:510
Async XLA Ops:
  10.8 7.9 %collective-permute-start.1 = (bf16[4,272,128]{2,1,0:T(8,128)(2,1)S(1)}, bf16[4,272,128]{2,1,0:T(8,128)(2,1)S(1)}, u32[]{:S(2)}, u32[]{:S(2)}) collective-permute-start(bf16[4,272,128]{2,1,0:T(8,128)(2,1)S(1)} %bitcast.2), channel_id=1, source_target_pairs={{4,8},{12,16},{20,24},{8,4},{16,12},{24,20},{5,9},{13,17},{21,25},... | collective-permute-start | bytes 835592 | tf_op jit(solution)/shard_map/ppermute | solution.py:447
  12.7 5.9 %collective-permute-start = (bf16[4,272,128]{2,1,0:T(8,128)(2,1)S(1)}, bf16[4,272,128]{2,1,0:T(8,128)(2,1)S(1)}, u32[]{:S(2)}, u32[]{:S(2)}) collective-permute-start(bf16[4,272,128]{2,1,0:T(8,128)(2,1)S(1)} %bitcast.3), channel_id=1, source_target_pairs={{0,4},{8,12},{16,20},{24,28},{4,0},{12,8},{20,16},{28,24},{1,5},{9... | collective-permute-start | bytes 835592 | tf_op jit(solution)/shard_map/ppermute | solution.py:448
  20.4 2.1 %collective-permute-start.2 = (bf16[256,256]{1,0:T(8,128)(2,1)S(1)}, bf16[256,256]{1,0:T(8,128)(2,1)S(1)}, u32[]{:S(2)}, u32[]{:S(2)}) collective-permute-start(bf16[256,256]{1,0:T(8,128)(2,1)S(1)} %get-tuple-element.20), channel_id=1, source_target_pairs={{0,4},{8,12},{16,20},{24,28},{4,0},{12,8},{20,16},{28,24},{1,5},{9... | collective-permute-start | bytes 393224 | tf_op jit(solution)/shard_map/ppermute | solution.py:488
  20.5 6.3 %collective-permute-start.3 = (bf16[256,256]{1,0:T(8,128)(2,1)S(1)}, bf16[256,256]{1,0:T(8,128)(2,1)S(1)}, u32[]{:S(2)}, u32[]{:S(2)}) collective-permute-start(bf16[256,256]{1,0:T(8,128)(2,1)S(1)} %get-tuple-element.20), channel_id=1, source_target_pairs={{4,8},{12,16},{20,24},{8,4},{16,12},{24,20},{5,9},{13,17},{21,25},... | collective-permute-start | bytes 393224 | tf_op jit(solution)/shard_map/ppermute | solution.py:489

commit v19 on v15

--- a/solution.py
+++ b/solution.py
@@ -208,6 +208,8 @@
     half = extent // 2
     modes = probe.shape[0]
     odd = lax.axis_index("row") % 2
+    me = lax.axis_index("row")
+    outer = ((me > 0) & (me < lax.axis_size("row") - 1)).astype(jnp.int32)
     source, col, row = (
         info[r : r + 1, :tile].astype(F32).astype(jnp.int32) for r in range(3)
     )
@@ -222,12 +224,16 @@
 
     def gather(s):
         rows = iota((STRIP, tile), 0) + s.start
-        from_first = (rows >= row).astype(jnp.int32) == odd
+        from_above = (rows >= row).astype(jnp.int32)
+        from_first = from_above == odd
+        from_second = from_above + 2 * (1 - outer) == 1 - odd
         for p in range(2):
             part = pl.ds(p * tile + s.start, STRIP)
             patch[p, s] = gather_columns(
                 lambda c: jnp.where(
-                    from_first, first[c, part].astype(F32), second[c, part].astype(F32)
+                    from_first,
+                    first[c, part].astype(F32),
+                    jnp.where(from_second, second[odd, c, part].astype(F32), 0.0),
                 ),
                 source, col, columns, (STRIP, tile),
             )
@@ -349,7 +355,7 @@
     tile = (band.shape[1] - INFO) // 2
     odd = lax.axis_index("row") % 2
     own_frame, first_frame, second_frame = (
-        frame_of(b) for b in (band, first_band, second_band)
+        frame_of(b) for b in (band, first_band, second_band.at[odd])
     )
     which = iota(second_info.shape, 0)
     second_info[...] = jnp.where(
@@ -430,7 +436,16 @@
     for start in (0, 1):
         pairs = [(i, i + 1) for i in range(start, rows - 1, 2)]
         swaps.append(pairs + [(b, a) for a, b in pairs])
-    second = lax.ppermute(band, "row", swaps[1])
+    ends = [r * columns + c for r in (0, rows - 1) for c in range(columns)]
+    pairs = [ends[i : i + 2] for i in range(0, 2 * columns, 2)]
+    pairs += [
+        [r * columns + c, (r + 1) * columns + c]
+        for r in range(1, rows - 1, 2) for c in range(columns)
+    ]
+    second = lax.all_to_all(
+        jnp.broadcast_to(band, (2,) + band.shape), ("row", "col"),
+        split_axis=0, concat_axis=0, axis_index_groups=pairs, tiled=True,
+    )
     first = lax.ppermute(band, "row", swaps[0])
     tables = dft_tables(extent)
     prepared = call(

time: 36.8 us -> 42.1 us (1.14); the launches traced: 36.6 us -> 41.3 us
  local copies, waits for them, and re-layouts: 0 us -> 5.31 us
  waiting for transfers between devices: 4.84 us -> 2.49 us
  starting transfers between devices: 5.74 us -> 7.78 us
    unnamed x0 -> x8, local copies, waits for them, and re-layouts: none -> 4.42 us
    all_to_all x0 -> x1, starting transfers between devices: none -> 3.49 us  [per_device(): lax.all_to_all(jnp.broadcast_to(band, (2,) + band.shape), ('row', 'col'),...]
    ppermute x1 -> x0, starting transfers between devices: 1.91 us -> none  [per_device(): second = lax.ppermute(band, 'row', swaps[1])]
    ppermute x1, starting transfers between devices: 1.74 us -> 0.07 us  [per_device(): first = lax.ppermute(band, 'row', swaps[0])]
    ppermute x1 -> x0, waiting for transfers between devices: 1.2 us -> none  [per_device(): second = lax.ppermute(band, 'row', swaps[1])]
    ppermute x1, starting transfers between devices: 1.91 us -> 3.09 us  [per_device(): from_second = lax.ppermute(to_rows, 'row', swaps[1])]
    ppermute x1, waiting for transfers between devices: 3.64 us -> 2.48 us  [per_device(): from_second = lax.ppermute(to_rows, 'row', swaps[1])]
    ppermute x1, starting transfers between devices: 0.18 us -> 1.13 us  [per_device(): from_first = lax.ppermute(to_rows, 'row', swaps[0])]
  transfers between devices with their start and end apart: 4 -> 4, of which waited for: 2 -> 1; matrix products, arithmetic and copies ran while one was open for 0% -> 0% of each run, Pallas kernels for 10% -> 9%
where the time goes in v19:
time: 42.1 us; the launch traced here: 41.3 us
  blocking collectives  17.8 us (42%)
  starting transfers between devices  7.78 us (18%)
  Pallas kernels  6.51 us (15%)
  local copies, waits for them, and re-layouts  5.31 us (13%)
  waiting for transfers between devices  2.49 us (6%)
  between operations  0.74 us (2%)
  other arithmetic  0.69 us (2%)
    all_gather x1, blocking collectives, per_device(): band = lax.all_gather(packed, 'col')  9.13 us
    all_to_all x1, blocking collectives, per_device(): lax.all_to_all(summed, 'col', split_axis=0, concat_axis=0, tiled=True)  8.66 us
    pallas_call x5, Pallas kernels, call(): pl.pallas_call(kernel, out_shape=out_shape, in_specs=in_specs, out_specs=...  6.51 us
    unnamed x8, local copies, waits for them, and re-layouts  4.42 us
    all_to_all x1, starting transfers between devices, per_device(): lax.all_to_all(jnp.broadcast_to(band, (2,) + band.shape), ('row', 'col'),...  3.49 us
    ppermute x1, starting transfers between devices, per_device(): from_second = lax.ppermute(to_rows, 'row', swaps[1])  3.09 us
    ppermute x1, waiting for transfers between devices, per_device(): from_second = lax.ppermute(to_rows, 'row', swaps[1])  2.48 us
    ppermute x1, starting transfers between devices, per_device(): from_first = lax.ppermute(to_rows, 'row', swaps[0])  1.13 us
  transfers between devices with their start and end apart: 4, of which 1 were waited for; matrix products, arithmetic and copies ran while one was open for 0% of the time, Pallas kernels for 9%

profile of v19, /device:TPU:8, one launch (start us, length us, event | category | flops | bytes accessed | tf_op | source)
XLA Modules:
  0.0 41.3 jit_solution(8058901982625686173)
XLA Ops:
  0.7 1.0 %pack.1 = bf16[272,128]{1,0:T(8,128)(2,1)S(1)} custom-call(f32[2,128,128]{2,1,0:T(8,128)} %specimen.1, s32[1,1,2,2]{3,2,1,0:T(2,128)} %centers.1, s32[1,1]{1,0:T(1,128)S(6)} %copy.8.cnt, s32[1,1,2]{2,1,0:T(1,128)} %helpers.1), custom_call_target="tpu_custom_call" | custom-call | flops 100000 | bytes 524288 | tf_op jit(solution)/shard_map/pack/pallas_call | solution.py:397
  1.6 9.1 %all-gather = bf16[1088,128]{1,0:T(8,128)(2,1)S(1)} all-gather(bf16[272,128]{1,0:T(8,128)(2,1)S(1)} %pack.1), channel_id=2, replica_groups=mesh['row'=8,'col'=4] {'col'}, dimensions={0}, use_global_device_ids=true | all-gather | bytes 348160 | tf_op jit(solution)/shard_map/all_gather | solution.py:432
  10.8 0.9 %broadcast_in_dim.3 = bf16[2,4,272,128]{3,2,1,0:T(8,128)(2,1)} broadcast(bf16[4,272,128]{2,1,0:T(8,128)(2,1)S(1)} %bitcast.2), dimensions={1,2,3} | broadcast | bytes 835584 | tf_op jit(solution)/shard_map/broadcast_in_dim | solution.py:446
  11.6 3.5 %all-to-all-start = ((bf16[2,4,272,128]{3,2,1,0:T(8,128)(2,1)}), bf16[2,4,272,128]{3,2,1,0:T(8,128)(2,1)S(1)}, u32[]{:S(2)}, u32[]{:S(2)}) async-start(bf16[2,4,272,128]{3,2,1,0:T(8,128)(2,1)} %broadcast_in_dim.3), calls=%async_computation | async-start | bytes 1114112 | tf_op jit(solution)/shard_map/all_to_all | solution.py:445
  15.1 0.1 collective-permute-start
  15.2 3.0 %prepare.1 = (bf16[16,256]{1,0:T(8,128)(2,1)S(1)}, f32[256,256]{1,0:T(8,128)S(1)}, bf16[8,256,256]{2,1,0:T(8,128)(2,1)S(1)}, f32[4,2,256,256]{3,2,1,0:T(8,128)S(1)}, f32[4,2,128,256]{3,2,1,0:T(8,128)S(1)}) custom-call(bf16[4,272,128]{2,1,0:T(8,128)(2,1)S(1)} %bitcast.4, f32[4,2,256,256]{3,2,1,0:T(8,128)} %probe.1, f32[1,1,1,256,256]{4,3,2,1,0:T(8,128)} %measured.1, ...), custom_call_target="tpu_custom_call" | custom-call | flops 1000000000 | bytes 4194304 | tf_op jit(solution)/shard_map/prepare/pallas_call | solution.py:397
  18.2 0.0 copy-start
  18.2 1.0 %copy-done = bf16[8,256,256]{2,1,0:T(8,128)(2,1)} copy-done((bf16[8,256,256]{2,1,0:T(8,128)(2,1)}, bf16[8,256,256]{2,1,0:T(8,128)(2,1)S(1)}, u32[]{:S(2)}) %copy-start) | copy-done | bytes 1048600
  19.2 0.0 copy-start.2
  19.2 1.0 %copy-done.2 = f32[4,2,128,256]{3,2,1,0:T(8,128)} copy-done((f32[4,2,128,256]{3,2,1,0:T(8,128)}, f32[4,2,128,256]{3,2,1,0:T(8,128)S(1)}, u32[]{:S(2)}) %copy-start.2) | copy-done | bytes 1048600
  20.2 0.0 collective-permute-done.first.first_band
  20.2 0.0 all-to-all-done.second.second_band
  20.2 0.0 copy-start.1
  20.2 1.2 %copy-done.1 = bf16[8,256,256]{2,1,0:T(8,128)(2,1)S(1)} copy-done((bf16[8,256,256]{2,1,0:T(8,128)(2,1)S(1)}, bf16[8,256,256]{2,1,0:T(8,128)(2,1)}, u32[]{:S(2)}) %copy-start.1) | copy-done | bytes 1048600
  21.4 0.0 copy-start.3
  21.4 1.2 %copy-done.3 = f32[4,2,128,256]{3,2,1,0:T(8,128)S(1)} copy-done((f32[4,2,128,256]{3,2,1,0:T(8,128)S(1)}, f32[4,2,128,256]{3,2,1,0:T(8,128)}, u32[]{:S(2)}) %copy-start.3) | copy-done | bytes 1048600
  22.6 1.8 %frame.1 = (bf16[256,256]{1,0:T(8,128)(2,1)S(1)}, bf16[4,2,256,256]{3,2,1,0:T(8,128)(2,1)S(1)}) custom-call(bf16[4,272,128]{2,1,0:T(8,128)(2,1)S(1)} %collective-permute-done.first.first_band, bf16[2,4,272,128]{3,2,1,0:T(8,128)(2,1)S(1)} %all-to-all-done.second.second_band, bf16[16,256]{1,0:T(8,128)(2,1)S(1)} %get-tuple-element.14.info, ...), custom_call_target="tpu_custom_call" | custom-call | flops 2000000000 | bytes 4194304 | tf_op jit(solution)/shard_map/frame/pallas_call | solution.py:397
  24.4 1.1 %collective-permute-start.1 = (bf16[256,256]{1,0:T(8,128)(2,1)S(1)}, bf16[256,256]{1,0:T(8,128)(2,1)S(1)}, u32[]{:S(2)}, u32[]{:S(2)}) collective-permute-start(bf16[256,256]{1,0:T(8,128)(2,1)S(1)} %get-tuple-element.20), channel_id=1, source_target_pairs={{0,4},{8,12},{16,20},{24,28},{4,0},{12,8},{20,16},{28,24},{1,5},{9... | collective-permute-start | bytes 393224 | tf_op jit(solution)/shard_map/ppermute | solution.py:489
  25.5 3.1 %collective-permute-start.2 = (bf16[256,256]{1,0:T(8,128)(2,1)S(1)}, bf16[256,256]{1,0:T(8,128)(2,1)S(1)}, u32[]{:S(2)}, u32[]{:S(2)}) collective-permute-start(bf16[256,256]{1,0:T(8,128)(2,1)S(1)} %get-tuple-element.20), channel_id=1, source_target_pairs={{4,8},{12,16},{20,24},{8,4},{16,12},{24,20},{5,9},{13,17},{21,25},... | collective-permute-start | bytes 393224 | tf_op jit(solution)/shard_map/ppermute | solution.py:490
  28.6 0.0 collective-permute-done.1.first
  28.7 0.7 %finish.1 = (f32[4,256,128]{2,1,0:T(8,128)S(1)}, s32[8,128]{1,0:T(8,128)S(1)}) custom-call(bf16[4,272,128]{2,1,0:T(8,128)(2,1)S(1)} %bitcast.5, bf16[4,272,128]{2,1,0:T(8,128)(2,1)S(1)} %collective-permute-done.first.first_band, bf16[2,4,272,128]{3,2,1,0:T(8,128)(2,1)S(1)} %all-to-all-done.second.second_band, ...), custom_call_target="tpu_custom_call" | custom-call | flops 500000000 | bytes 4194304 | tf_op jit(solution)/shard_map/finish/pallas_call | solution.py:397
  29.3 2.5 %collective-permute-done.2.second = bf16[256,256]{1,0:T(8,128)(2,1)S(1)} collective-permute-done((bf16[256,256]{1,0:T(8,128)(2,1)S(1)}, bf16[256,256]{1,0:T(8,128)(2,1)S(1)}, u32[]{:S(2)}, u32[]{:S(2)}) %collective-permute-start.2) | collective-permute-done | bytes 131104 | tf_op jit(solution)/shard_map/ppermute | solution.py:490
  31.8 0.1 fold.1
  31.9 8.7 %all_to_all.10 = bf16[4,256,128]{2,1,0:T(8,128)(2,1)S(1)} all-to-all(bf16[4,256,128]{2,1,0:T(8,128)(2,1)S(1)} %fold.1), channel_id=1, replica_groups=mesh['row'=8,'col'=4] {'col'}, dimensions={0} | all-to-all | bytes 524288 | tf_op jit(solution)/shard_map/all_to_all | solution.py:510
  40.6 0.7 %convert_reduce_fusion = f32[256,128]{1,0:T(8,128)} fusion(bf16[4,256,128]{2,1,0:T(8,128)(2,1)S(1)} %all_to_all.10), kind=kLoop, calls=%fused_computation | loop fusion | flops 229376 | bytes 393216 | tf_op jit(solution)/shard_map/reduce_sum | solution.py:511
Async XLA Ops:
  11.6 8.6 %all-to-all-start = ((bf16[2,4,272,128]{3,2,1,0:T(8,128)(2,1)}), bf16[2,4,272,128]{3,2,1,0:T(8,128)(2,1)S(1)}, u32[]{:S(2)}, u32[]{:S(2)}) async-start(bf16[2,4,272,128]{3,2,1,0:T(8,128)(2,1)} %broadcast_in_dim.3), calls=%async_computation | async-start | bytes 1114112 | tf_op jit(solution)/shard_map/all_to_all | solution.py:445
  15.1 5.1 %collective-permute-start = (bf16[4,272,128]{2,1,0:T(8,128)(2,1)S(1)}, bf16[4,272,128]{2,1,0:T(8,128)(2,1)S(1)}, u32[]{:S(2)}, u32[]{:S(2)}) collective-permute-start(bf16[4,272,128]{2,1,0:T(8,128)(2,1)S(1)} %bitcast.3), channel_id=1, source_target_pairs={{0,4},{8,12},{16,20},{24,28},{4,0},{12,8},{20,16},{28,24},{1,5},{9... | collective-permute-start | bytes 835592 | tf_op jit(solution)/shard_map/ppermute | solution.py:449
  18.2 1.0 %copy-start = (bf16[8,256,256]{2,1,0:T(8,128)(2,1)}, bf16[8,256,256]{2,1,0:T(8,128)(2,1)S(1)}, u32[]{:S(2)}) copy-start(bf16[8,256,256]{2,1,0:T(8,128)(2,1)S(1)} %get-tuple-element.16.tables) | copy-start | bytes 3145732
  19.2 1.0 %copy-start.2 = (f32[4,2,128,256]{3,2,1,0:T(8,128)}, f32[4,2,128,256]{3,2,1,0:T(8,128)S(1)}, u32[]{:S(2)}) copy-start(f32[4,2,128,256]{3,2,1,0:T(8,128)S(1)} %get-tuple-element.18.half_own) | copy-start | bytes 3145732
  20.2 1.2 %copy-start.1 = (bf16[8,256,256]{2,1,0:T(8,128)(2,1)S(1)}, bf16[8,256,256]{2,1,0:T(8,128)(2,1)}, u32[]{:S(2)}) copy-start(bf16[8,256,256]{2,1,0:T(8,128)(2,1)} %copy-done) | copy-start | bytes 3145732
  21.4 1.2 %copy-start.3 = (f32[4,2,128,256]{3,2,1,0:T(8,128)S(1)}, f32[4,2,128,256]{3,2,1,0:T(8,128)}, u32[]{:S(2)}) copy-start(f32[4,2,128,256]{3,2,1,0:T(8,128)} %copy-done.2) | copy-start | bytes 3145732
  24.4 4.2 %collective-permute-start.1 = (bf16[256,256]{1,0:T(8,128)(2,1)S(1)}, bf16[256,256]{1,0:T(8,128)(2,1)S(1)}, u32[]{:S(2)}, u32[]{:S(2)}) collective-permute-start(bf16[256,256]{1,0:T(8,128)(2,1)S(1)} %get-tuple-element.20), channel_id=1, source_target_pairs={{0,4},{8,12},{16,20},{24,28},{4,0},{12,8},{20,16},{28,24},{1,5},{9... | collective-permute-start | bytes 393224 | tf_op jit(solution)/shard_map/ppermute | solution.py:489
  25.5 6.3 %collective-permute-start.2 = (bf16[256,256]{1,0:T(8,128)(2,1)S(1)}, bf16[256,256]{1,0:T(8,128)(2,1)S(1)}, u32[]{:S(2)}, u32[]{:S(2)}) collective-permute-start(bf16[256,256]{1,0:T(8,128)(2,1)S(1)} %get-tuple-element.20), channel_id=1, source_target_pairs={{4,8},{12,16},{20,24},{8,4},{16,12},{24,20},{5,9},{13,17},{21,25},... | collective-permute-start | bytes 393224 | tf_op jit(solution)/shard_map/ppermute | solution.py:490

commit v20 on v15

--- a/solution.py
+++ b/solution.py
@@ -383,7 +383,24 @@
             out[c, s] = (partial[c, s] + other[c]).astype(BF16)
 
 
-def call(kernel, name, out_shape, in_specs, scratch, flops, moved, *args):
+def total_kernel(shares, out, total, sems):
+    planes, tile, _ = out.shape
+    pieces = sems.shape[0]
+    rows = planes * tile // pieces
+    copies = []
+    for i in range(pieces):
+        plane, start = i * rows // tile, i * rows % tile
+        part = pl.ds(i * rows, rows)
+        total[part] = sum(shares[c, part].astype(F32) for c in range(shares.shape[0]))
+        copies.append(
+            pltpu.make_async_copy(total.at[part], out.at[plane, pl.ds(start, rows)], sems.at[i])
+        )
+        copies[-1].start()
+    for copy in copies:
+        copy.wait()
+
+
+def call(kernel, name, out_shape, in_specs, scratch, flops, moved, *args, out_specs=None):
     args = [
         pltpu.with_memory_space_constraint(arg, pltpu.HBM) if spec is HBM else arg
         for arg, spec in zip(args, in_specs)
@@ -392,7 +409,7 @@
         kernel,
         out_shape=out_shape,
         in_specs=in_specs,
-        out_specs=jax.tree.map(lambda _: VMEM, out_shape),
+        out_specs=out_specs or jax.tree.map(lambda _: VMEM, out_shape),
         scratch_shapes=scratch,
         compiler_params=pltpu.CompilerParams(vmem_limit_bytes=32 * 2**20),
         cost_estimate=pl.CostEstimate(flops=flops, bytes_accessed=moved, transcendentals=0),
@@ -493,7 +510,15 @@
         partial, from_second, second_info,
     )
     shares = lax.all_to_all(summed, "col", split_axis=0, concat_axis=0, tiled=True)
-    return jnp.sum(shares.astype(F32), axis=0).reshape(2, tile, tile)
+    return call(
+        total_kernel, "total",
+        jax.ShapeDtypeStruct(specimen.shape, F32),
+        [VMEM],
+        [pltpu.VMEM((height, tile), F32), dma((4,))],
+        10**6, 2**18,
+        shares,
+        out_specs=HBM,
+    )
 
 
 def solution(mesh):

time: 36.8 us -> 36.8 us (level)
  other arithmetic: 0.69 us -> 0 us
  Pallas kernels: 6.52 us -> 7.2 us
    reduce_sum x1 -> x0, other arithmetic: 0.69 us -> none  [per_device(): return jnp.sum(shares.astype(F32), axis=0).reshape(2, tile, tile)]
    pallas_call x5 -> x6, Pallas kernels: 6.52 us -> 7.2 us  [call(): pl.pallas_call(kernel, out_shape=out_shape, in_specs=in_specs, out_specs=...]
where the time goes in v20:
time: 36.8 us; the launch traced here: 36.6 us
  blocking collectives  18.1 us (49%)
  Pallas kernels  7.2 us (20%)
  starting transfers between devices  5.74 us (16%)
  waiting for transfers between devices  4.85 us (13%)
  between operations  0.71 us (2%)
    all_gather x1, blocking collectives, per_device(): band = lax.all_gather(packed, 'col')  9.13 us
    all_to_all x1, blocking collectives, per_device(): lax.all_to_all(summed, 'col', split_axis=0, concat_axis=0, tiled=True)  8.94 us
    pallas_call x6, Pallas kernels, call(): pl.pallas_call(kernel, out_shape=out_shape, in_specs=in_specs, out_specs=...  7.2 us
    ppermute x1, waiting for transfers between devices, per_device(): from_second = lax.ppermute(to_rows, 'row', swaps[1])  3.64 us
    ppermute x1, starting transfers between devices, per_device(): second = lax.ppermute(band, 'row', swaps[1])  1.91 us
    ppermute x1, starting transfers between devices, per_device(): from_second = lax.ppermute(to_rows, 'row', swaps[1])  1.91 us
    ppermute x1, starting transfers between devices, per_device(): first = lax.ppermute(band, 'row', swaps[0])  1.74 us
    ppermute x1, waiting for transfers between devices, per_device(): second = lax.ppermute(band, 'row', swaps[1])  1.21 us
  transfers between devices with their start and end apart: 4, of which 2 were waited for; matrix products, arithmetic and copies ran while one was open for 0% of the time, Pallas kernels for 10%

profile of v20, /device:TPU:8, one launch (start us, length us, event | category | flops | bytes accessed | tf_op | source)
XLA Modules:
  0.0 36.6 jit_solution(9164626664213239081)
XLA Ops:
  0.7 1.0 %pack.1 = bf16[272,128]{1,0:T(8,128)(2,1)S(1)} custom-call(f32[2,128,128]{2,1,0:T(8,128)} %specimen.1, s32[1,1,2,2]{3,2,1,0:T(2,128)} %centers.1, s32[1,1]{1,0:T(1,128)S(6)} %copy.8.cnt, s32[1,1,2]{2,1,0:T(1,128)} %helpers.1), custom_call_target="tpu_custom_call" | custom-call | flops 100000 | bytes 524288 | tf_op jit(solution)/shard_map/pack/pallas_call | solution.py:408
  1.6 9.1 %all-gather = bf16[1088,128]{1,0:T(8,128)(2,1)S(1)} all-gather(bf16[272,128]{1,0:T(8,128)(2,1)S(1)} %pack.1), channel_id=2, replica_groups=mesh['row'=8,'col'=4] {'col'}, dimensions={0}, use_global_device_ids=true | all-gather | bytes 348160 | tf_op jit(solution)/shard_map/all_gather | solution.py:443
  10.8 1.9 %collective-permute-start.1 = (bf16[4,272,128]{2,1,0:T(8,128)(2,1)S(1)}, bf16[4,272,128]{2,1,0:T(8,128)(2,1)S(1)}, u32[]{:S(2)}, u32[]{:S(2)}) collective-permute-start(bf16[4,272,128]{2,1,0:T(8,128)(2,1)S(1)} %bitcast.1), channel_id=1, source_target_pairs={{4,8},{12,16},{20,24},{8,4},{16,12},{24,20},{5,9},{13,17},{21,25},... | collective-permute-start | bytes 835592 | tf_op jit(solution)/shard_map/ppermute | solution.py:450
  12.7 1.7 %collective-permute-start = (bf16[4,272,128]{2,1,0:T(8,128)(2,1)S(1)}, bf16[4,272,128]{2,1,0:T(8,128)(2,1)S(1)}, u32[]{:S(2)}, u32[]{:S(2)}) collective-permute-start(bf16[4,272,128]{2,1,0:T(8,128)(2,1)S(1)} %bitcast.2), channel_id=1, source_target_pairs={{0,4},{8,12},{16,20},{24,28},{4,0},{12,8},{20,16},{28,24},{1,5},{9... | collective-permute-start | bytes 835592 | tf_op jit(solution)/shard_map/ppermute | solution.py:451
  14.4 3.0 %prepare.1 = (bf16[16,256]{1,0:T(8,128)(2,1)S(1)}, f32[256,256]{1,0:T(8,128)S(1)}, bf16[8,256,256]{2,1,0:T(8,128)(2,1)S(1)}, f32[4,2,256,256]{3,2,1,0:T(8,128)S(1)}, f32[4,2,128,256]{3,2,1,0:T(8,128)S(1)}) custom-call(bf16[4,272,128]{2,1,0:T(8,128)(2,1)S(1)} %bitcast.3, f32[4,2,256,256]{3,2,1,0:T(8,128)} %probe.1, f32[1,1,1,256,256]{4,3,2,1,0:T(8,128)} %measured.1, ...), custom_call_target="tpu_custom_call" | custom-call | flops 1000000000 | bytes 4194304 | tf_op jit(solution)/shard_map/prepare/pallas_call | solution.py:408
  17.4 1.2 %collective-permute-done.1.second.second_band = bf16[4,272,128]{2,1,0:T(8,128)(2,1)S(1)} collective-permute-done((bf16[4,272,128]{2,1,0:T(8,128)(2,1)S(1)}, bf16[4,272,128]{2,1,0:T(8,128)(2,1)S(1)}, u32[]{:S(2)}, u32[]{:S(2)}) %collective-permute-start.1) | collective-permute-done | bytes 278560 | tf_op jit(solution)/shard_map/ppermute | solution.py:450
  18.6 0.0 collective-permute-done.first.first_band
  18.6 1.7 %frame.1 = (bf16[256,256]{1,0:T(8,128)(2,1)S(1)}, bf16[4,2,256,256]{3,2,1,0:T(8,128)(2,1)S(1)}) custom-call(bf16[4,272,128]{2,1,0:T(8,128)(2,1)S(1)} %collective-permute-done.first.first_band, bf16[4,272,128]{2,1,0:T(8,128)(2,1)S(1)} %collective-permute-done.1.second.second_band, bf16[16,256]{1,0:T(8,128)(2,1)S(1)} %get-tuple-element.14.info, ...), custom_call_target="tpu_custom_call" | custom-call | flops 2000000000 | bytes 4194304 | tf_op jit(solution)/shard_map/frame/pallas_call | solution.py:408
  20.4 0.2 collective-permute-start.2
  20.5 1.9 %collective-permute-start.3 = (bf16[256,256]{1,0:T(8,128)(2,1)S(1)}, bf16[256,256]{1,0:T(8,128)(2,1)S(1)}, u32[]{:S(2)}, u32[]{:S(2)}) collective-permute-start(bf16[256,256]{1,0:T(8,128)(2,1)S(1)} %get-tuple-element.20), channel_id=1, source_target_pairs={{4,8},{12,16},{20,24},{8,4},{16,12},{24,20},{5,9},{13,17},{21,25},... | collective-permute-start | bytes 393224 | tf_op jit(solution)/shard_map/ppermute | solution.py:492
  22.5 0.0 collective-permute-done.2.first
  22.5 0.7 %finish.1 = (f32[4,256,128]{2,1,0:T(8,128)S(1)}, s32[8,128]{1,0:T(8,128)S(1)}) custom-call(bf16[4,272,128]{2,1,0:T(8,128)(2,1)S(1)} %bitcast.4, bf16[4,272,128]{2,1,0:T(8,128)(2,1)S(1)} %collective-permute-done.first.first_band, bf16[4,272,128]{2,1,0:T(8,128)(2,1)S(1)} %collective-permute-done.1.second.second_band, ...), custom_call_target="tpu_custom_call" | custom-call | flops 500000000 | bytes 4194304 | tf_op jit(solution)/shard_map/finish/pallas_call | solution.py:408
  23.2 3.6 %collective-permute-done.3.second = bf16[256,256]{1,0:T(8,128)(2,1)S(1)} collective-permute-done((bf16[256,256]{1,0:T(8,128)(2,1)S(1)}, bf16[256,256]{1,0:T(8,128)(2,1)S(1)}, u32[]{:S(2)}, u32[]{:S(2)}) %collective-permute-start.3) | collective-permute-done | bytes 131104 | tf_op jit(solution)/shard_map/ppermute | solution.py:492
  26.8 0.1 fold.1
  26.9 8.9 %all_to_all.5.shares = bf16[4,256,128]{2,1,0:T(8,128)(2,1)S(1)} all-to-all(bf16[4,256,128]{2,1,0:T(8,128)(2,1)S(1)} %fold.1), channel_id=1, replica_groups=mesh['row'=8,'col'=4] {'col'}, dimensions={0} | all-to-all | bytes 524288 | tf_op jit(solution)/shard_map/all_to_all | solution.py:512
  35.9 0.7 %total.1 = f32[2,128,128]{2,1,0:T(8,128)} custom-call(bf16[4,256,128]{2,1,0:T(8,128)(2,1)S(1)} %all_to_all.5.shares), custom_call_target="tpu_custom_call" | custom-call | flops 1000000 | bytes 262144 | tf_op jit(solution)/shard_map/total/pallas_call | solution.py:408
Async XLA Ops:
  10.8 7.9 %collective-permute-start.1 = (bf16[4,272,128]{2,1,0:T(8,128)(2,1)S(1)}, bf16[4,272,128]{2,1,0:T(8,128)(2,1)S(1)}, u32[]{:S(2)}, u32[]{:S(2)}) collective-permute-start(bf16[4,272,128]{2,1,0:T(8,128)(2,1)S(1)} %bitcast.1), channel_id=1, source_target_pairs={{4,8},{12,16},{20,24},{8,4},{16,12},{24,20},{5,9},{13,17},{21,25},... | collective-permute-start | bytes 835592 | tf_op jit(solution)/shard_map/ppermute | solution.py:450
  12.7 5.9 %collective-permute-start = (bf16[4,272,128]{2,1,0:T(8,128)(2,1)S(1)}, bf16[4,272,128]{2,1,0:T(8,128)(2,1)S(1)}, u32[]{:S(2)}, u32[]{:S(2)}) collective-permute-start(bf16[4,272,128]{2,1,0:T(8,128)(2,1)S(1)} %bitcast.2), channel_id=1, source_target_pairs={{0,4},{8,12},{16,20},{24,28},{4,0},{12,8},{20,16},{28,24},{1,5},{9... | collective-permute-start | bytes 835592 | tf_op jit(solution)/shard_map/ppermute | solution.py:451
  20.4 2.1 %collective-permute-start.2 = (bf16[256,256]{1,0:T(8,128)(2,1)S(1)}, bf16[256,256]{1,0:T(8,128)(2,1)S(1)}, u32[]{:S(2)}, u32[]{:S(2)}) collective-permute-start(bf16[256,256]{1,0:T(8,128)(2,1)S(1)} %get-tuple-element.20), channel_id=1, source_target_pairs={{0,4},{8,12},{16,20},{24,28},{4,0},{12,8},{20,16},{28,24},{1,5},{9... | collective-permute-start | bytes 393224 | tf_op jit(solution)/shard_map/ppermute | solution.py:491
  20.5 6.3 %collective-permute-start.3 = (bf16[256,256]{1,0:T(8,128)(2,1)S(1)}, bf16[256,256]{1,0:T(8,128)(2,1)S(1)}, u32[]{:S(2)}, u32[]{:S(2)}) collective-permute-start(bf16[256,256]{1,0:T(8,128)(2,1)S(1)} %get-tuple-element.20), channel_id=1, source_target_pairs={{4,8},{12,16},{20,24},{8,4},{16,12},{24,20},{5,9},{13,17},{21,25},... | collective-permute-start | bytes 393224 | tf_op jit(solution)/shard_map/ppermute | solution.py:492

commit v21 on v15

--- a/solution.py
+++ b/solution.py
@@ -12,6 +12,7 @@
 F32 = jnp.float32
 BF16 = jnp.bfloat16
 INFO = 16
+COL = ("high", "low")
 STRIP = 16
 VMEM = pl.BlockSpec(memory_space=pltpu.VMEM)
 SMEM = pl.BlockSpec(memory_space=pltpu.SMEM)
@@ -104,7 +105,7 @@
 
 def frame_of(band):
     columns, height, lanes = band.shape
-    me = lax.axis_index("col").astype(F32)
+    me = lax.axis_index(COL).astype(F32)
     code = jnp.zeros((1, lanes), F32)
     for c in range(columns):
         info = band[c, height - INFO :].astype(F32)
@@ -405,7 +406,7 @@
     half = extent // 2
     tile = specimen.shape[1]
     modes = probe.shape[0]
-    columns = lax.axis_size("col")
+    columns = (lax.axis_size("high") * lax.axis_size("low"))
     height = 2 * tile
     part = jax.ShapeDtypeStruct((height, extent), BF16)
     dma = pltpu.SemaphoreType.DMA
@@ -423,7 +424,7 @@
         10**5, 2**19,
         specimen, centers, frame_counts, helper_cols,
     )
-    band = lax.all_gather(packed, "col")
+    band = lax.all_gather(packed, COL)
 
     rows = lax.axis_size("row")
     swaps = []
@@ -492,22 +493,27 @@
         10**7, 2**20,
         partial, from_second, second_info,
     )
-    shares = lax.all_to_all(summed, "col", split_axis=0, concat_axis=0, tiled=True)
+    shares = lax.all_to_all(summed, COL, split_axis=0, concat_axis=0, tiled=True)
     return jnp.sum(shares.astype(F32), axis=0).reshape(2, tile, tile)
 
 
 def solution(mesh):
+    rows, columns = mesh.devices.shape
+    low = math.gcd(columns, 2)
+    split = jax.sharding.Mesh(
+        mesh.devices.reshape(rows, columns // low, low), ("row",) + COL
+    )
     return jax.shard_map(
         per_device,
-        mesh=mesh,
+        mesh=split,
         in_specs=(
-            P(None, "row", "col"),
+            P(None, "row", COL),
             P(),
-            P("row", "col", None, None, None),
-            P("row", "col", None, None),
-            P("row", "col"),
-            P("row", "col", None),
+            P("row", COL, None, None, None),
+            P("row", COL, None, None),
+            P("row", COL),
+            P("row", COL, None),
         ),
-        out_specs=P(None, "row", "col"),
+        out_specs=P(None, "row", COL),
         check_vma=False,
     )

time: 36.8 us -> 36.8 us (level)
  no operation moved by 1% of the time
where the time goes in v21:
time: 36.8 us; the launch traced here: 36.6 us
  blocking collectives  18.1 us (49%)
  Pallas kernels  6.51 us (18%)
  starting transfers between devices  5.74 us (16%)
  waiting for transfers between devices  4.85 us (13%)
  between operations  0.71 us (2%)
  other arithmetic  0.69 us (2%)
    all_gather x1, blocking collectives, per_device(): band = lax.all_gather(packed, COL)  9.13 us
    all_to_all x1, blocking collectives, per_device(): lax.all_to_all(summed, COL, split_axis=0, concat_axis=0, tiled=True)  8.94 us
    pallas_call x5, Pallas kernels, call(): pl.pallas_call(kernel, out_shape=out_shape, in_specs=in_specs, out_specs=...  6.51 us
    ppermute x1, waiting for transfers between devices, per_device(): from_second = lax.ppermute(to_rows, 'row', swaps[1])  3.64 us
    ppermute x1, starting transfers between devices, per_device(): second = lax.ppermute(band, 'row', swaps[1])  1.91 us
    ppermute x1, starting transfers between devices, per_device(): from_second = lax.ppermute(to_rows, 'row', swaps[1])  1.91 us
    ppermute x1, starting transfers between devices, per_device(): first = lax.ppermute(band, 'row', swaps[0])  1.74 us
    ppermute x1, waiting for transfers between devices, per_device(): second = lax.ppermute(band, 'row', swaps[1])  1.21 us
  transfers between devices with their start and end apart: 4, of which 2 were waited for; matrix products, arithmetic and copies ran while one was open for 0% of the time, Pallas kernels for 10%

profile of v21, /device:TPU:8, one launch (start us, length us, event | category | flops | bytes accessed | tf_op | source)
XLA Modules:
  0.0 36.6 jit_solution(1396603259779469198)
XLA Ops:
  0.7 1.0 %pack.1 = bf16[272,128]{1,0:T(8,128)(2,1)S(1)} custom-call(f32[2,128,128]{2,1,0:T(8,128)} %specimen.1, s32[1,1,2,2]{3,2,1,0:T(2,128)} %centers.1, s32[1,1]{1,0:T(1,128)S(6)} %copy.8.cnt, s32[1,1,2]{2,1,0:T(1,128)} %helpers.1), custom_call_target="tpu_custom_call" | custom-call | flops 100000 | bytes 524288 | tf_op jit(solution)/shard_map/pack/pallas_call | solution.py:392
  1.6 9.1 %all-gather = bf16[1088,128]{1,0:T(8,128)(2,1)S(1)} all-gather(bf16[272,128]{1,0:T(8,128)(2,1)S(1)} %pack.1), channel_id=2, replica_groups=mesh['row'=8,'high'=2,'low'=2] {'high','low'}, dimensions={0}, use_global_device_ids=true | all-gather | bytes 348160 | tf_op jit(solution)/shard_map/all_gather | solution.py:427
  10.8 1.9 %collective-permute-start.1 = (bf16[4,272,128]{2,1,0:T(8,128)(2,1)S(1)}, bf16[4,272,128]{2,1,0:T(8,128)(2,1)S(1)}, u32[]{:S(2)}, u32[]{:S(2)}) collective-permute-start(bf16[4,272,128]{2,1,0:T(8,128)(2,1)S(1)} %bitcast.2), channel_id=1, source_target_pairs={{4,8},{12,16},{20,24},{8,4},{16,12},{24,20},{5,9},{13,17},{21,25},... | collective-permute-start | bytes 835592 | tf_op jit(solution)/shard_map/ppermute | solution.py:434
  12.7 1.7 %collective-permute-start = (bf16[4,272,128]{2,1,0:T(8,128)(2,1)S(1)}, bf16[4,272,128]{2,1,0:T(8,128)(2,1)S(1)}, u32[]{:S(2)}, u32[]{:S(2)}) collective-permute-start(bf16[4,272,128]{2,1,0:T(8,128)(2,1)S(1)} %bitcast.3), channel_id=1, source_target_pairs={{0,4},{8,12},{16,20},{24,28},{4,0},{12,8},{20,16},{28,24},{1,5},{9... | collective-permute-start | bytes 835592 | tf_op jit(solution)/shard_map/ppermute | solution.py:435
  14.4 3.0 %prepare.1 = (bf16[16,256]{1,0:T(8,128)(2,1)S(1)}, f32[256,256]{1,0:T(8,128)S(1)}, bf16[8,256,256]{2,1,0:T(8,128)(2,1)S(1)}, f32[4,2,256,256]{3,2,1,0:T(8,128)S(1)}, f32[4,2,128,256]{3,2,1,0:T(8,128)S(1)}) custom-call(bf16[4,272,128]{2,1,0:T(8,128)(2,1)S(1)} %bitcast.4, f32[4,2,256,256]{3,2,1,0:T(8,128)} %probe.1, f32[1,1,1,256,256]{4,3,2,1,0:T(8,128)} %measured.1, ...), custom_call_target="tpu_custom_call" | custom-call | flops 1000000000 | bytes 4194304 | tf_op jit(solution)/shard_map/prepare/pallas_call | solution.py:392
  17.4 1.2 %collective-permute-done.1.second.second_band = bf16[4,272,128]{2,1,0:T(8,128)(2,1)S(1)} collective-permute-done((bf16[4,272,128]{2,1,0:T(8,128)(2,1)S(1)}, bf16[4,272,128]{2,1,0:T(8,128)(2,1)S(1)}, u32[]{:S(2)}, u32[]{:S(2)}) %collective-permute-start.1) | collective-permute-done | bytes 278560 | tf_op jit(solution)/shard_map/ppermute | solution.py:434
  18.6 0.0 collective-permute-done.first.first_band
  18.6 1.7 %frame.1 = (bf16[256,256]{1,0:T(8,128)(2,1)S(1)}, bf16[4,2,256,256]{3,2,1,0:T(8,128)(2,1)S(1)}) custom-call(bf16[4,272,128]{2,1,0:T(8,128)(2,1)S(1)} %collective-permute-done.first.first_band, bf16[4,272,128]{2,1,0:T(8,128)(2,1)S(1)} %collective-permute-done.1.second.second_band, bf16[16,256]{1,0:T(8,128)(2,1)S(1)} %get-tuple-element.14.info, ...), custom_call_target="tpu_custom_call" | custom-call | flops 2000000000 | bytes 4194304 | tf_op jit(solution)/shard_map/frame/pallas_call | solution.py:392
  20.4 0.2 collective-permute-start.2
  20.5 1.9 %collective-permute-start.3 = (bf16[256,256]{1,0:T(8,128)(2,1)S(1)}, bf16[256,256]{1,0:T(8,128)(2,1)S(1)}, u32[]{:S(2)}, u32[]{:S(2)}) collective-permute-start(bf16[256,256]{1,0:T(8,128)(2,1)S(1)} %get-tuple-element.20), channel_id=1, source_target_pairs={{4,8},{12,16},{20,24},{8,4},{16,12},{24,20},{5,9},{13,17},{21,25},... | collective-permute-start | bytes 393224 | tf_op jit(solution)/shard_map/ppermute | solution.py:476
  22.5 0.0 collective-permute-done.2.first
  22.5 0.7 %finish.1 = (f32[4,256,128]{2,1,0:T(8,128)S(1)}, s32[8,128]{1,0:T(8,128)S(1)}) custom-call(bf16[4,272,128]{2,1,0:T(8,128)(2,1)S(1)} %bitcast.5, bf16[4,272,128]{2,1,0:T(8,128)(2,1)S(1)} %collective-permute-done.first.first_band, bf16[4,272,128]{2,1,0:T(8,128)(2,1)S(1)} %collective-permute-done.1.second.second_band, ...), custom_call_target="tpu_custom_call" | custom-call | flops 500000000 | bytes 4194304 | tf_op jit(solution)/shard_map/finish/pallas_call | solution.py:392
  23.2 3.6 %collective-permute-done.3.second = bf16[256,256]{1,0:T(8,128)(2,1)S(1)} collective-permute-done((bf16[256,256]{1,0:T(8,128)(2,1)S(1)}, bf16[256,256]{1,0:T(8,128)(2,1)S(1)}, u32[]{:S(2)}, u32[]{:S(2)}) %collective-permute-start.3) | collective-permute-done | bytes 131104 | tf_op jit(solution)/shard_map/ppermute | solution.py:476
  26.8 0.1 fold.1
  26.9 8.9 %all_to_all.5 = bf16[4,256,128]{2,1,0:T(8,128)(2,1)S(1)} all-to-all(bf16[4,256,128]{2,1,0:T(8,128)(2,1)S(1)} %fold.1), channel_id=1, replica_groups=mesh['row'=8,'high'=2,'low'=2] {'high','low'}, dimensions={0} | all-to-all | bytes 524288 | tf_op jit(solution)/shard_map/all_to_all | solution.py:496
  35.9 0.7 %convert_reduce_fusion = f32[256,128]{1,0:T(8,128)} fusion(bf16[4,256,128]{2,1,0:T(8,128)(2,1)S(1)} %all_to_all.5), kind=kLoop, calls=%fused_computation | loop fusion | flops 229376 | bytes 393216 | tf_op jit(solution)/shard_map/reduce_sum | solution.py:497
Async XLA Ops:
  10.8 7.9 %collective-permute-start.1 = (bf16[4,272,128]{2,1,0:T(8,128)(2,1)S(1)}, bf16[4,272,128]{2,1,0:T(8,128)(2,1)S(1)}, u32[]{:S(2)}, u32[]{:S(2)}) collective-permute-start(bf16[4,272,128]{2,1,0:T(8,128)(2,1)S(1)} %bitcast.2), channel_id=1, source_target_pairs={{4,8},{12,16},{20,24},{8,4},{16,12},{24,20},{5,9},{13,17},{21,25},... | collective-permute-start | bytes 835592 | tf_op jit(solution)/shard_map/ppermute | solution.py:434
  12.7 5.9 %collective-permute-start = (bf16[4,272,128]{2,1,0:T(8,128)(2,1)S(1)}, bf16[4,272,128]{2,1,0:T(8,128)(2,1)S(1)}, u32[]{:S(2)}, u32[]{:S(2)}) collective-permute-start(bf16[4,272,128]{2,1,0:T(8,128)(2,1)S(1)} %bitcast.3), channel_id=1, source_target_pairs={{0,4},{8,12},{16,20},{24,28},{4,0},{12,8},{20,16},{28,24},{1,5},{9... | collective-permute-start | bytes 835592 | tf_op jit(solution)/shard_map/ppermute | solution.py:435
  20.4 2.1 %collective-permute-start.2 = (bf16[256,256]{1,0:T(8,128)(2,1)S(1)}, bf16[256,256]{1,0:T(8,128)(2,1)S(1)}, u32[]{:S(2)}, u32[]{:S(2)}) collective-permute-start(bf16[256,256]{1,0:T(8,128)(2,1)S(1)} %get-tuple-element.20), channel_id=1, source_target_pairs={{0,4},{8,12},{16,20},{24,28},{4,0},{12,8},{20,16},{28,24},{1,5},{9... | collective-permute-start | bytes 393224 | tf_op jit(solution)/shard_map/ppermute | solution.py:475
  20.5 6.3 %collective-permute-start.3 = (bf16[256,256]{1,0:T(8,128)(2,1)S(1)}, bf16[256,256]{1,0:T(8,128)(2,1)S(1)}, u32[]{:S(2)}, u32[]{:S(2)}) collective-permute-start(bf16[256,256]{1,0:T(8,128)(2,1)S(1)} %get-tuple-element.20), channel_id=1, source_target_pairs={{4,8},{12,16},{20,24},{8,4},{16,12},{24,20},{5,9},{13,17},{21,25},... | collective-permute-start | bytes 393224 | tf_op jit(solution)/shard_map/ppermute | solution.py:476

commit v22 on v16

--- a/solution.py
+++ b/solution.py
@@ -103,9 +103,7 @@
 
 
 def ring(columns):
-    if columns & (columns - 1):
-        return list(range(columns))
-    return [i ^ (i >> 1) for i in range(columns)]
+    return list(range(0, columns, 2)) + list(range(1, columns, 2))
 
 
 def frame_of(band):

time: 38.7 us -> 36.8 us (0.951)
  blocking collectives: 20 us -> 18.1 us
    all_gather x1, blocking collectives: 11.1 us -> 9.13 us  [per_device(): band = lax.all_gather(packed, 'col', axis_index_groups=[ring(columns)])]
where the time goes in v22:
time: 36.8 us; the launch traced here: 36.6 us
  blocking collectives  18.1 us (49%)
  Pallas kernels  6.51 us (18%)
  starting transfers between devices  5.74 us (16%)
  waiting for transfers between devices  4.84 us (13%)
  between operations  0.71 us (2%)
  other arithmetic  0.69 us (2%)
    all_gather x1, blocking collectives, per_device(): band = lax.all_gather(packed, 'col', axis_index_groups=[ring(columns)])  9.13 us
    all_to_all x1, blocking collectives, per_device(): lax.all_to_all(summed, 'col', split_axis=0, concat_axis=0, tiled=True)  8.94 us
    pallas_call x5, Pallas kernels, call(): pl.pallas_call(kernel, out_shape=out_shape, in_specs=in_specs, out_specs=...  6.51 us
    ppermute x1, waiting for transfers between devices, per_device(): from_second = lax.ppermute(to_rows, 'row', swaps[1])  3.64 us
    ppermute x1, starting transfers between devices, per_device(): second = lax.ppermute(band, 'row', swaps[1])  1.91 us
    ppermute x1, starting transfers between devices, per_device(): from_second = lax.ppermute(to_rows, 'row', swaps[1])  1.91 us
    ppermute x1, starting transfers between devices, per_device(): first = lax.ppermute(band, 'row', swaps[0])  1.74 us
    ppermute x1, waiting for transfers between devices, per_device(): second = lax.ppermute(band, 'row', swaps[1])  1.2 us
  transfers between devices with their start and end apart: 4, of which 2 were waited for; matrix products, arithmetic and copies ran while one was open for 0% of the time, Pallas kernels for 10%

profile of v22, /device:TPU:8, one launch (start us, length us, event | category | flops | bytes accessed | tf_op | source)
XLA Modules:
  0.0 36.6 jit_solution(11103132305488821519)
XLA Ops:
  0.7 1.0 %pack.1 = bf16[272,128]{1,0:T(8,128)(2,1)S(1)} custom-call(f32[2,128,128]{2,1,0:T(8,128)} %specimen.1, s32[1,1,2,2]{3,2,1,0:T(2,128)} %centers.1, s32[1,1]{1,0:T(1,128)S(6)} %copy.8.cnt, s32[1,1,2]{2,1,0:T(1,128)} %helpers.1), custom_call_target="tpu_custom_call" | custom-call | flops 100000 | bytes 524288 | tf_op jit(solution)/shard_map/pack/pallas_call | solution.py:399
  1.6 9.1 %all-gather = bf16[1088,128]{1,0:T(8,128)(2,1)S(1)} all-gather(bf16[272,128]{1,0:T(8,128)(2,1)S(1)} %pack.1), channel_id=2, replica_groups={{0,2,1,3},{4,6,5,7},{8,10,9,11},{12,14,13,15},{16,18,17,19},{20,22,21,2..., dimensions={0}, use_global_device_ids=true | all-gather | bytes 348160 | tf_op jit(solution)/shard_map/all_gather | solution.py:434
  10.8 1.9 %collective-permute-start.1 = (bf16[4,272,128]{2,1,0:T(8,128)(2,1)S(1)}, bf16[4,272,128]{2,1,0:T(8,128)(2,1)S(1)}, u32[]{:S(2)}, u32[]{:S(2)}) collective-permute-start(bf16[4,272,128]{2,1,0:T(8,128)(2,1)S(1)} %bitcast.2), channel_id=1, source_target_pairs={{4,8},{12,16},{20,24},{8,4},{16,12},{24,20},{5,9},{13,17},{21,25},... | collective-permute-start | bytes 835592 | tf_op jit(solution)/shard_map/ppermute | solution.py:441
  12.7 1.7 %collective-permute-start = (bf16[4,272,128]{2,1,0:T(8,128)(2,1)S(1)}, bf16[4,272,128]{2,1,0:T(8,128)(2,1)S(1)}, u32[]{:S(2)}, u32[]{:S(2)}) collective-permute-start(bf16[4,272,128]{2,1,0:T(8,128)(2,1)S(1)} %bitcast.3), channel_id=1, source_target_pairs={{0,4},{8,12},{16,20},{24,28},{4,0},{12,8},{20,16},{28,24},{1,5},{9... | collective-permute-start | bytes 835592 | tf_op jit(solution)/shard_map/ppermute | solution.py:442
  14.4 3.0 %prepare.1 = (bf16[16,256]{1,0:T(8,128)(2,1)S(1)}, f32[256,256]{1,0:T(8,128)S(1)}, bf16[8,256,256]{2,1,0:T(8,128)(2,1)S(1)}, f32[4,2,256,256]{3,2,1,0:T(8,128)S(1)}, f32[4,2,128,256]{3,2,1,0:T(8,128)S(1)}) custom-call(bf16[4,272,128]{2,1,0:T(8,128)(2,1)S(1)} %bitcast.4, f32[4,2,256,256]{3,2,1,0:T(8,128)} %probe.1, f32[1,1,1,256,256]{4,3,2,1,0:T(8,128)} %measured.1, ...), custom_call_target="tpu_custom_call" | custom-call | flops 1000000000 | bytes 4194304 | tf_op jit(solution)/shard_map/prepare/pallas_call | solution.py:399
  17.4 1.2 %collective-permute-done.1.second.second_band = bf16[4,272,128]{2,1,0:T(8,128)(2,1)S(1)} collective-permute-done((bf16[4,272,128]{2,1,0:T(8,128)(2,1)S(1)}, bf16[4,272,128]{2,1,0:T(8,128)(2,1)S(1)}, u32[]{:S(2)}, u32[]{:S(2)}) %collective-permute-start.1) | collective-permute-done | bytes 278560 | tf_op jit(solution)/shard_map/ppermute | solution.py:441
  18.6 0.0 collective-permute-done.first.first_band
  18.6 1.7 %frame.1 = (bf16[256,256]{1,0:T(8,128)(2,1)S(1)}, bf16[4,2,256,256]{3,2,1,0:T(8,128)(2,1)S(1)}) custom-call(bf16[4,272,128]{2,1,0:T(8,128)(2,1)S(1)} %collective-permute-done.first.first_band, bf16[4,272,128]{2,1,0:T(8,128)(2,1)S(1)} %collective-permute-done.1.second.second_band, bf16[16,256]{1,0:T(8,128)(2,1)S(1)} %get-tuple-element.14.info, ...), custom_call_target="tpu_custom_call" | custom-call | flops 2000000000 | bytes 4194304 | tf_op jit(solution)/shard_map/frame/pallas_call | solution.py:399
  20.4 0.2 collective-permute-start.2
  20.5 1.9 %collective-permute-start.3 = (bf16[256,256]{1,0:T(8,128)(2,1)S(1)}, bf16[256,256]{1,0:T(8,128)(2,1)S(1)}, u32[]{:S(2)}, u32[]{:S(2)}) collective-permute-start(bf16[256,256]{1,0:T(8,128)(2,1)S(1)} %get-tuple-element.20), channel_id=1, source_target_pairs={{4,8},{12,16},{20,24},{8,4},{16,12},{24,20},{5,9},{13,17},{21,25},... | collective-permute-start | bytes 393224 | tf_op jit(solution)/shard_map/ppermute | solution.py:483
  22.5 0.0 collective-permute-done.2.first
  22.5 0.7 %finish.1 = (f32[4,256,128]{2,1,0:T(8,128)S(1)}, s32[8,128]{1,0:T(8,128)S(1)}) custom-call(bf16[4,272,128]{2,1,0:T(8,128)(2,1)S(1)} %bitcast.5, bf16[4,272,128]{2,1,0:T(8,128)(2,1)S(1)} %collective-permute-done.first.first_band, bf16[4,272,128]{2,1,0:T(8,128)(2,1)S(1)} %collective-permute-done.1.second.second_band, ...), custom_call_target="tpu_custom_call" | custom-call | flops 500000000 | bytes 4194304 | tf_op jit(solution)/shard_map/finish/pallas_call | solution.py:399
  23.2 3.6 %collective-permute-done.3.second = bf16[256,256]{1,0:T(8,128)(2,1)S(1)} collective-permute-done((bf16[256,256]{1,0:T(8,128)(2,1)S(1)}, bf16[256,256]{1,0:T(8,128)(2,1)S(1)}, u32[]{:S(2)}, u32[]{:S(2)}) %collective-permute-start.3) | collective-permute-done | bytes 131104 | tf_op jit(solution)/shard_map/ppermute | solution.py:483
  26.8 0.1 fold.1
  26.9 8.9 %all_to_all.5 = bf16[4,256,128]{2,1,0:T(8,128)(2,1)S(1)} all-to-all(bf16[4,256,128]{2,1,0:T(8,128)(2,1)S(1)} %fold.1), channel_id=1, replica_groups=mesh['row'=8,'col'=4] {'col'}, dimensions={0} | all-to-all | bytes 524288 | tf_op jit(solution)/shard_map/all_to_all | solution.py:503
  35.9 0.7 %convert_reduce_fusion = f32[256,128]{1,0:T(8,128)} fusion(bf16[4,256,128]{2,1,0:T(8,128)(2,1)S(1)} %all_to_all.5), kind=kLoop, calls=%fused_computation | loop fusion | flops 229376 | bytes 393216 | tf_op jit(solution)/shard_map/reduce_sum | solution.py:504
Async XLA Ops:
  10.8 7.9 %collective-permute-start.1 = (bf16[4,272,128]{2,1,0:T(8,128)(2,1)S(1)}, bf16[4,272,128]{2,1,0:T(8,128)(2,1)S(1)}, u32[]{:S(2)}, u32[]{:S(2)}) collective-permute-start(bf16[4,272,128]{2,1,0:T(8,128)(2,1)S(1)} %bitcast.2), channel_id=1, source_target_pairs={{4,8},{12,16},{20,24},{8,4},{16,12},{24,20},{5,9},{13,17},{21,25},... | collective-permute-start | bytes 835592 | tf_op jit(solution)/shard_map/ppermute | solution.py:441
  12.7 5.9 %collective-permute-start = (bf16[4,272,128]{2,1,0:T(8,128)(2,1)S(1)}, bf16[4,272,128]{2,1,0:T(8,128)(2,1)S(1)}, u32[]{:S(2)}, u32[]{:S(2)}) collective-permute-start(bf16[4,272,128]{2,1,0:T(8,128)(2,1)S(1)} %bitcast.3), channel_id=1, source_target_pairs={{0,4},{8,12},{16,20},{24,28},{4,0},{12,8},{20,16},{28,24},{1,5},{9... | collective-permute-start | bytes 835592 | tf_op jit(solution)/shard_map/ppermute | solution.py:442
  20.4 2.1 %collective-permute-start.2 = (bf16[256,256]{1,0:T(8,128)(2,1)S(1)}, bf16[256,256]{1,0:T(8,128)(2,1)S(1)}, u32[]{:S(2)}, u32[]{:S(2)}) collective-permute-start(bf16[256,256]{1,0:T(8,128)(2,1)S(1)} %get-tuple-element.20), channel_id=1, source_target_pairs={{0,4},{8,12},{16,20},{24,28},{4,0},{12,8},{20,16},{28,24},{1,5},{9... | collective-permute-start | bytes 393224 | tf_op jit(solution)/shard_map/ppermute | solution.py:482
  20.5 6.3 %collective-permute-start.3 = (bf16[256,256]{1,0:T(8,128)(2,1)S(1)}, bf16[256,256]{1,0:T(8,128)(2,1)S(1)}, u32[]{:S(2)}, u32[]{:S(2)}) collective-permute-start(bf16[256,256]{1,0:T(8,128)(2,1)S(1)} %get-tuple-element.20), channel_id=1, source_target_pairs={{4,8},{12,16},{20,24},{8,4},{16,12},{24,20},{5,9},{13,17},{21,25},... | collective-permute-start | bytes 393224 | tf_op jit(solution)/shard_map/ppermute | solution.py:483

commit v23 on v15

--- a/solution.py
+++ b/solution.py
@@ -200,7 +200,7 @@
 
 def frame_kernel(
     first, second, info, amplitude, tables, probe, half_own,
-    to_rows, mixed_back, patch, folded, half_far, mixed, far, corrected, product, chi,
+    to_second, to_first, mixed_back, patch, folded, half_far, mixed, far, corrected, product, chi,
 ):
     columns = first.shape[0]
     tile = (first.shape[1] - INFO) // 2
@@ -312,19 +312,20 @@
         mix_back(k, 1)
         back_along_columns(k)
     for s, t in zip(strips, lower):
-        accumulate(to_rows, chi, probe, s, t, s)
-
-
-def accumulate(out, chi, probe, s, t, rows):
-    tile = out.shape[0] // 2
+        accumulate((to_second, to_first), chi, probe, s, t, s)
+
+
+def accumulate(outs, chi, probe, s, t, rows):
+    tile = outs[0].shape[0] // 2
     re = im = 0.0
     for k in range(probe.shape[0]):
         pr, pi = probe[k, 0, rows], probe[k, 1, rows]
         cr, ci = chi[k, s], chi[k, t]
         re += pr * cr + pi * ci
         im += pr * ci - pi * cr
-    out[s] = re.astype(BF16)
-    out[pl.ds(tile + s.start, STRIP)] = im.astype(BF16)
+    for out in outs:
+        out[s] = re.astype(BF16)
+        out[pl.ds(tile + s.start, STRIP)] = im.astype(BF16)
 
 
 def place(block, columns, source, col, taken):
@@ -360,7 +361,7 @@
         chi[k] = dot(both_back, mixed_back[k].reshape(2 * extent, extent))
     for r in range(0, tile, STRIP):
         s, t = pl.ds(r, STRIP), pl.ds(tile + r, STRIP)
-        accumulate(centre, chi, probe, s, t, t)
+        accumulate((centre,), chi, probe, s, t, t)
         before = (iota((STRIP, tile), 0) + r < first_frame[1]).astype(jnp.int32)
         for part in (s, t):
             mine = place(centre[part].astype(F32), columns, own_frame[0], own_frame[2], None)
@@ -454,9 +455,9 @@
         band, probe, measured, tables,
     )
     full = (modes, 2, extent, extent)
-    to_rows, mixed_back = call(
+    to_second, to_first, mixed_back = call(
         frame_kernel, "frame",
-        (part, jax.ShapeDtypeStruct(full, BF16)),
+        (part, part, jax.ShapeDtypeStruct(full, BF16)),
         [VMEM] * 7,
         [
             pltpu.VMEM((2, tile, extent), F32),
@@ -471,8 +472,8 @@
         2 * 10**9, 2**22,
         first, second, *prepared,
     )
-    from_first = lax.ppermute(to_rows, "row", swaps[0])
-    from_second = lax.ppermute(to_rows, "row", swaps[1])
+    from_second = lax.ppermute(to_second, "row", swaps[1])
+    from_first = lax.ppermute(to_first, "row", swaps[0])
     partial, second_info = call(
         finish_kernel, "finish",
         (

time: 36.8 us -> 36.8 us (level)
  no operation moved by 1% of the time
where the time goes in v23:
time: 36.8 us; the launch traced here: 36.6 us
  blocking collectives  18.1 us (49%)
  Pallas kernels  6.52 us (18%)
  starting transfers between devices  5.74 us (16%)
  waiting for transfers between devices  4.84 us (13%)
  between operations  0.71 us (2%)
  other arithmetic  0.69 us (2%)
    all_gather x1, blocking collectives, per_device(): band = lax.all_gather(packed, 'col')  9.13 us
    all_to_all x1, blocking collectives, per_device(): lax.all_to_all(summed, 'col', split_axis=0, concat_axis=0, tiled=True)  8.94 us
    pallas_call x5, Pallas kernels, call(): pl.pallas_call(kernel, out_shape=out_shape, in_specs=in_specs, out_specs=...  6.52 us
    ppermute x1, waiting for transfers between devices, per_device(): from_second = lax.ppermute(to_second, 'row', swaps[1])  3.64 us
    ppermute x1, starting transfers between devices, per_device(): second = lax.ppermute(band, 'row', swaps[1])  1.91 us
    ppermute x1, starting transfers between devices, per_device(): from_second = lax.ppermute(to_second, 'row', swaps[1])  1.91 us
    ppermute x1, starting transfers between devices, per_device(): first = lax.ppermute(band, 'row', swaps[0])  1.74 us
    ppermute x1, waiting for transfers between devices, per_device(): second = lax.ppermute(band, 'row', swaps[1])  1.2 us
  transfers between devices with their start and end apart: 4, of which 2 were waited for; matrix products, arithmetic and copies ran while one was open for 0% of the time, Pallas kernels for 10%

profile of v23, /device:TPU:8, one launch (start us, length us, event | category | flops | bytes accessed | tf_op | source)
XLA Modules:
  0.0 36.6 jit_solution(9085718022258387636)
XLA Ops:
  0.7 1.0 %pack.1 = bf16[272,128]{1,0:T(8,128)(2,1)S(1)} custom-call(f32[2,128,128]{2,1,0:T(8,128)} %specimen.1, s32[1,1,2,2]{3,2,1,0:T(2,128)} %centers.1, s32[1,1]{1,0:T(1,128)S(6)} %copy.8.cnt, s32[1,1,2]{2,1,0:T(1,128)} %helpers.1), custom_call_target="tpu_custom_call" | custom-call | flops 100000 | bytes 524288 | tf_op jit(solution)/shard_map/pack/pallas_call | solution.py:392
  1.6 9.1 %all-gather = bf16[1088,128]{1,0:T(8,128)(2,1)S(1)} all-gather(bf16[272,128]{1,0:T(8,128)(2,1)S(1)} %pack.1), channel_id=2, replica_groups=mesh['row'=8,'col'=4] {'col'}, dimensions={0}, use_global_device_ids=true | all-gather | bytes 348160 | tf_op jit(solution)/shard_map/all_gather | solution.py:427
  10.8 1.9 %collective-permute-start.1 = (bf16[4,272,128]{2,1,0:T(8,128)(2,1)S(1)}, bf16[4,272,128]{2,1,0:T(8,128)(2,1)S(1)}, u32[]{:S(2)}, u32[]{:S(2)}) collective-permute-start(bf16[4,272,128]{2,1,0:T(8,128)(2,1)S(1)} %bitcast.2), channel_id=1, source_target_pairs={{4,8},{12,16},{20,24},{8,4},{16,12},{24,20},{5,9},{13,17},{21,25},... | collective-permute-start | bytes 835592 | tf_op jit(solution)/shard_map/ppermute | solution.py:434
  12.7 1.7 %collective-permute-start = (bf16[4,272,128]{2,1,0:T(8,128)(2,1)S(1)}, bf16[4,272,128]{2,1,0:T(8,128)(2,1)S(1)}, u32[]{:S(2)}, u32[]{:S(2)}) collective-permute-start(bf16[4,272,128]{2,1,0:T(8,128)(2,1)S(1)} %bitcast.3), channel_id=1, source_target_pairs={{0,4},{8,12},{16,20},{24,28},{4,0},{12,8},{20,16},{28,24},{1,5},{9... | collective-permute-start | bytes 835592 | tf_op jit(solution)/shard_map/ppermute | solution.py:435
  14.4 3.0 %prepare.1 = (bf16[16,256]{1,0:T(8,128)(2,1)S(1)}, f32[256,256]{1,0:T(8,128)S(1)}, bf16[8,256,256]{2,1,0:T(8,128)(2,1)S(1)}, f32[4,2,256,256]{3,2,1,0:T(8,128)S(1)}, f32[4,2,128,256]{3,2,1,0:T(8,128)S(1)}) custom-call(bf16[4,272,128]{2,1,0:T(8,128)(2,1)S(1)} %bitcast.4, f32[4,2,256,256]{3,2,1,0:T(8,128)} %probe.1, f32[1,1,1,256,256]{4,3,2,1,0:T(8,128)} %measured.1, ...), custom_call_target="tpu_custom_call" | custom-call | flops 1000000000 | bytes 4194304 | tf_op jit(solution)/shard_map/prepare/pallas_call | solution.py:392
  17.4 1.2 %collective-permute-done.1.second.second_band = bf16[4,272,128]{2,1,0:T(8,128)(2,1)S(1)} collective-permute-done((bf16[4,272,128]{2,1,0:T(8,128)(2,1)S(1)}, bf16[4,272,128]{2,1,0:T(8,128)(2,1)S(1)}, u32[]{:S(2)}, u32[]{:S(2)}) %collective-permute-start.1) | collective-permute-done | bytes 278560 | tf_op jit(solution)/shard_map/ppermute | solution.py:434
  18.6 0.0 collective-permute-done.first.first_band
  18.6 1.8 %frame.1 = (bf16[256,256]{1,0:T(8,128)(2,1)S(1)}, bf16[256,256]{1,0:T(8,128)(2,1)S(1)}, bf16[4,2,256,256]{3,2,1,0:T(8,128)(2,1)S(1)}) custom-call(bf16[4,272,128]{2,1,0:T(8,128)(2,1)S(1)} %collective-permute-done.first.first_band, bf16[4,272,128]{2,1,0:T(8,128)(2,1)S(1)} %collective-permute-done.1.second.second_band, ...), custom_call_target="tpu_custom_call" | custom-call | flops 2000000000 | bytes 4194304 | tf_op jit(solution)/shard_map/frame/pallas_call | solution.py:392
  20.4 0.2 collective-permute-start.2
  20.6 1.9 %collective-permute-start.3 = (bf16[256,256]{1,0:T(8,128)(2,1)S(1)}, bf16[256,256]{1,0:T(8,128)(2,1)S(1)}, u32[]{:S(2)}, u32[]{:S(2)}) collective-permute-start(bf16[256,256]{1,0:T(8,128)(2,1)S(1)} %get-tuple-element.23), channel_id=1, source_target_pairs={{4,8},{12,16},{20,24},{8,4},{16,12},{24,20},{5,9},{13,17},{21,25},... | collective-permute-start | bytes 393224 | tf_op jit(solution)/shard_map/ppermute | solution.py:475
  22.5 0.0 collective-permute-done.2.first
  22.5 0.7 %finish.1 = (f32[4,256,128]{2,1,0:T(8,128)S(1)}, s32[8,128]{1,0:T(8,128)S(1)}) custom-call(bf16[4,272,128]{2,1,0:T(8,128)(2,1)S(1)} %bitcast.5, bf16[4,272,128]{2,1,0:T(8,128)(2,1)S(1)} %collective-permute-done.first.first_band, bf16[4,272,128]{2,1,0:T(8,128)(2,1)S(1)} %collective-permute-done.1.second.second_band, ...), custom_call_target="tpu_custom_call" | custom-call | flops 500000000 | bytes 4194304 | tf_op jit(solution)/shard_map/finish/pallas_call | solution.py:392
  23.2 3.6 %collective-permute-done.3.second = bf16[256,256]{1,0:T(8,128)(2,1)S(1)} collective-permute-done((bf16[256,256]{1,0:T(8,128)(2,1)S(1)}, bf16[256,256]{1,0:T(8,128)(2,1)S(1)}, u32[]{:S(2)}, u32[]{:S(2)}) %collective-permute-start.3) | collective-permute-done | bytes 131104 | tf_op jit(solution)/shard_map/ppermute | solution.py:475
  26.8 0.1 fold.1
  26.9 8.9 %all_to_all.5 = bf16[4,256,128]{2,1,0:T(8,128)(2,1)S(1)} all-to-all(bf16[4,256,128]{2,1,0:T(8,128)(2,1)S(1)} %fold.1), channel_id=1, replica_groups=mesh['row'=8,'col'=4] {'col'}, dimensions={0} | all-to-all | bytes 524288 | tf_op jit(solution)/shard_map/all_to_all | solution.py:496
  35.9 0.7 %convert_reduce_fusion = f32[256,128]{1,0:T(8,128)} fusion(bf16[4,256,128]{2,1,0:T(8,128)(2,1)S(1)} %all_to_all.5), kind=kLoop, calls=%fused_computation | loop fusion | flops 229376 | bytes 393216 | tf_op jit(solution)/shard_map/reduce_sum | solution.py:497
Async XLA Ops:
  10.8 7.9 %collective-permute-start.1 = (bf16[4,272,128]{2,1,0:T(8,128)(2,1)S(1)}, bf16[4,272,128]{2,1,0:T(8,128)(2,1)S(1)}, u32[]{:S(2)}, u32[]{:S(2)}) collective-permute-start(bf16[4,272,128]{2,1,0:T(8,128)(2,1)S(1)} %bitcast.2), channel_id=1, source_target_pairs={{4,8},{12,16},{20,24},{8,4},{16,12},{24,20},{5,9},{13,17},{21,25},... | collective-permute-start | bytes 835592 | tf_op jit(solution)/shard_map/ppermute | solution.py:434
  12.7 5.9 %collective-permute-start = (bf16[4,272,128]{2,1,0:T(8,128)(2,1)S(1)}, bf16[4,272,128]{2,1,0:T(8,128)(2,1)S(1)}, u32[]{:S(2)}, u32[]{:S(2)}) collective-permute-start(bf16[4,272,128]{2,1,0:T(8,128)(2,1)S(1)} %bitcast.3), channel_id=1, source_target_pairs={{0,4},{8,12},{16,20},{24,28},{4,0},{12,8},{20,16},{28,24},{1,5},{9... | collective-permute-start | bytes 835592 | tf_op jit(solution)/shard_map/ppermute | solution.py:435
  20.4 2.1 %collective-permute-start.2 = (bf16[256,256]{1,0:T(8,128)(2,1)S(1)}, bf16[256,256]{1,0:T(8,128)(2,1)S(1)}, u32[]{:S(2)}, u32[]{:S(2)}) collective-permute-start(bf16[256,256]{1,0:T(8,128)(2,1)S(1)} %get-tuple-element.21), channel_id=1, source_target_pairs={{0,4},{8,12},{16,20},{24,28},{4,0},{12,8},{20,16},{28,24},{1,5},{9... | collective-permute-start | bytes 393224 | tf_op jit(solution)/shard_map/ppermute | solution.py:476
  20.6 6.3 %collective-permute-start.3 = (bf16[256,256]{1,0:T(8,128)(2,1)S(1)}, bf16[256,256]{1,0:T(8,128)(2,1)S(1)}, u32[]{:S(2)}, u32[]{:S(2)}) collective-permute-start(bf16[256,256]{1,0:T(8,128)(2,1)S(1)} %get-tuple-element.23), channel_id=1, source_target_pairs={{4,8},{12,16},{20,24},{8,4},{16,12},{24,20},{5,9},{13,17},{21,25},... | collective-permute-start | bytes 393224 | tf_op jit(solution)/shard_map/ppermute | solution.py:475

commit v24 on v15

--- a/solution.py
+++ b/solution.py
@@ -12,7 +12,7 @@
 F32 = jnp.float32
 BF16 = jnp.bfloat16
 INFO = 16
-STRIP = 16
+STRIP = 32
 VMEM = pl.BlockSpec(memory_space=pltpu.VMEM)
 SMEM = pl.BlockSpec(memory_space=pltpu.SMEM)
 HBM = pl.BlockSpec(memory_space=pltpu.HBM)

time: 36.8 us -> 36.8 us (level)
  no operation moved by 1% of the time
where the time goes in v24:
time: 36.8 us; the launch traced here: 36.6 us
  blocking collectives  18.1 us (49%)
  Pallas kernels  6.51 us (18%)
  starting transfers between devices  5.74 us (16%)
  waiting for transfers between devices  4.84 us (13%)
  between operations  0.71 us (2%)
  other arithmetic  0.69 us (2%)
    all_gather x1, blocking collectives, per_device(): band = lax.all_gather(packed, 'col')  9.13 us
    all_to_all x1, blocking collectives, per_device(): lax.all_to_all(summed, 'col', split_axis=0, concat_axis=0, tiled=True)  8.94 us
    pallas_call x5, Pallas kernels, call(): pl.pallas_call(kernel, out_shape=out_shape, in_specs=in_specs, out_specs=...  6.51 us
    ppermute x1, waiting for transfers between devices, per_device(): from_second = lax.ppermute(to_rows, 'row', swaps[1])  3.64 us
    ppermute x1, starting transfers between devices, per_device(): second = lax.ppermute(band, 'row', swaps[1])  1.91 us
    ppermute x1, starting transfers between devices, per_device(): from_second = lax.ppermute(to_rows, 'row', swaps[1])  1.91 us
    ppermute x1, starting transfers between devices, per_device(): first = lax.ppermute(band, 'row', swaps[0])  1.74 us
    ppermute x1, waiting for transfers between devices, per_device(): second = lax.ppermute(band, 'row', swaps[1])  1.2 us
  transfers between devices with their start and end apart: 4, of which 2 were waited for; matrix products, arithmetic and copies ran while one was open for 0% of the time, Pallas kernels for 10%

profile of v24, /device:TPU:8, one launch (start us, length us, event | category | flops | bytes accessed | tf_op | source)
XLA Modules:
  0.0 36.6 jit_solution(17942799533646863837)
XLA Ops:
  0.7 1.0 %pack.1 = bf16[272,128]{1,0:T(8,128)(2,1)S(1)} custom-call(f32[2,128,128]{2,1,0:T(8,128)} %specimen.1, s32[1,1,2,2]{3,2,1,0:T(2,128)} %centers.1, s32[1,1]{1,0:T(1,128)S(6)} %copy.8.cnt, s32[1,1,2]{2,1,0:T(1,128)} %helpers.1), custom_call_target="tpu_custom_call" | custom-call | flops 100000 | bytes 524288 | tf_op jit(solution)/shard_map/pack/pallas_call | solution.py:391
  1.6 9.1 %all-gather = bf16[1088,128]{1,0:T(8,128)(2,1)S(1)} all-gather(bf16[272,128]{1,0:T(8,128)(2,1)S(1)} %pack.1), channel_id=2, replica_groups=mesh['row'=8,'col'=4] {'col'}, dimensions={0}, use_global_device_ids=true | all-gather | bytes 348160 | tf_op jit(solution)/shard_map/all_gather | solution.py:426
  10.8 1.9 %collective-permute-start.1 = (bf16[4,272,128]{2,1,0:T(8,128)(2,1)S(1)}, bf16[4,272,128]{2,1,0:T(8,128)(2,1)S(1)}, u32[]{:S(2)}, u32[]{:S(2)}) collective-permute-start(bf16[4,272,128]{2,1,0:T(8,128)(2,1)S(1)} %bitcast.2), channel_id=1, source_target_pairs={{4,8},{12,16},{20,24},{8,4},{16,12},{24,20},{5,9},{13,17},{21,25},... | collective-permute-start | bytes 835592 | tf_op jit(solution)/shard_map/ppermute | solution.py:433
  12.7 1.7 %collective-permute-start = (bf16[4,272,128]{2,1,0:T(8,128)(2,1)S(1)}, bf16[4,272,128]{2,1,0:T(8,128)(2,1)S(1)}, u32[]{:S(2)}, u32[]{:S(2)}) collective-permute-start(bf16[4,272,128]{2,1,0:T(8,128)(2,1)S(1)} %bitcast.3), channel_id=1, source_target_pairs={{0,4},{8,12},{16,20},{24,28},{4,0},{12,8},{20,16},{28,24},{1,5},{9... | collective-permute-start | bytes 835592 | tf_op jit(solution)/shard_map/ppermute | solution.py:434
  14.4 3.0 %prepare.1 = (bf16[16,256]{1,0:T(8,128)(2,1)S(1)}, f32[256,256]{1,0:T(8,128)S(1)}, bf16[8,256,256]{2,1,0:T(8,128)(2,1)S(1)}, f32[4,2,256,256]{3,2,1,0:T(8,128)S(1)}, f32[4,2,128,256]{3,2,1,0:T(8,128)S(1)}) custom-call(bf16[4,272,128]{2,1,0:T(8,128)(2,1)S(1)} %bitcast.4, f32[4,2,256,256]{3,2,1,0:T(8,128)} %probe.1, f32[1,1,1,256,256]{4,3,2,1,0:T(8,128)} %measured.1, ...), custom_call_target="tpu_custom_call" | custom-call | flops 1000000000 | bytes 4194304 | tf_op jit(solution)/shard_map/prepare/pallas_call | solution.py:391
  17.4 1.2 %collective-permute-done.1.second.second_band = bf16[4,272,128]{2,1,0:T(8,128)(2,1)S(1)} collective-permute-done((bf16[4,272,128]{2,1,0:T(8,128)(2,1)S(1)}, bf16[4,272,128]{2,1,0:T(8,128)(2,1)S(1)}, u32[]{:S(2)}, u32[]{:S(2)}) %collective-permute-start.1) | collective-permute-done | bytes 278560 | tf_op jit(solution)/shard_map/ppermute | solution.py:433
  18.6 0.0 collective-permute-done.first.first_band
  18.6 1.7 %frame.1 = (bf16[256,256]{1,0:T(8,128)(2,1)S(1)}, bf16[4,2,256,256]{3,2,1,0:T(8,128)(2,1)S(1)}) custom-call(bf16[4,272,128]{2,1,0:T(8,128)(2,1)S(1)} %collective-permute-done.first.first_band, bf16[4,272,128]{2,1,0:T(8,128)(2,1)S(1)} %collective-permute-done.1.second.second_band, bf16[16,256]{1,0:T(8,128)(2,1)S(1)} %get-tuple-element.14.info, ...), custom_call_target="tpu_custom_call" | custom-call | flops 2000000000 | bytes 4194304 | tf_op jit(solution)/shard_map/frame/pallas_call | solution.py:391
  20.4 0.2 collective-permute-start.2
  20.5 1.9 %collective-permute-start.3 = (bf16[256,256]{1,0:T(8,128)(2,1)S(1)}, bf16[256,256]{1,0:T(8,128)(2,1)S(1)}, u32[]{:S(2)}, u32[]{:S(2)}) collective-permute-start(bf16[256,256]{1,0:T(8,128)(2,1)S(1)} %get-tuple-element.20), channel_id=1, source_target_pairs={{4,8},{12,16},{20,24},{8,4},{16,12},{24,20},{5,9},{13,17},{21,25},... | collective-permute-start | bytes 393224 | tf_op jit(solution)/shard_map/ppermute | solution.py:475
  22.5 0.0 collective-permute-done.2.first
  22.5 0.7 %finish.1 = (f32[4,256,128]{2,1,0:T(8,128)S(1)}, s32[8,128]{1,0:T(8,128)S(1)}) custom-call(bf16[4,272,128]{2,1,0:T(8,128)(2,1)S(1)} %bitcast.5, bf16[4,272,128]{2,1,0:T(8,128)(2,1)S(1)} %collective-permute-done.first.first_band, bf16[4,272,128]{2,1,0:T(8,128)(2,1)S(1)} %collective-permute-done.1.second.second_band, ...), custom_call_target="tpu_custom_call" | custom-call | flops 500000000 | bytes 4194304 | tf_op jit(solution)/shard_map/finish/pallas_call | solution.py:391
  23.2 3.6 %collective-permute-done.3.second = bf16[256,256]{1,0:T(8,128)(2,1)S(1)} collective-permute-done((bf16[256,256]{1,0:T(8,128)(2,1)S(1)}, bf16[256,256]{1,0:T(8,128)(2,1)S(1)}, u32[]{:S(2)}, u32[]{:S(2)}) %collective-permute-start.3) | collective-permute-done | bytes 131104 | tf_op jit(solution)/shard_map/ppermute | solution.py:475
  26.8 0.1 fold.1
  26.9 8.9 %all_to_all.5 = bf16[4,256,128]{2,1,0:T(8,128)(2,1)S(1)} all-to-all(bf16[4,256,128]{2,1,0:T(8,128)(2,1)S(1)} %fold.1), channel_id=1, replica_groups=mesh['row'=8,'col'=4] {'col'}, dimensions={0} | all-to-all | bytes 524288 | tf_op jit(solution)/shard_map/all_to_all | solution.py:495
  35.9 0.7 %convert_reduce_fusion = f32[256,128]{1,0:T(8,128)} fusion(bf16[4,256,128]{2,1,0:T(8,128)(2,1)S(1)} %all_to_all.5), kind=kLoop, calls=%fused_computation | loop fusion | flops 229376 | bytes 393216 | tf_op jit(solution)/shard_map/reduce_sum | solution.py:496
Async XLA Ops:
  10.8 7.9 %collective-permute-start.1 = (bf16[4,272,128]{2,1,0:T(8,128)(2,1)S(1)}, bf16[4,272,128]{2,1,0:T(8,128)(2,1)S(1)}, u32[]{:S(2)}, u32[]{:S(2)}) collective-permute-start(bf16[4,272,128]{2,1,0:T(8,128)(2,1)S(1)} %bitcast.2), channel_id=1, source_target_pairs={{4,8},{12,16},{20,24},{8,4},{16,12},{24,20},{5,9},{13,17},{21,25},... | collective-permute-start | bytes 835592 | tf_op jit(solution)/shard_map/ppermute | solution.py:433
  12.7 5.9 %collective-permute-start = (bf16[4,272,128]{2,1,0:T(8,128)(2,1)S(1)}, bf16[4,272,128]{2,1,0:T(8,128)(2,1)S(1)}, u32[]{:S(2)}, u32[]{:S(2)}) collective-permute-start(bf16[4,272,128]{2,1,0:T(8,128)(2,1)S(1)} %bitcast.3), channel_id=1, source_target_pairs={{0,4},{8,12},{16,20},{24,28},{4,0},{12,8},{20,16},{28,24},{1,5},{9... | collective-permute-start | bytes 835592 | tf_op jit(solution)/shard_map/ppermute | solution.py:434
  20.4 2.1 %collective-permute-start.2 = (bf16[256,256]{1,0:T(8,128)(2,1)S(1)}, bf16[256,256]{1,0:T(8,128)(2,1)S(1)}, u32[]{:S(2)}, u32[]{:S(2)}) collective-permute-start(bf16[256,256]{1,0:T(8,128)(2,1)S(1)} %get-tuple-element.20), channel_id=1, source_target_pairs={{0,4},{8,12},{16,20},{24,28},{4,0},{12,8},{20,16},{28,24},{1,5},{9... | collective-permute-start | bytes 393224 | tf_op jit(solution)/shard_map/ppermute | solution.py:474
  20.5 6.3 %collective-permute-start.3 = (bf16[256,256]{1,0:T(8,128)(2,1)S(1)}, bf16[256,256]{1,0:T(8,128)(2,1)S(1)}, u32[]{:S(2)}, u32[]{:S(2)}) collective-permute-start(bf16[256,256]{1,0:T(8,128)(2,1)S(1)} %get-tuple-element.20), channel_id=1, source_target_pairs={{4,8},{12,16},{20,24},{8,4},{16,12},{24,20},{5,9},{13,17},{21,25},... | collective-permute-start | bytes 393224 | tf_op jit(solution)/shard_map/ppermute | solution.py:475

commit v25 on v15

--- a/solution.py
+++ b/solution.py
@@ -198,19 +198,30 @@
             half_out[k, parity] = products[parity]
 
 
+def near_kernel(first, info, near):
+    columns = first.shape[0]
+    _, tile, _ = near.shape
+    source, col = (info[r : r + 1, :tile].astype(F32).astype(jnp.int32) for r in range(2))
+    for p in range(2):
+        for r in range(0, tile, STRIP):
+            part = pl.ds(p * tile + r, STRIP)
+            near[p, pl.ds(r, STRIP)] = gather_columns(
+                lambda c: first[c, part].astype(F32), source, col, columns, (STRIP, tile)
+            )
+
+
 def frame_kernel(
-    first, second, info, amplitude, tables, probe, half_own,
+    near, second, info, amplitude, tables, probe, half_own,
     to_rows, mixed_back, patch, folded, half_far, mixed, far, corrected, product, chi,
 ):
-    columns = first.shape[0]
-    tile = (first.shape[1] - INFO) // 2
+    columns = second.shape[0]
+    tile = (second.shape[1] - INFO) // 2
     extent = probe.shape[-1]
     half = extent // 2
     modes = probe.shape[0]
     odd = lax.axis_index("row") % 2
-    source, col, row = (
-        info[r : r + 1, :tile].astype(F32).astype(jnp.int32) for r in range(3)
-    )
+    source, col = (info[r : r + 1, :tile].astype(F32).astype(jnp.int32) for r in range(2))
+    center_row = info[2:3].astype(F32).astype(jnp.int32)
     strips = [pl.ds(r, STRIP) for r in range(0, half, STRIP)]
     lower = [pl.ds(half + r, STRIP) for r in range(0, half, STRIP)]
 
@@ -221,16 +232,15 @@
         return jnp.concatenate([x, y], 1).astype(BF16)
 
     def gather(s):
-        rows = iota((STRIP, tile), 0) + s.start
-        from_first = (rows >= row).astype(jnp.int32) == odd
+        rows = iota((STRIP, extent), 0) + s.start
+        from_first = (rows >= center_row).astype(jnp.int32) == odd
         for p in range(2):
             part = pl.ds(p * tile + s.start, STRIP)
-            patch[p, s] = gather_columns(
-                lambda c: jnp.where(
-                    from_first, first[c, part].astype(F32), second[c, part].astype(F32)
-                ),
+            far_rows = gather_columns(
+                lambda c: second[c, part].astype(F32),
                 source, col, columns, (STRIP, tile),
             )
+            patch[p, s] = jnp.where(from_first, near[p, s], far_rows)
 
     def wave(k):
         for s in strips:
@@ -453,6 +463,14 @@
         10**9, 2**22,
         band, probe, measured, tables,
     )
+    near = call(
+        near_kernel, "near",
+        jax.ShapeDtypeStruct((2, tile, extent), F32),
+        [VMEM] * 2,
+        [],
+        10**6, 2**19,
+        first, prepared[0],
+    )
     full = (modes, 2, extent, extent)
     to_rows, mixed_back = call(
         frame_kernel, "frame",
@@ -469,7 +487,7 @@
             pltpu.VMEM((modes, extent, extent), F32),
         ],
         2 * 10**9, 2**22,
-        first, second, *prepared,
+        near, second, *prepared,
     )
     from_first = lax.ppermute(to_rows, "row", swaps[0])
     from_second = lax.ppermute(to_rows, "row", swaps[1])

time: 36.8 us -> 36.9 us (level)
  waiting for transfers between devices: 4.84 us -> 5.89 us
  starting transfers between devices: 5.74 us -> 5.01 us
    ppermute x1, starting transfers between devices: 1.74 us -> 0.01 us  [per_device(): first = lax.ppermute(band, 'row', swaps[0])]
    ppermute x1, waiting for transfers between devices: 1.2 us -> 2.32 us  [per_device(): second = lax.ppermute(band, 'row', swaps[1])]
    ppermute x1, starting transfers between devices: 1.91 us -> 2.46 us  [per_device(): second = lax.ppermute(band, 'row', swaps[1])]
    ppermute x1, starting transfers between devices: 0.18 us -> 0.57 us  [per_device(): from_first = lax.ppermute(to_rows, 'row', swaps[0])]
    pallas_call x5 -> x6, Pallas kernels: 6.52 us -> 6.55 us  [call(): pl.pallas_call(kernel, out_shape=out_shape, in_specs=in_specs, out_specs=...]
where the time goes in v25:
time: 36.9 us; the launch traced here: 36.7 us
  blocking collectives  17.8 us (48%)
  Pallas kernels  6.55 us (18%)
  waiting for transfers between devices  5.89 us (16%)
  starting transfers between devices  5.01 us (14%)
  between operations  0.72 us (2%)
  other arithmetic  0.69 us (2%)
    all_gather x1, blocking collectives, per_device(): band = lax.all_gather(packed, 'col')  9.13 us
    all_to_all x1, blocking collectives, per_device(): lax.all_to_all(summed, 'col', split_axis=0, concat_axis=0, tiled=True)  8.66 us
    pallas_call x6, Pallas kernels, call(): pl.pallas_call(kernel, out_shape=out_shape, in_specs=in_specs, out_specs=...  6.55 us
    ppermute x1, waiting for transfers between devices, per_device(): from_second = lax.ppermute(to_rows, 'row', swaps[1])  3.57 us
    ppermute x1, starting transfers between devices, per_device(): second = lax.ppermute(band, 'row', swaps[1])  2.46 us
    ppermute x1, waiting for transfers between devices, per_device(): second = lax.ppermute(band, 'row', swaps[1])  2.32 us
    ppermute x1, starting transfers between devices, per_device(): from_second = lax.ppermute(to_rows, 'row', swaps[1])  1.98 us
  transfers between devices with their start and end apart: 4, of which 2 were waited for; matrix products, arithmetic and copies ran while one was open for 0% of the time, Pallas kernels for 10%

profile of v25, /device:TPU:8, one launch (start us, length us, event | category | flops | bytes accessed | tf_op | source)
XLA Modules:
  0.0 36.7 jit_solution(6647808869218986546)
XLA Ops:
  0.7 1.0 %pack.1 = bf16[272,128]{1,0:T(8,128)(2,1)S(1)} custom-call(f32[2,128,128]{2,1,0:T(8,128)} %specimen.1, s32[1,1,2,2]{3,2,1,0:T(2,128)} %centers.1, s32[1,1]{1,0:T(1,128)S(6)} %copy.8.cnt, s32[1,1,2]{2,1,0:T(1,128)} %helpers.1), custom_call_target="tpu_custom_call" | custom-call | flops 100000 | bytes 524288 | tf_op jit(solution)/shard_map/pack/pallas_call | solution.py:401
  1.6 9.1 %all-gather = bf16[1088,128]{1,0:T(8,128)(2,1)S(1)} all-gather(bf16[272,128]{1,0:T(8,128)(2,1)S(1)} %pack.1), channel_id=2, replica_groups=mesh['row'=8,'col'=4] {'col'}, dimensions={0}, use_global_device_ids=true | all-gather | bytes 348160 | tf_op jit(solution)/shard_map/all_gather | solution.py:436
  10.8 0.0 collective-permute-start
  10.8 2.5 %collective-permute-start.1 = (bf16[4,272,128]{2,1,0:T(8,128)(2,1)S(1)}, bf16[4,272,128]{2,1,0:T(8,128)(2,1)S(1)}, u32[]{:S(2)}, u32[]{:S(2)}) collective-permute-start(bf16[4,272,128]{2,1,0:T(8,128)(2,1)S(1)} %bitcast.3), channel_id=1, source_target_pairs={{4,8},{12,16},{20,24},{8,4},{16,12},{24,20},{5,9},{13,17},{21,25},... | collective-permute-start | bytes 835592 | tf_op jit(solution)/shard_map/ppermute | solution.py:443
  13.2 3.0 %prepare.1 = (bf16[16,256]{1,0:T(8,128)(2,1)S(1)}, f32[256,256]{1,0:T(8,128)S(1)}, bf16[8,256,256]{2,1,0:T(8,128)(2,1)S(1)}, f32[4,2,256,256]{3,2,1,0:T(8,128)S(1)}, f32[4,2,128,256]{3,2,1,0:T(8,128)S(1)}) custom-call(bf16[4,272,128]{2,1,0:T(8,128)(2,1)S(1)} %bitcast.4, f32[4,2,256,256]{3,2,1,0:T(8,128)} %probe.1, f32[1,1,1,256,256]{4,3,2,1,0:T(8,128)} %measured.1, ...), custom_call_target="tpu_custom_call" | custom-call | flops 1000000000 | bytes 4194304 | tf_op jit(solution)/shard_map/prepare/pallas_call | solution.py:401
  16.2 0.0 collective-permute-done.first.first_band
  16.2 0.1 near.1
  16.3 2.3 %collective-permute-done.1.second.second_band = bf16[4,272,128]{2,1,0:T(8,128)(2,1)S(1)} collective-permute-done((bf16[4,272,128]{2,1,0:T(8,128)(2,1)S(1)}, bf16[4,272,128]{2,1,0:T(8,128)(2,1)S(1)}, u32[]{:S(2)}, u32[]{:S(2)}) %collective-permute-start.1) | collective-permute-done | bytes 278560 | tf_op jit(solution)/shard_map/ppermute | solution.py:443
  18.6 1.7 %frame.1 = (bf16[256,256]{1,0:T(8,128)(2,1)S(1)}, bf16[4,2,256,256]{3,2,1,0:T(8,128)(2,1)S(1)}) custom-call(f32[2,128,256]{2,1,0:T(8,128)S(1)} %near.1, bf16[4,272,128]{2,1,0:T(8,128)(2,1)S(1)} %collective-permute-done.1.second.second_band, bf16[16,256]{1,0:T(8,128)(2,1)S(1)} %get-tuple-element.14.info, f32[256,256]{1,0:T(8,128)S(1)} %get-tuple-element.15.amplitude, ...), custom_call_target="tpu_custom_call" | custom-call | flops 2000000000 | bytes 4194304 | tf_op jit(solution)/shard_map/frame/pallas_call | solution.py:401
  20.3 0.6 %collective-permute-start.2 = (bf16[256,256]{1,0:T(8,128)(2,1)S(1)}, bf16[256,256]{1,0:T(8,128)(2,1)S(1)}, u32[]{:S(2)}, u32[]{:S(2)}) collective-permute-start(bf16[256,256]{1,0:T(8,128)(2,1)S(1)} %get-tuple-element.20), channel_id=1, source_target_pairs={{0,4},{8,12},{16,20},{24,28},{4,0},{12,8},{20,16},{28,24},{1,5},{9... | collective-permute-start | bytes 393224 | tf_op jit(solution)/shard_map/ppermute | solution.py:492
  20.9 2.0 %collective-permute-start.3 = (bf16[256,256]{1,0:T(8,128)(2,1)S(1)}, bf16[256,256]{1,0:T(8,128)(2,1)S(1)}, u32[]{:S(2)}, u32[]{:S(2)}) collective-permute-start(bf16[256,256]{1,0:T(8,128)(2,1)S(1)} %get-tuple-element.20), channel_id=1, source_target_pairs={{4,8},{12,16},{20,24},{8,4},{16,12},{24,20},{5,9},{13,17},{21,25},... | collective-permute-start | bytes 393224 | tf_op jit(solution)/shard_map/ppermute | solution.py:493
  22.9 0.0 collective-permute-done.2.first
  22.9 0.7 %finish.1 = (f32[4,256,128]{2,1,0:T(8,128)S(1)}, s32[8,128]{1,0:T(8,128)S(1)}) custom-call(bf16[4,272,128]{2,1,0:T(8,128)(2,1)S(1)} %bitcast.5, bf16[4,272,128]{2,1,0:T(8,128)(2,1)S(1)} %collective-permute-done.first.first_band, bf16[4,272,128]{2,1,0:T(8,128)(2,1)S(1)} %collective-permute-done.1.second.second_band, ...), custom_call_target="tpu_custom_call" | custom-call | flops 500000000 | bytes 4194304 | tf_op jit(solution)/shard_map/finish/pallas_call | solution.py:401
  23.6 3.6 %collective-permute-done.3.second = bf16[256,256]{1,0:T(8,128)(2,1)S(1)} collective-permute-done((bf16[256,256]{1,0:T(8,128)(2,1)S(1)}, bf16[256,256]{1,0:T(8,128)(2,1)S(1)}, u32[]{:S(2)}, u32[]{:S(2)}) %collective-permute-start.3) | collective-permute-done | bytes 131104 | tf_op jit(solution)/shard_map/ppermute | solution.py:493
  27.2 0.1 fold.1
  27.3 8.7 %all_to_all.5 = bf16[4,256,128]{2,1,0:T(8,128)(2,1)S(1)} all-to-all(bf16[4,256,128]{2,1,0:T(8,128)(2,1)S(1)} %fold.1), channel_id=1, replica_groups=mesh['row'=8,'col'=4] {'col'}, dimensions={0} | all-to-all | bytes 524288 | tf_op jit(solution)/shard_map/all_to_all | solution.py:513
  36.0 0.7 %convert_reduce_fusion = f32[256,128]{1,0:T(8,128)} fusion(bf16[4,256,128]{2,1,0:T(8,128)(2,1)S(1)} %all_to_all.5), kind=kLoop, calls=%fused_computation | loop fusion | flops 229376 | bytes 393216 | tf_op jit(solution)/shard_map/reduce_sum | solution.py:514
Async XLA Ops:
  10.8 5.5 %collective-permute-start = (bf16[4,272,128]{2,1,0:T(8,128)(2,1)S(1)}, bf16[4,272,128]{2,1,0:T(8,128)(2,1)S(1)}, u32[]{:S(2)}, u32[]{:S(2)}) collective-permute-start(bf16[4,272,128]{2,1,0:T(8,128)(2,1)S(1)} %bitcast.2), channel_id=1, source_target_pairs={{0,4},{8,12},{16,20},{24,28},{4,0},{12,8},{20,16},{28,24},{1,5},{9... | collective-permute-start | bytes 835592 | tf_op jit(solution)/shard_map/ppermute | solution.py:444
  10.8 7.9 %collective-permute-start.1 = (bf16[4,272,128]{2,1,0:T(8,128)(2,1)S(1)}, bf16[4,272,128]{2,1,0:T(8,128)(2,1)S(1)}, u32[]{:S(2)}, u32[]{:S(2)}) collective-permute-start(bf16[4,272,128]{2,1,0:T(8,128)(2,1)S(1)} %bitcast.3), channel_id=1, source_target_pairs={{4,8},{12,16},{20,24},{8,4},{16,12},{24,20},{5,9},{13,17},{21,25},... | collective-permute-start | bytes 835592 | tf_op jit(solution)/shard_map/ppermute | solution.py:443
  20.3 2.6 %collective-permute-start.2 = (bf16[256,256]{1,0:T(8,128)(2,1)S(1)}, bf16[256,256]{1,0:T(8,128)(2,1)S(1)}, u32[]{:S(2)}, u32[]{:S(2)}) collective-permute-start(bf16[256,256]{1,0:T(8,128)(2,1)S(1)} %get-tuple-element.20), channel_id=1, source_target_pairs={{0,4},{8,12},{16,20},{24,28},{4,0},{12,8},{20,16},{28,24},{1,5},{9... | collective-permute-start | bytes 393224 | tf_op jit(solution)/shard_map/ppermute | solution.py:492
  20.9 6.3 %collective-permute-start.3 = (bf16[256,256]{1,0:T(8,128)(2,1)S(1)}, bf16[256,256]{1,0:T(8,128)(2,1)S(1)}, u32[]{:S(2)}, u32[]{:S(2)}) collective-permute-start(bf16[256,256]{1,0:T(8,128)(2,1)S(1)} %get-tuple-element.20), channel_id=1, source_target_pairs={{4,8},{12,16},{20,24},{8,4},{16,12},{24,20},{5,9},{13,17},{21,25},... | collective-permute-start | bytes 393224 | tf_op jit(solution)/shard_map/ppermute | solution.py:493

commit v26 on v25

--- a/solution.py
+++ b/solution.py
@@ -351,8 +351,8 @@
 
 
 def finish_kernel(
-    band, first_band, second_band, mixed_back, tables, probe, first,
-    partial, second_info, chi, centre,
+    band, first_band, second_band, mixed_back, tables, probe, first, pair,
+    out, chi, centre,
 ):
     columns = band.shape[0]
     extent = probe.shape[-1]
@@ -361,36 +361,27 @@
     own_frame, first_frame, second_frame = (
         frame_of(b) for b in (band, first_band, second_band)
     )
-    which = iota(second_info.shape, 0)
-    second_info[...] = jnp.where(
-        which == 0, second_frame[0], jnp.where(which == 1, second_frame[1], second_frame[2])
-    )
+    me = lax.axis_index("row")
+    outer = ((me > 0) & (me < lax.axis_size("row") - 1)).astype(jnp.int32)
     both_back = jnp.concatenate([tables[6], -tables[7]], 1)
     for k in range(probe.shape[0]):
         chi[k] = dot(both_back, mixed_back[k].reshape(2 * extent, extent))
     for r in range(0, tile, STRIP):
         s, t = pl.ds(r, STRIP), pl.ds(tile + r, STRIP)
         accumulate(centre, chi, probe, s, t, t)
-        before = (iota((STRIP, tile), 0) + r < first_frame[1]).astype(jnp.int32)
+        rows = iota((STRIP, tile), 0) + r
+        from_first = (rows < first_frame[1]).astype(jnp.int32) == odd
+        from_second = (rows < second_frame[1]).astype(jnp.int32) + 2 * (1 - outer) == 1 - odd
         for part in (s, t):
-            mine = place(centre[part].astype(F32), columns, own_frame[0], own_frame[2], None)
+            own = place(centre[part].astype(F32), columns, own_frame[0], own_frame[2], None)
+            close = place(
+                first[part].astype(F32), columns, first_frame[0], first_frame[2], from_first
+            )
             other = place(
-                first[part].astype(F32), columns, first_frame[0], first_frame[2], before == odd
+                pair[odd, part].astype(F32), columns, second_frame[0], second_frame[2], from_second
             )
             for c in range(columns):
-                partial[c, part] = mine[c] + other[c]
-
-
-def fold_kernel(partial, second, second_info, out):
-    columns, height, tile = out.shape
-    odd = lax.axis_index("row") % 2
-    source, row, col = (second_info[r : r + 1] for r in range(3))
-    for r in range(0, height, STRIP):
-        s = pl.ds(r, STRIP)
-        before = (iota((STRIP, tile), 0) + r % tile < row).astype(jnp.int32)
-        other = place(second[s].astype(F32), columns, source, col, before == 1 - odd)
-        for c in range(columns):
-            out[c, s] = (partial[c, s] + other[c]).astype(BF16)
+                out[c, part] = (own[c] + close[c] + other[c]).astype(BF16)
 
 
 def call(kernel, name, out_shape, in_specs, scratch, flops, moved, *args):
@@ -490,25 +481,20 @@
         near, second, *prepared,
     )
     from_first = lax.ppermute(to_rows, "row", swaps[0])
-    from_second = lax.ppermute(to_rows, "row", swaps[1])
-    partial, second_info = call(
+    ends = [r * columns + c for r in (0, rows - 1) for c in range(columns)]
+    pairs = [ends[i : i + 2] for i in range(0, 2 * columns, 2)]
+    pairs += [
+        [r * columns + c, (r + 1) * columns + c]
+        for r in range(1, rows - 1, 2) for c in range(columns)
+    ]
+    pair = lax.all_gather(to_rows, ("row", "col"), axis_index_groups=pairs)
+    summed = call(
         finish_kernel, "finish",
-        (
-            jax.ShapeDtypeStruct((columns, height, tile), F32),
-            jax.ShapeDtypeStruct((8, tile), jnp.int32),
-        ),
-        [VMEM] * 7,
+        jax.ShapeDtypeStruct((columns, height, tile), BF16),
+        [VMEM] * 8,
         [pltpu.VMEM((modes, extent, extent), F32), pltpu.VMEM((height, extent), BF16)],
         5 * 10**8, 2**22,
-        band, first, second, mixed_back, prepared[2], prepared[3], from_first,
-    )
-    summed = call(
-        fold_kernel, "fold",
-        jax.ShapeDtypeStruct((columns, height, tile), BF16),
-        [VMEM] * 3,
-        [],
-        10**7, 2**20,
-        partial, from_second, second_info,
+        band, first, second, mixed_back, prepared[2], prepared[3], from_first, pair,
     )
     shares = lax.all_to_all(summed, "col", split_axis=0, concat_axis=0, tiled=True)
     return jnp.sum(shares.astype(F32), axis=0).reshape(2, tile, tile)

time: 36.9 us -> 38.1 us (1.033)
  the two profiles are of different devices: /device:TPU:8 before, /device:TPU:0 now
where the time goes in v26:
time: 38.1 us; the launch traced here: 37.8 us
  blocking collectives  24.5 us (64%)
  Pallas kernels  6.6 us (17%)
  starting transfers between devices  5.34 us (14%)
  between operations  0.71 us (2%)
  other arithmetic  0.69 us (2%)
    all_gather x1, blocking collectives, per_device(): band = lax.all_gather(packed, 'col')  10.6 us
    all_to_all x1, blocking collectives, per_device(): lax.all_to_all(summed, 'col', split_axis=0, concat_axis=0, tiled=True)  8.29 us
    pallas_call x5, Pallas kernels, call(): pl.pallas_call(kernel, out_shape=out_shape, in_specs=in_specs, out_specs=...  6.6 us
    all_gather x1, blocking collectives, per_device(): pair = lax.all_gather(to_rows, ('row', 'col'), axis_index_groups=pairs)  5.63 us
    ppermute x1, starting transfers between devices, per_device(): from_first = lax.ppermute(to_rows, 'row', swaps[0])  4.67 us
  transfers between devices with their start and end apart: 3, of which 0 were waited for; matrix products, arithmetic and copies ran while one was open for 0% of the time, Pallas kernels for 8%

profile of v26, /device:TPU:0, one launch (start us, length us, event | category | flops | bytes accessed | tf_op | source)
XLA Modules:
  0.0 37.8 jit_solution(7273190126080176103)
XLA Ops:
  0.7 1.0 %pack.1 = bf16[272,128]{1,0:T(8,128)(2,1)S(1)} custom-call(f32[2,128,128]{2,1,0:T(8,128)} %specimen.1, s32[1,1,2,2]{3,2,1,0:T(2,128)} %centers.1, s32[1,1]{1,0:T(1,128)S(6)} %copy.8.cnt, s32[1,1,2]{2,1,0:T(1,128)} %helpers.1), custom_call_target="tpu_custom_call" | custom-call | flops 100000 | bytes 524288 | tf_op jit(solution)/shard_map/pack/pallas_call | solution.py:392
  1.6 10.6 %all-gather = bf16[1088,128]{1,0:T(8,128)(2,1)S(1)} all-gather(bf16[272,128]{1,0:T(8,128)(2,1)S(1)} %pack.1), channel_id=2, replica_groups=mesh['row'=8,'col'=4] {'col'}, dimensions={0}, use_global_device_ids=true | all-gather | bytes 348160 | tf_op jit(solution)/shard_map/all_gather | solution.py:427
  12.2 0.0 collective-permute-start
  12.2 0.7 %collective-permute-start.1 = (bf16[4,272,128]{2,1,0:T(8,128)(2,1)S(1)}, bf16[4,272,128]{2,1,0:T(8,128)(2,1)S(1)}, u32[]{:S(2)}, u32[]{:S(2)}) collective-permute-start(bf16[4,272,128]{2,1,0:T(8,128)(2,1)S(1)} %bitcast.4), channel_id=1, source_target_pairs={{4,8},{12,16},{20,24},{8,4},{16,12},{24,20},{5,9},{13,17},{21,25},... | collective-permute-start | bytes 835592 | tf_op jit(solution)/shard_map/ppermute | solution.py:434
  12.9 3.0 %prepare.1 = (bf16[16,256]{1,0:T(8,128)(2,1)S(1)}, f32[256,256]{1,0:T(8,128)S(1)}, bf16[8,256,256]{2,1,0:T(8,128)(2,1)S(1)}, f32[4,2,256,256]{3,2,1,0:T(8,128)S(1)}, f32[4,2,128,256]{3,2,1,0:T(8,128)S(1)}) custom-call(bf16[4,272,128]{2,1,0:T(8,128)(2,1)S(1)} %bitcast.5, f32[4,2,256,256]{3,2,1,0:T(8,128)} %probe.1, f32[1,1,1,256,256]{4,3,2,1,0:T(8,128)} %measured.1, ...), custom_call_target="tpu_custom_call" | custom-call | flops 1000000000 | bytes 4194304 | tf_op jit(solution)/shard_map/prepare/pallas_call | solution.py:392
  15.9 0.0 collective-permute-done.first.first_band
  15.9 0.1 near.1
  15.9 0.0 collective-permute-done.1.second.second_band
  16.0 1.7 %frame.1 = (bf16[256,256]{1,0:T(8,128)(2,1)S(1)}, bf16[4,2,256,256]{3,2,1,0:T(8,128)(2,1)S(1)}) custom-call(f32[2,128,256]{2,1,0:T(8,128)S(1)} %near.1, bf16[4,272,128]{2,1,0:T(8,128)(2,1)S(1)} %collective-permute-done.1.second.second_band, bf16[16,256]{1,0:T(8,128)(2,1)S(1)} %get-tuple-element.12.info, f32[256,256]{1,0:T(8,128)S(1)} %get-tuple-element.13.amplitude, ...), custom_call_target="tpu_custom_call" | custom-call | flops 2000000000 | bytes 4194304 | tf_op jit(solution)/shard_map/frame/pallas_call | solution.py:392
  17.7 4.7 %collective-permute-start.2 = (bf16[256,256]{1,0:T(8,128)(2,1)S(1)}, bf16[256,256]{1,0:T(8,128)(2,1)S(1)}, u32[]{:S(2)}, u32[]{:S(2)}) collective-permute-start(bf16[256,256]{1,0:T(8,128)(2,1)S(1)} %get-tuple-element.18), channel_id=1, source_target_pairs={{0,4},{8,12},{16,20},{24,28},{4,0},{12,8},{20,16},{28,24},{1,5},{9... | collective-permute-start | bytes 393224 | tf_op jit(solution)/shard_map/ppermute | solution.py:483
  22.4 5.6 %all-gather.1 = bf16[512,256]{1,0:T(8,128)(2,1)S(1)} all-gather(bf16[256,256]{1,0:T(8,128)(2,1)S(1)} %get-tuple-element.18), channel_id=3, replica_groups={{0,1},{2,3},{28,29},{30,31},{4,8},{5,9},{6,10},{7,11},{12,16},{13,17},{..., dimensions={0}, use_global_device_ids=true | all-gather | bytes 393216 | tf_op jit(solution)/shard_map/all_gather | solution.py:490
  28.0 0.0 collective-permute-done.2.first
  28.0 0.9 %finish.1 = bf16[4,256,128]{2,1,0:T(8,128)(2,1)S(1)} custom-call(bf16[4,272,128]{2,1,0:T(8,128)(2,1)S(1)} %bitcast.6, bf16[4,272,128]{2,1,0:T(8,128)(2,1)S(1)} %collective-permute-done.first.first_band, bf16[4,272,128]{2,1,0:T(8,128)(2,1)S(1)} %collective-permute-done.1.second.second_band, bf16[4,2,256,256]{3,2,1,0:T(8,128)(2,1)S(1)} %get-tuple-element.17.mixed_back, ...), custom_call_target="tpu_custom_call" | custom-call | flops 500000000 | bytes 4194304 | tf_op jit(solution)/shard_map/finish/pallas_call | solution.py:392
  28.9 8.3 %all_to_all.5 = bf16[4,256,128]{2,1,0:T(8,128)(2,1)S(1)} all-to-all(bf16[4,256,128]{2,1,0:T(8,128)(2,1)S(1)} %finish.1), channel_id=1, replica_groups=mesh['row'=8,'col'=4] {'col'}, dimensions={0} | all-to-all | bytes 524288 | tf_op jit(solution)/shard_map/all_to_all | solution.py:499
  37.2 0.7 %convert_reduce_fusion = f32[256,128]{1,0:T(8,128)} fusion(bf16[4,256,128]{2,1,0:T(8,128)(2,1)S(1)} %all_to_all.5), kind=kLoop, calls=%fused_computation | loop fusion | flops 229376 | bytes 393216 | tf_op jit(solution)/shard_map/reduce_sum | solution.py:500
Async XLA Ops:
  12.2 3.7 %collective-permute-start = (bf16[4,272,128]{2,1,0:T(8,128)(2,1)S(1)}, bf16[4,272,128]{2,1,0:T(8,128)(2,1)S(1)}, u32[]{:S(2)}, u32[]{:S(2)}) collective-permute-start(bf16[4,272,128]{2,1,0:T(8,128)(2,1)S(1)} %bitcast.3), channel_id=1, source_target_pairs={{0,4},{8,12},{16,20},{24,28},{4,0},{12,8},{20,16},{28,24},{1,5},{9... | collective-permute-start | bytes 835592 | tf_op jit(solution)/shard_map/ppermute | solution.py:435
  12.2 3.7 %collective-permute-start.1 = (bf16[4,272,128]{2,1,0:T(8,128)(2,1)S(1)}, bf16[4,272,128]{2,1,0:T(8,128)(2,1)S(1)}, u32[]{:S(2)}, u32[]{:S(2)}) collective-permute-start(bf16[4,272,128]{2,1,0:T(8,128)(2,1)S(1)} %bitcast.4), channel_id=1, source_target_pairs={{4,8},{12,16},{20,24},{8,4},{16,12},{24,20},{5,9},{13,17},{21,25},... | collective-permute-start | bytes 835592 | tf_op jit(solution)/shard_map/ppermute | solution.py:434
  17.7 10.3 %collective-permute-start.2 = (bf16[256,256]{1,0:T(8,128)(2,1)S(1)}, bf16[256,256]{1,0:T(8,128)(2,1)S(1)}, u32[]{:S(2)}, u32[]{:S(2)}) collective-permute-start(bf16[256,256]{1,0:T(8,128)(2,1)S(1)} %get-tuple-element.18), channel_id=1, source_target_pairs={{0,4},{8,12},{16,20},{24,28},{4,0},{12,8},{20,16},{28,24},{1,5},{9... | collective-permute-start | bytes 393224 | tf_op jit(solution)/shard_map/ppermute | solution.py:483

commit v27 on v25

--- a/solution.py
+++ b/solution.py
@@ -12,7 +12,7 @@
 F32 = jnp.float32
 BF16 = jnp.bfloat16
 INFO = 16
-STRIP = 16
+STRIP = 32
 VMEM = pl.BlockSpec(memory_space=pltpu.VMEM)
 SMEM = pl.BlockSpec(memory_space=pltpu.SMEM)
 HBM = pl.BlockSpec(memory_space=pltpu.HBM)

time: 36.9 us -> 36.9 us (level)
  no operation moved by 1% of the time
where the time goes in v27:
time: 36.9 us; the launch traced here: 36.7 us
  blocking collectives  17.8 us (48%)
  Pallas kernels  6.55 us (18%)
  waiting for transfers between devices  5.89 us (16%)
  starting transfers between devices  5.01 us (14%)
  between operations  0.72 us (2%)
  other arithmetic  0.69 us (2%)
    all_gather x1, blocking collectives, per_device(): band = lax.all_gather(packed, 'col')  9.13 us
    all_to_all x1, blocking collectives, per_device(): lax.all_to_all(summed, 'col', split_axis=0, concat_axis=0, tiled=True)  8.66 us
    pallas_call x6, Pallas kernels, call(): pl.pallas_call(kernel, out_shape=out_shape, in_specs=in_specs, out_specs=...  6.55 us
    ppermute x1, waiting for transfers between devices, per_device(): from_second = lax.ppermute(to_rows, 'row', swaps[1])  3.57 us
    ppermute x1, starting transfers between devices, per_device(): second = lax.ppermute(band, 'row', swaps[1])  2.46 us
    ppermute x1, waiting for transfers between devices, per_device(): second = lax.ppermute(band, 'row', swaps[1])  2.32 us
    ppermute x1, starting transfers between devices, per_device(): from_second = lax.ppermute(to_rows, 'row', swaps[1])  1.98 us
  transfers between devices with their start and end apart: 4, of which 2 were waited for; matrix products, arithmetic and copies ran while one was open for 0% of the time, Pallas kernels for 10%

profile of v27, /device:TPU:8, one launch (start us, length us, event | category | flops | bytes accessed | tf_op | source)
XLA Modules:
  0.0 36.7 jit_solution(8679977352063868558)
XLA Ops:
  0.7 1.0 %pack.1 = bf16[272,128]{1,0:T(8,128)(2,1)S(1)} custom-call(f32[2,128,128]{2,1,0:T(8,128)} %specimen.1, s32[1,1,2,2]{3,2,1,0:T(2,128)} %centers.1, s32[1,1]{1,0:T(1,128)S(6)} %copy.8.cnt, s32[1,1,2]{2,1,0:T(1,128)} %helpers.1), custom_call_target="tpu_custom_call" | custom-call | flops 100000 | bytes 524288 | tf_op jit(solution)/shard_map/pack/pallas_call | solution.py:401
  1.6 9.1 %all-gather = bf16[1088,128]{1,0:T(8,128)(2,1)S(1)} all-gather(bf16[272,128]{1,0:T(8,128)(2,1)S(1)} %pack.1), channel_id=2, replica_groups=mesh['row'=8,'col'=4] {'col'}, dimensions={0}, use_global_device_ids=true | all-gather | bytes 348160 | tf_op jit(solution)/shard_map/all_gather | solution.py:436
  10.8 0.0 collective-permute-start
  10.8 2.5 %collective-permute-start.1 = (bf16[4,272,128]{2,1,0:T(8,128)(2,1)S(1)}, bf16[4,272,128]{2,1,0:T(8,128)(2,1)S(1)}, u32[]{:S(2)}, u32[]{:S(2)}) collective-permute-start(bf16[4,272,128]{2,1,0:T(8,128)(2,1)S(1)} %bitcast.3), channel_id=1, source_target_pairs={{4,8},{12,16},{20,24},{8,4},{16,12},{24,20},{5,9},{13,17},{21,25},... | collective-permute-start | bytes 835592 | tf_op jit(solution)/shard_map/ppermute | solution.py:443
  13.2 3.0 %prepare.1 = (bf16[16,256]{1,0:T(8,128)(2,1)S(1)}, f32[256,256]{1,0:T(8,128)S(1)}, bf16[8,256,256]{2,1,0:T(8,128)(2,1)S(1)}, f32[4,2,256,256]{3,2,1,0:T(8,128)S(1)}, f32[4,2,128,256]{3,2,1,0:T(8,128)S(1)}) custom-call(bf16[4,272,128]{2,1,0:T(8,128)(2,1)S(1)} %bitcast.4, f32[4,2,256,256]{3,2,1,0:T(8,128)} %probe.1, f32[1,1,1,256,256]{4,3,2,1,0:T(8,128)} %measured.1, ...), custom_call_target="tpu_custom_call" | custom-call | flops 1000000000 | bytes 4194304 | tf_op jit(solution)/shard_map/prepare/pallas_call | solution.py:401
  16.2 0.0 collective-permute-done.first.first_band
  16.2 0.1 near.1
  16.3 2.3 %collective-permute-done.1.second.second_band = bf16[4,272,128]{2,1,0:T(8,128)(2,1)S(1)} collective-permute-done((bf16[4,272,128]{2,1,0:T(8,128)(2,1)S(1)}, bf16[4,272,128]{2,1,0:T(8,128)(2,1)S(1)}, u32[]{:S(2)}, u32[]{:S(2)}) %collective-permute-start.1) | collective-permute-done | bytes 278560 | tf_op jit(solution)/shard_map/ppermute | solution.py:443
  18.6 1.7 %frame.1 = (bf16[256,256]{1,0:T(8,128)(2,1)S(1)}, bf16[4,2,256,256]{3,2,1,0:T(8,128)(2,1)S(1)}) custom-call(f32[2,128,256]{2,1,0:T(8,128)S(1)} %near.1, bf16[4,272,128]{2,1,0:T(8,128)(2,1)S(1)} %collective-permute-done.1.second.second_band, bf16[16,256]{1,0:T(8,128)(2,1)S(1)} %get-tuple-element.14.info, f32[256,256]{1,0:T(8,128)S(1)} %get-tuple-element.15.amplitude, ...), custom_call_target="tpu_custom_call" | custom-call | flops 2000000000 | bytes 4194304 | tf_op jit(solution)/shard_map/frame/pallas_call | solution.py:401
  20.3 0.6 %collective-permute-start.2 = (bf16[256,256]{1,0:T(8,128)(2,1)S(1)}, bf16[256,256]{1,0:T(8,128)(2,1)S(1)}, u32[]{:S(2)}, u32[]{:S(2)}) collective-permute-start(bf16[256,256]{1,0:T(8,128)(2,1)S(1)} %get-tuple-element.20), channel_id=1, source_target_pairs={{0,4},{8,12},{16,20},{24,28},{4,0},{12,8},{20,16},{28,24},{1,5},{9... | collective-permute-start | bytes 393224 | tf_op jit(solution)/shard_map/ppermute | solution.py:492
  20.9 2.0 %collective-permute-start.3 = (bf16[256,256]{1,0:T(8,128)(2,1)S(1)}, bf16[256,256]{1,0:T(8,128)(2,1)S(1)}, u32[]{:S(2)}, u32[]{:S(2)}) collective-permute-start(bf16[256,256]{1,0:T(8,128)(2,1)S(1)} %get-tuple-element.20), channel_id=1, source_target_pairs={{4,8},{12,16},{20,24},{8,4},{16,12},{24,20},{5,9},{13,17},{21,25},... | collective-permute-start | bytes 393224 | tf_op jit(solution)/shard_map/ppermute | solution.py:493
  22.9 0.0 collective-permute-done.2.first
  22.9 0.7 %finish.1 = (f32[4,256,128]{2,1,0:T(8,128)S(1)}, s32[8,128]{1,0:T(8,128)S(1)}) custom-call(bf16[4,272,128]{2,1,0:T(8,128)(2,1)S(1)} %bitcast.5, bf16[4,272,128]{2,1,0:T(8,128)(2,1)S(1)} %collective-permute-done.first.first_band, bf16[4,272,128]{2,1,0:T(8,128)(2,1)S(1)} %collective-permute-done.1.second.second_band, ...), custom_call_target="tpu_custom_call" | custom-call | flops 500000000 | bytes 4194304 | tf_op jit(solution)/shard_map/finish/pallas_call | solution.py:401
  23.6 3.6 %collective-permute-done.3.second = bf16[256,256]{1,0:T(8,128)(2,1)S(1)} collective-permute-done((bf16[256,256]{1,0:T(8,128)(2,1)S(1)}, bf16[256,256]{1,0:T(8,128)(2,1)S(1)}, u32[]{:S(2)}, u32[]{:S(2)}) %collective-permute-start.3) | collective-permute-done | bytes 131104 | tf_op jit(solution)/shard_map/ppermute | solution.py:493
  27.2 0.1 fold.1
  27.3 8.7 %all_to_all.5 = bf16[4,256,128]{2,1,0:T(8,128)(2,1)S(1)} all-to-all(bf16[4,256,128]{2,1,0:T(8,128)(2,1)S(1)} %fold.1), channel_id=1, replica_groups=mesh['row'=8,'col'=4] {'col'}, dimensions={0} | all-to-all | bytes 524288 | tf_op jit(solution)/shard_map/all_to_all | solution.py:513
  36.0 0.7 %convert_reduce_fusion = f32[256,128]{1,0:T(8,128)} fusion(bf16[4,256,128]{2,1,0:T(8,128)(2,1)S(1)} %all_to_all.5), kind=kLoop, calls=%fused_computation | loop fusion | flops 229376 | bytes 393216 | tf_op jit(solution)/shard_map/reduce_sum | solution.py:514
Async XLA Ops:
  10.8 5.5 %collective-permute-start = (bf16[4,272,128]{2,1,0:T(8,128)(2,1)S(1)}, bf16[4,272,128]{2,1,0:T(8,128)(2,1)S(1)}, u32[]{:S(2)}, u32[]{:S(2)}) collective-permute-start(bf16[4,272,128]{2,1,0:T(8,128)(2,1)S(1)} %bitcast.2), channel_id=1, source_target_pairs={{0,4},{8,12},{16,20},{24,28},{4,0},{12,8},{20,16},{28,24},{1,5},{9... | collective-permute-start | bytes 835592 | tf_op jit(solution)/shard_map/ppermute | solution.py:444
  10.8 7.9 %collective-permute-start.1 = (bf16[4,272,128]{2,1,0:T(8,128)(2,1)S(1)}, bf16[4,272,128]{2,1,0:T(8,128)(2,1)S(1)}, u32[]{:S(2)}, u32[]{:S(2)}) collective-permute-start(bf16[4,272,128]{2,1,0:T(8,128)(2,1)S(1)} %bitcast.3), channel_id=1, source_target_pairs={{4,8},{12,16},{20,24},{8,4},{16,12},{24,20},{5,9},{13,17},{21,25},... | collective-permute-start | bytes 835592 | tf_op jit(solution)/shard_map/ppermute | solution.py:443
  20.3 2.6 %collective-permute-start.2 = (bf16[256,256]{1,0:T(8,128)(2,1)S(1)}, bf16[256,256]{1,0:T(8,128)(2,1)S(1)}, u32[]{:S(2)}, u32[]{:S(2)}) collective-permute-start(bf16[256,256]{1,0:T(8,128)(2,1)S(1)} %get-tuple-element.20), channel_id=1, source_target_pairs={{0,4},{8,12},{16,20},{24,28},{4,0},{12,8},{20,16},{28,24},{1,5},{9... | collective-permute-start | bytes 393224 | tf_op jit(solution)/shard_map/ppermute | solution.py:492
  20.9 6.3 %collective-permute-start.3 = (bf16[256,256]{1,0:T(8,128)(2,1)S(1)}, bf16[256,256]{1,0:T(8,128)(2,1)S(1)}, u32[]{:S(2)}, u32[]{:S(2)}) collective-permute-start(bf16[256,256]{1,0:T(8,128)(2,1)S(1)} %get-tuple-element.20), channel_id=1, source_target_pairs={{4,8},{12,16},{20,24},{8,4},{16,12},{24,20},{5,9},{13,17},{21,25},... | collective-permute-start | bytes 393224 | tf_op jit(solution)/shard_map/ppermute | solution.py:493
